TPU v7x, 32 devices: a whole 2x2x4 slice. The times are simulated.
32 devices in a mesh: ctx: 16 (over z, x, core), tp: 2 (over y).
Axes of the slice: x: 2, y: 2, z: 4, core: 2. Of those that a mesh axis runs over, the one named last changes fastest.
Arguments:
- features: bfloat16 [3, 2048, 8192], P(None, 'ctx', 'tp'), may hold values from -6 to 6
- conv_weight: float32 [3, 3, 8192], replicated, may hold values from -3 to 3
- decay_rates: float32 [16, 8192], P(None, ('tp', 'ctx')), may hold values from 1e-05 to 0.03
- residues: float32 [16, 8192], P(None, ('tp', 'ctx')), may hold values from -1.5 to 1.5
- skip_gain: float32 [8192], P(('tp', 'ctx')), may hold values from -1 to 1
- out_weight: bfloat16 [8192, 8192], P('tp', 'ctx'), may hold values from -0.0625 to 0.0625
Outputs:
- mixed: bfloat16 [2048, 8192], P('ctx', 'tp')
All inputs are finite; a program needn't handle non-finite values.
Results may differ from a plain program's by a relative error of at most 0.014.
Values may be sent and summed in bfloat16 or wider, within the bound.
No kernel may reach another device: no remote copies, remote signals or barrier semaphores. Data moves between devices by JAX's collectives and lax.ppermute only.
A program may use at most 192 MiB of HBM per device.

v0:
```python
import functools

import jax
import jax.numpy as jnp
from jax import lax
from jax.experimental import pallas as pl
from jax.experimental.pallas import tpu as pltpu
from jax.sharding import PartitionSpec as P

LANES = 128
SUBLANES = 8
GROUP = LANES * SUBLANES
HALO = 2
TAPS = 3
SIDE = 2
SLAB = SIDE * SIDE
F32 = jnp.float32
BF16 = jnp.bfloat16


def spread(scratch, halo, block, pitch):
    tokens = block.shape[0]
    for tile in range(SUBLANES):
        lanes = pl.ds(tile * LANES, LANES)
        scratch[pl.ds(tile * pitch + SUBLANES - HALO, HALO), :] = halo[:, lanes].astype(F32)
        scratch[pl.ds(tile * pitch + SUBLANES, tokens), :] = block[:, lanes].astype(F32)


def token(scratch, index, pitch):
    return scratch[pl.ds(index, SUBLANES, stride=pitch), :]


def tree_sum(terms):
    while len(terms) > 1:
        terms = [a + b for a, b in zip(terms[::2], terms[1::2])] + terms[len(terms) & ~1 :]
    return terms[0]


def filter_kernel(here, features, halo, taps, u_ref, query_ref, tap_rows, *rows):
    tokens = features.shape[1]
    pitch = tokens + SUBLANES
    for tile in range(SUBLANES):
        for which in range(3):
            for j in range(TAPS):
                row = which * TAPS + j
                tap_rows[row, tile : tile + 1] = taps[which, j : j + 1, tile * LANES : (tile + 1) * LANES]
    for which in range(3):
        spread(rows[which], halo.at[which], features.at[which], pitch)
    weights = [[tap_rows[which * TAPS + j] for j in range(TAPS)] for which in range(3)]

    def step(index, carry):
        carry = list(carry)
        for inner in range(SUBLANES):
            now = index * SUBLANES + inner
            filtered = []
            for which in range(3):
                last, before = carry[which]
                fresh = token(rows[which], now + SUBLANES, pitch)
                filtered.append(
                    weights[which][0] * fresh + weights[which][1] * last + weights[which][2] * before
                )
                carry[which] = (fresh, last)
            query_ref[0, now] = filtered[0]
            u_ref[0, now] = (filtered[1] * filtered[2]).astype(BF16).astype(F32)
        return tuple(carry)

    start = tuple(
        (token(rows[which], SUBLANES - 1, pitch), token(rows[which], SUBLANES - 2, pitch))
        for which in range(3)
    )
    lax.fori_loop(0, tokens // SUBLANES, step, start)


def registers(refs, rank, wide, first, count):
    pitch = wide.shape[0] // SUBLANES
    each = SUBLANES // SLAB
    for d in range(SLAB):
        for j in range(each):
            start = pl.multiple_of(((d ^ rank) * each + j) * pitch, SUBLANES)
            rows = refs[d][0, first : first + count, j * LANES : (j + 1) * LANES]
            wide[pl.ds(start, count), :] = rows.astype(F32)
    return [wide[pl.ds(m, SUBLANES, stride=pitch), :] for m in range(count)]


def state_kernel(modes, here, u_ref, *refs):
    rates, outs, wide = refs[:SLAB], refs[SLAB : 2 * SLAB], refs[-1]
    rank = here[1]
    tokens = u_ref.shape[1]
    decay = [jnp.exp(-rate) for rate in registers(rates, rank, wide, 0, modes)]

    def step(index, states):
        for inner in range(SUBLANES):
            u = u_ref[0, index * SUBLANES + inner]
            states = tuple(states[m] * decay[m] + u for m in range(modes))
        return states

    zero = tuple(jnp.zeros((SUBLANES, LANES), F32) for _ in range(modes))
    states = lax.fori_loop(0, tokens // SUBLANES, step, zero)
    each = SUBLANES // SLAB
    pitch = wide.shape[0] // SUBLANES
    for m in range(modes):
        wide[pl.ds(m, SUBLANES, stride=pitch), :] = states[m]
    for d in range(SLAB):
        for j in range(each):
            start = pl.multiple_of(((d ^ rank) * each + j) * pitch, SUBLANES)
            outs[d][0, :, j * LANES : (j + 1) * LANES] = wide[pl.ds(start, modes), :].astype(BF16)


def slab_kernel(tokens, here, rates, *refs):
    states, out = refs[:SLAB], refs[SLAB]
    slabs = rates.shape[0]
    for g in range(slabs):
        rate = rates[lax.rem(g - here[0] + slabs, slabs), : states[0].shape[1]]
        total = None
        for d in range(SLAB):
            later = (SLAB - 1 - (here[1] ^ d)).astype(F32) * float(tokens)
            term = jnp.exp(-later * rate) * states[d][g].astype(F32)
            total = term if total is None else total + term
        out[g] = total.astype(BF16)


def incoming_kernel(tokens, here, rates, *refs):
    slabs = rates.shape[0]
    states, earlier, outs = refs[:SLAB], refs[SLAB : SLAB + slabs - 1], refs[SLAB + slabs - 1 :]
    for g in range(slabs):
        rate = rates[lax.rem(g - here[0] + slabs, slabs), : states[0].shape[1]]
        entering = earlier[0][g].astype(F32)
        for k in range(1, slabs - 1):
            entering += jnp.exp(-float(k * SLAB * tokens) * rate) * earlier[k][g].astype(F32)
        for d in range(SLAB):
            block = here[1] ^ d
            total = jnp.exp(-(block.astype(F32) * float(tokens)) * rate) * entering
            for e in range(SLAB):
                if e != d:
                    between = block - 1 - (here[1] ^ e)
                    factor = jnp.exp(-(jnp.maximum(between, 0).astype(F32) * float(tokens)) * rate)
                    factor = jnp.where(between >= 0, factor, jnp.zeros_like(factor))
                    total += factor * states[e][g].astype(F32)
            outs[d][g] = total.astype(BF16)


def local_kernel(modes, here, u_ref, *refs):
    rates, y_ref, wide = refs[:SLAB], refs[-2], refs[-1]
    tokens = u_ref.shape[1]
    rate = registers(rates, here[1], wide, 0, modes)
    rest = registers(rates, here[1], wide, modes, modes + 1)
    decay = [jnp.exp(-r) for r in rate]
    weight = [rest[m] * jnp.sqrt(2.0 * rate[m]) for m in range(modes)]
    skip = rest[modes]

    def step(index, states):
        for inner in range(SUBLANES):
            now = index * SUBLANES + inner
            u = u_ref[0, now]
            states = tuple(states[m] * decay[m] + u for m in range(modes))
            y_ref[0, now] = tree_sum([weight[m] * states[m] for m in range(modes)] + [skip * u])
        return states

    zero = tuple(jnp.zeros((SUBLANES, LANES), F32) for _ in range(modes))
    lax.fori_loop(0, tokens // SUBLANES, step, zero)


def gated_kernel(modes, here, query_ref, y_ref, *refs):
    rates, incoming = refs[:SLAB], refs[SLAB : 2 * SLAB]
    out_ref, wide, out_rows = refs[2 * SLAB :]
    tokens = query_ref.shape[1]
    pitch = tokens + SUBLANES
    rate = registers(rates, here[1], wide, 0, modes)
    rest = registers(rates, here[1], wide, modes, modes)
    state = registers(incoming, here[1], wide, 0, modes)
    decay = [jnp.exp(-r) for r in rate]
    weighted = tuple(rest[m] * jnp.sqrt(2.0 * rate[m]) * state[m] for m in range(modes))

    def step(index, weighted):
        for inner in range(SUBLANES):
            now = index * SUBLANES + inner
            weighted = tuple(weighted[m] * decay[m] for m in range(modes))
            long_out = tree_sum([y_ref[0, now], *weighted])
            long_out = long_out.astype(BF16).astype(F32)
            out_rows[pl.ds(now, SUBLANES, stride=pitch), :] = query_ref[0, now] * long_out
        return weighted

    lax.fori_loop(0, tokens // SUBLANES, step, weighted)
    for tile in range(SUBLANES):
        out_ref[:, pl.ds(tile * LANES, LANES)] = out_rows[pl.ds(tile * pitch, tokens), :].astype(BF16)


def project_kernel(count, picks, here, *refs):
    out_ref, slots, sems = refs[-3:]
    depth, share = slots.shape[1:]
    blocks, sources = refs[: SIDE * count], refs[SIDE * count : -3]
    half = depth // SIDE
    columns = pl.ds(pl.multiple_of(here[0] * share, share), share)
    copies = []
    for i, (which, rank) in enumerate(picks):
        if rank is None:
            source = sources[which].at[:, columns]
        else:
            source = sources[which].at[here[rank], :, columns]
        copies.append(pltpu.make_async_copy(source, slots.at[i], sems.at[i]))
        copies[-1].start()
    for i in range(len(picks)):
        copies[i].wait()
        for j in range(count):
            total = None
            for h in range(SIDE):
                term = jnp.dot(
                    blocks[SIDE * j + h][...],
                    slots[i, h * half : (h + 1) * half],
                    preferred_element_type=F32,
                )
                total = term if total is None else total + term
            out_ref[j, i] = total.astype(BF16)


def place_kernel(kept, steps, here, *refs):
    per_pair = 2 * steps
    sources, out_ref = refs[: SIDE * per_pair], refs[-1]
    share = sources[0].shape[2]
    tp_me, rank = here[0], here[1]
    for slot in range(kept):
        step = here[2 + slot]
        for pair in range(SIDE):
            mine = sources[pair * per_pair : (pair + 1) * per_pair]
            for near in range(SIDE):
                piece = rank ^ (SIDE * pair + near)
                for t in range(SIDE):
                    start = ((slot * SLAB + piece) * SIDE + t) * share
                    target = pl.ds(pl.multiple_of(start, share), share)
                    own = jnp.logical_and(step == 0, tp_me == t)
                    moved = jnp.logical_and(step == 0, tp_me != t)
                    choices = [(own, mine[0]), (moved, mine[1])]
                    choices += [(step == k, mine[2 * k + t]) for k in range(1, steps)]
                    for chosen, source in choices:
                        index = near if source.shape[0] == SIDE else SIDE * pair + near

                        @pl.when(chosen)
                        def _(source=source, index=index, target=target):
                            out_ref[:, target] = source[index]


def ring_order(count):
    return [0] + list(range(1, count, 2)) + [i for i in range(count - 1, 0, -1) if i % 2 == 0]


def any_size(features, conv_weight, decay_rates, residues, skip_gain, out_weight):
    tokens, width = features.shape[1:]
    ctx, tp = lax.axis_size("ctx"), lax.axis_size("tp")
    me, tp_me = lax.axis_index("ctx"), lax.axis_index("tp")
    halo = lax.ppermute(features[:, tokens - HALO :], "ctx", [(i, i + 1) for i in range(ctx - 1)])
    extended = jnp.concatenate([halo, features], axis=1).astype(F32)
    taps = lax.dynamic_slice_in_dim(conv_weight, tp_me * width, width, 2)
    filtered = sum(taps[:, j, None] * extended[:, HALO - j : HALO - j + tokens] for j in range(TAPS))
    u = (filtered[1] * filtered[2]).astype(BF16).astype(F32)
    rates, weights, skip = (
        lax.all_gather(a, "ctx", axis=a.ndim - 1, tiled=True) for a in (decay_rates, residues, skip_gain)
    )
    weights = weights * jnp.sqrt(2.0 * rates)
    decay = jnp.exp(-rates)
    zero = jnp.zeros(rates.shape, F32)
    left = lax.fori_loop(0, tokens, lambda t, s: s * decay + u[t], zero)
    lefts = lax.all_gather(left, "ctx")
    block_decay = jnp.exp(-float(tokens) * rates)
    entering = lax.fori_loop(0, me, lambda b, s: s * block_decay + lefts[b], zero)

    def advance(states, now):
        states = states * decay + now
        return states, jnp.sum(weights * states, axis=0) + skip * now

    long_out = lax.scan(advance, entering, u)[1].astype(BF16).astype(F32)
    gated = (filtered[0] * long_out).astype(BF16)
    whole = lax.all_gather(gated, "ctx", axis=0, tiled=True)
    partial = jnp.dot(whole, out_weight, preferred_element_type=F32).astype(BF16)
    share = partial.shape[1] // tp
    partial = partial.reshape(ctx * tokens, tp, share).transpose(1, 0, 2)
    partial = lax.all_to_all(partial, "tp", split_axis=0, concat_axis=0, tiled=True)
    summed = jnp.sum(partial.astype(F32), axis=0).astype(BF16).reshape(ctx, tokens, share)
    summed = lax.all_to_all(summed, "ctx", split_axis=0, concat_axis=0, tiled=True)
    placed = lax.all_to_all(
        summed.reshape(tp, ctx // tp, tokens, share), "tp", split_axis=0, concat_axis=0, tiled=True
    )
    return placed.transpose(2, 1, 0, 3).reshape(tokens, width)


def per_device(features, conv_weight, decay_rates, residues, skip_gain, out_weight):
    tokens, width = features.shape[1:]
    modes, owned = decay_rates.shape
    ctx, tp = lax.axis_size("ctx"), lax.axis_size("tp")
    depth, columns = out_weight.shape
    share = columns // tp
    if owned * SLAB != GROUP or tp != SIDE or share % LANES or ctx // SLAB < 3:
        return any_size(features, conv_weight, decay_rates, residues, skip_gain, out_weight)
    slabs = ctx // SLAB
    groups = width // GROUP
    me, tp_me = lax.axis_index("ctx"), lax.axis_index("tp")
    z_me, rank = me // SLAB, me % SLAB
    order = ring_order(slabs)
    place = [order.index(z) for z in range(slabs)]
    here = jnp.stack([z_me, rank, tp_me]).astype(jnp.int32)

    def within_slab(array, mask):
        return lax.ppermute(array, "ctx", [(i, i ^ mask) for i in range(ctx)])

    def from_slab(array, by):
        return lax.ppermute(array, "ctx", [(i, (i - by * SLAB) % ctx) for i in range(ctx)])

    def ring(array):
        pairs = []
        for i in range(ctx):
            z, rest = divmod(i, SLAB)
            pairs.append((i, order[(place[z] + 1) % slabs] * SLAB + rest))
        return lax.ppermute(array, "ctx", pairs)

    halo = lax.ppermute(
        features[:, tokens - HALO :, :], "ctx", [(i, i + 1) for i in range(ctx - 1)]
    )
    rows = jnp.concatenate([decay_rates, residues, skip_gain[None]], axis=0)
    rows = jnp.stack([rows] + [from_slab(rows, by) for by in range(1, slabs)])
    rows, halo = lax.optimization_barrier((rows, halo))
    rates = [rows, within_slab(rows, 1), within_slab(rows, 2)]

    beside = within_slab(out_weight, 1)
    slab_weights = lax.all_gather(
        out_weight,
        "ctx",
        axis_index_groups=[list(range(z * SLAB, (z + 1) * SLAB)) for z in range(slabs)],
    )

    limit = pltpu.CompilerParams(vmem_limit_bytes=16 * 1024 * 1024)
    large = pltpu.CompilerParams(vmem_limit_bytes=48 * 1024 * 1024)
    light = pl.CostEstimate(flops=1, bytes_accessed=1, transcendentals=0)
    series_shape = jax.ShapeDtypeStruct((groups, tokens, SUBLANES, LANES), F32)
    state_shape = jax.ShapeDtypeStruct((groups, modes, owned), BF16)
    scratch_rows = pltpu.VMEM((SUBLANES * (tokens + SUBLANES), LANES), F32)
    wide = pltpu.VMEM((SUBLANES * (modes + SUBLANES), LANES), F32)
    series = pl.BlockSpec((1, tokens, SUBLANES, LANES), lambda g, here: (g, 0, 0, 0))
    state_spec = pl.BlockSpec((1, modes, owned), lambda g, here: (g, 0, 0))
    rate_spec = pl.BlockSpec(
        (1, 2 * modes + 1, owned), lambda g, here: (lax.rem(g - here[0] + slabs, slabs), 0, 0)
    )

    def grouped(kernel, name, in_specs, out_specs, out_shape, scratch, groups=groups):
        return pl.pallas_call(
            kernel,
            grid_spec=pltpu.PrefetchScalarGridSpec(
                num_scalar_prefetch=1,
                grid=(groups,),
                in_specs=in_specs,
                out_specs=out_specs,
                scratch_shapes=scratch,
            ),
            out_shape=out_shape,
            compiler_params=limit,
            cost_estimate=light,
            name=name,
        )

    u, query = grouped(
        filter_kernel,
        "short_filters",
        [
            pl.BlockSpec((3, tokens, GROUP), lambda g, here: (0, 0, g)),
            pl.BlockSpec((3, HALO, GROUP), lambda g, here: (0, 0, g)),
            pl.BlockSpec((3, TAPS, GROUP), lambda g, here: (0, 0, here[2] * groups + g)),
        ],
        [series, series],
        [series_shape, series_shape],
        [pltpu.VMEM((3 * TAPS, SUBLANES, LANES), F32), scratch_rows, scratch_rows, scratch_rows],
    )(here, features, halo, conv_weight)

    passed, u = lax.optimization_barrier((rates[2], u))
    rates.append(within_slab(passed, 1))

    left = grouped(
        functools.partial(state_kernel, modes),
        "block_states",
        [series] + [rate_spec] * SLAB,
        [state_spec] * SLAB,
        [state_shape] * SLAB,
        [wide],
    )(here, u, *rates)
    left = [left[0]] + [within_slab(left[d], d) for d in range(1, SLAB)]

    smem = pl.BlockSpec(memory_space=pltpu.SMEM)
    vmem = pl.BlockSpec(memory_space=pltpu.VMEM)
    slab_left = pl.pallas_call(
        functools.partial(slab_kernel, tokens),
        in_specs=[smem] + [vmem] * (1 + SLAB),
        out_specs=vmem,
        out_shape=state_shape,
        compiler_params=limit,
        cost_estimate=light,
        name="slab_states",
    )(here, rates[0], *left)
    earlier = [
        lax.ppermute(slab_left, "ctx", [(i, i + by * SLAB) for i in range(ctx - by * SLAB)])
        for by in range(1, slabs)
    ]

    local = grouped(
        functools.partial(local_kernel, modes),
        "local_convolution",
        [series] + [rate_spec] * SLAB,
        series,
        series_shape,
        [wide],
    )(here, u, *rates)
    earlier, local = lax.optimization_barrier((earlier, local))

    incoming = pl.pallas_call(
        functools.partial(incoming_kernel, tokens),
        in_specs=[smem] + [vmem] * (SLAB + slabs),
        out_specs=[vmem] * SLAB,
        out_shape=[state_shape] * SLAB,
        compiler_params=limit,
        cost_estimate=light,
        name="incoming_states",
    )(here, rates[0], *left, *earlier)
    incoming = [incoming[0]] + [within_slab(incoming[d], d) for d in range(1, SLAB)]

    def gated_half(half):
        count = groups // SIDE
        first = half * count

        def shifted(spec):
            return pl.BlockSpec(spec.block_shape, lambda g, here: spec.index_map(g + first, here))

        return grouped(
            functools.partial(gated_kernel, modes),
            "gated_block",
            [shifted(s) for s in [series] * 2 + [rate_spec] * SLAB + [state_spec] * SLAB],
            pl.BlockSpec((tokens, GROUP), lambda g, here: (0, g)),
            jax.ShapeDtypeStruct((tokens, width // SIDE), BF16),
            [wide, scratch_rows],
            count,
        )(here, query, local, *rates, *incoming)

    def project(blocks, sources, picks, share_index):
        scalars = jnp.stack([share_index, rank ^ 2, rank ^ 3]).astype(jnp.int32)
        return pl.pallas_call(
            functools.partial(project_kernel, len(blocks), picks),
            in_specs=[smem]
            + [vmem] * (SIDE * len(blocks))
            + [pl.BlockSpec(memory_space=pltpu.HBM)] * len(sources),
            out_specs=vmem,
            out_shape=jax.ShapeDtypeStruct((len(blocks), len(picks), tokens, share), BF16),
            scratch_shapes=[
                pltpu.VMEM((len(picks), depth, share), BF16),
                pltpu.SemaphoreType.DMA((len(picks),)),
            ],
            compiler_params=large,
            cost_estimate=light,
            name="project_block",
        )(scalars, *[h for b in blocks for h in b], *sources)

    def project_away(blocks, sources, picks):
        away = project(blocks, sources, picks, 1 - tp_me)
        return away, lax.ppermute(away, "tp", [(0, 1), (1, 0)])

    def project_mine(blocks, sources, picks, after):
        blocks, _ = lax.optimization_barrier((blocks, after))
        return project(blocks, sources, picks, tp_me)

    def total(mine, got):
        return (mine.astype(F32) + got.astype(F32)).astype(BF16)

    half_of = [z * tp // slabs for z in range(slabs)]

    def deliver(summed, by):
        pairs = [[], []]
        for i in range(ctx):
            z, rest = divmod(i, SLAB)
            target = order[(place[z] - by) % slabs] * SLAB + rest
            for t in range(tp):
                pairs[t].append((i * tp + t, target * tp + half_of[z]))
        if by == 0:
            moves = [p for p in pairs[0] + pairs[1] if p[0] != p[1]]
            return [summed, lax.ppermute(summed, ("ctx", "tp"), moves)]
        return [lax.ppermute(summed, ("ctx", "tp"), moves) for moves in pairs]

    near, far, both = (
        ((0, None), (1, None)),
        ((0, 1), (0, 2)),
        ((0, None), (1, None), (2, 1), (2, 2)),
    )
    near, far, both = (
        ((0, None), (1, None)),
        ((0, 1), (0, 2)),
        ((0, None), (1, None), (2, 1), (2, 2)),
    )
    blocks = [[gated_half(h) for h in range(SIDE)]]
    arrived = [[], []]
    for step in range(slabs - 1):
        if step:
            blocks[step], summed, arrived[0] = lax.optimization_barrier(
                (blocks[step], summed, arrived[0])
            )
            arrived[0] += deliver(summed, step - 1)
        blocks.append([ring(h) for h in blocks[step]])
        away, got = project_away([blocks[step]], [out_weight, beside], near)
        mine = project_mine([blocks[step]], [out_weight, beside], near, away)
        summed = total(mine, got)[0]
    slab_weights, summed = lax.optimization_barrier((slab_weights, summed))
    away, got = project_away(blocks[: slabs - 1], [slab_weights], far)
    mine = project_mine(blocks[: slabs - 1], [slab_weights], far, away)
    block, _ = lax.optimization_barrier((blocks[-1], mine))
    sources = [out_weight, beside, slab_weights]
    last_away, last_got = project_away([block], sources, both)
    last_mine = project_mine([block], sources, both, last_away)
    batch = total(mine, got)
    for step in range(slabs - 2):
        arrived[1] += deliver(batch[step], step)
    late = deliver(jnp.concatenate([summed, batch[slabs - 2]]), slabs - 2)
    late += deliver(total(last_mine, last_got)[0], slabs - 1)
    arrived = [a + late for a in arrived]

    def place_of(z):
        return sum(jnp.where(z == k, place[k], 0) for k in range(slabs))

    kept = slabs // tp
    steps = [
        lax.rem(place_of(tp_me * kept + j) - place_of(z_me) + slabs, slabs) for j in range(kept)
    ]
    return pl.pallas_call(
        functools.partial(place_kernel, kept, slabs),
        in_specs=[smem] + [vmem] * (SIDE * 2 * slabs),
        out_specs=vmem,
        out_shape=jax.ShapeDtypeStruct((tokens, width), BF16),
        compiler_params=limit,
        cost_estimate=light,
        name="place_columns",
    )(jnp.stack([tp_me, rank, *steps]).astype(jnp.int32), *arrived[0], *arrived[1])


def solution(mesh):
    in_specs = (
        P(None, "ctx", "tp"),
        P(),
        P(None, ("tp", "ctx")),
        P(None, ("tp", "ctx")),
        P(("tp", "ctx")),
        P("tp", "ctx"),
    )
    out_specs = P("ctx", "tp")
    return jax.shard_map(
        per_device, mesh=mesh, in_specs=in_specs, out_specs=out_specs, check_vma=False
    )
```

profile of v0, /device:TPU:0, one launch (start us, length us, event | category | flops | bytes accessed | tf_op | source)
XLA Modules:
  0.0 195.1 jit_solution(222647231373609646)
XLA Ops:
  7.8 4.7 %collective-permute-start = (f32[33,256]{1,0:T(8,128)S(1)}, f32[33,256]{1,0:T(8,128)S(1)}, u32[]{:S(2)}, u32[]{:S(2)}) collective-permute-start(f32[33,256]{1,0:T(8,128)S(1)} %get-tuple-element.97), channel_id=1, source_target_pairs={{0,24},{2,26},{4,28},{6,30},{8,0},{10,2},{12,4},{14,6},{16,8},{18,... | collective-permute-start | bytes 101384 | tf_op jit(solution)/shard_map/ppermute | solution.py:305
  18.3 3.1 %collective-permute-start.4 = (f32[4,33,256]{2,1,0:T(8,128)S(1)}, f32[4,33,256]{2,1,0:T(8,128)S(1)}, u32[]{:S(2)}, u32[]{:S(2)}) collective-permute-start(f32[4,33,256]{2,1,0:T(8,128)S(1)} %pad_maximum_fusion.1.refs_0_.rates), channel_id=1, source_target_pairs={{0,4},{2,6},{4,0},{6,2},{8,12},{10,14},{12,8},{14,10},{16,20},{18,... | collective-permute-start | bytes 405512 | tf_op jit(solution)/shard_map/ppermute | solution.py:302
  24.0 3.3 %short_filters.1 = (f32[4,128,8,128]{3,2,1,0:T(8,128)S(1)}, f32[4,128,8,128]{3,2,1,0:T(8,128)S(1)}) custom-call(s32[3]{0:T(128)S(1)} %pad_add_fusion.1.here, bf16[3,128,4096]{2,1,0:T(8,128)(2,1)S(1)} %copy-done.2, bf16[3,2,4096]{2,1,0:T(2,128)(2,1)S(1)} %collective-permute-done.3.halo, f32[3,3,8192]{2,1,0:T(4,128)S(1)} %copy-done.3), custom_call_target="tpu_custom_call" | custom-call | flops 1 | bytes 1 | tf_op jit(solution)/shard_map/short_filters/pallas_call | solution.py:358
  29.5 3.1 %block_states.1 = (bf16[4,16,256]{2,1,0:T(8,128)(2,1)S(1)}, bf16[4,16,256]{2,1,0:T(8,128)(2,1)S(1)}, bf16[4,16,256]{2,1,0:T(8,128)(2,1)S(1)}, bf16[4,16,256]{2,1,0:T(8,128)(2,1)S(1)}) custom-call(s32[3]{0:T(128)S(1)} %pad_add_fusion.1.here, f32[4,128,8,128]{3,2,1,0:T(8,128)S(1)} %get-tuple-element.53.u_ref, ...), custom_call_target="tpu_custom_call" | custom-call | flops 1 | bytes 1 | tf_op jit(solution)/shard_map/block_states/pallas_call | solution.py:374
  40.2 4.5 %collective-permute-start.10 = (bf16[4,16,256]{2,1,0:T(8,128)(2,1)S(1)}, bf16[4,16,256]{2,1,0:T(8,128)(2,1)S(1)}, u32[]{:S(2)}, u32[]{:S(2)}) collective-permute-start(bf16[4,16,256]{2,1,0:T(8,128)(2,1)S(1)} %slab_states.1), channel_id=1, source_target_pairs={{0,8},{2,10},{4,12},{6,14},{8,16},{10,18},{12,20},{14,22},{16,24},... | collective-permute-start | bytes 98312 | tf_op jit(solution)/shard_map/ppermute | solution.py:396
  47.6 5.6 %local_convolution.1.y_ref = f32[4,128,8,128]{3,2,1,0:T(8,128)S(1)} custom-call(s32[3]{0:T(128)S(1)} %pad_add_fusion.1.here, f32[4,128,8,128]{3,2,1,0:T(8,128)S(1)} %get-tuple-element.53.u_ref, f32[4,33,256]{2,1,0:T(8,128)S(1)} %pad_maximum_fusion.1.refs_0_.rates, f32[4,33,256]{2,1,0:T(8,128)S(1)} %collective-permute-done.5.refs_1_, ...), custom_call_target="tpu_custom_call" | custom-call | flops 1 | bytes 1 | tf_op jit(solution)/shard_map/local_convolution/pallas_call | solution.py:400
  56.0 3.3 %collective-permute-done.14.refs_6_ = bf16[4,16,256]{2,1,0:T(8,128)(2,1)S(1)} collective-permute-done((bf16[4,16,256]{2,1,0:T(8,128)(2,1)S(1)}, bf16[4,16,256]{2,1,0:T(8,128)(2,1)S(1)}, u32[]{:S(2)}, u32[]{:S(2)}) %collective-permute-start.14) | collective-permute-done | bytes 32800 | tf_op jit(solution)/shard_map/ppermute | solution.py:302
  67.6 3.0 %project_block.10 = bf16[1,2,128,256]{3,2,1,0:T(8,128)(2,1)S(1)} custom-call(s32[3]{0:T(128)S(1)} %add_add_fusion.1.here, bf16[128,2048]{1,0:T(8,128)(2,1)S(1)} %gated_block.2.refs_0_, bf16[128,2048]{1,0:T(8,128)(2,1)S(1)} %gated_block.3.refs_1_, bf16[4096,512]{1,0:T(8,128)(2,1)S(1)} %copy-done, bf16[4096,512]{1,0:T(8,128)(2,1)} %collective-permute-done.18.refs_3_), custom_call_target="tpu_custom_call" | custom-call | flops 1 | bytes 1 | tf_op jit(solution)/shard_map/project_block/pallas_call | solution.py:440
  72.3 3.0 %project_block.11 = bf16[1,2,128,256]{3,2,1,0:T(8,128)(2,1)S(1)} custom-call(s32[3]{0:T(128)S(1)} %add_add_fusion.here, bf16[128,2048]{1,0:T(8,128)(2,1)S(1)} %gated_block.2.refs_0_, bf16[128,2048]{1,0:T(8,128)(2,1)S(1)} %gated_block.3.refs_1_, bf16[4096,512]{1,0:T(8,128)(2,1)S(1)} %copy-done, bf16[4096,512]{1,0:T(8,128)(2,1)} %collective-permute-done.18.refs_3_), custom_call_target="tpu_custom_call" | custom-call | flops 1 | bytes 1 | tf_op jit(solution)/shard_map/project_block/pallas_call | solution.py:440
  78.0 11.1 %collective-permute-done.16.refs_0_.refs_2_ = bf16[128,2048]{1,0:T(8,128)(2,1)S(1)} collective-permute-done((bf16[128,2048]{1,0:T(8,128)(2,1)S(1)}, bf16[128,2048]{1,0:T(8,128)(2,1)S(1)}, u32[]{:S(2)}, u32[]{:S(2)}) %collective-permute-start.16) | collective-permute-done | bytes 524320 | tf_op jit(solution)/shard_map/ppermute | solution.py:312
  89.6 3.0 %project_block.12 = bf16[1,2,128,256]{3,2,1,0:T(8,128)(2,1)S(1)} custom-call(s32[3]{0:T(128)S(1)} %add_add_fusion.1.here, bf16[128,2048]{1,0:T(8,128)(2,1)S(1)} %collective-permute-done.16.refs_0_.refs_2_, bf16[128,2048]{1,0:T(8,128)(2,1)S(1)} %collective-permute-done.17.refs_1_.refs_3_, bf16[4096,512]{1,0:T(8,128)(2,1)S(1)} %copy-done, ...), custom_call_target="tpu_custom_call" | custom-call | flops 1 | bytes 1 | tf_op jit(solution)/shard_map/project_block/pallas_call | solution.py:440
  95.4 3.0 %project_block.13 = bf16[1,2,128,256]{3,2,1,0:T(8,128)(2,1)S(1)} custom-call(s32[3]{0:T(128)S(1)} %add_add_fusion.here, bf16[128,2048]{1,0:T(8,128)(2,1)S(1)} %collective-permute-done.16.refs_0_.refs_2_, bf16[128,2048]{1,0:T(8,128)(2,1)S(1)} %collective-permute-done.17.refs_1_.refs_3_, bf16[4096,512]{1,0:T(8,128)(2,1)S(1)} %copy-done, ...), custom_call_target="tpu_custom_call" | custom-call | flops 1 | bytes 1 | tf_op jit(solution)/shard_map/project_block/pallas_call | solution.py:440
  101.0 3.8 %collective-permute-done.20.refs_0_.refs_4_ = bf16[128,2048]{1,0:T(8,128)(2,1)S(1)} collective-permute-done((bf16[128,2048]{1,0:T(8,128)(2,1)S(1)}, bf16[128,2048]{1,0:T(8,128)(2,1)S(1)}, u32[]{:S(2)}, u32[]{:S(2)}) %collective-permute-start.20) | collective-permute-done | bytes 524320 | tf_op jit(solution)/shard_map/ppermute | solution.py:312
  104.8 10.3 %collective-permute-done.21.refs_1_.refs_5_ = bf16[128,2048]{1,0:T(8,128)(2,1)S(1)} collective-permute-done((bf16[128,2048]{1,0:T(8,128)(2,1)S(1)}, bf16[128,2048]{1,0:T(8,128)(2,1)S(1)}, u32[]{:S(2)}, u32[]{:S(2)}) %collective-permute-start.21) | collective-permute-done | bytes 524320 | tf_op jit(solution)/shard_map/ppermute | solution.py:312
  115.4 3.0 %project_block.14 = bf16[1,2,128,256]{3,2,1,0:T(8,128)(2,1)S(1)} custom-call(s32[3]{0:T(128)S(1)} %add_add_fusion.1.here, bf16[128,2048]{1,0:T(8,128)(2,1)S(1)} %collective-permute-done.20.refs_0_.refs_4_, bf16[128,2048]{1,0:T(8,128)(2,1)S(1)} %collective-permute-done.21.refs_1_.refs_5_, bf16[4096,512]{1,0:T(8,128)(2,1)S(1)} %copy-done, ...), custom_call_target="tpu_custom_call" | custom-call | flops 1 | bytes 1 | tf_op jit(solution)/shard_map/project_block/pallas_call | solution.py:440
  120.0 3.0 %project_block.15 = bf16[1,2,128,256]{3,2,1,0:T(8,128)(2,1)S(1)} custom-call(s32[3]{0:T(128)S(1)} %add_add_fusion.here, bf16[128,2048]{1,0:T(8,128)(2,1)S(1)} %collective-permute-done.20.refs_0_.refs_4_, bf16[128,2048]{1,0:T(8,128)(2,1)S(1)} %collective-permute-done.21.refs_1_.refs_5_, bf16[4096,512]{1,0:T(8,128)(2,1)S(1)} %copy-done, ...), custom_call_target="tpu_custom_call" | custom-call | flops 1 | bytes 1 | tf_op jit(solution)/shard_map/project_block/pallas_call | solution.py:440
  123.5 4.7 %project_block.16 = bf16[3,2,128,256]{3,2,1,0:T(8,128)(2,1)S(1)} custom-call(s32[3]{0:T(128)S(1)} %add_add_fusion.1.here, bf16[128,2048]{1,0:T(8,128)(2,1)S(1)} %gated_block.2.refs_0_, bf16[128,2048]{1,0:T(8,128)(2,1)S(1)} %gated_block.3.refs_1_, bf16[128,2048]{1,0:T(8,128)(2,1)S(1)} %collective-permute-done.16.refs_0_.refs_2_, ...), custom_call_target="tpu_custom_call" | custom-call | flops 1 | bytes 1 | tf_op jit(solution)/shard_map/project_block/pallas_call | solution.py:440
  128.2 4.9 %project_block.17 = bf16[3,2,128,256]{3,2,1,0:T(8,128)(2,1)S(1)} custom-call(s32[3]{0:T(128)S(1)} %add_add_fusion.here, bf16[128,2048]{1,0:T(8,128)(2,1)S(1)} %gated_block.2.refs_0_, bf16[128,2048]{1,0:T(8,128)(2,1)S(1)} %gated_block.3.refs_1_, bf16[128,2048]{1,0:T(8,128)(2,1)S(1)} %collective-permute-done.16.refs_0_.refs_2_, ...), custom_call_target="tpu_custom_call" | custom-call | flops 1 | bytes 1 | tf_op jit(solution)/shard_map/project_block/pallas_call | solution.py:440
  133.2 7.1 %collective-permute-done.31.refs_1_ = bf16[128,2048]{1,0:T(8,128)(2,1)} collective-permute-done((bf16[128,2048]{1,0:T(8,128)(2,1)S(1)}, bf16[128,2048]{1,0:T(8,128)(2,1)}, u32[]{:S(2)}, u32[]{:S(2)}) %collective-permute-start.31) | collective-permute-done | bytes 524320 | tf_op jit(solution)/shard_map/ppermute | solution.py:312
  140.3 5.0 %project_block.18 = bf16[1,4,128,256]{3,2,1,0:T(8,128)(2,1)S(1)} custom-call(s32[3]{0:T(128)S(1)} %add_add_fusion.1.here, bf16[128,2048]{1,0:T(8,128)(2,1)} %collective-permute-done.30.refs_0_, bf16[128,2048]{1,0:T(8,128)(2,1)} %collective-permute-done.31.refs_1_, bf16[4096,512]{1,0:T(8,128)(2,1)S(1)} %copy-done.1, ...), custom_call_target="tpu_custom_call" | custom-call | flops 1 | bytes 1 | tf_op jit(solution)/shard_map/project_block/pallas_call | solution.py:440
  150.6 5.1 %project_block.19 = bf16[1,4,128,256]{3,2,1,0:T(8,128)(2,1)S(1)} custom-call(s32[3]{0:T(128)S(1)} %add_add_fusion.here, bf16[128,2048]{1,0:T(8,128)(2,1)} %collective-permute-done.30.refs_0_, bf16[128,2048]{1,0:T(8,128)(2,1)} %collective-permute-done.31.refs_1_, bf16[4096,512]{1,0:T(8,128)(2,1)S(1)} %copy-done.1, ...), custom_call_target="tpu_custom_call" | custom-call | flops 1 | bytes 1 | tf_op jit(solution)/shard_map/project_block/pallas_call | solution.py:440
  159.8 3.3 %collective-permute-done.27 = bf16[3,2,128,256]{3,2,1,0:T(8,128)(2,1)S(1)} collective-permute-done((bf16[3,2,128,256]{3,2,1,0:T(8,128)(2,1)S(1)}, bf16[3,2,128,256]{3,2,1,0:T(8,128)(2,1)S(1)}, u32[]{:S(2)}, u32[]{:S(2)}) %collective-permute-start.27) | collective-permute-done | bytes 393248 | tf_op jit(solution)/shard_map/ppermute | solution.py:458
  166.6 12.0 %collective-permute-start.36 = (bf16[2,128,256]{2,1,0:T(8,128)(2,1)S(1)}, bf16[2,128,256]{2,1,0:T(8,128)(2,1)S(1)}, u32[]{:S(2)}, u32[]{:S(2)}) collective-permute-start(bf16[2,128,256]{2,1,0:T(8,128)(2,1)S(1)} %get-tuple-element.93), channel_id=1, source_target_pairs={{0,16},{2,18},{4,20},{6,22},{8,0},{10,2},{12,4},{14,6},{16,25},{18... | collective-permute-start | bytes 393224 | tf_op jit(solution)/shard_map/ppermute | solution.py:479
  181.1 5.3 %collective-permute-done.37.refs_11_ = bf16[2,128,256]{2,1,0:T(8,128)(2,1)S(1)} collective-permute-done((bf16[2,128,256]{2,1,0:T(8,128)(2,1)S(1)}, bf16[2,128,256]{2,1,0:T(8,128)(2,1)S(1)}, u32[]{:S(2)}, u32[]{:S(2)}) %collective-permute-start.37) | collective-permute-done | bytes 131104 | tf_op jit(solution)/shard_map/ppermute | solution.py:479
  (103 shorter events, 63.2 us)
Async XLA Ops:
  6.5 117.0 %all-gather.3.cloned.1.call-start = ((), (), s32[]{:S(2)}) async-start(), calls=%async_computation | async-start | bytes 20971520 | tf_op jit(solution)/shard_map/all_gather | solution.py:323
  7.3 58.2 %collective-permute-start.18 = (bf16[4096,512]{1,0:T(8,128)(2,1)}, bf16[4096,512]{1,0:T(8,128)(2,1)}, u32[]{:S(2)}, u32[]{:S(2)}) collective-permute-start(bf16[4096,512]{1,0:T(8,128)(2,1)} %refs_2_.15), channel_id=1, source_target_pairs={{0,2},{2,0},{4,6},{6,4},{8,10},{10,8},{12,14},{14,12},{16,18},{18,... | collective-permute-start | bytes 12582920 | tf_op jit(solution)/shard_map/ppermute | solution.py:302
  7.8 8.2 %collective-permute-start = (f32[33,256]{1,0:T(8,128)S(1)}, f32[33,256]{1,0:T(8,128)S(1)}, u32[]{:S(2)}, u32[]{:S(2)}) collective-permute-start(f32[33,256]{1,0:T(8,128)S(1)} %get-tuple-element.97), channel_id=1, source_target_pairs={{0,24},{2,26},{4,28},{6,30},{8,0},{10,2},{12,4},{14,6},{16,8},{18,... | collective-permute-start | bytes 101384 | tf_op jit(solution)/shard_map/ppermute | solution.py:305
  18.3 9.5 %collective-permute-start.4 = (f32[4,33,256]{2,1,0:T(8,128)S(1)}, f32[4,33,256]{2,1,0:T(8,128)S(1)}, u32[]{:S(2)}, u32[]{:S(2)}) collective-permute-start(f32[4,33,256]{2,1,0:T(8,128)S(1)} %pad_maximum_fusion.1.refs_0_.rates), channel_id=1, source_target_pairs={{0,4},{2,6},{4,0},{6,2},{8,12},{10,14},{12,8},{14,10},{16,20},{18,... | collective-permute-start | bytes 405512 | tf_op jit(solution)/shard_map/ppermute | solution.py:302
  40.2 13.0 %collective-permute-start.10 = (bf16[4,16,256]{2,1,0:T(8,128)(2,1)S(1)}, bf16[4,16,256]{2,1,0:T(8,128)(2,1)S(1)}, u32[]{:S(2)}, u32[]{:S(2)}) collective-permute-start(bf16[4,16,256]{2,1,0:T(8,128)(2,1)S(1)} %slab_states.1), channel_id=1, source_target_pairs={{0,8},{2,10},{4,12},{6,14},{8,16},{10,18},{12,20},{14,22},{16,24},... | collective-permute-start | bytes 98312 | tf_op jit(solution)/shard_map/ppermute | solution.py:396
  44.7 8.5 %collective-permute-start.11 = (bf16[4,16,256]{2,1,0:T(8,128)(2,1)S(1)}, bf16[4,16,256]{2,1,0:T(8,128)(2,1)S(1)}, u32[]{:S(2)}, u32[]{:S(2)}) collective-permute-start(bf16[4,16,256]{2,1,0:T(8,128)(2,1)S(1)} %slab_states.1), channel_id=1, source_target_pairs={{0,16},{2,18},{4,20},{6,22},{8,24},{10,26},{12,28},{14,30},{1,17},... | collective-permute-start | bytes 98312 | tf_op jit(solution)/shard_map/ppermute | solution.py:396
  46.3 6.9 %collective-permute-start.12 = (bf16[4,16,256]{2,1,0:T(8,128)(2,1)S(1)}, bf16[4,16,256]{2,1,0:T(8,128)(2,1)S(1)}, u32[]{:S(2)}, u32[]{:S(2)}) collective-permute-start(bf16[4,16,256]{2,1,0:T(8,128)(2,1)S(1)} %slab_states.1), channel_id=1, source_target_pairs={{0,24},{2,26},{4,28},{6,30},{1,25},{3,27},{5,29},{7,31}} | collective-permute-start | bytes 98312 | tf_op jit(solution)/shard_map/ppermute | solution.py:396
  62.2 15.7 %collective-permute-start.17 = (bf16[128,2048]{1,0:T(8,128)(2,1)S(1)}, bf16[128,2048]{1,0:T(8,128)(2,1)S(1)}, u32[]{:S(2)}, u32[]{:S(2)}) collective-permute-start(bf16[128,2048]{1,0:T(8,128)(2,1)S(1)} %gated_block.3.refs_1_), channel_id=1, source_target_pairs={{0,8},{2,10},{4,12},{6,14},{8,24},{10,26},{12,28},{14,30},{16,0},{... | collective-permute-start | bytes 1572872 | tf_op jit(solution)/shard_map/ppermute | solution.py:312
  64.7 24.4 %collective-permute-start.16 = (bf16[128,2048]{1,0:T(8,128)(2,1)S(1)}, bf16[128,2048]{1,0:T(8,128)(2,1)S(1)}, u32[]{:S(2)}, u32[]{:S(2)}) collective-permute-start(bf16[128,2048]{1,0:T(8,128)(2,1)S(1)} %gated_block.2.refs_0_), channel_id=1, source_target_pairs={{0,8},{2,10},{4,12},{6,14},{8,24},{10,26},{12,28},{14,30},{16,0},{... | collective-permute-start | bytes 1572872 | tf_op jit(solution)/shard_map/ppermute | solution.py:312
  89.1 15.7 %collective-permute-start.20 = (bf16[128,2048]{1,0:T(8,128)(2,1)S(1)}, bf16[128,2048]{1,0:T(8,128)(2,1)S(1)}, u32[]{:S(2)}, u32[]{:S(2)}) collective-permute-start(bf16[128,2048]{1,0:T(8,128)(2,1)S(1)} %collective-permute-done.16.refs_0_.refs_2_), channel_id=1, source_target_pairs={{0,8},{2,10},{4,12},{6,14},{8,24},{10,26},{12,28},{14,30},{16,0},{... | collective-permute-start | bytes 1572872 | tf_op jit(solution)/shard_map/ppermute | solution.py:312
  89.1 25.9 %collective-permute-start.21 = (bf16[128,2048]{1,0:T(8,128)(2,1)S(1)}, bf16[128,2048]{1,0:T(8,128)(2,1)S(1)}, u32[]{:S(2)}, u32[]{:S(2)}) collective-permute-start(bf16[128,2048]{1,0:T(8,128)(2,1)S(1)} %collective-permute-done.17.refs_1_.refs_3_), channel_id=1, source_target_pairs={{0,8},{2,10},{4,12},{6,14},{8,24},{10,26},{12,28},{14,30},{16,0},{... | collective-permute-start | bytes 1572872 | tf_op jit(solution)/shard_map/ppermute | solution.py:312
  115.1 18.1 %collective-permute-start.30 = (bf16[128,2048]{1,0:T(8,128)(2,1)S(1)}, bf16[128,2048]{1,0:T(8,128)(2,1)}, u32[]{:S(2)}, u32[]{:S(2)}) collective-permute-start(bf16[128,2048]{1,0:T(8,128)(2,1)S(1)} %collective-permute-done.20.refs_0_.refs_4_), channel_id=1, source_target_pairs={{0,8},{2,10},{4,12},{6,14},{8,24},{10,26},{12,28},{14,30},{16,0},{... | collective-permute-start | bytes 1572872 | tf_op jit(solution)/shard_map/ppermute | solution.py:312
  115.1 25.2 %collective-permute-start.31 = (bf16[128,2048]{1,0:T(8,128)(2,1)S(1)}, bf16[128,2048]{1,0:T(8,128)(2,1)}, u32[]{:S(2)}, u32[]{:S(2)}) collective-permute-start(bf16[128,2048]{1,0:T(8,128)(2,1)S(1)} %collective-permute-done.21.refs_1_.refs_5_), channel_id=1, source_target_pairs={{0,8},{2,10},{4,12},{6,14},{8,24},{10,26},{12,28},{14,30},{16,0},{... | collective-permute-start | bytes 1572872 | tf_op jit(solution)/shard_map/ppermute | solution.py:312
  145.3 12.1 %collective-permute-start.32 = (bf16[1,4,128,256]{3,2,1,0:T(8,128)(2,1)S(1)}, bf16[1,4,128,256]{3,2,1,0:T(8,128)(2,1)S(1)}, u32[]{:S(2)}, u32[]{:S(2)}) collective-permute-start(bf16[1,4,128,256]{3,2,1,0:T(8,128)(2,1)S(1)} %project_block.18), channel_id=1, source_target_pairs={{0,1},{1,0},{2,3},{3,2},{4,5},{5,4},{6,7},{7,6},{8,9},{9,8},{10,11... | collective-permute-start | bytes 786440 | tf_op jit(solution)/shard_map/ppermute | solution.py:458
  146.8 16.2 %collective-permute-start.27 = (bf16[3,2,128,256]{3,2,1,0:T(8,128)(2,1)S(1)}, bf16[3,2,128,256]{3,2,1,0:T(8,128)(2,1)S(1)}, u32[]{:S(2)}, u32[]{:S(2)}) collective-permute-start(bf16[3,2,128,256]{3,2,1,0:T(8,128)(2,1)S(1)} %project_block.16), channel_id=1, source_target_pairs={{0,1},{1,0},{2,3},{3,2},{4,5},{5,4},{6,7},{7,6},{8,9},{9,8},{10,11... | collective-permute-start | bytes 1179656 | tf_op jit(solution)/shard_map/ppermute | solution.py:458
  147.4 17.1 %collective-permute-start.24 = (bf16[2,128,256]{2,1,0:T(8,128)(2,1)S(1)}, bf16[2,128,256]{2,1,0:T(8,128)(2,1)S(1)}, u32[]{:S(2)}, u32[]{:S(2)}) collective-permute-start(bf16[2,128,256]{2,1,0:T(8,128)(2,1)S(1)} %copy-done.4), channel_id=1, source_target_pairs={{0,16},{2,18},{4,20},{6,22},{8,0},{10,2},{12,4},{14,6},{16,25},{18... | collective-permute-start | bytes 393224 | tf_op jit(solution)/shard_map/ppermute | solution.py:479
  149.3 15.9 %collective-permute-start.25 = (bf16[2,128,256]{2,1,0:T(8,128)(2,1)S(1)}, bf16[2,128,256]{2,1,0:T(8,128)(2,1)S(1)}, u32[]{:S(2)}, u32[]{:S(2)}) collective-permute-start(bf16[2,128,256]{2,1,0:T(8,128)(2,1)S(1)} %copy-done.4), channel_id=1, source_target_pairs={{1,16},{3,18},{5,20},{7,22},{9,0},{11,2},{13,4},{15,6},{17,25},{19... | collective-permute-start | bytes 393224 | tf_op jit(solution)/shard_map/ppermute | solution.py:479
  157.5 9.0 %collective-permute-start.33 = (bf16[4,128,256]{2,1,0:T(8,128)(2,1)S(1)}, bf16[4,128,256]{2,1,0:T(8,128)(2,1)S(1)}, u32[]{:S(2)}, u32[]{:S(2)}) collective-permute-start(bf16[4,128,256]{2,1,0:T(8,128)(2,1)S(1)} %fusion), channel_id=1, source_target_pairs={{0,8},{2,10},{4,12},{6,14},{8,24},{10,26},{12,28},{14,30},{16,1},{... | collective-permute-start | bytes 786440 | tf_op jit(solution)/shard_map/ppermute | solution.py:479
  159.1 19.5 %collective-permute-start.34 = (bf16[4,128,256]{2,1,0:T(8,128)(2,1)S(1)}, bf16[4,128,256]{2,1,0:T(8,128)(2,1)S(1)}, u32[]{:S(2)}, u32[]{:S(2)}) collective-permute-start(bf16[4,128,256]{2,1,0:T(8,128)(2,1)S(1)} %fusion), channel_id=1, source_target_pairs={{1,8},{3,10},{5,12},{7,14},{9,24},{11,26},{13,28},{15,30},{17,1},{... | collective-permute-start | bytes 786440 | tf_op jit(solution)/shard_map/ppermute | solution.py:479
  163.2 23.2 %collective-permute-start.28 = (bf16[4,128,256]{2,1,0:T(8,128)(2,1)S(1)}, bf16[4,128,256]{2,1,0:T(8,128)(2,1)S(1)}, u32[]{:S(2)}, u32[]{:S(2)}) collective-permute-start(bf16[4,128,256]{2,1,0:T(8,128)(2,1)S(1)} %pad_maximum_fusion), channel_id=1, source_target_pairs={{0,24},{2,26},{4,28},{6,30},{8,16},{10,18},{12,20},{14,22},{16,9},... | collective-permute-start | bytes 786440 | tf_op jit(solution)/shard_map/ppermute | solution.py:479
  164.5 21.8 %collective-permute-start.29 = (bf16[4,128,256]{2,1,0:T(8,128)(2,1)S(1)}, bf16[4,128,256]{2,1,0:T(8,128)(2,1)S(1)}, u32[]{:S(2)}, u32[]{:S(2)}) collective-permute-start(bf16[4,128,256]{2,1,0:T(8,128)(2,1)S(1)} %pad_maximum_fusion), channel_id=1, source_target_pairs={{1,24},{3,26},{5,28},{7,30},{9,16},{11,18},{13,20},{15,22},{17,9},... | collective-permute-start | bytes 786440 | tf_op jit(solution)/shard_map/ppermute | solution.py:479
  165.2 14.8 %collective-permute-start.35 = (bf16[2,128,256]{2,1,0:T(8,128)(2,1)S(1)}, bf16[2,128,256]{2,1,0:T(8,128)(2,1)S(1)}, u32[]{:S(2)}, u32[]{:S(2)}) collective-permute-start(bf16[2,128,256]{2,1,0:T(8,128)(2,1)S(1)} %get-tuple-element.94.refs_8_), channel_id=1, source_target_pairs={{16,17},{18,19},{20,21},{22,23},{24,25},{26,27},{28,29},{30,31},{1... | collective-permute-start | bytes 393224 | tf_op jit(solution)/shard_map/ppermute | solution.py:478
  166.6 14.5 %collective-permute-start.36 = (bf16[2,128,256]{2,1,0:T(8,128)(2,1)S(1)}, bf16[2,128,256]{2,1,0:T(8,128)(2,1)S(1)}, u32[]{:S(2)}, u32[]{:S(2)}) collective-permute-start(bf16[2,128,256]{2,1,0:T(8,128)(2,1)S(1)} %get-tuple-element.93), channel_id=1, source_target_pairs={{0,16},{2,18},{4,20},{6,22},{8,0},{10,2},{12,4},{14,6},{16,25},{18... | collective-permute-start | bytes 393224 | tf_op jit(solution)/shard_map/ppermute | solution.py:479
  178.6 7.8 %collective-permute-start.37 = (bf16[2,128,256]{2,1,0:T(8,128)(2,1)S(1)}, bf16[2,128,256]{2,1,0:T(8,128)(2,1)S(1)}, u32[]{:S(2)}, u32[]{:S(2)}) collective-permute-start(bf16[2,128,256]{2,1,0:T(8,128)(2,1)S(1)} %get-tuple-element.93), channel_id=1, source_target_pairs={{1,16},{3,18},{5,20},{7,22},{9,0},{11,2},{13,4},{15,6},{17,25},{19... | collective-permute-start | bytes 393224 | tf_op jit(solution)/shard_map/ppermute | solution.py:479
  (23 other events, 119.7 us)
Sparse Core Ops, SparseCore 0:
  8.9 111.8 all-gather.2
where the time goes:
time: 196 us; the launch traced here: 195 us
  waiting for transfers between devices  61.9 us (32%)
  Pallas kernels  57.8 us (29%)
  starting transfers between devices  54.6 us (28%)
  between operations  13.9 us (7%)
  local copies, waits for them, and re-layouts  5.68 us (3%)
    pallas_call x10, Pallas kernels, project(): pl.pallas_call(functools.partial(project_kernel, len(blocks), picks), in_...  37.7 us
    ppermute x6, waiting for transfers between devices, ring(): return lax.ppermute(array, 'ctx', pairs)  33.8 us
    ppermute x8, starting transfers between devices, deliver(): return [lax.ppermute(summed, ('ctx', 'tp'), moves) for moves in pairs]  20.8 us
    ppermute x10, waiting for transfers between devices, within_slab(): return lax.ppermute(array, 'ctx', [(i, i ^ mask) for i in range(ctx)])  10.3 us
    ppermute x10, starting transfers between devices, within_slab(): return lax.ppermute(array, 'ctx', [(i, i ^ mask) for i in range(ctx)])  8.25 us
    ppermute x3, starting transfers between devices, per_device(): lax.ppermute(slab_left, 'ctx', [(i, i + by * SLAB) for i in range(ctx - b...  7.36 us
    ppermute x5, starting transfers between devices, project_away(): return (away, lax.ppermute(away, 'tp', [(0, 1), (1, 0)]))  6.83 us
    ppermute x5, waiting for transfers between devices, project_away(): return (away, lax.ppermute(away, 'tp', [(0, 1), (1, 0)]))  6.59 us
  transfers between devices with their start and end apart: 39, of which 20 were waited for; matrix products, arithmetic and copies ran while one was open for 1% of the time, Pallas kernels for 26%

commit v1 on v0

--- a/solution.py
+++ b/solution.py
@@ -185,58 +185,57 @@
         out_ref[:, pl.ds(tile * LANES, LANES)] = out_rows[pl.ds(tile * pitch, tokens), :].astype(BF16)
 
 
-def project_kernel(count, picks, here, *refs):
+def project_kernel(count, picks, first, added, here, *refs):
     out_ref, slots, sems = refs[-3:]
     depth, share = slots.shape[1:]
-    blocks, sources = refs[: SIDE * count], refs[SIDE * count : -3]
-    half = depth // SIDE
+    blocks, sources = refs[:-3], refs[:-3]
+    runs = depth // blocks[0].shape[1]
+    blocks, sources = blocks[: runs * count], sources[runs * count :]
+    rows = pl.ds(first, depth)
     columns = pl.ds(pl.multiple_of(here[0] * share, share), share)
     copies = []
     for i, (which, rank) in enumerate(picks):
-        if rank is None:
-            source = sources[which].at[:, columns]
-        else:
-            source = sources[which].at[here[rank], :, columns]
-        copies.append(pltpu.make_async_copy(source, slots.at[i], sems.at[i]))
+        source = sources[which] if rank is None else sources[which].at[here[rank]]
+        copies.append(pltpu.make_async_copy(source.at[rows, columns], slots.at[i], sems.at[i]))
         copies[-1].start()
     for i in range(len(picks)):
         copies[i].wait()
         for j in range(count):
-            total = None
-            for h in range(SIDE):
+            total = sources[-1][here[0], j, i] if added else None
+            for h in range(runs):
+                size = depth // runs
                 term = jnp.dot(
-                    blocks[SIDE * j + h][...],
-                    slots[i, h * half : (h + 1) * half],
+                    blocks[runs * j + h][...],
+                    slots[i, h * size : (h + 1) * size],
                     preferred_element_type=F32,
                 )
                 total = term if total is None else total + term
-            out_ref[j, i] = total.astype(BF16)
+            if out_ref.ndim == 4:
+                out_ref[j, i] = total.astype(out_ref.dtype)
+            else:
+                part = out_ref.shape[-1]
+                for t in range(out_ref.shape[0]):
+                    out_ref[t, j, i] = total[:, t * part : (t + 1) * part].astype(out_ref.dtype)
 
 
 def place_kernel(kept, steps, here, *refs):
-    per_pair = 2 * steps
-    sources, out_ref = refs[: SIDE * per_pair], refs[-1]
+    sources, out_ref = refs[:-1], refs[-1]
     share = sources[0].shape[2]
     tp_me, rank = here[0], here[1]
     for slot in range(kept):
         step = here[2 + slot]
-        for pair in range(SIDE):
-            mine = sources[pair * per_pair : (pair + 1) * per_pair]
-            for near in range(SIDE):
-                piece = rank ^ (SIDE * pair + near)
-                for t in range(SIDE):
-                    start = ((slot * SLAB + piece) * SIDE + t) * share
-                    target = pl.ds(pl.multiple_of(start, share), share)
-                    own = jnp.logical_and(step == 0, tp_me == t)
-                    moved = jnp.logical_and(step == 0, tp_me != t)
-                    choices = [(own, mine[0]), (moved, mine[1])]
-                    choices += [(step == k, mine[2 * k + t]) for k in range(1, steps)]
-                    for chosen, source in choices:
-                        index = near if source.shape[0] == SIDE else SIDE * pair + near
-
-                        @pl.when(chosen)
-                        def _(source=source, index=index, target=target):
-                            out_ref[:, target] = source[index]
+        for t in range(SIDE):
+            own = jnp.logical_and(step == 0, tp_me == t)
+            moved = jnp.logical_and(step == 0, tp_me != t)
+            choices = [(own, sources[0]), (moved, sources[1])]
+            choices += [(step == k, sources[2 * k + t]) for k in range(1, steps)]
+            for chosen, source in choices:
+
+                @pl.when(chosen)
+                def _(source=source, slot=slot, t=t):
+                    for piece in range(SLAB):
+                        start = ((slot * SLAB + (rank ^ piece)) * SIDE + t) * share
+                        out_ref[:, pl.ds(pl.multiple_of(start, share), share)] = source[piece]
 
 
 def ring_order(count):
@@ -435,23 +434,38 @@
             count,
         )(here, query, local, *rates, *incoming)
 
-    def project(blocks, sources, picks, share_index):
-        scalars = jnp.stack([share_index, rank ^ 2, rank ^ 3]).astype(jnp.int32)
+    def project(blocks, sources, picks, share_index, partial=None, halves=(0, 1)):
+        scalars = jnp.stack([share_index if share_index is not None else 0, rank ^ 2, rank ^ 3])
+        run = depth // SIDE
+        wide_share = columns if share_index is None else share
+        shape = (len(blocks), len(picks), tokens, share)
+        if share_index is None:
+            out = jax.ShapeDtypeStruct((tp, *shape), F32)
+        else:
+            out = jax.ShapeDtypeStruct(shape, BF16)
         return pl.pallas_call(
-            functools.partial(project_kernel, len(blocks), picks),
+            functools.partial(
+                project_kernel, len(blocks), picks, halves[0] * run, partial is not None
+            ),
             in_specs=[smem]
-            + [vmem] * (SIDE * len(blocks))
-            + [pl.BlockSpec(memory_space=pltpu.HBM)] * len(sources),
+            + [vmem] * (len(halves) * len(blocks))
+            + [pl.BlockSpec(memory_space=pltpu.HBM)] * len(sources)
+            + ([vmem] if partial is not None else []),
             out_specs=vmem,
-            out_shape=jax.ShapeDtypeStruct((len(blocks), len(picks), tokens, share), BF16),
+            out_shape=out,
             scratch_shapes=[
-                pltpu.VMEM((len(picks), depth, share), BF16),
+                pltpu.VMEM((len(picks), len(halves) * run, wide_share), BF16),
                 pltpu.SemaphoreType.DMA((len(picks),)),
             ],
             compiler_params=large,
             cost_estimate=light,
             name="project_block",
-        )(scalars, *[h for b in blocks for h in b], *sources)
+        )(
+            scalars.astype(jnp.int32),
+            *[b[h] for b in blocks for h in halves],
+            *sources,
+            *([partial] if partial is not None else []),
+        )
 
     def project_away(blocks, sources, picks):
         away = project(blocks, sources, picks, 1 - tp_me)
@@ -489,30 +503,35 @@
         ((0, None), (1, None), (2, 1), (2, 2)),
     )
     blocks = [[gated_half(h) for h in range(SIDE)]]
-    arrived = [[], []]
+    sums = []
     for step in range(slabs - 1):
         if step:
-            blocks[step], summed, arrived[0] = lax.optimization_barrier(
-                (blocks[step], summed, arrived[0])
-            )
-            arrived[0] += deliver(summed, step - 1)
+            blocks[step], summed = lax.optimization_barrier((blocks[step], summed))
+            sums.append(summed)
         blocks.append([ring(h) for h in blocks[step]])
         away, got = project_away([blocks[step]], [out_weight, beside], near)
         mine = project_mine([blocks[step]], [out_weight, beside], near, away)
         summed = total(mine, got)[0]
-    slab_weights, summed = lax.optimization_barrier((slab_weights, summed))
+    slab_weights, _ = lax.optimization_barrier((slab_weights, mine))
+    earlier_mine, earlier_got = mine, got
     away, got = project_away(blocks[: slabs - 1], [slab_weights], far)
     mine = project_mine(blocks[: slabs - 1], [slab_weights], far, away)
-    block, _ = lax.optimization_barrier((blocks[-1], mine))
     sources = [out_weight, beside, slab_weights]
-    last_away, last_got = project_away([block], sources, both)
-    last_mine = project_mine([block], sources, both, last_away)
+    head, _ = lax.optimization_barrier((blocks[-1][0], mine))
+    partial = project([[head]], sources, both, None, None, (0,))
+    tail, partial, got, earlier_got = lax.optimization_barrier(
+        (blocks[-1][1], partial, got, earlier_got)
+    )
+    sums.append(total(earlier_mine, earlier_got)[0])
+    last_away = project([[None, tail]], sources, both, 1 - tp_me, partial, (1,))
+    last_got = lax.ppermute(last_away, "tp", [(0, 1), (1, 0)])
+    tail, _ = lax.optimization_barrier((tail, last_away))
+    last_mine = project([[None, tail]], sources, both, tp_me, partial, (1,))
     batch = total(mine, got)
-    for step in range(slabs - 2):
-        arrived[1] += deliver(batch[step], step)
-    late = deliver(jnp.concatenate([summed, batch[slabs - 2]]), slabs - 2)
-    late += deliver(total(last_mine, last_got)[0], slabs - 1)
-    arrived = [a + late for a in arrived]
+    arrived = []
+    for step in range(slabs - 1):
+        arrived += deliver(jnp.concatenate([sums[step], batch[step]]), step)
+    arrived += deliver(total(last_mine, last_got)[0], slabs - 1)
 
     def place_of(z):
         return sum(jnp.where(z == k, place[k], 0) for k in range(slabs))
@@ -523,13 +542,13 @@
     ]
     return pl.pallas_call(
         functools.partial(place_kernel, kept, slabs),
-        in_specs=[smem] + [vmem] * (SIDE * 2 * slabs),
+        in_specs=[smem] + [vmem] * (SIDE * slabs),
         out_specs=vmem,
         out_shape=jax.ShapeDtypeStruct((tokens, width), BF16),
         compiler_params=limit,
         cost_estimate=light,
         name="place_columns",
-    )(jnp.stack([tp_me, rank, *steps]).astype(jnp.int32), *arrived[0], *arrived[1])
+    )(jnp.stack([tp_me, rank, *steps]).astype(jnp.int32), *arrived)
 
 
 def solution(mesh):

time: 196 us -> 190 us (0.969)
  the two profiles are of different devices: /device:TPU:0 before, /device:TPU:4 now
where the time goes in v1:
time: 190 us
  waiting for transfers between devices  62.3 us (33%)
  Pallas kernels  59.3 us (31%)
  starting transfers between devices  47.1 us (25%)
  between operations  14 us (7%)
  local copies, waits for them, and re-layouts  5.67 us (3%)
    pallas_call x11, Pallas kernels, project(): pl.pallas_call(functools.partial(project_kernel, len(blocks), picks, halv...  39.4 us
    ppermute x6, waiting for transfers between devices, ring(): return lax.ppermute(array, 'ctx', pairs)  30.5 us
    ppermute x6, starting transfers between devices, deliver(): return [lax.ppermute(summed, ('ctx', 'tp'), moves) for moves in pairs]  15.8 us
    ppermute x6, waiting for transfers between devices, deliver(): return [lax.ppermute(summed, ('ctx', 'tp'), moves) for moves in pairs]  14.7 us
    ppermute x3, starting transfers between devices, per_device(): lax.ppermute(slab_left, 'ctx', [(i, i + by * SLAB) for i in range(ctx - b...  9.37 us
    ppermute x10, waiting for transfers between devices, within_slab(): return lax.ppermute(array, 'ctx', [(i, i ^ mask) for i in range(ctx)])  8.84 us
    ppermute x10, starting transfers between devices, within_slab(): return lax.ppermute(array, 'ctx', [(i, i ^ mask) for i in range(ctx)])  7.22 us
    pallas_call x1, Pallas kernels, per_device(): grouped(functools.partial(local_kernel, modes), 'local_convolution', [ser...  5.61 us
  transfers between devices with their start and end apart: 36, of which 16 were waited for; matrix products, arithmetic and copies ran while one was open for 1% of the time, Pallas kernels for 30%

profile of v1, /device:TPU:4, one launch (start us, length us, event | category | flops | bytes accessed | tf_op | source)
XLA Modules:
  0.0 189.7 jit_solution(8704582484059205947)
XLA Ops:
  22.5 3.3 %short_filters.1 = (f32[4,128,8,128]{3,2,1,0:T(8,128)S(1)}, f32[4,128,8,128]{3,2,1,0:T(8,128)S(1)}) custom-call(s32[3]{0:T(128)S(1)} %pad_add_fusion.1.here, bf16[3,128,4096]{2,1,0:T(8,128)(2,1)S(1)} %copy-done.2, bf16[3,2,4096]{2,1,0:T(2,128)(2,1)S(1)} %collective-permute-done.3.halo, f32[3,3,8192]{2,1,0:T(4,128)S(1)} %copy-done.3), custom_call_target="tpu_custom_call" | custom-call | flops 1 | bytes 1 | tf_op jit(solution)/shard_map/short_filters/pallas_call | solution.py:357
  27.6 3.1 %block_states.1 = (bf16[4,16,256]{2,1,0:T(8,128)(2,1)S(1)}, bf16[4,16,256]{2,1,0:T(8,128)(2,1)S(1)}, bf16[4,16,256]{2,1,0:T(8,128)(2,1)S(1)}, bf16[4,16,256]{2,1,0:T(8,128)(2,1)S(1)}) custom-call(s32[3]{0:T(128)S(1)} %pad_add_fusion.1.here, f32[4,128,8,128]{3,2,1,0:T(8,128)S(1)} %get-tuple-element.52.u_ref, ...), custom_call_target="tpu_custom_call" | custom-call | flops 1 | bytes 1 | tf_op jit(solution)/shard_map/block_states/pallas_call | solution.py:373
  32.7 3.4 %collective-permute-done.8.refs_2_ = bf16[4,16,256]{2,1,0:T(8,128)(2,1)S(1)} collective-permute-done((bf16[4,16,256]{2,1,0:T(8,128)(2,1)S(1)}, bf16[4,16,256]{2,1,0:T(8,128)(2,1)S(1)}, u32[]{:S(2)}, u32[]{:S(2)}) %collective-permute-start.8) | collective-permute-done | bytes 32800 | tf_op jit(solution)/shard_map/ppermute | solution.py:301
  37.0 5.6 %collective-permute-start.12 = (bf16[4,16,256]{2,1,0:T(8,128)(2,1)S(1)}, bf16[4,16,256]{2,1,0:T(8,128)(2,1)S(1)}, u32[]{:S(2)}, u32[]{:S(2)}) collective-permute-start(bf16[4,16,256]{2,1,0:T(8,128)(2,1)S(1)} %slab_states.1), channel_id=1, source_target_pairs={{0,24},{2,26},{4,28},{6,30},{1,25},{3,27},{5,29},{7,31}} | collective-permute-start | bytes 98312 | tf_op jit(solution)/shard_map/ppermute | solution.py:395
  46.4 5.6 %local_convolution.1.y_ref = f32[4,128,8,128]{3,2,1,0:T(8,128)S(1)} custom-call(s32[3]{0:T(128)S(1)} %pad_add_fusion.1.here, f32[4,128,8,128]{3,2,1,0:T(8,128)S(1)} %get-tuple-element.52.u_ref, f32[4,33,256]{2,1,0:T(8,128)S(1)} %pad_maximum_fusion.3.refs_0_.rates, f32[4,33,256]{2,1,0:T(8,128)S(1)} %collective-permute-done.5.refs_1_, ...), custom_call_target="tpu_custom_call" | custom-call | flops 1 | bytes 1 | tf_op jit(solution)/shard_map/local_convolution/pallas_call | solution.py:399
  54.8 3.1 %collective-permute-done.14.refs_6_ = bf16[4,16,256]{2,1,0:T(8,128)(2,1)S(1)} collective-permute-done((bf16[4,16,256]{2,1,0:T(8,128)(2,1)S(1)}, bf16[4,16,256]{2,1,0:T(8,128)(2,1)S(1)}, u32[]{:S(2)}, u32[]{:S(2)}) %collective-permute-start.14) | collective-permute-done | bytes 32800 | tf_op jit(solution)/shard_map/ppermute | solution.py:301
  66.2 3.0 %project_block.11 = bf16[1,2,128,256]{3,2,1,0:T(8,128)(2,1)S(1)} custom-call(s32[3]{0:T(128)S(1)} %add_add_fusion.1.here, bf16[128,2048]{1,0:T(8,128)(2,1)S(1)} %gated_block.2.refs_0_, bf16[128,2048]{1,0:T(8,128)(2,1)S(1)} %gated_block.3.refs_1_, bf16[4096,512]{1,0:T(8,128)(2,1)S(1)} %copy-done, bf16[4096,512]{1,0:T(8,128)(2,1)} %collective-permute-done.18.refs_3_.refs_2_), custom_call_target="tpu_custom_call" | custom-call | flops 1 | bytes 1 | tf_op jit(solution)/shard_map/project_block/pallas_call | solution.py:446
  69.8 3.0 %project_block.12 = bf16[1,2,128,256]{3,2,1,0:T(8,128)(2,1)S(1)} custom-call(s32[3]{0:T(128)S(1)} %add_add_fusion.here, bf16[128,2048]{1,0:T(8,128)(2,1)S(1)} %gated_block.2.refs_0_, bf16[128,2048]{1,0:T(8,128)(2,1)S(1)} %gated_block.3.refs_1_, bf16[4096,512]{1,0:T(8,128)(2,1)S(1)} %copy-done, bf16[4096,512]{1,0:T(8,128)(2,1)} %collective-permute-done.18.refs_3_.refs_2_), custom_call_target="tpu_custom_call" | custom-call | flops 1 | bytes 1 | tf_op jit(solution)/shard_map/project_block/pallas_call | solution.py:446
  76.8 11.0 %collective-permute-done.17.refs_1_.refs_3_ = bf16[128,2048]{1,0:T(8,128)(2,1)S(1)} collective-permute-done((bf16[128,2048]{1,0:T(8,128)(2,1)S(1)}, bf16[128,2048]{1,0:T(8,128)(2,1)S(1)}, u32[]{:S(2)}, u32[]{:S(2)}) %collective-permute-start.17) | collective-permute-done | bytes 524320 | tf_op jit(solution)/shard_map/ppermute | solution.py:311
  88.2 3.0 %project_block.13 = bf16[1,2,128,256]{3,2,1,0:T(8,128)(2,1)S(1)} custom-call(s32[3]{0:T(128)S(1)} %add_add_fusion.1.here, bf16[128,2048]{1,0:T(8,128)(2,1)S(1)} %collective-permute-done.16.refs_0_.refs_2_, bf16[128,2048]{1,0:T(8,128)(2,1)S(1)} %collective-permute-done.17.refs_1_.refs_3_, bf16[4096,512]{1,0:T(8,128)(2,1)S(1)} %copy-done, ...), custom_call_target="tpu_custom_call" | custom-call | flops 1 | bytes 1 | tf_op jit(solution)/shard_map/project_block/pallas_call | solution.py:446
  91.8 3.0 %project_block.14 = bf16[1,2,128,256]{3,2,1,0:T(8,128)(2,1)S(1)} custom-call(s32[3]{0:T(128)S(1)} %add_add_fusion.here, bf16[128,2048]{1,0:T(8,128)(2,1)S(1)} %collective-permute-done.16.refs_0_.refs_2_, bf16[128,2048]{1,0:T(8,128)(2,1)S(1)} %collective-permute-done.17.refs_1_.refs_3_, bf16[4096,512]{1,0:T(8,128)(2,1)S(1)} %copy-done, ...), custom_call_target="tpu_custom_call" | custom-call | flops 1 | bytes 1 | tf_op jit(solution)/shard_map/project_block/pallas_call | solution.py:446
  96.9 6.6 %collective-permute-done.20.refs_0_.refs_4_ = bf16[128,2048]{1,0:T(8,128)(2,1)S(1)} collective-permute-done((bf16[128,2048]{1,0:T(8,128)(2,1)S(1)}, bf16[128,2048]{1,0:T(8,128)(2,1)S(1)}, u32[]{:S(2)}, u32[]{:S(2)}) %collective-permute-start.20) | collective-permute-done | bytes 524320 | tf_op jit(solution)/shard_map/ppermute | solution.py:311
  103.5 10.1 %collective-permute-done.21.refs_1_.refs_5_ = bf16[128,2048]{1,0:T(8,128)(2,1)S(1)} collective-permute-done((bf16[128,2048]{1,0:T(8,128)(2,1)S(1)}, bf16[128,2048]{1,0:T(8,128)(2,1)S(1)}, u32[]{:S(2)}, u32[]{:S(2)}) %collective-permute-start.21) | collective-permute-done | bytes 524320 | tf_op jit(solution)/shard_map/ppermute | solution.py:311
  114.1 3.0 %project_block.15 = bf16[1,2,128,256]{3,2,1,0:T(8,128)(2,1)S(1)} custom-call(s32[3]{0:T(128)S(1)} %add_add_fusion.1.here, bf16[128,2048]{1,0:T(8,128)(2,1)S(1)} %collective-permute-done.20.refs_0_.refs_4_, bf16[128,2048]{1,0:T(8,128)(2,1)S(1)} %collective-permute-done.21.refs_1_.refs_5_, bf16[4096,512]{1,0:T(8,128)(2,1)S(1)} %copy-done, ...), custom_call_target="tpu_custom_call" | custom-call | flops 1 | bytes 1 | tf_op jit(solution)/shard_map/project_block/pallas_call | solution.py:446
  117.1 3.0 %project_block.16 = bf16[1,2,128,256]{3,2,1,0:T(8,128)(2,1)S(1)} custom-call(s32[3]{0:T(128)S(1)} %add_add_fusion.here, bf16[128,2048]{1,0:T(8,128)(2,1)S(1)} %collective-permute-done.20.refs_0_.refs_4_, bf16[128,2048]{1,0:T(8,128)(2,1)S(1)} %collective-permute-done.21.refs_1_.refs_5_, bf16[4096,512]{1,0:T(8,128)(2,1)S(1)} %copy-done, ...), custom_call_target="tpu_custom_call" | custom-call | flops 1 | bytes 1 | tf_op jit(solution)/shard_map/project_block/pallas_call | solution.py:446
  120.2 4.7 %project_block.17 = bf16[3,2,128,256]{3,2,1,0:T(8,128)(2,1)S(1)} custom-call(s32[3]{0:T(128)S(1)} %add_add_fusion.1.here, bf16[128,2048]{1,0:T(8,128)(2,1)S(1)} %gated_block.2.refs_0_, bf16[128,2048]{1,0:T(8,128)(2,1)S(1)} %gated_block.3.refs_1_, bf16[128,2048]{1,0:T(8,128)(2,1)S(1)} %collective-permute-done.16.refs_0_.refs_2_, ...), custom_call_target="tpu_custom_call" | custom-call | flops 1 | bytes 1 | tf_op jit(solution)/shard_map/project_block/pallas_call | solution.py:446
  127.0 4.9 %project_block.18 = bf16[3,2,128,256]{3,2,1,0:T(8,128)(2,1)S(1)} custom-call(s32[3]{0:T(128)S(1)} %add_add_fusion.here, bf16[128,2048]{1,0:T(8,128)(2,1)S(1)} %gated_block.2.refs_0_, bf16[128,2048]{1,0:T(8,128)(2,1)S(1)} %gated_block.3.refs_1_, bf16[128,2048]{1,0:T(8,128)(2,1)S(1)} %collective-permute-done.16.refs_0_.refs_2_, ...), custom_call_target="tpu_custom_call" | custom-call | flops 1 | bytes 1 | tf_op jit(solution)/shard_map/project_block/pallas_call | solution.py:446
  132.0 4.6 %project_block.19.refs_4_ = f32[2,1,4,128,256]{4,3,2,1,0:T(8,128)S(1)} custom-call(s32[3]{0:T(128)S(1)} %add_add_fusion.2.here, bf16[128,2048]{1,0:T(8,128)(2,1)} %collective-permute-done.24.refs_0_, bf16[4096,512]{1,0:T(8,128)(2,1)S(1)} %copy-done.1, bf16[4096,512]{1,0:T(8,128)(2,1)} %collective-permute-done.18.refs_3_.refs_2_, bf16[4,4096,512]{2,1,0:T(8,128)(2,1)} %bitcast.31), custom_call_target="tpu_custom_call" | custom-call | flops 1 | bytes 1 | tf_op jit(solution)/shard_map/project_block/pallas_call | solution.py:446
  139.0 3.3 %collective-permute-start.29 = (bf16[4,128,256]{2,1,0:T(8,128)(2,1)S(1)}, bf16[4,128,256]{2,1,0:T(8,128)(2,1)S(1)}, u32[]{:S(2)}, u32[]{:S(2)}) collective-permute-start(bf16[4,128,256]{2,1,0:T(8,128)(2,1)S(1)} %pad_maximum_fusion.1), channel_id=1, source_target_pairs={{1,16},{3,18},{5,20},{7,22},{9,0},{11,2},{13,4},{15,6},{17,25},{19... | collective-permute-start | bytes 786440 | tf_op jit(solution)/shard_map/ppermute | solution.py:493
  142.9 3.7 %project_block.20 = bf16[1,4,128,256]{3,2,1,0:T(8,128)(2,1)S(1)} custom-call(s32[3]{0:T(128)S(1)} %add_add_fusion.1.here, bf16[128,2048]{1,0:T(8,128)(2,1)} %collective-permute-done.23.refs_0_, bf16[4096,512]{1,0:T(8,128)(2,1)S(1)} %copy-done.1, bf16[4096,512]{1,0:T(8,128)(2,1)} %collective-permute-done.18.refs_3_.refs_2_, bf16[4,4096,512]{2,1,0:T(8,128)(2,1)} %bitcast.32, ...), custom_call_target="tpu_custom_call" | custom-call | flops 1 | bytes 1 | tf_op jit(solution)/shard_map/project_block/pallas_call | solution.py:446
  150.7 7.0 %collective-permute-start.31 = (bf16[4,128,256]{2,1,0:T(8,128)(2,1)S(1)}, bf16[4,128,256]{2,1,0:T(8,128)(2,1)S(1)}, u32[]{:S(2)}, u32[]{:S(2)}) collective-permute-start(bf16[4,128,256]{2,1,0:T(8,128)(2,1)S(1)} %pad_maximum_fusion.2), channel_id=1, source_target_pairs={{1,24},{3,26},{5,28},{7,30},{9,16},{11,18},{13,20},{15,22},{17,9},... | collective-permute-start | bytes 786440 | tf_op jit(solution)/shard_map/ppermute | solution.py:493
  157.7 3.7 %project_block.21 = bf16[1,4,128,256]{3,2,1,0:T(8,128)(2,1)S(1)} custom-call(s32[3]{0:T(128)S(1)} %add_add_fusion.here, bf16[128,2048]{1,0:T(8,128)(2,1)} %collective-permute-done.23.refs_0_, bf16[4096,512]{1,0:T(8,128)(2,1)S(1)} %copy-done.1, bf16[4096,512]{1,0:T(8,128)(2,1)} %collective-permute-done.18.refs_3_.refs_2_, bf16[4,4096,512]{2,1,0:T(8,128)(2,1)} %bitcast.33, ...), custom_call_target="tpu_custom_call" | custom-call | flops 1 | bytes 1 | tf_op jit(solution)/shard_map/project_block/pallas_call | solution.py:446
  166.5 8.7 %collective-permute-done.30.refs_4_ = bf16[4,128,256]{2,1,0:T(8,128)(2,1)S(1)} collective-permute-done((bf16[4,128,256]{2,1,0:T(8,128)(2,1)S(1)}, bf16[4,128,256]{2,1,0:T(8,128)(2,1)S(1)}, u32[]{:S(2)}, u32[]{:S(2)}) %collective-permute-start.30) | collective-permute-done | bytes 262176 | tf_op jit(solution)/shard_map/ppermute | solution.py:493
  175.2 6.0 %collective-permute-done.33.refs_6_ = bf16[4,128,256]{2,1,0:T(8,128)(2,1)S(1)} collective-permute-done((bf16[4,128,256]{2,1,0:T(8,128)(2,1)S(1)}, bf16[4,128,256]{2,1,0:T(8,128)(2,1)S(1)}, u32[]{:S(2)}, u32[]{:S(2)}) %collective-permute-start.33) | collective-permute-done | bytes 262176 | tf_op jit(solution)/shard_map/ppermute | solution.py:493
  (101 shorter events, 59.5 us)
Async XLA Ops:
  6.5 113.6 %all-gather.3.cloned.1.call-start = ((), (), s32[]{:S(2)}) async-start(), calls=%async_computation | async-start | bytes 20971520 | tf_op jit(solution)/shard_map/all_gather | solution.py:322
  7.3 56.7 %collective-permute-start.18 = (bf16[4096,512]{1,0:T(8,128)(2,1)}, bf16[4096,512]{1,0:T(8,128)(2,1)}, u32[]{:S(2)}, u32[]{:S(2)}) collective-permute-start(bf16[4096,512]{1,0:T(8,128)(2,1)} %refs_1_.5), channel_id=1, source_target_pairs={{0,2},{2,0},{4,6},{6,4},{8,10},{10,8},{12,14},{14,12},{16,18},{18,... | collective-permute-start | bytes 12582920 | tf_op jit(solution)/shard_map/ppermute | solution.py:301
  7.4 7.2 %collective-permute-start.1 = (f32[33,256]{1,0:T(8,128)S(1)}, f32[33,256]{1,0:T(8,128)S(1)}, u32[]{:S(2)}, u32[]{:S(2)}) collective-permute-start(f32[33,256]{1,0:T(8,128)S(1)} %get-tuple-element.95), channel_id=1, source_target_pairs={{0,16},{2,18},{4,20},{6,22},{8,24},{10,26},{12,28},{14,30},{16,0},... | collective-permute-start | bytes 101384 | tf_op jit(solution)/shard_map/ppermute | solution.py:304
  17.2 8.6 %collective-permute-start.4 = (f32[4,33,256]{2,1,0:T(8,128)S(1)}, f32[4,33,256]{2,1,0:T(8,128)S(1)}, u32[]{:S(2)}, u32[]{:S(2)}) collective-permute-start(f32[4,33,256]{2,1,0:T(8,128)S(1)} %pad_maximum_fusion.3.refs_0_.rates), channel_id=1, source_target_pairs={{0,4},{2,6},{4,0},{6,2},{8,12},{10,14},{12,8},{14,10},{16,20},{18,... | collective-permute-start | bytes 405512 | tf_op jit(solution)/shard_map/ppermute | solution.py:301
  20.0 6.3 %collective-permute-start.5 = (f32[4,33,256]{2,1,0:T(8,128)S(1)}, f32[4,33,256]{2,1,0:T(8,128)S(1)}, u32[]{:S(2)}, u32[]{:S(2)}) collective-permute-start(f32[4,33,256]{2,1,0:T(8,128)S(1)} %pad_maximum_fusion.3.refs_0_.rates), channel_id=1, source_target_pairs={{0,2},{2,0},{4,6},{6,4},{8,10},{10,8},{12,14},{14,12},{16,18},{18,... | collective-permute-start | bytes 405512 | tf_op jit(solution)/shard_map/ppermute | solution.py:301
  37.0 15.0 %collective-permute-start.12 = (bf16[4,16,256]{2,1,0:T(8,128)(2,1)S(1)}, bf16[4,16,256]{2,1,0:T(8,128)(2,1)S(1)}, u32[]{:S(2)}, u32[]{:S(2)}) collective-permute-start(bf16[4,16,256]{2,1,0:T(8,128)(2,1)S(1)} %slab_states.1), channel_id=1, source_target_pairs={{0,24},{2,26},{4,28},{6,30},{1,25},{3,27},{5,29},{7,31}} | collective-permute-start | bytes 98312 | tf_op jit(solution)/shard_map/ppermute | solution.py:395
  42.6 9.4 %collective-permute-start.11 = (bf16[4,16,256]{2,1,0:T(8,128)(2,1)S(1)}, bf16[4,16,256]{2,1,0:T(8,128)(2,1)S(1)}, u32[]{:S(2)}, u32[]{:S(2)}) collective-permute-start(bf16[4,16,256]{2,1,0:T(8,128)(2,1)S(1)} %slab_states.1), channel_id=1, source_target_pairs={{0,16},{2,18},{4,20},{6,22},{8,24},{10,26},{12,28},{14,30},{1,17},... | collective-permute-start | bytes 98312 | tf_op jit(solution)/shard_map/ppermute | solution.py:395
  43.9 8.1 %collective-permute-start.10 = (bf16[4,16,256]{2,1,0:T(8,128)(2,1)S(1)}, bf16[4,16,256]{2,1,0:T(8,128)(2,1)S(1)}, u32[]{:S(2)}, u32[]{:S(2)}) collective-permute-start(bf16[4,16,256]{2,1,0:T(8,128)(2,1)S(1)} %slab_states.1), channel_id=1, source_target_pairs={{0,8},{2,10},{4,12},{6,14},{8,16},{10,18},{12,20},{14,22},{16,24},... | collective-permute-start | bytes 98312 | tf_op jit(solution)/shard_map/ppermute | solution.py:395
  61.1 15.7 %collective-permute-start.16 = (bf16[128,2048]{1,0:T(8,128)(2,1)S(1)}, bf16[128,2048]{1,0:T(8,128)(2,1)S(1)}, u32[]{:S(2)}, u32[]{:S(2)}) collective-permute-start(bf16[128,2048]{1,0:T(8,128)(2,1)S(1)} %gated_block.2.refs_0_), channel_id=1, source_target_pairs={{0,8},{2,10},{4,12},{6,14},{8,24},{10,26},{12,28},{14,30},{16,0},{... | collective-permute-start | bytes 1572872 | tf_op jit(solution)/shard_map/ppermute | solution.py:311
  63.8 24.0 %collective-permute-start.17 = (bf16[128,2048]{1,0:T(8,128)(2,1)S(1)}, bf16[128,2048]{1,0:T(8,128)(2,1)S(1)}, u32[]{:S(2)}, u32[]{:S(2)}) collective-permute-start(bf16[128,2048]{1,0:T(8,128)(2,1)S(1)} %gated_block.3.refs_1_), channel_id=1, source_target_pairs={{0,8},{2,10},{4,12},{6,14},{8,24},{10,26},{12,28},{14,30},{16,0},{... | collective-permute-start | bytes 1572872 | tf_op jit(solution)/shard_map/ppermute | solution.py:311
  87.8 15.7 %collective-permute-start.20 = (bf16[128,2048]{1,0:T(8,128)(2,1)S(1)}, bf16[128,2048]{1,0:T(8,128)(2,1)S(1)}, u32[]{:S(2)}, u32[]{:S(2)}) collective-permute-start(bf16[128,2048]{1,0:T(8,128)(2,1)S(1)} %collective-permute-done.16.refs_0_.refs_2_), channel_id=1, source_target_pairs={{0,8},{2,10},{4,12},{6,14},{8,24},{10,26},{12,28},{14,30},{16,0},{... | collective-permute-start | bytes 1572872 | tf_op jit(solution)/shard_map/ppermute | solution.py:311
  87.8 25.9 %collective-permute-start.21 = (bf16[128,2048]{1,0:T(8,128)(2,1)S(1)}, bf16[128,2048]{1,0:T(8,128)(2,1)S(1)}, u32[]{:S(2)}, u32[]{:S(2)}) collective-permute-start(bf16[128,2048]{1,0:T(8,128)(2,1)S(1)} %collective-permute-done.17.refs_1_.refs_3_), channel_id=1, source_target_pairs={{0,8},{2,10},{4,12},{6,14},{8,24},{10,26},{12,28},{14,30},{16,0},{... | collective-permute-start | bytes 1572872 | tf_op jit(solution)/shard_map/ppermute | solution.py:311
  113.7 18.3 %collective-permute-start.24 = (bf16[128,2048]{1,0:T(8,128)(2,1)S(1)}, bf16[128,2048]{1,0:T(8,128)(2,1)}, u32[]{:S(2)}, u32[]{:S(2)}) collective-permute-start(bf16[128,2048]{1,0:T(8,128)(2,1)S(1)} %collective-permute-done.20.refs_0_.refs_4_), channel_id=1, source_target_pairs={{0,8},{2,10},{4,12},{6,14},{8,24},{10,26},{12,28},{14,30},{16,0},{... | collective-permute-start | bytes 1572872 | tf_op jit(solution)/shard_map/ppermute | solution.py:311
  113.7 25.1 %collective-permute-start.23 = (bf16[128,2048]{1,0:T(8,128)(2,1)S(1)}, bf16[128,2048]{1,0:T(8,128)(2,1)}, u32[]{:S(2)}, u32[]{:S(2)}) collective-permute-start(bf16[128,2048]{1,0:T(8,128)(2,1)S(1)} %collective-permute-done.21.refs_1_.refs_5_), channel_id=1, source_target_pairs={{0,8},{2,10},{4,12},{6,14},{8,24},{10,26},{12,28},{14,30},{16,0},{... | collective-permute-start | bytes 1572872 | tf_op jit(solution)/shard_map/ppermute | solution.py:311
  124.8 13.9 %collective-permute-start.25 = (bf16[3,2,128,256]{3,2,1,0:T(8,128)(2,1)S(1)}, bf16[3,2,128,256]{3,2,1,0:T(8,128)(2,1)S(1)}, u32[]{:S(2)}, u32[]{:S(2)}) collective-permute-start(bf16[3,2,128,256]{3,2,1,0:T(8,128)(2,1)S(1)} %project_block.17), channel_id=1, source_target_pairs={{0,1},{1,0},{2,3},{3,2},{4,5},{5,4},{6,7},{7,6},{8,9},{9,8},{10,11... | collective-permute-start | bytes 1179656 | tf_op jit(solution)/shard_map/ppermute | solution.py:472
  125.4 12.3 %collective-permute-start.26 = (bf16[1,2,128,256]{3,2,1,0:T(8,128)(2,1)S(1)}, bf16[1,2,128,256]{3,2,1,0:T(8,128)(2,1)S(1)}, u32[]{:S(2)}, u32[]{:S(2)}) collective-permute-start(bf16[1,2,128,256]{3,2,1,0:T(8,128)(2,1)S(1)} %project_block.15), channel_id=1, source_target_pairs={{0,1},{1,0},{2,3},{3,2},{4,5},{5,4},{6,7},{7,6},{8,9},{9,8},{10,11... | collective-permute-start | bytes 393224 | tf_op jit(solution)/shard_map/ppermute | solution.py:472
  139.0 26.1 %collective-permute-start.29 = (bf16[4,128,256]{2,1,0:T(8,128)(2,1)S(1)}, bf16[4,128,256]{2,1,0:T(8,128)(2,1)S(1)}, u32[]{:S(2)}, u32[]{:S(2)}) collective-permute-start(bf16[4,128,256]{2,1,0:T(8,128)(2,1)S(1)} %pad_maximum_fusion.1), channel_id=1, source_target_pairs={{1,16},{3,18},{5,20},{7,22},{9,0},{11,2},{13,4},{15,6},{17,25},{19... | collective-permute-start | bytes 786440 | tf_op jit(solution)/shard_map/ppermute | solution.py:493
  142.2 24.3 %collective-permute-start.28 = (bf16[4,128,256]{2,1,0:T(8,128)(2,1)S(1)}, bf16[4,128,256]{2,1,0:T(8,128)(2,1)S(1)}, u32[]{:S(2)}, u32[]{:S(2)}) collective-permute-start(bf16[4,128,256]{2,1,0:T(8,128)(2,1)S(1)} %pad_maximum_fusion.1), channel_id=1, source_target_pairs={{0,16},{2,18},{4,20},{6,22},{8,0},{10,2},{12,4},{14,6},{16,25},{18... | collective-permute-start | bytes 786440 | tf_op jit(solution)/shard_map/ppermute | solution.py:493
  146.6 14.8 %collective-permute-start.32 = (bf16[1,4,128,256]{3,2,1,0:T(8,128)(2,1)S(1)}, bf16[1,4,128,256]{3,2,1,0:T(8,128)(2,1)S(1)}, u32[]{:S(2)}, u32[]{:S(2)}) collective-permute-start(bf16[1,4,128,256]{3,2,1,0:T(8,128)(2,1)S(1)} %project_block.20), channel_id=1, source_target_pairs={{0,1},{1,0},{2,3},{3,2},{4,5},{5,4},{6,7},{7,6},{8,9},{9,8},{10,11... | collective-permute-start | bytes 786440 | tf_op jit(solution)/shard_map/ppermute | solution.py:527
  147.8 14.9 %collective-permute-start.27 = (bf16[4,128,256]{2,1,0:T(8,128)(2,1)S(1)}, bf16[4,128,256]{2,1,0:T(8,128)(2,1)S(1)}, u32[]{:S(2)}, u32[]{:S(2)}) collective-permute-start(bf16[4,128,256]{2,1,0:T(8,128)(2,1)S(1)} %pad_maximum_fusion.refs_0_), channel_id=1, source_target_pairs={{16,17},{18,19},{20,21},{22,23},{24,25},{26,27},{28,29},{30,31},{1... | collective-permute-start | bytes 786440 | tf_op jit(solution)/shard_map/ppermute | solution.py:492
  150.7 15.8 %collective-permute-start.31 = (bf16[4,128,256]{2,1,0:T(8,128)(2,1)S(1)}, bf16[4,128,256]{2,1,0:T(8,128)(2,1)S(1)}, u32[]{:S(2)}, u32[]{:S(2)}) collective-permute-start(bf16[4,128,256]{2,1,0:T(8,128)(2,1)S(1)} %pad_maximum_fusion.2), channel_id=1, source_target_pairs={{1,24},{3,26},{5,28},{7,30},{9,16},{11,18},{13,20},{15,22},{17,9},... | collective-permute-start | bytes 786440 | tf_op jit(solution)/shard_map/ppermute | solution.py:493
  161.4 13.8 %collective-permute-start.30 = (bf16[4,128,256]{2,1,0:T(8,128)(2,1)S(1)}, bf16[4,128,256]{2,1,0:T(8,128)(2,1)S(1)}, u32[]{:S(2)}, u32[]{:S(2)}) collective-permute-start(bf16[4,128,256]{2,1,0:T(8,128)(2,1)S(1)} %pad_maximum_fusion.2), channel_id=1, source_target_pairs={{0,24},{2,26},{4,28},{6,30},{8,16},{10,18},{12,20},{14,22},{16,9},... | collective-permute-start | bytes 786440 | tf_op jit(solution)/shard_map/ppermute | solution.py:493
  162.8 12.5 %collective-permute-start.34 = (bf16[4,128,256]{2,1,0:T(8,128)(2,1)S(1)}, bf16[4,128,256]{2,1,0:T(8,128)(2,1)S(1)}, u32[]{:S(2)}, u32[]{:S(2)}) collective-permute-start(bf16[4,128,256]{2,1,0:T(8,128)(2,1)S(1)} %fusion), channel_id=1, source_target_pairs={{1,8},{3,10},{5,12},{7,14},{9,24},{11,26},{13,28},{15,30},{17,1},{... | collective-permute-start | bytes 786440 | tf_op jit(solution)/shard_map/ppermute | solution.py:493
  165.1 16.2 %collective-permute-start.33 = (bf16[4,128,256]{2,1,0:T(8,128)(2,1)S(1)}, bf16[4,128,256]{2,1,0:T(8,128)(2,1)S(1)}, u32[]{:S(2)}, u32[]{:S(2)}) collective-permute-start(bf16[4,128,256]{2,1,0:T(8,128)(2,1)S(1)} %fusion), channel_id=1, source_target_pairs={{0,8},{2,10},{4,12},{6,14},{8,24},{10,26},{12,28},{14,30},{16,1},{... | collective-permute-start | bytes 786440 | tf_op jit(solution)/shard_map/ppermute | solution.py:493
  (20 other events, 82.5 us)
Sparse Core Ops, SparseCore 0:
  8.9 109.9 all-gather.2

commit v2 on v1

--- a/solution.py
+++ b/solution.py
@@ -503,34 +503,36 @@
         ((0, None), (1, None), (2, 1), (2, 2)),
     )
     blocks = [[gated_half(h) for h in range(SIDE)]]
-    sums = []
+    kept_parts, got_parts = [], []
+    mine = None
     for step in range(slabs - 1):
+        first, second = block = blocks[step]
         if step:
-            blocks[step], summed = lax.optimization_barrier((blocks[step], summed))
-            sums.append(summed)
-        blocks.append([ring(h) for h in blocks[step]])
-        away, got = project_away([blocks[step]], [out_weight, beside], near)
-        mine = project_mine([blocks[step]], [out_weight, beside], near, away)
-        summed = total(mine, got)[0]
-    slab_weights, _ = lax.optimization_barrier((slab_weights, mine))
-    earlier_mine, earlier_got = mine, got
+            second, mine = lax.optimization_barrier((second, mine))
+            block, _ = lax.optimization_barrier((block, mine))
+        if step > 1:
+            block, _ = lax.optimization_barrier((block, got_parts[: step - 1]))
+        blocks.append([ring(first), ring(second)])
+        away, got = project_away([block], [out_weight, beside], near)
+        mine = project_mine([block], [out_weight, beside], near, away)
+        kept_parts.append(mine)
+        got_parts.append(got)
+    slab_weights, _ = lax.optimization_barrier((slab_weights, (mine, got_parts[:-1])))
     away, got = project_away(blocks[: slabs - 1], [slab_weights], far)
     mine = project_mine(blocks[: slabs - 1], [slab_weights], far, away)
     sources = [out_weight, beside, slab_weights]
     head, _ = lax.optimization_barrier((blocks[-1][0], mine))
     partial = project([[head]], sources, both, None, None, (0,))
-    tail, partial, got, earlier_got = lax.optimization_barrier(
-        (blocks[-1][1], partial, got, earlier_got)
-    )
-    sums.append(total(earlier_mine, earlier_got)[0])
+    tail, partial = lax.optimization_barrier((blocks[-1][1], partial))
     last_away = project([[None, tail]], sources, both, 1 - tp_me, partial, (1,))
     last_got = lax.ppermute(last_away, "tp", [(0, 1), (1, 0)])
-    tail, _ = lax.optimization_barrier((tail, last_away))
+    tail, got, got_parts, _ = lax.optimization_barrier((tail, got, got_parts, last_away))
     last_mine = project([[None, tail]], sources, both, tp_me, partial, (1,))
     batch = total(mine, got)
     arrived = []
     for step in range(slabs - 1):
-        arrived += deliver(jnp.concatenate([sums[step], batch[step]]), step)
+        summed = total(kept_parts[step], got_parts[step])[0]
+        arrived += deliver(jnp.concatenate([summed, batch[step]]), step)
     arrived += deliver(total(last_mine, last_got)[0], slabs - 1)
 
     def place_of(z):

time: 190 us -> 196 us (1.032)
  the two profiles are of different devices: /device:TPU:4 before, /device:TPU:0 now
where the time goes in v2:
time: 196 us; the launch traced here: 195 us
  waiting for transfers between devices  66.7 us (34%)
  Pallas kernels  59.3 us (30%)
  starting transfers between devices  46.9 us (24%)
  between operations  14 us (7%)
  local copies, waits for them, and re-layouts  6.24 us (3%)
    pallas_call x11, Pallas kernels, project(): pl.pallas_call(functools.partial(project_kernel, len(blocks), picks, halv...  39.4 us
    ppermute x6, waiting for transfers between devices, ring(): return lax.ppermute(array, 'ctx', pairs)  32 us
    ppermute x6, starting transfers between devices, deliver(): return [lax.ppermute(summed, ('ctx', 'tp'), moves) for moves in pairs]  16.2 us
    ppermute x4, waiting for transfers between devices, project_away(): return (away, lax.ppermute(away, 'tp', [(0, 1), (1, 0)]))  11.6 us
    ppermute x10, waiting for transfers between devices, within_slab(): return lax.ppermute(array, 'ctx', [(i, i ^ mask) for i in range(ctx)])  10.7 us
    ppermute x10, starting transfers between devices, within_slab(): return lax.ppermute(array, 'ctx', [(i, i ^ mask) for i in range(ctx)])  8.97 us
    ppermute x3, starting transfers between devices, from_slab(): lax.ppermute(array, 'ctx', [(i, (i - by * SLAB) % ctx) for i in range(ctx)])  7.52 us
    ppermute x6, waiting for transfers between devices, deliver(): return [lax.ppermute(summed, ('ctx', 'tp'), moves) for moves in pairs]  6.53 us
  transfers between devices with their start and end apart: 36, of which 16 were waited for; matrix products, arithmetic and copies ran while one was open for 1% of the time, Pallas kernels for 30%

profile of v2, /device:TPU:0, one launch (start us, length us, event | category | flops | bytes accessed | tf_op | source)
XLA Modules:
  0.0 194.8 jit_solution(7194817736360715455)
XLA Ops:
  7.8 3.7 %collective-permute-start.1 = (f32[33,256]{1,0:T(8,128)S(1)}, f32[33,256]{1,0:T(8,128)S(1)}, u32[]{:S(2)}, u32[]{:S(2)}) collective-permute-start(f32[33,256]{1,0:T(8,128)S(1)} %get-tuple-element.103), channel_id=1, source_target_pairs={{0,16},{2,18},{4,20},{6,22},{8,24},{10,26},{12,28},{14,30},{16,0},... | collective-permute-start | bytes 101384 | tf_op jit(solution)/shard_map/ppermute | solution.py:304
  18.7 4.5 %collective-permute-start.4 = (f32[4,33,256]{2,1,0:T(8,128)S(1)}, f32[4,33,256]{2,1,0:T(8,128)S(1)}, u32[]{:S(2)}, u32[]{:S(2)}) collective-permute-start(f32[4,33,256]{2,1,0:T(8,128)S(1)} %pad_maximum_fusion.3.refs_0_.rates), channel_id=1, source_target_pairs={{0,4},{2,6},{4,0},{6,2},{8,12},{10,14},{12,8},{14,10},{16,20},{18,... | collective-permute-start | bytes 405512 | tf_op jit(solution)/shard_map/ppermute | solution.py:301
  25.7 3.3 %short_filters.1 = (f32[4,128,8,128]{3,2,1,0:T(8,128)S(1)}, f32[4,128,8,128]{3,2,1,0:T(8,128)S(1)}) custom-call(s32[3]{0:T(128)S(1)} %pad_add_fusion.1.here, bf16[3,128,4096]{2,1,0:T(8,128)(2,1)S(1)} %copy-done.2, bf16[3,2,4096]{2,1,0:T(2,128)(2,1)S(1)} %collective-permute-done.3.halo, f32[3,3,8192]{2,1,0:T(4,128)S(1)} %copy-done.3), custom_call_target="tpu_custom_call" | custom-call | flops 1 | bytes 1 | tf_op jit(solution)/shard_map/short_filters/pallas_call | solution.py:357
  31.5 3.1 %block_states.1 = (bf16[4,16,256]{2,1,0:T(8,128)(2,1)S(1)}, bf16[4,16,256]{2,1,0:T(8,128)(2,1)S(1)}, bf16[4,16,256]{2,1,0:T(8,128)(2,1)S(1)}, bf16[4,16,256]{2,1,0:T(8,128)(2,1)S(1)}) custom-call(s32[3]{0:T(128)S(1)} %pad_add_fusion.1.here, f32[4,128,8,128]{3,2,1,0:T(8,128)S(1)} %get-tuple-element.56.u_ref, ...), custom_call_target="tpu_custom_call" | custom-call | flops 1 | bytes 1 | tf_op jit(solution)/shard_map/block_states/pallas_call | solution.py:373
  46.5 5.6 %local_convolution.1.y_ref = f32[4,128,8,128]{3,2,1,0:T(8,128)S(1)} custom-call(s32[3]{0:T(128)S(1)} %pad_add_fusion.1.here, f32[4,128,8,128]{3,2,1,0:T(8,128)S(1)} %get-tuple-element.56.u_ref, f32[4,33,256]{2,1,0:T(8,128)S(1)} %pad_maximum_fusion.3.refs_0_.rates, f32[4,33,256]{2,1,0:T(8,128)S(1)} %collective-permute-done.5.refs_1_, ...), custom_call_target="tpu_custom_call" | custom-call | flops 1 | bytes 1 | tf_op jit(solution)/shard_map/local_convolution/pallas_call | solution.py:399
  54.9 3.1 %collective-permute-done.14.refs_6_ = bf16[4,16,256]{2,1,0:T(8,128)(2,1)S(1)} collective-permute-done((bf16[4,16,256]{2,1,0:T(8,128)(2,1)S(1)}, bf16[4,16,256]{2,1,0:T(8,128)(2,1)S(1)}, u32[]{:S(2)}, u32[]{:S(2)}) %collective-permute-start.14) | collective-permute-done | bytes 32800 | tf_op jit(solution)/shard_map/ppermute | solution.py:301
  64.4 12.5 %collective-permute-done.19.refs_0_.refs_2_ = bf16[128,2048]{1,0:T(8,128)(2,1)S(1)} collective-permute-done((bf16[128,2048]{1,0:T(8,128)(2,1)S(1)}, bf16[128,2048]{1,0:T(8,128)(2,1)S(1)}, u32[]{:S(2)}, u32[]{:S(2)}) %collective-permute-start.19) | collective-permute-done | bytes 524320 | tf_op jit(solution)/shard_map/ppermute | solution.py:311
  79.1 3.0 %project_block.11 = bf16[1,2,128,256]{3,2,1,0:T(8,128)(2,1)S(1)} custom-call(s32[3]{0:T(128)S(1)} %add_add_fusion.1.here, bf16[128,2048]{1,0:T(8,128)(2,1)S(1)} %gated_block.2.refs_0_, bf16[128,2048]{1,0:T(8,128)(2,1)S(1)} %gated_block.3.refs_1_, bf16[4096,512]{1,0:T(8,128)(2,1)S(1)} %copy-done, bf16[4096,512]{1,0:T(8,128)(2,1)} %collective-permute-done.16.refs_3_.refs_2_), custom_call_target="tpu_custom_call" | custom-call | flops 1 | bytes 1 | tf_op jit(solution)/shard_map/project_block/pallas_call | solution.py:446
  82.1 3.0 %project_block.12 = bf16[1,2,128,256]{3,2,1,0:T(8,128)(2,1)S(1)} custom-call(s32[3]{0:T(128)S(1)} %add_add_fusion.here, bf16[128,2048]{1,0:T(8,128)(2,1)S(1)} %gated_block.2.refs_0_, bf16[128,2048]{1,0:T(8,128)(2,1)S(1)} %gated_block.3.refs_1_, bf16[4096,512]{1,0:T(8,128)(2,1)S(1)} %copy-done, bf16[4096,512]{1,0:T(8,128)(2,1)} %collective-permute-done.16.refs_3_.refs_2_), custom_call_target="tpu_custom_call" | custom-call | flops 1 | bytes 1 | tf_op jit(solution)/shard_map/project_block/pallas_call | solution.py:446
  85.1 3.1 %collective-permute-done.17.refs_1_.refs_3_ = bf16[128,2048]{1,0:T(8,128)(2,1)S(1)} collective-permute-done((bf16[128,2048]{1,0:T(8,128)(2,1)S(1)}, bf16[128,2048]{1,0:T(8,128)(2,1)S(1)}, u32[]{:S(2)}, u32[]{:S(2)}) %collective-permute-start.17) | collective-permute-done | bytes 524320 | tf_op jit(solution)/shard_map/ppermute | solution.py:311
  88.2 11.2 %collective-permute-done.21.refs_0_.refs_4_ = bf16[128,2048]{1,0:T(8,128)(2,1)S(1)} collective-permute-done((bf16[128,2048]{1,0:T(8,128)(2,1)S(1)}, bf16[128,2048]{1,0:T(8,128)(2,1)S(1)}, u32[]{:S(2)}, u32[]{:S(2)}) %collective-permute-start.21) | collective-permute-done | bytes 524320 | tf_op jit(solution)/shard_map/ppermute | solution.py:311
  105.4 5.3 %collective-permute-done.18.refs_1_.refs_5_ = bf16[128,2048]{1,0:T(8,128)(2,1)S(1)} collective-permute-done((bf16[128,2048]{1,0:T(8,128)(2,1)S(1)}, bf16[128,2048]{1,0:T(8,128)(2,1)S(1)}, u32[]{:S(2)}, u32[]{:S(2)}) %collective-permute-start.18) | collective-permute-done | bytes 524320 | tf_op jit(solution)/shard_map/ppermute | solution.py:311
  112.7 4.4 %collective-permute-done.23 = bf16[1,2,128,256]{3,2,1,0:T(8,128)(2,1)S(1)} collective-permute-done((bf16[1,2,128,256]{3,2,1,0:T(8,128)(2,1)S(1)}, bf16[1,2,128,256]{3,2,1,0:T(8,128)(2,1)S(1)}, u32[]{:S(2)}, u32[]{:S(2)}) %collective-permute-start.23) | collective-permute-done | bytes 131104 | tf_op jit(solution)/shard_map/ppermute | solution.py:472
  123.7 4.7 %project_block.17 = bf16[3,2,128,256]{3,2,1,0:T(8,128)(2,1)S(1)} custom-call(s32[3]{0:T(128)S(1)} %add_add_fusion.1.here, bf16[128,2048]{1,0:T(8,128)(2,1)S(1)} %gated_block.2.refs_0_, bf16[128,2048]{1,0:T(8,128)(2,1)S(1)} %gated_block.3.refs_1_, bf16[128,2048]{1,0:T(8,128)(2,1)S(1)} %collective-permute-done.19.refs_0_.refs_2_, ...), custom_call_target="tpu_custom_call" | custom-call | flops 1 | bytes 1 | tf_op jit(solution)/shard_map/project_block/pallas_call | solution.py:446
  130.1 4.9 %project_block.18 = bf16[3,2,128,256]{3,2,1,0:T(8,128)(2,1)S(1)} custom-call(s32[3]{0:T(128)S(1)} %add_add_fusion.here, bf16[128,2048]{1,0:T(8,128)(2,1)S(1)} %gated_block.2.refs_0_, bf16[128,2048]{1,0:T(8,128)(2,1)S(1)} %gated_block.3.refs_1_, bf16[128,2048]{1,0:T(8,128)(2,1)S(1)} %collective-permute-done.19.refs_0_.refs_2_, ...), custom_call_target="tpu_custom_call" | custom-call | flops 1 | bytes 1 | tf_op jit(solution)/shard_map/project_block/pallas_call | solution.py:446
  135.0 4.5 %project_block.19.refs_4_ = f32[2,1,4,128,256]{4,3,2,1,0:T(8,128)S(1)} custom-call(s32[3]{0:T(128)S(1)} %add_add_fusion.2.here, bf16[128,2048]{1,0:T(8,128)(2,1)} %collective-permute-done.22.refs_0_, bf16[4096,512]{1,0:T(8,128)(2,1)S(1)} %copy-done.1, bf16[4096,512]{1,0:T(8,128)(2,1)} %collective-permute-done.16.refs_3_.refs_2_, bf16[4,4096,512]{2,1,0:T(8,128)(2,1)} %bitcast.31), custom_call_target="tpu_custom_call" | custom-call | flops 1 | bytes 1 | tf_op jit(solution)/shard_map/project_block/pallas_call | solution.py:446
  139.6 3.7 %project_block.20 = bf16[1,4,128,256]{3,2,1,0:T(8,128)(2,1)S(1)} custom-call(s32[3]{0:T(128)S(1)} %add_add_fusion.1.here, bf16[128,2048]{1,0:T(8,128)(2,1)} %collective-permute-done.20.refs_0_, bf16[4096,512]{1,0:T(8,128)(2,1)S(1)} %copy-done.1, bf16[4096,512]{1,0:T(8,128)(2,1)} %collective-permute-done.16.refs_3_.refs_2_, bf16[4,4096,512]{2,1,0:T(8,128)(2,1)} %bitcast.32, ...), custom_call_target="tpu_custom_call" | custom-call | flops 1 | bytes 1 | tf_op jit(solution)/shard_map/project_block/pallas_call | solution.py:446
  145.4 7.2 %collective-permute-done.26 = bf16[1,2,128,256]{3,2,1,0:T(8,128)(2,1)S(1)} collective-permute-done((bf16[1,2,128,256]{3,2,1,0:T(8,128)(2,1)S(1)}, bf16[1,2,128,256]{3,2,1,0:T(8,128)(2,1)S(1)}, u32[]{:S(2)}, u32[]{:S(2)}) %collective-permute-start.26) | collective-permute-done | bytes 131104 | tf_op jit(solution)/shard_map/ppermute | solution.py:472
  152.6 3.7 %project_block.21 = bf16[1,4,128,256]{3,2,1,0:T(8,128)(2,1)S(1)} custom-call(s32[3]{0:T(128)S(1)} %add_add_fusion.here, bf16[128,2048]{1,0:T(8,128)(2,1)} %collective-permute-done.20.refs_0_, bf16[4096,512]{1,0:T(8,128)(2,1)S(1)} %copy-done.1, bf16[4096,512]{1,0:T(8,128)(2,1)} %collective-permute-done.16.refs_3_.refs_2_, bf16[4,4096,512]{2,1,0:T(8,128)(2,1)} %bitcast.33, ...), custom_call_target="tpu_custom_call" | custom-call | flops 1 | bytes 1 | tf_op jit(solution)/shard_map/project_block/pallas_call | solution.py:446
  159.8 5.0 %collective-permute-start.30 = (bf16[4,128,256]{2,1,0:T(8,128)(2,1)S(1)}, bf16[4,128,256]{2,1,0:T(8,128)(2,1)S(1)}, u32[]{:S(2)}, u32[]{:S(2)}) collective-permute-start(bf16[4,128,256]{2,1,0:T(8,128)(2,1)S(1)} %pad_maximum_fusion.2), channel_id=1, source_target_pairs={{0,24},{2,26},{4,28},{6,30},{8,16},{10,18},{12,20},{14,22},{16,9},... | collective-permute-start | bytes 786440 | tf_op jit(solution)/shard_map/ppermute | solution.py:493
  166.4 6.1 %collective-permute-start.28 = (bf16[4,128,256]{2,1,0:T(8,128)(2,1)S(1)}, bf16[4,128,256]{2,1,0:T(8,128)(2,1)S(1)}, u32[]{:S(2)}, u32[]{:S(2)}) collective-permute-start(bf16[4,128,256]{2,1,0:T(8,128)(2,1)S(1)} %pad_maximum_fusion.1), channel_id=1, source_target_pairs={{0,16},{2,18},{4,20},{6,22},{8,0},{10,2},{12,4},{14,6},{16,25},{18... | collective-permute-start | bytes 786440 | tf_op jit(solution)/shard_map/ppermute | solution.py:493
  175.4 3.3 %collective-permute-done.28.refs_2_ = bf16[4,128,256]{2,1,0:T(8,128)(2,1)S(1)} collective-permute-done((bf16[4,128,256]{2,1,0:T(8,128)(2,1)S(1)}, bf16[4,128,256]{2,1,0:T(8,128)(2,1)S(1)}, u32[]{:S(2)}, u32[]{:S(2)}) %collective-permute-start.28) | collective-permute-done | bytes 262176 | tf_op jit(solution)/shard_map/ppermute | solution.py:493
  178.6 3.2 %collective-permute-done.29.refs_3_ = bf16[4,128,256]{2,1,0:T(8,128)(2,1)S(1)} collective-permute-done((bf16[4,128,256]{2,1,0:T(8,128)(2,1)S(1)}, bf16[4,128,256]{2,1,0:T(8,128)(2,1)S(1)}, u32[]{:S(2)}, u32[]{:S(2)}) %collective-permute-start.29) | collective-permute-done | bytes 262176 | tf_op jit(solution)/shard_map/ppermute | solution.py:493
  181.9 4.4 %collective-permute-done.27.refs_1_ = bf16[4,128,256]{2,1,0:T(8,128)(2,1)S(1)} collective-permute-done((bf16[4,128,256]{2,1,0:T(8,128)(2,1)S(1)}, bf16[4,128,256]{2,1,0:T(8,128)(2,1)S(1)}, u32[]{:S(2)}, u32[]{:S(2)}) %collective-permute-start.27) | collective-permute-done | bytes 262176 | tf_op jit(solution)/shard_map/ppermute | solution.py:492
  (107 shorter events, 64.5 us)
Async XLA Ops:
  6.5 117.2 %all-gather.3.cloned.1.call-start = ((), (), s32[]{:S(2)}) async-start(), calls=%async_computation | async-start | bytes 20971520 | tf_op jit(solution)/shard_map/all_gather | solution.py:322
  7.3 69.7 %collective-permute-start.16 = (bf16[4096,512]{1,0:T(8,128)(2,1)}, bf16[4096,512]{1,0:T(8,128)(2,1)}, u32[]{:S(2)}, u32[]{:S(2)}) collective-permute-start(bf16[4096,512]{1,0:T(8,128)(2,1)} %refs_1_.5), channel_id=1, source_target_pairs={{0,2},{2,0},{4,6},{6,4},{8,10},{10,8},{12,14},{14,12},{16,18},{18,... | collective-permute-start | bytes 12582920 | tf_op jit(solution)/shard_map/ppermute | solution.py:301
  7.8 10.0 %collective-permute-start.1 = (f32[33,256]{1,0:T(8,128)S(1)}, f32[33,256]{1,0:T(8,128)S(1)}, u32[]{:S(2)}, u32[]{:S(2)}) collective-permute-start(f32[33,256]{1,0:T(8,128)S(1)} %get-tuple-element.103), channel_id=1, source_target_pairs={{0,16},{2,18},{4,20},{6,22},{8,24},{10,26},{12,28},{14,30},{16,0},... | collective-permute-start | bytes 101384 | tf_op jit(solution)/shard_map/ppermute | solution.py:304
  18.7 11.2 %collective-permute-start.4 = (f32[4,33,256]{2,1,0:T(8,128)S(1)}, f32[4,33,256]{2,1,0:T(8,128)S(1)}, u32[]{:S(2)}, u32[]{:S(2)}) collective-permute-start(f32[4,33,256]{2,1,0:T(8,128)S(1)} %pad_maximum_fusion.3.refs_0_.rates), channel_id=1, source_target_pairs={{0,4},{2,6},{4,0},{6,2},{8,12},{10,14},{12,8},{14,10},{16,20},{18,... | collective-permute-start | bytes 405512 | tf_op jit(solution)/shard_map/ppermute | solution.py:301
  41.5 10.6 %collective-permute-start.10 = (bf16[4,16,256]{2,1,0:T(8,128)(2,1)S(1)}, bf16[4,16,256]{2,1,0:T(8,128)(2,1)S(1)}, u32[]{:S(2)}, u32[]{:S(2)}) collective-permute-start(bf16[4,16,256]{2,1,0:T(8,128)(2,1)S(1)} %slab_states.1), channel_id=1, source_target_pairs={{0,8},{2,10},{4,12},{6,14},{8,16},{10,18},{12,20},{14,22},{16,24},... | collective-permute-start | bytes 98312 | tf_op jit(solution)/shard_map/ppermute | solution.py:395
  42.8 9.3 %collective-permute-start.11 = (bf16[4,16,256]{2,1,0:T(8,128)(2,1)S(1)}, bf16[4,16,256]{2,1,0:T(8,128)(2,1)S(1)}, u32[]{:S(2)}, u32[]{:S(2)}) collective-permute-start(bf16[4,16,256]{2,1,0:T(8,128)(2,1)S(1)} %slab_states.1), channel_id=1, source_target_pairs={{0,16},{2,18},{4,20},{6,22},{8,24},{10,26},{12,28},{14,30},{1,17},... | collective-permute-start | bytes 98312 | tf_op jit(solution)/shard_map/ppermute | solution.py:395
  45.2 6.9 %collective-permute-start.12 = (bf16[4,16,256]{2,1,0:T(8,128)(2,1)S(1)}, bf16[4,16,256]{2,1,0:T(8,128)(2,1)S(1)}, u32[]{:S(2)}, u32[]{:S(2)}) collective-permute-start(bf16[4,16,256]{2,1,0:T(8,128)(2,1)S(1)} %slab_states.1), channel_id=1, source_target_pairs={{0,24},{2,26},{4,28},{6,30},{1,25},{3,27},{5,29},{7,31}} | collective-permute-start | bytes 98312 | tf_op jit(solution)/shard_map/ppermute | solution.py:395
  61.2 15.7 %collective-permute-start.19 = (bf16[128,2048]{1,0:T(8,128)(2,1)S(1)}, bf16[128,2048]{1,0:T(8,128)(2,1)S(1)}, u32[]{:S(2)}, u32[]{:S(2)}) collective-permute-start(bf16[128,2048]{1,0:T(8,128)(2,1)S(1)} %gated_block.2.refs_0_), channel_id=1, source_target_pairs={{0,8},{2,10},{4,12},{6,14},{8,24},{10,26},{12,28},{14,30},{16,0},{... | collective-permute-start | bytes 1572872 | tf_op jit(solution)/shard_map/ppermute | solution.py:311
  63.7 24.5 %collective-permute-start.17 = (bf16[128,2048]{1,0:T(8,128)(2,1)S(1)}, bf16[128,2048]{1,0:T(8,128)(2,1)S(1)}, u32[]{:S(2)}, u32[]{:S(2)}) collective-permute-start(bf16[128,2048]{1,0:T(8,128)(2,1)S(1)} %gated_block.3.refs_1_), channel_id=1, source_target_pairs={{0,8},{2,10},{4,12},{6,14},{8,24},{10,26},{12,28},{14,30},{16,0},{... | collective-permute-start | bytes 1572872 | tf_op jit(solution)/shard_map/ppermute | solution.py:311
  76.9 22.5 %collective-permute-start.21 = (bf16[128,2048]{1,0:T(8,128)(2,1)S(1)}, bf16[128,2048]{1,0:T(8,128)(2,1)S(1)}, u32[]{:S(2)}, u32[]{:S(2)}) collective-permute-start(bf16[128,2048]{1,0:T(8,128)(2,1)S(1)} %collective-permute-done.19.refs_0_.refs_2_), channel_id=1, source_target_pairs={{0,8},{2,10},{4,12},{6,14},{8,24},{10,26},{12,28},{14,30},{16,0},{... | collective-permute-start | bytes 1572872 | tf_op jit(solution)/shard_map/ppermute | solution.py:311
  88.2 22.5 %collective-permute-start.18 = (bf16[128,2048]{1,0:T(8,128)(2,1)S(1)}, bf16[128,2048]{1,0:T(8,128)(2,1)S(1)}, u32[]{:S(2)}, u32[]{:S(2)}) collective-permute-start(bf16[128,2048]{1,0:T(8,128)(2,1)S(1)} %collective-permute-done.17.refs_1_.refs_3_), channel_id=1, source_target_pairs={{0,8},{2,10},{4,12},{6,14},{8,24},{10,26},{12,28},{14,30},{16,0},{... | collective-permute-start | bytes 1572872 | tf_op jit(solution)/shard_map/ppermute | solution.py:311
  99.4 35.6 %collective-permute-start.22 = (bf16[128,2048]{1,0:T(8,128)(2,1)S(1)}, bf16[128,2048]{1,0:T(8,128)(2,1)}, u32[]{:S(2)}, u32[]{:S(2)}) collective-permute-start(bf16[128,2048]{1,0:T(8,128)(2,1)S(1)} %collective-permute-done.21.refs_0_.refs_4_), channel_id=1, source_target_pairs={{0,8},{2,10},{4,12},{6,14},{8,24},{10,26},{12,28},{14,30},{16,0},{... | collective-permute-start | bytes 1572872 | tf_op jit(solution)/shard_map/ppermute | solution.py:311
  110.6 29.0 %collective-permute-start.20 = (bf16[128,2048]{1,0:T(8,128)(2,1)S(1)}, bf16[128,2048]{1,0:T(8,128)(2,1)}, u32[]{:S(2)}, u32[]{:S(2)}) collective-permute-start(bf16[128,2048]{1,0:T(8,128)(2,1)S(1)} %collective-permute-done.18.refs_1_.refs_5_), channel_id=1, source_target_pairs={{0,8},{2,10},{4,12},{6,14},{8,24},{10,26},{12,28},{14,30},{16,0},{... | collective-permute-start | bytes 1572872 | tf_op jit(solution)/shard_map/ppermute | solution.py:311
  112.2 11.5 %collective-permute-start.24 = (bf16[1,2,128,256]{3,2,1,0:T(8,128)(2,1)S(1)}, bf16[1,2,128,256]{3,2,1,0:T(8,128)(2,1)}, u32[]{:S(2)}, u32[]{:S(2)}) collective-permute-start(bf16[1,2,128,256]{3,2,1,0:T(8,128)(2,1)S(1)} %project_block.13), channel_id=1, source_target_pairs={{0,1},{1,0},{2,3},{3,2},{4,5},{5,4},{6,7},{7,6},{8,9},{9,8},{10,11... | collective-permute-start | bytes 393224 | tf_op jit(solution)/shard_map/ppermute | solution.py:472
  128.4 24.2 %collective-permute-start.25 = (bf16[3,2,128,256]{3,2,1,0:T(8,128)(2,1)S(1)}, bf16[3,2,128,256]{3,2,1,0:T(8,128)(2,1)S(1)}, u32[]{:S(2)}, u32[]{:S(2)}) collective-permute-start(bf16[3,2,128,256]{3,2,1,0:T(8,128)(2,1)S(1)} %project_block.17), channel_id=1, source_target_pairs={{0,1},{1,0},{2,3},{3,2},{4,5},{5,4},{6,7},{7,6},{8,9},{9,8},{10,11... | collective-permute-start | bytes 1179656 | tf_op jit(solution)/shard_map/ppermute | solution.py:472
  143.3 12.9 %collective-permute-start.32 = (bf16[1,4,128,256]{3,2,1,0:T(8,128)(2,1)S(1)}, bf16[1,4,128,256]{3,2,1,0:T(8,128)(2,1)S(1)}, u32[]{:S(2)}, u32[]{:S(2)}) collective-permute-start(bf16[1,4,128,256]{3,2,1,0:T(8,128)(2,1)S(1)} %project_block.20), channel_id=1, source_target_pairs={{0,1},{1,0},{2,3},{3,2},{4,5},{5,4},{6,7},{7,6},{8,9},{9,8},{10,11... | collective-permute-start | bytes 786440 | tf_op jit(solution)/shard_map/ppermute | solution.py:528
  143.9 8.7 %collective-permute-start.26 = (bf16[1,2,128,256]{3,2,1,0:T(8,128)(2,1)S(1)}, bf16[1,2,128,256]{3,2,1,0:T(8,128)(2,1)S(1)}, u32[]{:S(2)}, u32[]{:S(2)}) collective-permute-start(bf16[1,2,128,256]{3,2,1,0:T(8,128)(2,1)S(1)} %copy-done.5), channel_id=1, source_target_pairs={{0,1},{1,0},{2,3},{3,2},{4,5},{5,4},{6,7},{7,6},{8,9},{9,8},{10,11... | collective-permute-start | bytes 393224 | tf_op jit(solution)/shard_map/ppermute | solution.py:472
  156.3 16.2 %collective-permute-start.33 = (bf16[4,128,256]{2,1,0:T(8,128)(2,1)S(1)}, bf16[4,128,256]{2,1,0:T(8,128)(2,1)S(1)}, u32[]{:S(2)}, u32[]{:S(2)}) collective-permute-start(bf16[4,128,256]{2,1,0:T(8,128)(2,1)S(1)} %fusion), channel_id=1, source_target_pairs={{0,8},{2,10},{4,12},{6,14},{8,24},{10,26},{12,28},{14,30},{16,1},{... | collective-permute-start | bytes 786440 | tf_op jit(solution)/shard_map/ppermute | solution.py:493
  158.9 15.0 %collective-permute-start.34 = (bf16[4,128,256]{2,1,0:T(8,128)(2,1)S(1)}, bf16[4,128,256]{2,1,0:T(8,128)(2,1)S(1)}, u32[]{:S(2)}, u32[]{:S(2)}) collective-permute-start(bf16[4,128,256]{2,1,0:T(8,128)(2,1)S(1)} %fusion), channel_id=1, source_target_pairs={{1,8},{3,10},{5,12},{7,14},{9,24},{11,26},{13,28},{15,30},{17,1},{... | collective-permute-start | bytes 786440 | tf_op jit(solution)/shard_map/ppermute | solution.py:493
  159.8 15.5 %collective-permute-start.30 = (bf16[4,128,256]{2,1,0:T(8,128)(2,1)S(1)}, bf16[4,128,256]{2,1,0:T(8,128)(2,1)S(1)}, u32[]{:S(2)}, u32[]{:S(2)}) collective-permute-start(bf16[4,128,256]{2,1,0:T(8,128)(2,1)S(1)} %pad_maximum_fusion.2), channel_id=1, source_target_pairs={{0,24},{2,26},{4,28},{6,30},{8,16},{10,18},{12,20},{14,22},{16,9},... | collective-permute-start | bytes 786440 | tf_op jit(solution)/shard_map/ppermute | solution.py:493
  164.8 10.6 %collective-permute-start.31 = (bf16[4,128,256]{2,1,0:T(8,128)(2,1)S(1)}, bf16[4,128,256]{2,1,0:T(8,128)(2,1)S(1)}, u32[]{:S(2)}, u32[]{:S(2)}) collective-permute-start(bf16[4,128,256]{2,1,0:T(8,128)(2,1)S(1)} %pad_maximum_fusion.2), channel_id=1, source_target_pairs={{1,24},{3,26},{5,28},{7,30},{9,16},{11,18},{13,20},{15,22},{17,9},... | collective-permute-start | bytes 786440 | tf_op jit(solution)/shard_map/ppermute | solution.py:493
  166.4 12.2 %collective-permute-start.28 = (bf16[4,128,256]{2,1,0:T(8,128)(2,1)S(1)}, bf16[4,128,256]{2,1,0:T(8,128)(2,1)S(1)}, u32[]{:S(2)}, u32[]{:S(2)}) collective-permute-start(bf16[4,128,256]{2,1,0:T(8,128)(2,1)S(1)} %pad_maximum_fusion.1), channel_id=1, source_target_pairs={{0,16},{2,18},{4,20},{6,22},{8,0},{10,2},{12,4},{14,6},{16,25},{18... | collective-permute-start | bytes 786440 | tf_op jit(solution)/shard_map/ppermute | solution.py:493
  172.6 9.3 %collective-permute-start.29 = (bf16[4,128,256]{2,1,0:T(8,128)(2,1)S(1)}, bf16[4,128,256]{2,1,0:T(8,128)(2,1)S(1)}, u32[]{:S(2)}, u32[]{:S(2)}) collective-permute-start(bf16[4,128,256]{2,1,0:T(8,128)(2,1)S(1)} %pad_maximum_fusion.1), channel_id=1, source_target_pairs={{1,16},{3,18},{5,20},{7,22},{9,0},{11,2},{13,4},{15,6},{17,25},{19... | collective-permute-start | bytes 786440 | tf_op jit(solution)/shard_map/ppermute | solution.py:493
  173.9 12.4 %collective-permute-start.27 = (bf16[4,128,256]{2,1,0:T(8,128)(2,1)S(1)}, bf16[4,128,256]{2,1,0:T(8,128)(2,1)S(1)}, u32[]{:S(2)}, u32[]{:S(2)}) collective-permute-start(bf16[4,128,256]{2,1,0:T(8,128)(2,1)S(1)} %pad_maximum_fusion.refs_0_), channel_id=1, source_target_pairs={{16,17},{18,19},{20,21},{22,23},{24,25},{26,27},{28,29},{30,31},{1... | collective-permute-start | bytes 786440 | tf_op jit(solution)/shard_map/ppermute | solution.py:492
  (23 other events, 104.8 us)
Sparse Core Ops, SparseCore 0:
  8.9 112.9 all-gather.2

commit v3 on v2

--- a/solution.py
+++ b/solution.py
@@ -504,35 +504,35 @@
     )
     blocks = [[gated_half(h) for h in range(SIDE)]]
     kept_parts, got_parts = [], []
-    mine = None
+    mine, got = None, None
     for step in range(slabs - 1):
         first, second = block = blocks[step]
         if step:
             second, mine = lax.optimization_barrier((second, mine))
             block, _ = lax.optimization_barrier((block, mine))
-        if step > 1:
-            block, _ = lax.optimization_barrier((block, got_parts[: step - 1]))
         blocks.append([ring(first), ring(second)])
-        away, got = project_away([block], [out_weight, beside], near)
-        mine = project_mine([block], [out_weight, beside], near, away)
+        away, coming = project_away([block], [out_weight, beside], near)
+        mine = project_mine([block], [out_weight, beside], near, (away, got))
+        got = coming
         kept_parts.append(mine)
         got_parts.append(got)
-    slab_weights, _ = lax.optimization_barrier((slab_weights, (mine, got_parts[:-1])))
-    away, got = project_away(blocks[: slabs - 1], [slab_weights], far)
-    mine = project_mine(blocks[: slabs - 1], [slab_weights], far, away)
+    slab_weights, _ = lax.optimization_barrier((slab_weights, mine))
+    away, batch_got = project_away(blocks[: slabs - 1], [slab_weights], far)
     sources = [out_weight, beside, slab_weights]
-    head, _ = lax.optimization_barrier((blocks[-1][0], mine))
+    head, _ = lax.optimization_barrier((blocks[-1][0], away))
     partial = project([[head]], sources, both, None, None, (0,))
-    tail, partial = lax.optimization_barrier((blocks[-1][1], partial))
+    tail = blocks[-1][1]
     last_away = project([[None, tail]], sources, both, 1 - tp_me, partial, (1,))
     last_got = lax.ppermute(last_away, "tp", [(0, 1), (1, 0)])
-    tail, got, got_parts, _ = lax.optimization_barrier((tail, got, got_parts, last_away))
-    last_mine = project([[None, tail]], sources, both, tp_me, partial, (1,))
-    batch = total(mine, got)
+    batch_mine = project_mine(blocks[: slabs - 1], [slab_weights], far, (last_away, got))
+    batch_got, got_parts, _ = lax.optimization_barrier((batch_got, got_parts, last_away))
+    batch = total(batch_mine, batch_got)
     arrived = []
     for step in range(slabs - 1):
         summed = total(kept_parts[step], got_parts[step])[0]
         arrived += deliver(jnp.concatenate([summed, batch[step]]), step)
+    tail, _ = lax.optimization_barrier((tail, (batch_mine, arrived[2])))
+    last_mine = project([[None, tail]], sources, both, tp_me, partial, (1,))
     arrived += deliver(total(last_mine, last_got)[0], slabs - 1)
 
     def place_of(z):

time: 196 us -> 187 us (0.954)
  the two profiles are of different devices: /device:TPU:0 before, /device:TPU:4 now
where the time goes in v3:
time: 187 us; the launch traced here: 186 us
  Pallas kernels  59.4 us (32%)
  waiting for transfers between devices  58.1 us (31%)
  starting transfers between devices  47.2 us (25%)
  between operations  14 us (7%)
  local copies, waits for them, and re-layouts  6.98 us (4%)
    pallas_call x11, Pallas kernels, project(): pl.pallas_call(functools.partial(project_kernel, len(blocks), picks, halv...  39.5 us
    ppermute x6, waiting for transfers between devices, ring(): return lax.ppermute(array, 'ctx', pairs)  33.5 us
    ppermute x6, starting transfers between devices, deliver(): return [lax.ppermute(summed, ('ctx', 'tp'), moves) for moves in pairs]  17.2 us
    ppermute x6, waiting for transfers between devices, deliver(): return [lax.ppermute(summed, ('ctx', 'tp'), moves) for moves in pairs]  10.6 us
    ppermute x3, starting transfers between devices, per_device(): lax.ppermute(slab_left, 'ctx', [(i, i + by * SLAB) for i in range(ctx - b...  9.37 us
    ppermute x10, waiting for transfers between devices, within_slab(): return lax.ppermute(array, 'ctx', [(i, i ^ mask) for i in range(ctx)])  8.84 us
    ppermute x10, starting transfers between devices, within_slab(): return lax.ppermute(array, 'ctx', [(i, i ^ mask) for i in range(ctx)])  7.22 us
    unnamed x26, local copies, waits for them, and re-layouts  5.97 us
  transfers between devices with their start and end apart: 36, of which 16 were waited for; matrix products, arithmetic and copies ran while one was open for 1% of the time, Pallas kernels for 31%

profile of v3, /device:TPU:4, one launch (start us, length us, event | category | flops | bytes accessed | tf_op | source)
XLA Modules:
  0.0 186.5 jit_solution(10593671176691941648)
XLA Ops:
  22.5 3.3 %short_filters.1 = (f32[4,128,8,128]{3,2,1,0:T(8,128)S(1)}, f32[4,128,8,128]{3,2,1,0:T(8,128)S(1)}) custom-call(s32[3]{0:T(128)S(1)} %pad_add_fusion.1.here, bf16[3,128,4096]{2,1,0:T(8,128)(2,1)S(1)} %copy-done.2, bf16[3,2,4096]{2,1,0:T(2,128)(2,1)S(1)} %collective-permute-done.3.halo, f32[3,3,8192]{2,1,0:T(4,128)S(1)} %copy-done.3), custom_call_target="tpu_custom_call" | custom-call | flops 1 | bytes 1 | tf_op jit(solution)/shard_map/short_filters/pallas_call | solution.py:357
  27.6 3.1 %block_states.1 = (bf16[4,16,256]{2,1,0:T(8,128)(2,1)S(1)}, bf16[4,16,256]{2,1,0:T(8,128)(2,1)S(1)}, bf16[4,16,256]{2,1,0:T(8,128)(2,1)S(1)}, bf16[4,16,256]{2,1,0:T(8,128)(2,1)S(1)}) custom-call(s32[3]{0:T(128)S(1)} %pad_add_fusion.1.here, f32[4,128,8,128]{3,2,1,0:T(8,128)S(1)} %get-tuple-element.52.u_ref, ...), custom_call_target="tpu_custom_call" | custom-call | flops 1 | bytes 1 | tf_op jit(solution)/shard_map/block_states/pallas_call | solution.py:373
  32.7 3.4 %collective-permute-done.8.refs_2_ = bf16[4,16,256]{2,1,0:T(8,128)(2,1)S(1)} collective-permute-done((bf16[4,16,256]{2,1,0:T(8,128)(2,1)S(1)}, bf16[4,16,256]{2,1,0:T(8,128)(2,1)S(1)}, u32[]{:S(2)}, u32[]{:S(2)}) %collective-permute-start.8) | collective-permute-done | bytes 32800 | tf_op jit(solution)/shard_map/ppermute | solution.py:301
  37.0 5.6 %collective-permute-start.12 = (bf16[4,16,256]{2,1,0:T(8,128)(2,1)S(1)}, bf16[4,16,256]{2,1,0:T(8,128)(2,1)S(1)}, u32[]{:S(2)}, u32[]{:S(2)}) collective-permute-start(bf16[4,16,256]{2,1,0:T(8,128)(2,1)S(1)} %slab_states.1), channel_id=1, source_target_pairs={{0,24},{2,26},{4,28},{6,30},{1,25},{3,27},{5,29},{7,31}} | collective-permute-start | bytes 98312 | tf_op jit(solution)/shard_map/ppermute | solution.py:395
  46.4 5.6 %local_convolution.1.y_ref = f32[4,128,8,128]{3,2,1,0:T(8,128)S(1)} custom-call(s32[3]{0:T(128)S(1)} %pad_add_fusion.1.here, f32[4,128,8,128]{3,2,1,0:T(8,128)S(1)} %get-tuple-element.52.u_ref, f32[4,33,256]{2,1,0:T(8,128)S(1)} %pad_maximum_fusion.3.refs_0_.rates, f32[4,33,256]{2,1,0:T(8,128)S(1)} %collective-permute-done.5.refs_1_, ...), custom_call_target="tpu_custom_call" | custom-call | flops 1 | bytes 1 | tf_op jit(solution)/shard_map/local_convolution/pallas_call | solution.py:399
  54.8 3.1 %collective-permute-done.14.refs_6_ = bf16[4,16,256]{2,1,0:T(8,128)(2,1)S(1)} collective-permute-done((bf16[4,16,256]{2,1,0:T(8,128)(2,1)S(1)}, bf16[4,16,256]{2,1,0:T(8,128)(2,1)S(1)}, u32[]{:S(2)}, u32[]{:S(2)}) %collective-permute-start.14) | collective-permute-done | bytes 32800 | tf_op jit(solution)/shard_map/ppermute | solution.py:301
  64.0 12.8 %collective-permute-done.17.refs_0_.refs_2_ = bf16[128,2048]{1,0:T(8,128)(2,1)S(1)} collective-permute-done((bf16[128,2048]{1,0:T(8,128)(2,1)S(1)}, bf16[128,2048]{1,0:T(8,128)(2,1)S(1)}, u32[]{:S(2)}, u32[]{:S(2)}) %collective-permute-start.17) | collective-permute-done | bytes 524320 | tf_op jit(solution)/shard_map/ppermute | solution.py:311
  79.0 3.0 %project_block.11 = bf16[1,2,128,256]{3,2,1,0:T(8,128)(2,1)S(1)} custom-call(s32[3]{0:T(128)S(1)} %add_add_fusion.1.here, bf16[128,2048]{1,0:T(8,128)(2,1)S(1)} %gated_block.2.refs_0_, bf16[128,2048]{1,0:T(8,128)(2,1)S(1)} %gated_block.3.refs_1_, bf16[4096,512]{1,0:T(8,128)(2,1)S(1)} %copy-done, bf16[4096,512]{1,0:T(8,128)(2,1)} %collective-permute-done.16.refs_3_.refs_2_), custom_call_target="tpu_custom_call" | custom-call | flops 1 | bytes 1 | tf_op jit(solution)/shard_map/project_block/pallas_call | solution.py:446
  85.0 3.1 %collective-permute-done.18.refs_1_.refs_3_ = bf16[128,2048]{1,0:T(8,128)(2,1)S(1)} collective-permute-done((bf16[128,2048]{1,0:T(8,128)(2,1)S(1)}, bf16[128,2048]{1,0:T(8,128)(2,1)S(1)}, u32[]{:S(2)}, u32[]{:S(2)}) %collective-permute-start.18) | collective-permute-done | bytes 524320 | tf_op jit(solution)/shard_map/ppermute | solution.py:311
  88.6 10.7 %collective-permute-done.19.refs_0_.refs_4_ = bf16[128,2048]{1,0:T(8,128)(2,1)S(1)} collective-permute-done((bf16[128,2048]{1,0:T(8,128)(2,1)S(1)}, bf16[128,2048]{1,0:T(8,128)(2,1)S(1)}, u32[]{:S(2)}, u32[]{:S(2)}) %collective-permute-start.19) | collective-permute-done | bytes 524320 | tf_op jit(solution)/shard_map/ppermute | solution.py:311
  102.3 3.0 %project_block.17 = bf16[1,2,128,256]{3,2,1,0:T(8,128)(2,1)S(1)} custom-call(s32[3]{0:T(128)S(1)} %add_add_fusion.here, bf16[128,2048]{1,0:T(8,128)(2,1)S(1)} %collective-permute-done.17.refs_0_.refs_2_, bf16[128,2048]{1,0:T(8,128)(2,1)S(1)} %collective-permute-done.18.refs_1_.refs_3_, bf16[4096,512]{1,0:T(8,128)(2,1)S(1)} %copy-done, ...), custom_call_target="tpu_custom_call" | custom-call | flops 1 | bytes 1 | tf_op jit(solution)/shard_map/project_block/pallas_call | solution.py:446
  105.3 5.2 %collective-permute-done.20.refs_1_.refs_5_ = bf16[128,2048]{1,0:T(8,128)(2,1)S(1)} collective-permute-done((bf16[128,2048]{1,0:T(8,128)(2,1)S(1)}, bf16[128,2048]{1,0:T(8,128)(2,1)S(1)}, u32[]{:S(2)}, u32[]{:S(2)}) %collective-permute-start.20) | collective-permute-done | bytes 524320 | tf_op jit(solution)/shard_map/ppermute | solution.py:311
  116.2 3.1 %project_block.15 = bf16[1,2,128,256]{3,2,1,0:T(8,128)(2,1)S(1)} custom-call(s32[3]{0:T(128)S(1)} %add_add_fusion.here, bf16[128,2048]{1,0:T(8,128)(2,1)S(1)} %collective-permute-done.19.refs_0_.refs_4_, bf16[128,2048]{1,0:T(8,128)(2,1)S(1)} %collective-permute-done.20.refs_1_.refs_5_, bf16[4096,512]{1,0:T(8,128)(2,1)S(1)} %copy-done, ...), custom_call_target="tpu_custom_call" | custom-call | flops 1 | bytes 1 | tf_op jit(solution)/shard_map/project_block/pallas_call | solution.py:446
  119.4 5.0 %project_block.16 = bf16[3,2,128,256]{3,2,1,0:T(8,128)(2,1)S(1)} custom-call(s32[3]{0:T(128)S(1)} %add_add_fusion.1.here, bf16[128,2048]{1,0:T(8,128)(2,1)S(1)} %gated_block.2.refs_0_, bf16[128,2048]{1,0:T(8,128)(2,1)S(1)} %gated_block.3.refs_1_, bf16[128,2048]{1,0:T(8,128)(2,1)S(1)} %collective-permute-done.17.refs_0_.refs_2_, ...), custom_call_target="tpu_custom_call" | custom-call | flops 1 | bytes 1 | tf_op jit(solution)/shard_map/project_block/pallas_call | solution.py:446
  126.6 4.5 %project_block.18.refs_4_ = f32[2,1,4,128,256]{4,3,2,1,0:T(8,128)S(1)} custom-call(s32[3]{0:T(128)S(1)} %add_add_fusion.2.here, bf16[128,2048]{1,0:T(8,128)(2,1)} %collective-permute-done.26.refs_0_, bf16[4096,512]{1,0:T(8,128)(2,1)S(1)} %copy-done.1, bf16[4096,512]{1,0:T(8,128)(2,1)} %collective-permute-done.16.refs_3_.refs_2_, bf16[4,4096,512]{2,1,0:T(8,128)(2,1)} %bitcast.30), custom_call_target="tpu_custom_call" | custom-call | flops 1 | bytes 1 | tf_op jit(solution)/shard_map/project_block/pallas_call | solution.py:446
  132.9 3.6 %project_block.19 = bf16[1,4,128,256]{3,2,1,0:T(8,128)(2,1)S(1)} custom-call(s32[3]{0:T(128)S(1)} %add_add_fusion.1.here, bf16[128,2048]{1,0:T(8,128)(2,1)} %collective-permute-done.25.refs_0_, bf16[4096,512]{1,0:T(8,128)(2,1)S(1)} %copy-done.1, bf16[4096,512]{1,0:T(8,128)(2,1)} %collective-permute-done.16.refs_3_.refs_2_, bf16[4,4096,512]{2,1,0:T(8,128)(2,1)} %bitcast.31, ...), custom_call_target="tpu_custom_call" | custom-call | flops 1 | bytes 1 | tf_op jit(solution)/shard_map/project_block/pallas_call | solution.py:446
  138.0 4.7 %project_block.20 = bf16[3,2,128,256]{3,2,1,0:T(8,128)(2,1)S(1)} custom-call(s32[3]{0:T(128)S(1)} %add_add_fusion.here, bf16[128,2048]{1,0:T(8,128)(2,1)S(1)} %gated_block.2.refs_0_, bf16[128,2048]{1,0:T(8,128)(2,1)S(1)} %gated_block.3.refs_1_, bf16[128,2048]{1,0:T(8,128)(2,1)S(1)} %collective-permute-done.17.refs_0_.refs_2_, ...), custom_call_target="tpu_custom_call" | custom-call | flops 1 | bytes 1 | tf_op jit(solution)/shard_map/project_block/pallas_call | solution.py:446
  142.9 5.6 %collective-permute-start.29 = (bf16[4,128,256]{2,1,0:T(8,128)(2,1)S(1)}, bf16[4,128,256]{2,1,0:T(8,128)(2,1)S(1)}, u32[]{:S(2)}, u32[]{:S(2)}) collective-permute-start(bf16[4,128,256]{2,1,0:T(8,128)(2,1)S(1)} %pad_maximum_fusion.1), channel_id=1, source_target_pairs={{1,16},{3,18},{5,20},{7,22},{9,0},{11,2},{13,4},{15,6},{17,25},{19... | collective-permute-start | bytes 786440 | tf_op jit(solution)/shard_map/ppermute | solution.py:493
  149.3 3.1 %collective-permute-start.27 = (bf16[4,128,256]{2,1,0:T(8,128)(2,1)S(1)}, bf16[4,128,256]{2,1,0:T(8,128)(2,1)S(1)}, u32[]{:S(2)}, u32[]{:S(2)}) collective-permute-start(bf16[4,128,256]{2,1,0:T(8,128)(2,1)S(1)} %pad_maximum_fusion.refs_0_), channel_id=1, source_target_pairs={{16,17},{18,19},{20,21},{22,23},{24,25},{26,27},{28,29},{30,31},{1... | collective-permute-start | bytes 786440 | tf_op jit(solution)/shard_map/ppermute | solution.py:492
  152.5 4.4 %collective-permute-start.31 = (bf16[4,128,256]{2,1,0:T(8,128)(2,1)S(1)}, bf16[4,128,256]{2,1,0:T(8,128)(2,1)S(1)}, u32[]{:S(2)}, u32[]{:S(2)}) collective-permute-start(bf16[4,128,256]{2,1,0:T(8,128)(2,1)S(1)} %pad_maximum_fusion.2), channel_id=1, source_target_pairs={{1,24},{3,26},{5,28},{7,30},{9,16},{11,18},{13,20},{15,22},{17,9},... | collective-permute-start | bytes 786440 | tf_op jit(solution)/shard_map/ppermute | solution.py:493
  158.2 3.7 %project_block.21 = bf16[1,4,128,256]{3,2,1,0:T(8,128)(2,1)S(1)} custom-call(s32[3]{0:T(128)S(1)} %add_add_fusion.here, bf16[128,2048]{1,0:T(8,128)(2,1)} %collective-permute-done.25.refs_0_, bf16[4096,512]{1,0:T(8,128)(2,1)S(1)} %copy-done.1, bf16[4096,512]{1,0:T(8,128)(2,1)} %collective-permute-done.16.refs_3_.refs_2_, bf16[4,4096,512]{2,1,0:T(8,128)(2,1)} %bitcast.33, ...), custom_call_target="tpu_custom_call" | custom-call | flops 1 | bytes 1 | tf_op jit(solution)/shard_map/project_block/pallas_call | solution.py:446
  161.9 3.9 %collective-permute-start.34 = (bf16[4,128,256]{2,1,0:T(8,128)(2,1)S(1)}, bf16[4,128,256]{2,1,0:T(8,128)(2,1)S(1)}, u32[]{:S(2)}, u32[]{:S(2)}) collective-permute-start(bf16[4,128,256]{2,1,0:T(8,128)(2,1)S(1)} %fusion), channel_id=1, source_target_pairs={{1,8},{3,10},{5,12},{7,14},{9,24},{11,26},{13,28},{15,30},{17,1},{... | collective-permute-start | bytes 786440 | tf_op jit(solution)/shard_map/ppermute | solution.py:493
  167.9 4.1 %collective-permute-done.34.refs_7_ = bf16[4,128,256]{2,1,0:T(8,128)(2,1)S(1)} collective-permute-done((bf16[4,128,256]{2,1,0:T(8,128)(2,1)S(1)}, bf16[4,128,256]{2,1,0:T(8,128)(2,1)S(1)}, u32[]{:S(2)}, u32[]{:S(2)}) %collective-permute-start.34) | collective-permute-done | bytes 262176 | tf_op jit(solution)/shard_map/ppermute | solution.py:493
  171.9 6.1 %collective-permute-done.33.refs_6_ = bf16[4,128,256]{2,1,0:T(8,128)(2,1)S(1)} collective-permute-done((bf16[4,128,256]{2,1,0:T(8,128)(2,1)S(1)}, bf16[4,128,256]{2,1,0:T(8,128)(2,1)S(1)}, u32[]{:S(2)}, u32[]{:S(2)}) %collective-permute-start.33) | collective-permute-done | bytes 262176 | tf_op jit(solution)/shard_map/ppermute | solution.py:493
  (111 shorter events, 58.9 us)
Async XLA Ops:
  6.5 112.8 %all-gather.3.cloned.1.call-start = ((), (), s32[]{:S(2)}) async-start(), calls=%async_computation | async-start | bytes 20971520 | tf_op jit(solution)/shard_map/all_gather | solution.py:322
  7.3 69.5 %collective-permute-start.16 = (bf16[4096,512]{1,0:T(8,128)(2,1)}, bf16[4096,512]{1,0:T(8,128)(2,1)}, u32[]{:S(2)}, u32[]{:S(2)}) collective-permute-start(bf16[4096,512]{1,0:T(8,128)(2,1)} %refs_1_.5), channel_id=1, source_target_pairs={{0,2},{2,0},{4,6},{6,4},{8,10},{10,8},{12,14},{14,12},{16,18},{18,... | collective-permute-start | bytes 12582920 | tf_op jit(solution)/shard_map/ppermute | solution.py:301
  7.4 7.2 %collective-permute-start.1 = (f32[33,256]{1,0:T(8,128)S(1)}, f32[33,256]{1,0:T(8,128)S(1)}, u32[]{:S(2)}, u32[]{:S(2)}) collective-permute-start(f32[33,256]{1,0:T(8,128)S(1)} %get-tuple-element.95), channel_id=1, source_target_pairs={{0,16},{2,18},{4,20},{6,22},{8,24},{10,26},{12,28},{14,30},{16,0},... | collective-permute-start | bytes 101384 | tf_op jit(solution)/shard_map/ppermute | solution.py:304
  17.2 8.6 %collective-permute-start.4 = (f32[4,33,256]{2,1,0:T(8,128)S(1)}, f32[4,33,256]{2,1,0:T(8,128)S(1)}, u32[]{:S(2)}, u32[]{:S(2)}) collective-permute-start(f32[4,33,256]{2,1,0:T(8,128)S(1)} %pad_maximum_fusion.3.refs_0_.rates), channel_id=1, source_target_pairs={{0,4},{2,6},{4,0},{6,2},{8,12},{10,14},{12,8},{14,10},{16,20},{18,... | collective-permute-start | bytes 405512 | tf_op jit(solution)/shard_map/ppermute | solution.py:301
  37.0 15.0 %collective-permute-start.12 = (bf16[4,16,256]{2,1,0:T(8,128)(2,1)S(1)}, bf16[4,16,256]{2,1,0:T(8,128)(2,1)S(1)}, u32[]{:S(2)}, u32[]{:S(2)}) collective-permute-start(bf16[4,16,256]{2,1,0:T(8,128)(2,1)S(1)} %slab_states.1), channel_id=1, source_target_pairs={{0,24},{2,26},{4,28},{6,30},{1,25},{3,27},{5,29},{7,31}} | collective-permute-start | bytes 98312 | tf_op jit(solution)/shard_map/ppermute | solution.py:395
  42.6 9.4 %collective-permute-start.11 = (bf16[4,16,256]{2,1,0:T(8,128)(2,1)S(1)}, bf16[4,16,256]{2,1,0:T(8,128)(2,1)S(1)}, u32[]{:S(2)}, u32[]{:S(2)}) collective-permute-start(bf16[4,16,256]{2,1,0:T(8,128)(2,1)S(1)} %slab_states.1), channel_id=1, source_target_pairs={{0,16},{2,18},{4,20},{6,22},{8,24},{10,26},{12,28},{14,30},{1,17},... | collective-permute-start | bytes 98312 | tf_op jit(solution)/shard_map/ppermute | solution.py:395
  43.9 8.1 %collective-permute-start.10 = (bf16[4,16,256]{2,1,0:T(8,128)(2,1)S(1)}, bf16[4,16,256]{2,1,0:T(8,128)(2,1)S(1)}, u32[]{:S(2)}, u32[]{:S(2)}) collective-permute-start(bf16[4,16,256]{2,1,0:T(8,128)(2,1)S(1)} %slab_states.1), channel_id=1, source_target_pairs={{0,8},{2,10},{4,12},{6,14},{8,16},{10,18},{12,20},{14,22},{16,24},... | collective-permute-start | bytes 98312 | tf_op jit(solution)/shard_map/ppermute | solution.py:395
  61.1 15.7 %collective-permute-start.17 = (bf16[128,2048]{1,0:T(8,128)(2,1)S(1)}, bf16[128,2048]{1,0:T(8,128)(2,1)S(1)}, u32[]{:S(2)}, u32[]{:S(2)}) collective-permute-start(bf16[128,2048]{1,0:T(8,128)(2,1)S(1)} %gated_block.2.refs_0_), channel_id=1, source_target_pairs={{0,8},{2,10},{4,12},{6,14},{8,24},{10,26},{12,28},{14,30},{16,0},{... | collective-permute-start | bytes 1572872 | tf_op jit(solution)/shard_map/ppermute | solution.py:311
  63.8 24.2 %collective-permute-start.18 = (bf16[128,2048]{1,0:T(8,128)(2,1)S(1)}, bf16[128,2048]{1,0:T(8,128)(2,1)S(1)}, u32[]{:S(2)}, u32[]{:S(2)}) collective-permute-start(bf16[128,2048]{1,0:T(8,128)(2,1)S(1)} %gated_block.3.refs_1_), channel_id=1, source_target_pairs={{0,8},{2,10},{4,12},{6,14},{8,24},{10,26},{12,28},{14,30},{16,0},{... | collective-permute-start | bytes 1572872 | tf_op jit(solution)/shard_map/ppermute | solution.py:311
  76.8 22.5 %collective-permute-start.19 = (bf16[128,2048]{1,0:T(8,128)(2,1)S(1)}, bf16[128,2048]{1,0:T(8,128)(2,1)S(1)}, u32[]{:S(2)}, u32[]{:S(2)}) collective-permute-start(bf16[128,2048]{1,0:T(8,128)(2,1)S(1)} %collective-permute-done.17.refs_0_.refs_2_), channel_id=1, source_target_pairs={{0,8},{2,10},{4,12},{6,14},{8,24},{10,26},{12,28},{14,30},{16,0},{... | collective-permute-start | bytes 1572872 | tf_op jit(solution)/shard_map/ppermute | solution.py:311
  88.0 22.5 %collective-permute-start.20 = (bf16[128,2048]{1,0:T(8,128)(2,1)S(1)}, bf16[128,2048]{1,0:T(8,128)(2,1)S(1)}, u32[]{:S(2)}, u32[]{:S(2)}) collective-permute-start(bf16[128,2048]{1,0:T(8,128)(2,1)S(1)} %collective-permute-done.18.refs_1_.refs_3_), channel_id=1, source_target_pairs={{0,8},{2,10},{4,12},{6,14},{8,24},{10,26},{12,28},{14,30},{16,0},{... | collective-permute-start | bytes 1572872 | tf_op jit(solution)/shard_map/ppermute | solution.py:311
  88.1 14.2 %collective-permute-start.23 = (bf16[1,2,128,256]{3,2,1,0:T(8,128)(2,1)S(1)}, bf16[1,2,128,256]{3,2,1,0:T(8,128)(2,1)S(1)}, u32[]{:S(2)}, u32[]{:S(2)}) collective-permute-start(bf16[1,2,128,256]{3,2,1,0:T(8,128)(2,1)S(1)} %project_block.11), channel_id=1, source_target_pairs={{0,1},{1,0},{2,3},{3,2},{4,5},{5,4},{6,7},{7,6},{8,9},{9,8},{10,11... | collective-permute-start | bytes 393224 | tf_op jit(solution)/shard_map/ppermute | solution.py:472
  99.3 27.3 %collective-permute-start.26 = (bf16[128,2048]{1,0:T(8,128)(2,1)S(1)}, bf16[128,2048]{1,0:T(8,128)(2,1)}, u32[]{:S(2)}, u32[]{:S(2)}) collective-permute-start(bf16[128,2048]{1,0:T(8,128)(2,1)S(1)} %collective-permute-done.19.refs_0_.refs_4_), channel_id=1, source_target_pairs={{0,8},{2,10},{4,12},{6,14},{8,24},{10,26},{12,28},{14,30},{16,0},{... | collective-permute-start | bytes 1572872 | tf_op jit(solution)/shard_map/ppermute | solution.py:311
  110.5 22.4 %collective-permute-start.25 = (bf16[128,2048]{1,0:T(8,128)(2,1)S(1)}, bf16[128,2048]{1,0:T(8,128)(2,1)}, u32[]{:S(2)}, u32[]{:S(2)}) collective-permute-start(bf16[128,2048]{1,0:T(8,128)(2,1)S(1)} %collective-permute-done.20.refs_1_.refs_5_), channel_id=1, source_target_pairs={{0,8},{2,10},{4,12},{6,14},{8,24},{10,26},{12,28},{14,30},{16,0},{... | collective-permute-start | bytes 1572872 | tf_op jit(solution)/shard_map/ppermute | solution.py:311
  124.4 18.3 %collective-permute-start.22 = (bf16[3,2,128,256]{3,2,1,0:T(8,128)(2,1)S(1)}, bf16[3,2,128,256]{3,2,1,0:T(8,128)(2,1)S(1)}, u32[]{:S(2)}, u32[]{:S(2)}) collective-permute-start(bf16[3,2,128,256]{3,2,1,0:T(8,128)(2,1)S(1)} %project_block.16), channel_id=1, source_target_pairs={{0,1},{1,0},{2,3},{3,2},{4,5},{5,4},{6,7},{7,6},{8,9},{9,8},{10,11... | collective-permute-start | bytes 1179656 | tf_op jit(solution)/shard_map/ppermute | solution.py:472
  125.1 13.0 %collective-permute-start.24 = (bf16[1,2,128,256]{3,2,1,0:T(8,128)(2,1)S(1)}, bf16[1,2,128,256]{3,2,1,0:T(8,128)(2,1)S(1)}, u32[]{:S(2)}, u32[]{:S(2)}) collective-permute-start(bf16[1,2,128,256]{3,2,1,0:T(8,128)(2,1)S(1)} %copy-done.5), channel_id=1, source_target_pairs={{0,1},{1,0},{2,3},{3,2},{4,5},{5,4},{6,7},{7,6},{8,9},{9,8},{10,11... | collective-permute-start | bytes 393224 | tf_op jit(solution)/shard_map/ppermute | solution.py:472
  136.6 25.3 %collective-permute-start.32 = (bf16[1,4,128,256]{3,2,1,0:T(8,128)(2,1)S(1)}, bf16[1,4,128,256]{3,2,1,0:T(8,128)(2,1)S(1)}, u32[]{:S(2)}, u32[]{:S(2)}) collective-permute-start(bf16[1,4,128,256]{3,2,1,0:T(8,128)(2,1)S(1)} %project_block.19), channel_id=1, source_target_pairs={{0,1},{1,0},{2,3},{3,2},{4,5},{5,4},{6,7},{7,6},{8,9},{9,8},{10,11... | collective-permute-start | bytes 786440 | tf_op jit(solution)/shard_map/ppermute | solution.py:526
  142.9 24.4 %collective-permute-start.29 = (bf16[4,128,256]{2,1,0:T(8,128)(2,1)S(1)}, bf16[4,128,256]{2,1,0:T(8,128)(2,1)S(1)}, u32[]{:S(2)}, u32[]{:S(2)}) collective-permute-start(bf16[4,128,256]{2,1,0:T(8,128)(2,1)S(1)} %pad_maximum_fusion.1), channel_id=1, source_target_pairs={{1,16},{3,18},{5,20},{7,22},{9,0},{11,2},{13,4},{15,6},{17,25},{19... | collective-permute-start | bytes 786440 | tf_op jit(solution)/shard_map/ppermute | solution.py:493
  148.6 8.3 %collective-permute-start.28 = (bf16[4,128,256]{2,1,0:T(8,128)(2,1)S(1)}, bf16[4,128,256]{2,1,0:T(8,128)(2,1)S(1)}, u32[]{:S(2)}, u32[]{:S(2)}) collective-permute-start(bf16[4,128,256]{2,1,0:T(8,128)(2,1)S(1)} %pad_maximum_fusion.1), channel_id=1, source_target_pairs={{0,16},{2,18},{4,20},{6,22},{8,0},{10,2},{12,4},{14,6},{16,25},{18... | collective-permute-start | bytes 786440 | tf_op jit(solution)/shard_map/ppermute | solution.py:493
  149.3 16.5 %collective-permute-start.27 = (bf16[4,128,256]{2,1,0:T(8,128)(2,1)S(1)}, bf16[4,128,256]{2,1,0:T(8,128)(2,1)S(1)}, u32[]{:S(2)}, u32[]{:S(2)}) collective-permute-start(bf16[4,128,256]{2,1,0:T(8,128)(2,1)S(1)} %pad_maximum_fusion.refs_0_), channel_id=1, source_target_pairs={{16,17},{18,19},{20,21},{22,23},{24,25},{26,27},{28,29},{30,31},{1... | collective-permute-start | bytes 786440 | tf_op jit(solution)/shard_map/ppermute | solution.py:492
  152.5 14.8 %collective-permute-start.31 = (bf16[4,128,256]{2,1,0:T(8,128)(2,1)S(1)}, bf16[4,128,256]{2,1,0:T(8,128)(2,1)S(1)}, u32[]{:S(2)}, u32[]{:S(2)}) collective-permute-start(bf16[4,128,256]{2,1,0:T(8,128)(2,1)S(1)} %pad_maximum_fusion.2), channel_id=1, source_target_pairs={{1,24},{3,26},{5,28},{7,30},{9,16},{11,18},{13,20},{15,22},{17,9},... | collective-permute-start | bytes 786440 | tf_op jit(solution)/shard_map/ppermute | solution.py:493
  156.9 11.0 %collective-permute-start.30 = (bf16[4,128,256]{2,1,0:T(8,128)(2,1)S(1)}, bf16[4,128,256]{2,1,0:T(8,128)(2,1)S(1)}, u32[]{:S(2)}, u32[]{:S(2)}) collective-permute-start(bf16[4,128,256]{2,1,0:T(8,128)(2,1)S(1)} %pad_maximum_fusion.2), channel_id=1, source_target_pairs={{0,24},{2,26},{4,28},{6,30},{8,16},{10,18},{12,20},{14,22},{16,9},... | collective-permute-start | bytes 786440 | tf_op jit(solution)/shard_map/ppermute | solution.py:493
  161.9 10.0 %collective-permute-start.34 = (bf16[4,128,256]{2,1,0:T(8,128)(2,1)S(1)}, bf16[4,128,256]{2,1,0:T(8,128)(2,1)S(1)}, u32[]{:S(2)}, u32[]{:S(2)}) collective-permute-start(bf16[4,128,256]{2,1,0:T(8,128)(2,1)S(1)} %fusion), channel_id=1, source_target_pairs={{1,8},{3,10},{5,12},{7,14},{9,24},{11,26},{13,28},{15,30},{17,1},{... | collective-permute-start | bytes 786440 | tf_op jit(solution)/shard_map/ppermute | solution.py:493
  165.9 12.1 %collective-permute-start.33 = (bf16[4,128,256]{2,1,0:T(8,128)(2,1)S(1)}, bf16[4,128,256]{2,1,0:T(8,128)(2,1)S(1)}, u32[]{:S(2)}, u32[]{:S(2)}) collective-permute-start(bf16[4,128,256]{2,1,0:T(8,128)(2,1)S(1)} %fusion), channel_id=1, source_target_pairs={{0,8},{2,10},{4,12},{6,14},{8,24},{10,26},{12,28},{14,30},{16,1},{... | collective-permute-start | bytes 786440 | tf_op jit(solution)/shard_map/ppermute | solution.py:493
  (25 other events, 107.1 us)
Sparse Core Ops, SparseCore 0:
  8.9 109.9 all-gather.2

commit v4 on v3

--- a/solution.py
+++ b/solution.py
@@ -124,9 +124,10 @@
     states, earlier, outs = refs[:SLAB], refs[SLAB : SLAB + slabs - 1], refs[SLAB + slabs - 1 :]
     for g in range(slabs):
         rate = rates[lax.rem(g - here[0] + slabs, slabs), : states[0].shape[1]]
-        entering = earlier[0][g].astype(F32)
-        for k in range(1, slabs - 1):
-            entering += jnp.exp(-float(k * SLAB * tokens) * rate) * earlier[k][g].astype(F32)
+        entering = jnp.zeros(rate.shape, F32)
+        for k in range(slabs - 1):
+            term = jnp.exp(-float(k * SLAB * tokens) * rate) * earlier[k][g].astype(F32)
+            entering += jnp.where(here[0] > k, term, jnp.zeros_like(term))
         for d in range(SLAB):
             block = here[1] ^ d
             total = jnp.exp(-(block.astype(F32) * float(tokens)) * rate) * entering
@@ -218,24 +219,22 @@
                     out_ref[t, j, i] = total[:, t * part : (t + 1) * part].astype(out_ref.dtype)
 
 
-def place_kernel(kept, steps, here, *refs):
-    sources, out_ref = refs[:-1], refs[-1]
-    share = sources[0].shape[2]
-    tp_me, rank = here[0], here[1]
+def place_kernel(kept, counts, here, *refs):
+    out_ref = refs[-1]
+    share = refs[0].shape[2]
+    rank = here[0]
+    starts = [sum(counts[:k]) for k in range(len(counts))]
     for slot in range(kept):
-        step = here[2 + slot]
         for t in range(SIDE):
-            own = jnp.logical_and(step == 0, tp_me == t)
-            moved = jnp.logical_and(step == 0, tp_me != t)
-            choices = [(own, sources[0]), (moved, sources[1])]
-            choices += [(step == k, sources[2 * k + t]) for k in range(1, steps)]
-            for chosen, source in choices:
-
-                @pl.when(chosen)
-                def _(source=source, slot=slot, t=t):
+            for k, count in enumerate(counts):
+
+                @pl.when(here[1 + slot * SIDE + t] == k)
+                def _(slot=slot, t=t, k=k, count=count):
                     for piece in range(SLAB):
+                        each = SLAB // count
+                        source = refs[starts[k] + piece // each]
                         start = ((slot * SLAB + (rank ^ piece)) * SIDE + t) * share
-                        out_ref[:, pl.ds(pl.multiple_of(start, share), share)] = source[piece]
+                        out_ref[:, pl.ds(pl.multiple_of(start, share), share)] = source[piece % each]
 
 
 def ring_order(count):
@@ -287,7 +286,7 @@
     ctx, tp = lax.axis_size("ctx"), lax.axis_size("tp")
     depth, columns = out_weight.shape
     share = columns // tp
-    if owned * SLAB != GROUP or tp != SIDE or share % LANES or ctx // SLAB < 3:
+    if owned * SLAB != GROUP or tp != SIDE or share % LANES or ctx // SLAB < 4 or ctx // SLAB % 2:
         return any_size(features, conv_weight, decay_rates, residues, skip_gain, out_weight)
     slabs = ctx // SLAB
     groups = width // GROUP
@@ -380,6 +379,16 @@
     )(here, u, *rates)
     left = [left[0]] + [within_slab(left[d], d) for d in range(1, SLAB)]
 
+    local = grouped(
+        functools.partial(local_kernel, modes),
+        "local_convolution",
+        [series] + [rate_spec] * SLAB,
+        series,
+        series_shape,
+        [wide],
+    )(here, u, *rates)
+    left, local = lax.optimization_barrier((left, local))
+
     smem = pl.BlockSpec(memory_space=pltpu.SMEM)
     vmem = pl.BlockSpec(memory_space=pltpu.VMEM)
     slab_left = pl.pallas_call(
@@ -391,20 +400,7 @@
         cost_estimate=light,
         name="slab_states",
     )(here, rates[0], *left)
-    earlier = [
-        lax.ppermute(slab_left, "ctx", [(i, i + by * SLAB) for i in range(ctx - by * SLAB)])
-        for by in range(1, slabs)
-    ]
-
-    local = grouped(
-        functools.partial(local_kernel, modes),
-        "local_convolution",
-        [series] + [rate_spec] * SLAB,
-        series,
-        series_shape,
-        [wide],
-    )(here, u, *rates)
-    earlier, local = lax.optimization_barrier((earlier, local))
+    earlier = [from_slab(slab_left, -by) for by in range(1, slabs)]
 
     incoming = pl.pallas_call(
         functools.partial(incoming_kernel, tokens),
@@ -480,17 +476,15 @@
 
     half_of = [z * tp // slabs for z in range(slabs)]
 
-    def deliver(summed, by):
-        pairs = [[], []]
+    def deliver(classes, by):
+        pairs = []
         for i in range(ctx):
             z, rest = divmod(i, SLAB)
-            target = order[(place[z] - by) % slabs] * SLAB + rest
             for t in range(tp):
-                pairs[t].append((i * tp + t, target * tp + half_of[z]))
-        if by == 0:
-            moves = [p for p in pairs[0] + pairs[1] if p[0] != p[1]]
-            return [summed, lax.ppermute(summed, ("ctx", "tp"), moves)]
-        return [lax.ppermute(summed, ("ctx", "tp"), moves) for moves in pairs]
+                target = order[(place[z] - by - t * slabs // tp) % slabs] * SLAB + rest
+                pairs.append((i * tp + t, target * tp + half_of[z]))
+        moved = jnp.where(tp_me == 0, classes[by], classes[(by + slabs // tp) % slabs])
+        return lax.ppermute(moved, ("ctx", "tp"), pairs)
 
     near, far, both = (
         ((0, None), (1, None)),
@@ -518,39 +512,44 @@
         got_parts.append(got)
     slab_weights, _ = lax.optimization_barrier((slab_weights, mine))
     away, batch_got = project_away(blocks[: slabs - 1], [slab_weights], far)
+    batch_mine = project_mine(blocks[: slabs - 1], [slab_weights], far, away)
     sources = [out_weight, beside, slab_weights]
-    head, _ = lax.optimization_barrier((blocks[-1][0], away))
+    head, _ = lax.optimization_barrier((blocks[-1][0], batch_mine))
     partial = project([[head]], sources, both, None, None, (0,))
     tail = blocks[-1][1]
     last_away = project([[None, tail]], sources, both, 1 - tp_me, partial, (1,))
     last_got = lax.ppermute(last_away, "tp", [(0, 1), (1, 0)])
-    batch_mine = project_mine(blocks[: slabs - 1], [slab_weights], far, (last_away, got))
     batch_got, got_parts, _ = lax.optimization_barrier((batch_got, got_parts, last_away))
-    batch = total(batch_mine, batch_got)
-    arrived = []
-    for step in range(slabs - 1):
-        summed = total(kept_parts[step], got_parts[step])[0]
-        arrived += deliver(jnp.concatenate([summed, batch[step]]), step)
-    tail, _ = lax.optimization_barrier((tail, (batch_mine, arrived[2])))
+    near_sums = [total(m, g)[0] for m, g in zip(kept_parts, got_parts)]
+    sums = [jnp.concatenate(parts) for parts in zip(near_sums, total(batch_mine, batch_got))]
+    late = ((slabs - 1) % (slabs // tp), slabs - 1)
+    arrived = {by: [deliver(sums, by)] for by in range(slabs) if by not in late}
+    tail, _ = lax.optimization_barrier((tail, (last_away, arrived[0])))
     last_mine = project([[None, tail]], sources, both, tp_me, partial, (1,))
-    arrived += deliver(total(last_mine, last_got)[0], slabs - 1)
+    sums.append(total(last_mine, last_got)[0])
+    for by in late:
+        arrived[by] = [deliver(sums, by)]
+    arrived = [arrived[by] for by in range(slabs)]
 
     def place_of(z):
         return sum(jnp.where(z == k, place[k], 0) for k in range(slabs))
 
     kept = slabs // tp
-    steps = [
-        lax.rem(place_of(tp_me * kept + j) - place_of(z_me) + slabs, slabs) for j in range(kept)
+    which = [
+        lax.rem(place_of(tp_me * kept + j) - place_of(z_me) + slabs + t * slabs // tp, slabs)
+        for j in range(kept)
+        for t in range(tp)
     ]
+    counts = [len(parts) for parts in arrived]
     return pl.pallas_call(
-        functools.partial(place_kernel, kept, slabs),
-        in_specs=[smem] + [vmem] * (SIDE * slabs),
+        functools.partial(place_kernel, kept, counts),
+        in_specs=[smem] + [vmem] * sum(counts),
         out_specs=vmem,
         out_shape=jax.ShapeDtypeStruct((tokens, width), BF16),
         compiler_params=limit,
         cost_estimate=light,
         name="place_columns",
-    )(jnp.stack([tp_me, rank, *steps]).astype(jnp.int32), *arrived)
+    )(jnp.stack([rank, *which]).astype(jnp.int32), *[a for parts in arrived for a in parts])
 
 
 def solution(mesh):

time: 187 us -> 187 us (level)
  starting transfers between devices: 47.2 us -> 41.1 us
  other arithmetic: 0.76 us -> 3.52 us
    ppermute x10 -> x4, starting transfers between devices: 29.6 us -> 13 us  [deliver(): return lax.ppermute(moved, ('ctx', 'tp'), pairs)]
    ppermute x6, waiting for transfers between devices: 33.5 us -> 27 us  [ring(): return lax.ppermute(array, 'ctx', pairs)]
    all_gather x1, waiting for transfers between devices: 0.02 us -> 5.76 us  [per_device(): lax.all_gather(out_weight, 'ctx', axis_index_groups=[list(range(z * SLAB,...]
    ppermute x3 -> x6, starting transfers between devices: 4.68 us -> 10.4 us  [from_slab(): lax.ppermute(array, 'ctx', [(i, (i - by * SLAB) % ctx) for i in range(ctx)])]
    ppermute x6, starting transfers between devices: 0.43 us -> 4.72 us  [ring(): return lax.ppermute(array, 'ctx', pairs)]
    ppermute x10, waiting for transfers between devices: 8.84 us -> 5.62 us  [within_slab(): return lax.ppermute(array, 'ctx', [(i, i ^ mask) for i in range(ctx)])]
    ppermute x1, waiting for transfers between devices: 0.01 us -> 2.76 us  [per_device(): last_got = lax.ppermute(last_away, 'tp', [(0, 1), (1, 0)])]
    ppermute x10 -> x4, waiting for transfers between devices: 10.7 us -> 13.1 us  [deliver(): return lax.ppermute(moved, ('ctx', 'tp'), pairs)]
  transfers between devices with their start and end apart: 36 -> 33, of which waited for: 16 -> 16; matrix products, arithmetic and copies ran while one was open for 1% -> 1% of each run, Pallas kernels for 31% -> 32%
where the time goes in v4:
time: 187 us; the launch traced here: 185 us
  Pallas kernels  60.7 us (32%)
  waiting for transfers between devices  59.9 us (32%)
  starting transfers between devices  41.1 us (22%)
  between operations  13.8 us (7%)
  local copies, waits for them, and re-layouts  5.78 us (3%)
  other arithmetic  3.52 us (2%)
    pallas_call x11, Pallas kernels, project(): pl.pallas_call(functools.partial(project_kernel, len(blocks), picks, halv...  40.8 us
    ppermute x6, waiting for transfers between devices, ring(): return lax.ppermute(array, 'ctx', pairs)  27 us
    ppermute x4, waiting for transfers between devices, deliver(): return lax.ppermute(moved, ('ctx', 'tp'), pairs)  13.1 us
    ppermute x4, starting transfers between devices, deliver(): return lax.ppermute(moved, ('ctx', 'tp'), pairs)  13 us
    ppermute x6, starting transfers between devices, from_slab(): lax.ppermute(array, 'ctx', [(i, (i - by * SLAB) % ctx) for i in range(ctx)])  10.4 us
    ppermute x10, starting transfers between devices, within_slab(): return lax.ppermute(array, 'ctx', [(i, i ^ mask) for i in range(ctx)])  8.01 us
    all_gather x1, waiting for transfers between devices, per_device(): lax.all_gather(out_weight, 'ctx', axis_index_groups=[list(range(z * SLAB,...  5.76 us
    ppermute x10, waiting for transfers between devices, within_slab(): return lax.ppermute(array, 'ctx', [(i, i ^ mask) for i in range(ctx)])  5.62 us
  transfers between devices with their start and end apart: 33, of which 16 were waited for; matrix products, arithmetic and copies ran while one was open for 1% of the time, Pallas kernels for 32%

profile of v4, /device:TPU:4, one launch (start us, length us, event | category | flops | bytes accessed | tf_op | source)
XLA Modules:
  0.0 184.8 jit_solution(5795572851536290971)
XLA Ops:
  7.4 3.7 %collective-permute-start = (f32[33,256]{1,0:T(8,128)S(1)}, f32[33,256]{1,0:T(8,128)S(1)}, u32[]{:S(2)}, u32[]{:S(2)}) collective-permute-start(f32[33,256]{1,0:T(8,128)S(1)} %get-tuple-element.101), channel_id=1, source_target_pairs={{0,24},{2,26},{4,28},{6,30},{8,0},{10,2},{12,4},{14,6},{16,8},{18,... | collective-permute-start | bytes 101384 | tf_op jit(solution)/shard_map/ppermute | solution.py:303
  16.9 3.1 %collective-permute-start.4 = (f32[4,33,256]{2,1,0:T(8,128)S(1)}, f32[4,33,256]{2,1,0:T(8,128)S(1)}, u32[]{:S(2)}, u32[]{:S(2)}) collective-permute-start(f32[4,33,256]{2,1,0:T(8,128)S(1)} %pad_maximum_fusion.3.refs_0_.rates), channel_id=1, source_target_pairs={{0,4},{2,6},{4,0},{6,2},{8,12},{10,14},{12,8},{14,10},{16,20},{18,... | collective-permute-start | bytes 405512 | tf_op jit(solution)/shard_map/ppermute | solution.py:300
  22.5 3.3 %short_filters.1 = (f32[4,128,8,128]{3,2,1,0:T(8,128)S(1)}, f32[4,128,8,128]{3,2,1,0:T(8,128)S(1)}) custom-call(s32[3]{0:T(128)S(1)} %pad_add_fusion.here, bf16[3,128,4096]{2,1,0:T(8,128)(2,1)S(1)} %copy-done.2, bf16[3,2,4096]{2,1,0:T(2,128)(2,1)S(1)} %collective-permute-done.3.halo, f32[3,3,8192]{2,1,0:T(4,128)S(1)} %copy-done.3), custom_call_target="tpu_custom_call" | custom-call | flops 1 | bytes 1 | tf_op jit(solution)/shard_map/short_filters/pallas_call | solution.py:356
  27.8 3.1 %block_states.1 = (bf16[4,16,256]{2,1,0:T(8,128)(2,1)S(1)}, bf16[4,16,256]{2,1,0:T(8,128)(2,1)S(1)}, bf16[4,16,256]{2,1,0:T(8,128)(2,1)S(1)}, bf16[4,16,256]{2,1,0:T(8,128)(2,1)S(1)}) custom-call(s32[3]{0:T(128)S(1)} %pad_add_fusion.here, f32[4,128,8,128]{3,2,1,0:T(8,128)S(1)} %get-tuple-element.53.u_ref, f32[4,33,256]{2,1,0:T(8,128)S(1)} %pad_maximum_fusion.3.refs_0_.rates, ...), custom_call_target="tpu_custom_call" | custom-call | flops 1 | bytes 1 | tf_op jit(solution)/shard_map/block_states/pallas_call | solution.py:372
  33.6 5.6 %local_convolution.1.y_ref = f32[4,128,8,128]{3,2,1,0:T(8,128)S(1)} custom-call(s32[3]{0:T(128)S(1)} %pad_add_fusion.here, f32[4,128,8,128]{3,2,1,0:T(8,128)S(1)} %get-tuple-element.53.u_ref, f32[4,33,256]{2,1,0:T(8,128)S(1)} %pad_maximum_fusion.3.refs_0_.rates, f32[4,33,256]{2,1,0:T(8,128)S(1)} %collective-permute-done.5.refs_1_, ...), custom_call_target="tpu_custom_call" | custom-call | flops 1 | bytes 1 | tf_op jit(solution)/shard_map/local_convolution/pallas_call | solution.py:382
  39.9 3.3 %collective-permute-start.10 = (bf16[4,16,256]{2,1,0:T(8,128)(2,1)S(1)}, bf16[4,16,256]{2,1,0:T(8,128)(2,1)S(1)}, u32[]{:S(2)}, u32[]{:S(2)}) collective-permute-start(bf16[4,16,256]{2,1,0:T(8,128)(2,1)S(1)} %slab_states.1), channel_id=1, source_target_pairs={{0,8},{2,10},{4,12},{6,14},{8,16},{10,18},{12,20},{14,22},{16,24},... | collective-permute-start | bytes 98312 | tf_op jit(solution)/shard_map/ppermute | solution.py:303
  51.1 3.1 %collective-permute-done.14.refs_6_ = bf16[4,16,256]{2,1,0:T(8,128)(2,1)S(1)} collective-permute-done((bf16[4,16,256]{2,1,0:T(8,128)(2,1)S(1)}, bf16[4,16,256]{2,1,0:T(8,128)(2,1)S(1)}, u32[]{:S(2)}, u32[]{:S(2)}) %collective-permute-start.14) | collective-permute-done | bytes 32800 | tf_op jit(solution)/shard_map/ppermute | solution.py:300
  63.6 9.5 %collective-permute-done.17.refs_0_.refs_2_ = bf16[128,2048]{1,0:T(8,128)(2,1)S(1)} collective-permute-done((bf16[128,2048]{1,0:T(8,128)(2,1)S(1)}, bf16[128,2048]{1,0:T(8,128)(2,1)S(1)}, u32[]{:S(2)}, u32[]{:S(2)}) %collective-permute-start.17) | collective-permute-done | bytes 524320 | tf_op jit(solution)/shard_map/ppermute | solution.py:310
  75.5 3.0 %project_block.11 = bf16[1,2,128,256]{3,2,1,0:T(8,128)(2,1)S(1)} custom-call(s32[3]{0:T(128)S(1)} %add_add_fusion.1.here, bf16[128,2048]{1,0:T(8,128)(2,1)S(1)} %gated_block.2.refs_0_, bf16[128,2048]{1,0:T(8,128)(2,1)S(1)} %gated_block.3.refs_1_, bf16[4096,512]{1,0:T(8,128)(2,1)S(1)} %copy-done, bf16[4096,512]{1,0:T(8,128)(2,1)} %collective-permute-done.16.refs_3_.refs_2_), custom_call_target="tpu_custom_call" | custom-call | flops 1 | bytes 1 | tf_op jit(solution)/shard_map/project_block/pallas_call | solution.py:442
  78.5 3.0 %project_block.12 = bf16[1,2,128,256]{3,2,1,0:T(8,128)(2,1)S(1)} custom-call(s32[3]{0:T(128)S(1)} %add_add_fusion.here, bf16[128,2048]{1,0:T(8,128)(2,1)S(1)} %gated_block.2.refs_0_, bf16[128,2048]{1,0:T(8,128)(2,1)S(1)} %gated_block.3.refs_1_, bf16[4096,512]{1,0:T(8,128)(2,1)S(1)} %copy-done, bf16[4096,512]{1,0:T(8,128)(2,1)} %collective-permute-done.16.refs_3_.refs_2_), custom_call_target="tpu_custom_call" | custom-call | flops 1 | bytes 1 | tf_op jit(solution)/shard_map/project_block/pallas_call | solution.py:442
  85.5 10.1 %collective-permute-done.19.refs_0_.refs_4_ = bf16[128,2048]{1,0:T(8,128)(2,1)S(1)} collective-permute-done((bf16[128,2048]{1,0:T(8,128)(2,1)S(1)}, bf16[128,2048]{1,0:T(8,128)(2,1)S(1)}, u32[]{:S(2)}, u32[]{:S(2)}) %collective-permute-start.19) | collective-permute-done | bytes 524320 | tf_op jit(solution)/shard_map/ppermute | solution.py:310
  102.4 4.5 %collective-permute-done.20.refs_1_.refs_5_ = bf16[128,2048]{1,0:T(8,128)(2,1)S(1)} collective-permute-done((bf16[128,2048]{1,0:T(8,128)(2,1)S(1)}, bf16[128,2048]{1,0:T(8,128)(2,1)S(1)}, u32[]{:S(2)}, u32[]{:S(2)}) %collective-permute-start.20) | collective-permute-done | bytes 524320 | tf_op jit(solution)/shard_map/ppermute | solution.py:310
  107.0 3.6 %project_block.13 = bf16[1,2,128,256]{3,2,1,0:T(8,128)(2,1)} custom-call(s32[3]{0:T(128)S(1)} %add_add_fusion.1.here, bf16[128,2048]{1,0:T(8,128)(2,1)S(1)} %collective-permute-done.19.refs_0_.refs_4_, bf16[128,2048]{1,0:T(8,128)(2,1)S(1)} %collective-permute-done.20.refs_1_.refs_5_, bf16[4096,512]{1,0:T(8,128)(2,1)S(1)} %copy-done, ...), custom_call_target="tpu_custom_call" | custom-call | flops 1 | bytes 1 | tf_op jit(solution)/shard_map/project_block/pallas_call | solution.py:442
  113.6 5.8 %all-gather.3.cloned.1.call-done = bf16[16384,512]{1,0:T(8,128)(2,1)} async-done(((bf16[4096,512]{1,0:T(8,128)(2,1)}), bf16[16384,512]{1,0:T(8,128)(2,1)}) %all-gather.3.cloned.1.call-update) | async-done | bytes 16777232 | tf_op jit(solution)/shard_map/all_gather | solution.py:321
  119.4 5.4 %project_block.16 = bf16[3,2,128,256]{3,2,1,0:T(8,128)(2,1)} custom-call(s32[3]{0:T(128)S(1)} %add_add_fusion.1.here, bf16[128,2048]{1,0:T(8,128)(2,1)S(1)} %gated_block.2.refs_0_, bf16[128,2048]{1,0:T(8,128)(2,1)S(1)} %gated_block.3.refs_1_, bf16[128,2048]{1,0:T(8,128)(2,1)S(1)} %collective-permute-done.17.refs_0_.refs_2_, ...), custom_call_target="tpu_custom_call" | custom-call | flops 1 | bytes 1 | tf_op jit(solution)/shard_map/project_block/pallas_call | solution.py:442
  127.0 4.9 %project_block.18 = bf16[3,2,128,256]{3,2,1,0:T(8,128)(2,1)S(1)} custom-call(s32[3]{0:T(128)S(1)} %add_add_fusion.here, bf16[128,2048]{1,0:T(8,128)(2,1)S(1)} %gated_block.2.refs_0_, bf16[128,2048]{1,0:T(8,128)(2,1)S(1)} %gated_block.3.refs_1_, bf16[128,2048]{1,0:T(8,128)(2,1)S(1)} %collective-permute-done.17.refs_0_.refs_2_, ...), custom_call_target="tpu_custom_call" | custom-call | flops 1 | bytes 1 | tf_op jit(solution)/shard_map/project_block/pallas_call | solution.py:442
  131.9 4.5 %project_block.19.refs_4_ = f32[2,1,4,128,256]{4,3,2,1,0:T(8,128)S(1)} custom-call(s32[3]{0:T(128)S(1)} %add_add_fusion.2.here, bf16[128,2048]{1,0:T(8,128)(2,1)} %collective-permute-done.26.refs_0_, bf16[4096,512]{1,0:T(8,128)(2,1)S(1)} %copy-done.1, bf16[4096,512]{1,0:T(8,128)(2,1)} %collective-permute-done.16.refs_3_.refs_2_, bf16[4,4096,512]{2,1,0:T(8,128)(2,1)} %bitcast.37), custom_call_target="tpu_custom_call" | custom-call | flops 1 | bytes 1 | tf_op jit(solution)/shard_map/project_block/pallas_call | solution.py:442
  136.5 3.7 %project_block.20 = bf16[1,4,128,256]{3,2,1,0:T(8,128)(2,1)S(1)} custom-call(s32[3]{0:T(128)S(1)} %add_add_fusion.1.here, bf16[128,2048]{1,0:T(8,128)(2,1)} %collective-permute-done.25.refs_0_, bf16[4096,512]{1,0:T(8,128)(2,1)S(1)} %copy-done.1, bf16[4096,512]{1,0:T(8,128)(2,1)} %collective-permute-done.16.refs_3_.refs_2_, bf16[4,4096,512]{2,1,0:T(8,128)(2,1)} %bitcast.38, ...), custom_call_target="tpu_custom_call" | custom-call | flops 1 | bytes 1 | tf_op jit(solution)/shard_map/project_block/pallas_call | solution.py:442
  142.4 4.8 %collective-permute-start.27 = (bf16[4,128,256]{2,1,0:T(8,128)(2,1)S(1)}, bf16[4,128,256]{2,1,0:T(8,128)(2,1)S(1)}, u32[]{:S(2)}, u32[]{:S(2)}) collective-permute-start(bf16[4,128,256]{2,1,0:T(8,128)(2,1)S(1)} %get-tuple-element.96), channel_id=1, source_target_pairs={{0,0},{1,24},{2,2},{3,26},{4,4},{5,28},{6,6},{7,30},{8,8},{9,16},{... | collective-permute-start | bytes 786440 | tf_op jit(solution)/shard_map/ppermute | solution.py:487
  147.3 3.9 %collective-permute-start.30 = (bf16[4,128,256]{2,1,0:T(8,128)(2,1)S(1)}, bf16[4,128,256]{2,1,0:T(8,128)(2,1)S(1)}, u32[]{:S(2)}, u32[]{:S(2)}) collective-permute-start(bf16[4,128,256]{2,1,0:T(8,128)(2,1)S(1)} %get-tuple-element.95), channel_id=1, source_target_pairs={{0,24},{1,0},{2,26},{3,2},{4,28},{5,4},{6,30},{7,6},{8,16},{9,8},{... | collective-permute-start | bytes 786440 | tf_op jit(solution)/shard_map/ppermute | solution.py:487
  154.1 3.6 %project_block.21 = bf16[1,4,128,256]{3,2,1,0:T(8,128)(2,1)S(1)} custom-call(s32[3]{0:T(128)S(1)} %add_add_fusion.here, bf16[128,2048]{1,0:T(8,128)(2,1)} %collective-permute-done.25.refs_0_, bf16[4096,512]{1,0:T(8,128)(2,1)S(1)} %copy-done.1, bf16[4096,512]{1,0:T(8,128)(2,1)} %collective-permute-done.16.refs_3_.refs_2_, bf16[4,4096,512]{2,1,0:T(8,128)(2,1)} %bitcast.39, ...), custom_call_target="tpu_custom_call" | custom-call | flops 1 | bytes 1 | tf_op jit(solution)/shard_map/project_block/pallas_call | solution.py:442
  160.7 4.3 %collective-permute-start.31 = (bf16[4,128,256]{2,1,0:T(8,128)(2,1)S(1)}, bf16[4,128,256]{2,1,0:T(8,128)(2,1)S(1)}, u32[]{:S(2)}, u32[]{:S(2)}) collective-permute-start(bf16[4,128,256]{2,1,0:T(8,128)(2,1)S(1)} %get-tuple-element.93), channel_id=1, source_target_pairs={{0,8},{1,16},{2,10},{3,18},{4,12},{5,20},{6,14},{7,22},{8,24},{9,0... | collective-permute-start | bytes 786440 | tf_op jit(solution)/shard_map/ppermute | solution.py:487
  165.1 4.5 %collective-permute-done.29.refs_1_ = bf16[4,128,256]{2,1,0:T(8,128)(2,1)S(1)} collective-permute-done((bf16[4,128,256]{2,1,0:T(8,128)(2,1)S(1)}, bf16[4,128,256]{2,1,0:T(8,128)(2,1)S(1)}, u32[]{:S(2)}, u32[]{:S(2)}) %collective-permute-start.29) | collective-permute-done | bytes 262176 | tf_op jit(solution)/shard_map/ppermute | solution.py:487
  169.6 6.6 %collective-permute-done.31.refs_3_ = bf16[4,128,256]{2,1,0:T(8,128)(2,1)S(1)} collective-permute-done((bf16[4,128,256]{2,1,0:T(8,128)(2,1)S(1)}, bf16[4,128,256]{2,1,0:T(8,128)(2,1)S(1)}, u32[]{:S(2)}, u32[]{:S(2)}) %collective-permute-start.31) | collective-permute-done | bytes 262176 | tf_op jit(solution)/shard_map/ppermute | solution.py:487
  (94 shorter events, 60.0 us)
Async XLA Ops:
  6.5 112.8 %all-gather.3.cloned.1.call-start = ((), (), s32[]{:S(2)}) async-start(), calls=%async_computation | async-start | bytes 20971520 | tf_op jit(solution)/shard_map/all_gather | solution.py:321
  7.3 66.0 %collective-permute-start.16 = (bf16[4096,512]{1,0:T(8,128)(2,1)}, bf16[4096,512]{1,0:T(8,128)(2,1)}, u32[]{:S(2)}, u32[]{:S(2)}) collective-permute-start(bf16[4096,512]{1,0:T(8,128)(2,1)} %refs_1_.5), channel_id=1, source_target_pairs={{0,2},{2,0},{4,6},{6,4},{8,10},{10,8},{12,14},{14,12},{16,18},{18,... | collective-permute-start | bytes 12582920 | tf_op jit(solution)/shard_map/ppermute | solution.py:300
  7.4 7.2 %collective-permute-start = (f32[33,256]{1,0:T(8,128)S(1)}, f32[33,256]{1,0:T(8,128)S(1)}, u32[]{:S(2)}, u32[]{:S(2)}) collective-permute-start(f32[33,256]{1,0:T(8,128)S(1)} %get-tuple-element.101), channel_id=1, source_target_pairs={{0,24},{2,26},{4,28},{6,30},{8,0},{10,2},{12,4},{14,6},{16,8},{18,... | collective-permute-start | bytes 101384 | tf_op jit(solution)/shard_map/ppermute | solution.py:303
  11.1 5.8 %collective-permute-start.2 = (f32[33,256]{1,0:T(8,128)S(1)}, f32[33,256]{1,0:T(8,128)S(1)}, u32[]{:S(2)}, u32[]{:S(2)}) collective-permute-start(f32[33,256]{1,0:T(8,128)S(1)} %get-tuple-element.101), channel_id=1, source_target_pairs={{0,8},{2,10},{4,12},{6,14},{8,16},{10,18},{12,20},{14,22},{16,24},... | collective-permute-start | bytes 101384 | tf_op jit(solution)/shard_map/ppermute | solution.py:303
  16.9 9.3 %collective-permute-start.4 = (f32[4,33,256]{2,1,0:T(8,128)S(1)}, f32[4,33,256]{2,1,0:T(8,128)S(1)}, u32[]{:S(2)}, u32[]{:S(2)}) collective-permute-start(f32[4,33,256]{2,1,0:T(8,128)S(1)} %pad_maximum_fusion.3.refs_0_.rates), channel_id=1, source_target_pairs={{0,4},{2,6},{4,0},{6,2},{8,12},{10,14},{12,8},{14,10},{16,20},{18,... | collective-permute-start | bytes 405512 | tf_op jit(solution)/shard_map/ppermute | solution.py:300
  20.0 6.3 %collective-permute-start.5 = (f32[4,33,256]{2,1,0:T(8,128)S(1)}, f32[4,33,256]{2,1,0:T(8,128)S(1)}, u32[]{:S(2)}, u32[]{:S(2)}) collective-permute-start(f32[4,33,256]{2,1,0:T(8,128)S(1)} %pad_maximum_fusion.3.refs_0_.rates), channel_id=1, source_target_pairs={{0,2},{2,0},{4,6},{6,4},{8,10},{10,8},{12,14},{14,12},{16,18},{18,... | collective-permute-start | bytes 405512 | tf_op jit(solution)/shard_map/ppermute | solution.py:300
  30.9 8.3 %collective-permute-start.7 = (bf16[4,16,256]{2,1,0:T(8,128)(2,1)S(1)}, bf16[4,16,256]{2,1,0:T(8,128)(2,1)S(1)}, u32[]{:S(2)}, u32[]{:S(2)}) collective-permute-start(bf16[4,16,256]{2,1,0:T(8,128)(2,1)S(1)} %get-tuple-element.56), channel_id=1, source_target_pairs={{0,2},{2,0},{4,6},{6,4},{8,10},{10,8},{12,14},{14,12},{16,18},{18,... | collective-permute-start | bytes 98312 | tf_op jit(solution)/shard_map/ppermute | solution.py:300
  31.2 8.1 %collective-permute-start.8 = (bf16[4,16,256]{2,1,0:T(8,128)(2,1)S(1)}, bf16[4,16,256]{2,1,0:T(8,128)(2,1)S(1)}, u32[]{:S(2)}, u32[]{:S(2)}) collective-permute-start(bf16[4,16,256]{2,1,0:T(8,128)(2,1)S(1)} %get-tuple-element.57), channel_id=1, source_target_pairs={{0,4},{2,6},{4,0},{6,2},{8,12},{10,14},{12,8},{14,10},{16,20},{18,... | collective-permute-start | bytes 98312 | tf_op jit(solution)/shard_map/ppermute | solution.py:300
  39.9 5.8 %collective-permute-start.10 = (bf16[4,16,256]{2,1,0:T(8,128)(2,1)S(1)}, bf16[4,16,256]{2,1,0:T(8,128)(2,1)S(1)}, u32[]{:S(2)}, u32[]{:S(2)}) collective-permute-start(bf16[4,16,256]{2,1,0:T(8,128)(2,1)S(1)} %slab_states.1), channel_id=1, source_target_pairs={{0,8},{2,10},{4,12},{6,14},{8,16},{10,18},{12,20},{14,22},{16,24},... | collective-permute-start | bytes 98312 | tf_op jit(solution)/shard_map/ppermute | solution.py:303
  57.4 15.7 %collective-permute-start.17 = (bf16[128,2048]{1,0:T(8,128)(2,1)S(1)}, bf16[128,2048]{1,0:T(8,128)(2,1)S(1)}, u32[]{:S(2)}, u32[]{:S(2)}) collective-permute-start(bf16[128,2048]{1,0:T(8,128)(2,1)S(1)} %gated_block.2.refs_0_), channel_id=1, source_target_pairs={{0,8},{2,10},{4,12},{6,14},{8,24},{10,26},{12,28},{14,30},{16,0},{... | collective-permute-start | bytes 1572872 | tf_op jit(solution)/shard_map/ppermute | solution.py:310
  60.8 23.6 %collective-permute-start.18 = (bf16[128,2048]{1,0:T(8,128)(2,1)S(1)}, bf16[128,2048]{1,0:T(8,128)(2,1)S(1)}, u32[]{:S(2)}, u32[]{:S(2)}) collective-permute-start(bf16[128,2048]{1,0:T(8,128)(2,1)S(1)} %gated_block.3.refs_1_), channel_id=1, source_target_pairs={{0,8},{2,10},{4,12},{6,14},{8,24},{10,26},{12,28},{14,30},{16,0},{... | collective-permute-start | bytes 1572872 | tf_op jit(solution)/shard_map/ppermute | solution.py:310
  73.1 22.5 %collective-permute-start.19 = (bf16[128,2048]{1,0:T(8,128)(2,1)S(1)}, bf16[128,2048]{1,0:T(8,128)(2,1)S(1)}, u32[]{:S(2)}, u32[]{:S(2)}) collective-permute-start(bf16[128,2048]{1,0:T(8,128)(2,1)S(1)} %collective-permute-done.17.refs_0_.refs_2_), channel_id=1, source_target_pairs={{0,8},{2,10},{4,12},{6,14},{8,24},{10,26},{12,28},{14,30},{16,0},{... | collective-permute-start | bytes 1572872 | tf_op jit(solution)/shard_map/ppermute | solution.py:310
  84.3 22.5 %collective-permute-start.20 = (bf16[128,2048]{1,0:T(8,128)(2,1)S(1)}, bf16[128,2048]{1,0:T(8,128)(2,1)S(1)}, u32[]{:S(2)}, u32[]{:S(2)}) collective-permute-start(bf16[128,2048]{1,0:T(8,128)(2,1)S(1)} %collective-permute-done.18.refs_1_.refs_3_), channel_id=1, source_target_pairs={{0,8},{2,10},{4,12},{6,14},{8,24},{10,26},{12,28},{14,30},{16,0},{... | collective-permute-start | bytes 1572872 | tf_op jit(solution)/shard_map/ppermute | solution.py:310
  84.9 14.5 %collective-permute-start.23 = (bf16[1,2,128,256]{3,2,1,0:T(8,128)(2,1)S(1)}, bf16[1,2,128,256]{3,2,1,0:T(8,128)(2,1)S(1)}, u32[]{:S(2)}, u32[]{:S(2)}) collective-permute-start(bf16[1,2,128,256]{3,2,1,0:T(8,128)(2,1)S(1)} %project_block.11), channel_id=1, source_target_pairs={{0,1},{1,0},{2,3},{3,2},{4,5},{5,4},{6,7},{7,6},{8,9},{9,8},{10,11... | collective-permute-start | bytes 393224 | tf_op jit(solution)/shard_map/ppermute | solution.py:468
  95.6 36.3 %collective-permute-start.26 = (bf16[128,2048]{1,0:T(8,128)(2,1)S(1)}, bf16[128,2048]{1,0:T(8,128)(2,1)}, u32[]{:S(2)}, u32[]{:S(2)}) collective-permute-start(bf16[128,2048]{1,0:T(8,128)(2,1)S(1)} %collective-permute-done.19.refs_0_.refs_4_), channel_id=1, source_target_pairs={{0,8},{2,10},{4,12},{6,14},{8,24},{10,26},{12,28},{14,30},{16,0},{... | collective-permute-start | bytes 1572872 | tf_op jit(solution)/shard_map/ppermute | solution.py:310
  98.7 11.9 %collective-permute-start.21 = (bf16[1,2,128,256]{3,2,1,0:T(8,128)(2,1)S(1)}, bf16[1,2,128,256]{3,2,1,0:T(8,128)(2,1)}, u32[]{:S(2)}, u32[]{:S(2)}) collective-permute-start(bf16[1,2,128,256]{3,2,1,0:T(8,128)(2,1)S(1)} %project_block.14), channel_id=1, source_target_pairs={{0,1},{1,0},{2,3},{3,2},{4,5},{5,4},{6,7},{7,6},{8,9},{9,8},{10,11... | collective-permute-start | bytes 393224 | tf_op jit(solution)/shard_map/ppermute | solution.py:468
  106.8 29.7 %collective-permute-start.25 = (bf16[128,2048]{1,0:T(8,128)(2,1)S(1)}, bf16[128,2048]{1,0:T(8,128)(2,1)}, u32[]{:S(2)}, u32[]{:S(2)}) collective-permute-start(bf16[128,2048]{1,0:T(8,128)(2,1)S(1)} %collective-permute-done.20.refs_1_.refs_5_), channel_id=1, source_target_pairs={{0,8},{2,10},{4,12},{6,14},{8,24},{10,26},{12,28},{14,30},{16,0},{... | collective-permute-start | bytes 1572872 | tf_op jit(solution)/shard_map/ppermute | solution.py:310
  124.8 15.4 %collective-permute-start.22 = (bf16[3,2,128,256]{3,2,1,0:T(8,128)(2,1)}, bf16[3,2,128,256]{3,2,1,0:T(8,128)(2,1)}, u32[]{:S(2)}, u32[]{:S(2)}) collective-permute-start(bf16[3,2,128,256]{3,2,1,0:T(8,128)(2,1)} %project_block.16), channel_id=1, source_target_pairs={{0,1},{1,0},{2,3},{3,2},{4,5},{5,4},{6,7},{7,6},{8,9},{9,8},{10,11... | collective-permute-start | bytes 1179656 | tf_op jit(solution)/shard_map/ppermute | solution.py:468
  125.4 14.8 %collective-permute-start.24 = (bf16[1,2,128,256]{3,2,1,0:T(8,128)(2,1)}, bf16[1,2,128,256]{3,2,1,0:T(8,128)(2,1)}, u32[]{:S(2)}, u32[]{:S(2)}) collective-permute-start(bf16[1,2,128,256]{3,2,1,0:T(8,128)(2,1)} %project_block.13), channel_id=1, source_target_pairs={{0,1},{1,0},{2,3},{3,2},{4,5},{5,4},{6,7},{7,6},{8,9},{9,8},{10,11... | collective-permute-start | bytes 393224 | tf_op jit(solution)/shard_map/ppermute | solution.py:468
  142.4 11.7 %collective-permute-start.27 = (bf16[4,128,256]{2,1,0:T(8,128)(2,1)S(1)}, bf16[4,128,256]{2,1,0:T(8,128)(2,1)S(1)}, u32[]{:S(2)}, u32[]{:S(2)}) collective-permute-start(bf16[4,128,256]{2,1,0:T(8,128)(2,1)S(1)} %get-tuple-element.96), channel_id=1, source_target_pairs={{0,0},{1,24},{2,2},{3,26},{4,4},{5,28},{6,6},{7,30},{8,8},{9,16},{... | collective-permute-start | bytes 786440 | tf_op jit(solution)/shard_map/ppermute | solution.py:487
  147.2 13.3 %collective-permute-start.28 = (bf16[1,4,128,256]{3,2,1,0:T(8,128)(2,1)S(1)}, bf16[1,4,128,256]{3,2,1,0:T(8,128)(2,1)S(1)}, u32[]{:S(2)}, u32[]{:S(2)}) collective-permute-start(bf16[1,4,128,256]{3,2,1,0:T(8,128)(2,1)S(1)} %project_block.20), channel_id=1, source_target_pairs={{0,1},{1,0},{2,3},{3,2},{4,5},{5,4},{6,7},{7,6},{8,9},{9,8},{10,11... | collective-permute-start | bytes 786440 | tf_op jit(solution)/shard_map/ppermute | solution.py:521
  147.3 17.8 %collective-permute-start.30 = (bf16[4,128,256]{2,1,0:T(8,128)(2,1)S(1)}, bf16[4,128,256]{2,1,0:T(8,128)(2,1)S(1)}, u32[]{:S(2)}, u32[]{:S(2)}) collective-permute-start(bf16[4,128,256]{2,1,0:T(8,128)(2,1)S(1)} %get-tuple-element.95), channel_id=1, source_target_pairs={{0,24},{1,0},{2,26},{3,2},{4,28},{5,4},{6,30},{7,6},{8,16},{9,8},{... | collective-permute-start | bytes 786440 | tf_op jit(solution)/shard_map/ppermute | solution.py:487
  160.7 8.9 %collective-permute-start.29 = (bf16[4,128,256]{2,1,0:T(8,128)(2,1)S(1)}, bf16[4,128,256]{2,1,0:T(8,128)(2,1)S(1)}, u32[]{:S(2)}, u32[]{:S(2)}) collective-permute-start(bf16[4,128,256]{2,1,0:T(8,128)(2,1)S(1)} %get-tuple-element.94), channel_id=1, source_target_pairs={{0,16},{1,8},{2,18},{3,10},{4,20},{5,12},{6,22},{7,14},{8,0},{9,24... | collective-permute-start | bytes 786440 | tf_op jit(solution)/shard_map/ppermute | solution.py:487
  160.7 15.5 %collective-permute-start.31 = (bf16[4,128,256]{2,1,0:T(8,128)(2,1)S(1)}, bf16[4,128,256]{2,1,0:T(8,128)(2,1)S(1)}, u32[]{:S(2)}, u32[]{:S(2)}) collective-permute-start(bf16[4,128,256]{2,1,0:T(8,128)(2,1)S(1)} %get-tuple-element.93), channel_id=1, source_target_pairs={{0,8},{1,16},{2,10},{3,18},{4,12},{5,20},{6,14},{7,22},{8,24},{9,0... | collective-permute-start | bytes 786440 | tf_op jit(solution)/shard_map/ppermute | solution.py:487
  (18 other events, 72.0 us)
Sparse Core Ops, SparseCore 0:
  8.9 110.4 all-gather.2

commit v5 on v4

--- a/solution.py
+++ b/solution.py
@@ -199,18 +199,22 @@
         source = sources[which] if rank is None else sources[which].at[here[rank]]
         copies.append(pltpu.make_async_copy(source.at[rows, columns], slots.at[i], sems.at[i]))
         copies[-1].start()
+    tokens, size = blocks[0].shape
+    stacked = [
+        jnp.concatenate([blocks[runs * j + h][...] for j in range(count)], axis=0) for h in range(runs)
+    ]
     for i in range(len(picks)):
         copies[i].wait()
+        products = None
+        for h in range(runs):
+            term = jnp.dot(
+                stacked[h], slots[i, h * size : (h + 1) * size], preferred_element_type=F32
+            )
+            products = term if products is None else products + term
         for j in range(count):
-            total = sources[-1][here[0], j, i] if added else None
-            for h in range(runs):
-                size = depth // runs
-                term = jnp.dot(
-                    blocks[runs * j + h][...],
-                    slots[i, h * size : (h + 1) * size],
-                    preferred_element_type=F32,
-                )
-                total = term if total is None else total + term
+            total = products[j * tokens : (j + 1) * tokens]
+            if added:
+                total = sources[-1][here[0], j, i] + total
             if out_ref.ndim == 4:
                 out_ref[j, i] = total.astype(out_ref.dtype)
             else:
@@ -486,11 +490,6 @@
         moved = jnp.where(tp_me == 0, classes[by], classes[(by + slabs // tp) % slabs])
         return lax.ppermute(moved, ("ctx", "tp"), pairs)
 
-    near, far, both = (
-        ((0, None), (1, None)),
-        ((0, 1), (0, 2)),
-        ((0, None), (1, None), (2, 1), (2, 2)),
-    )
     near, far, both = (
         ((0, None), (1, None)),
         ((0, 1), (0, 2)),

time: 187 us -> 189 us (1.011)
  Pallas kernels: 60.7 us -> 62.8 us
    pallas_call x11, Pallas kernels: 40.8 us -> 42.8 us  [project(): pl.pallas_call(functools.partial(project_kernel, len(blocks), picks, halv...]
  transfers between devices with their start and end apart: 33 -> 33, of which waited for: 16 -> 16; matrix products, arithmetic and copies ran while one was open for 1% -> 1% of each run, Pallas kernels for 32% -> 33%
where the time goes in v5:
time: 189 us; the launch traced here: 187 us
  Pallas kernels  62.8 us (33%)
  waiting for transfers between devices  59.9 us (32%)
  starting transfers between devices  41.1 us (22%)
  between operations  13.8 us (7%)
  local copies, waits for them, and re-layouts  5.78 us (3%)
  other arithmetic  3.52 us (2%)
    pallas_call x11, Pallas kernels, project(): pl.pallas_call(functools.partial(project_kernel, len(blocks), picks, halv...  42.8 us
    ppermute x6, waiting for transfers between devices, ring(): return lax.ppermute(array, 'ctx', pairs)  27 us
    ppermute x4, waiting for transfers between devices, deliver(): return lax.ppermute(moved, ('ctx', 'tp'), pairs)  13.1 us
    ppermute x4, starting transfers between devices, deliver(): return lax.ppermute(moved, ('ctx', 'tp'), pairs)  13 us
    ppermute x6, starting transfers between devices, from_slab(): lax.ppermute(array, 'ctx', [(i, (i - by * SLAB) % ctx) for i in range(ctx)])  10.4 us
    ppermute x10, starting transfers between devices, within_slab(): return lax.ppermute(array, 'ctx', [(i, i ^ mask) for i in range(ctx)])  8.01 us
    all_gather x1, waiting for transfers between devices, per_device(): lax.all_gather(out_weight, 'ctx', axis_index_groups=[list(range(z * SLAB,...  5.75 us
    ppermute x10, waiting for transfers between devices, within_slab(): return lax.ppermute(array, 'ctx', [(i, i ^ mask) for i in range(ctx)])  5.62 us
  transfers between devices with their start and end apart: 33, of which 16 were waited for; matrix products, arithmetic and copies ran while one was open for 1% of the time, Pallas kernels for 33%

profile of v5, /device:TPU:4, one launch (start us, length us, event | category | flops | bytes accessed | tf_op | source)
XLA Modules:
  0.0 186.9 jit_solution(9026440212648817110)
XLA Ops:
  7.4 3.7 %collective-permute-start = (f32[33,256]{1,0:T(8,128)S(1)}, f32[33,256]{1,0:T(8,128)S(1)}, u32[]{:S(2)}, u32[]{:S(2)}) collective-permute-start(f32[33,256]{1,0:T(8,128)S(1)} %get-tuple-element.101), channel_id=1, source_target_pairs={{0,24},{2,26},{4,28},{6,30},{8,0},{10,2},{12,4},{14,6},{16,8},{18,... | collective-permute-start | bytes 101384 | tf_op jit(solution)/shard_map/ppermute | solution.py:307
  16.9 3.1 %collective-permute-start.4 = (f32[4,33,256]{2,1,0:T(8,128)S(1)}, f32[4,33,256]{2,1,0:T(8,128)S(1)}, u32[]{:S(2)}, u32[]{:S(2)}) collective-permute-start(f32[4,33,256]{2,1,0:T(8,128)S(1)} %pad_maximum_fusion.3.refs_0_.rates), channel_id=1, source_target_pairs={{0,4},{2,6},{4,0},{6,2},{8,12},{10,14},{12,8},{14,10},{16,20},{18,... | collective-permute-start | bytes 405512 | tf_op jit(solution)/shard_map/ppermute | solution.py:304
  22.5 3.3 %short_filters.1 = (f32[4,128,8,128]{3,2,1,0:T(8,128)S(1)}, f32[4,128,8,128]{3,2,1,0:T(8,128)S(1)}) custom-call(s32[3]{0:T(128)S(1)} %pad_add_fusion.here, bf16[3,128,4096]{2,1,0:T(8,128)(2,1)S(1)} %copy-done.2, bf16[3,2,4096]{2,1,0:T(2,128)(2,1)S(1)} %collective-permute-done.3.halo, f32[3,3,8192]{2,1,0:T(4,128)S(1)} %copy-done.3), custom_call_target="tpu_custom_call" | custom-call | flops 1 | bytes 1 | tf_op jit(solution)/shard_map/short_filters/pallas_call | solution.py:360
  27.8 3.1 %block_states.1 = (bf16[4,16,256]{2,1,0:T(8,128)(2,1)S(1)}, bf16[4,16,256]{2,1,0:T(8,128)(2,1)S(1)}, bf16[4,16,256]{2,1,0:T(8,128)(2,1)S(1)}, bf16[4,16,256]{2,1,0:T(8,128)(2,1)S(1)}) custom-call(s32[3]{0:T(128)S(1)} %pad_add_fusion.here, f32[4,128,8,128]{3,2,1,0:T(8,128)S(1)} %get-tuple-element.53.u_ref, f32[4,33,256]{2,1,0:T(8,128)S(1)} %pad_maximum_fusion.3.refs_0_.rates, ...), custom_call_target="tpu_custom_call" | custom-call | flops 1 | bytes 1 | tf_op jit(solution)/shard_map/block_states/pallas_call | solution.py:376
  33.6 5.6 %local_convolution.1.y_ref = f32[4,128,8,128]{3,2,1,0:T(8,128)S(1)} custom-call(s32[3]{0:T(128)S(1)} %pad_add_fusion.here, f32[4,128,8,128]{3,2,1,0:T(8,128)S(1)} %get-tuple-element.53.u_ref, f32[4,33,256]{2,1,0:T(8,128)S(1)} %pad_maximum_fusion.3.refs_0_.rates, f32[4,33,256]{2,1,0:T(8,128)S(1)} %collective-permute-done.5.refs_1_, ...), custom_call_target="tpu_custom_call" | custom-call | flops 1 | bytes 1 | tf_op jit(solution)/shard_map/local_convolution/pallas_call | solution.py:386
  39.9 3.3 %collective-permute-start.10 = (bf16[4,16,256]{2,1,0:T(8,128)(2,1)S(1)}, bf16[4,16,256]{2,1,0:T(8,128)(2,1)S(1)}, u32[]{:S(2)}, u32[]{:S(2)}) collective-permute-start(bf16[4,16,256]{2,1,0:T(8,128)(2,1)S(1)} %slab_states.1), channel_id=1, source_target_pairs={{0,8},{2,10},{4,12},{6,14},{8,16},{10,18},{12,20},{14,22},{16,24},... | collective-permute-start | bytes 98312 | tf_op jit(solution)/shard_map/ppermute | solution.py:307
  51.1 3.1 %collective-permute-done.14.refs_6_ = bf16[4,16,256]{2,1,0:T(8,128)(2,1)S(1)} collective-permute-done((bf16[4,16,256]{2,1,0:T(8,128)(2,1)S(1)}, bf16[4,16,256]{2,1,0:T(8,128)(2,1)S(1)}, u32[]{:S(2)}, u32[]{:S(2)}) %collective-permute-start.14) | collective-permute-done | bytes 32800 | tf_op jit(solution)/shard_map/ppermute | solution.py:304
  63.6 9.5 %collective-permute-done.17.refs_0_.refs_2_ = bf16[128,2048]{1,0:T(8,128)(2,1)S(1)} collective-permute-done((bf16[128,2048]{1,0:T(8,128)(2,1)S(1)}, bf16[128,2048]{1,0:T(8,128)(2,1)S(1)}, u32[]{:S(2)}, u32[]{:S(2)}) %collective-permute-start.17) | collective-permute-done | bytes 524320 | tf_op jit(solution)/shard_map/ppermute | solution.py:314
  75.5 3.0 %project_block.11 = bf16[1,2,128,256]{3,2,1,0:T(8,128)(2,1)S(1)} custom-call(s32[3]{0:T(128)S(1)} %add_add_fusion.1.here, bf16[128,2048]{1,0:T(8,128)(2,1)S(1)} %gated_block.2.refs_0_, bf16[128,2048]{1,0:T(8,128)(2,1)S(1)} %gated_block.3.refs_1_, bf16[4096,512]{1,0:T(8,128)(2,1)S(1)} %copy-done, bf16[4096,512]{1,0:T(8,128)(2,1)} %collective-permute-done.16.refs_3_.refs_2_), custom_call_target="tpu_custom_call" | custom-call | flops 1 | bytes 1 | tf_op jit(solution)/shard_map/project_block/pallas_call | solution.py:446
  85.5 10.1 %collective-permute-done.19.refs_0_.refs_4_ = bf16[128,2048]{1,0:T(8,128)(2,1)S(1)} collective-permute-done((bf16[128,2048]{1,0:T(8,128)(2,1)S(1)}, bf16[128,2048]{1,0:T(8,128)(2,1)S(1)}, u32[]{:S(2)}, u32[]{:S(2)}) %collective-permute-start.19) | collective-permute-done | bytes 524320 | tf_op jit(solution)/shard_map/ppermute | solution.py:314
  99.4 3.0 %project_block.17 = bf16[1,2,128,256]{3,2,1,0:T(8,128)(2,1)S(1)} custom-call(s32[3]{0:T(128)S(1)} %add_add_fusion.here, bf16[128,2048]{1,0:T(8,128)(2,1)S(1)} %collective-permute-done.17.refs_0_.refs_2_, bf16[128,2048]{1,0:T(8,128)(2,1)S(1)} %collective-permute-done.18.refs_1_.refs_3_, bf16[4096,512]{1,0:T(8,128)(2,1)S(1)} %copy-done, ...), custom_call_target="tpu_custom_call" | custom-call | flops 1 | bytes 1 | tf_op jit(solution)/shard_map/project_block/pallas_call | solution.py:446
  102.4 4.5 %collective-permute-done.20.refs_1_.refs_5_ = bf16[128,2048]{1,0:T(8,128)(2,1)S(1)} collective-permute-done((bf16[128,2048]{1,0:T(8,128)(2,1)S(1)}, bf16[128,2048]{1,0:T(8,128)(2,1)S(1)}, u32[]{:S(2)}, u32[]{:S(2)}) %collective-permute-start.20) | collective-permute-done | bytes 524320 | tf_op jit(solution)/shard_map/ppermute | solution.py:314
  107.0 3.6 %project_block.13 = bf16[1,2,128,256]{3,2,1,0:T(8,128)(2,1)} custom-call(s32[3]{0:T(128)S(1)} %add_add_fusion.1.here, bf16[128,2048]{1,0:T(8,128)(2,1)S(1)} %collective-permute-done.19.refs_0_.refs_4_, bf16[128,2048]{1,0:T(8,128)(2,1)S(1)} %collective-permute-done.20.refs_1_.refs_5_, bf16[4096,512]{1,0:T(8,128)(2,1)S(1)} %copy-done, ...), custom_call_target="tpu_custom_call" | custom-call | flops 1 | bytes 1 | tf_op jit(solution)/shard_map/project_block/pallas_call | solution.py:446
  113.6 5.8 %all-gather.3.cloned.1.call-done = bf16[16384,512]{1,0:T(8,128)(2,1)} async-done(((bf16[4096,512]{1,0:T(8,128)(2,1)}), bf16[16384,512]{1,0:T(8,128)(2,1)}) %all-gather.3.cloned.1.call-update) | async-done | bytes 16777232 | tf_op jit(solution)/shard_map/all_gather | solution.py:325
  119.4 6.4 %project_block.16 = bf16[3,2,128,256]{3,2,1,0:T(8,128)(2,1)} custom-call(s32[3]{0:T(128)S(1)} %add_add_fusion.1.here, bf16[128,2048]{1,0:T(8,128)(2,1)S(1)} %gated_block.2.refs_0_, bf16[128,2048]{1,0:T(8,128)(2,1)S(1)} %gated_block.3.refs_1_, bf16[128,2048]{1,0:T(8,128)(2,1)S(1)} %collective-permute-done.17.refs_0_.refs_2_, ...), custom_call_target="tpu_custom_call" | custom-call | flops 1 | bytes 1 | tf_op jit(solution)/shard_map/project_block/pallas_call | solution.py:446
  128.0 6.0 %project_block.18 = bf16[3,2,128,256]{3,2,1,0:T(8,128)(2,1)S(1)} custom-call(s32[3]{0:T(128)S(1)} %add_add_fusion.here, bf16[128,2048]{1,0:T(8,128)(2,1)S(1)} %gated_block.2.refs_0_, bf16[128,2048]{1,0:T(8,128)(2,1)S(1)} %gated_block.3.refs_1_, bf16[128,2048]{1,0:T(8,128)(2,1)S(1)} %collective-permute-done.17.refs_0_.refs_2_, ...), custom_call_target="tpu_custom_call" | custom-call | flops 1 | bytes 1 | tf_op jit(solution)/shard_map/project_block/pallas_call | solution.py:446
  134.0 4.5 %project_block.19.refs_4_ = f32[2,1,4,128,256]{4,3,2,1,0:T(8,128)S(1)} custom-call(s32[3]{0:T(128)S(1)} %add_add_fusion.2.here, bf16[128,2048]{1,0:T(8,128)(2,1)} %collective-permute-done.26.refs_0_, bf16[4096,512]{1,0:T(8,128)(2,1)S(1)} %copy-done.1, bf16[4096,512]{1,0:T(8,128)(2,1)} %collective-permute-done.16.refs_3_.refs_2_, bf16[4,4096,512]{2,1,0:T(8,128)(2,1)} %bitcast.37), custom_call_target="tpu_custom_call" | custom-call | flops 1 | bytes 1 | tf_op jit(solution)/shard_map/project_block/pallas_call | solution.py:446
  138.6 3.7 %project_block.20 = bf16[1,4,128,256]{3,2,1,0:T(8,128)(2,1)S(1)} custom-call(s32[3]{0:T(128)S(1)} %add_add_fusion.1.here, bf16[128,2048]{1,0:T(8,128)(2,1)} %collective-permute-done.25.refs_0_, bf16[4096,512]{1,0:T(8,128)(2,1)S(1)} %copy-done.1, bf16[4096,512]{1,0:T(8,128)(2,1)} %collective-permute-done.16.refs_3_.refs_2_, bf16[4,4096,512]{2,1,0:T(8,128)(2,1)} %bitcast.38, ...), custom_call_target="tpu_custom_call" | custom-call | flops 1 | bytes 1 | tf_op jit(solution)/shard_map/project_block/pallas_call | solution.py:446
  144.5 4.8 %collective-permute-start.27 = (bf16[4,128,256]{2,1,0:T(8,128)(2,1)S(1)}, bf16[4,128,256]{2,1,0:T(8,128)(2,1)S(1)}, u32[]{:S(2)}, u32[]{:S(2)}) collective-permute-start(bf16[4,128,256]{2,1,0:T(8,128)(2,1)S(1)} %get-tuple-element.96), channel_id=1, source_target_pairs={{0,0},{1,24},{2,2},{3,26},{4,4},{5,28},{6,6},{7,30},{8,8},{9,16},{... | collective-permute-start | bytes 786440 | tf_op jit(solution)/shard_map/ppermute | solution.py:491
  149.3 3.9 %collective-permute-start.30 = (bf16[4,128,256]{2,1,0:T(8,128)(2,1)S(1)}, bf16[4,128,256]{2,1,0:T(8,128)(2,1)S(1)}, u32[]{:S(2)}, u32[]{:S(2)}) collective-permute-start(bf16[4,128,256]{2,1,0:T(8,128)(2,1)S(1)} %get-tuple-element.95), channel_id=1, source_target_pairs={{0,24},{1,0},{2,26},{3,2},{4,28},{5,4},{6,30},{7,6},{8,16},{9,8},{... | collective-permute-start | bytes 786440 | tf_op jit(solution)/shard_map/ppermute | solution.py:491
  156.2 3.7 %project_block.21 = bf16[1,4,128,256]{3,2,1,0:T(8,128)(2,1)S(1)} custom-call(s32[3]{0:T(128)S(1)} %add_add_fusion.here, bf16[128,2048]{1,0:T(8,128)(2,1)} %collective-permute-done.25.refs_0_, bf16[4096,512]{1,0:T(8,128)(2,1)S(1)} %copy-done.1, bf16[4096,512]{1,0:T(8,128)(2,1)} %collective-permute-done.16.refs_3_.refs_2_, bf16[4,4096,512]{2,1,0:T(8,128)(2,1)} %bitcast.39, ...), custom_call_target="tpu_custom_call" | custom-call | flops 1 | bytes 1 | tf_op jit(solution)/shard_map/project_block/pallas_call | solution.py:446
  162.8 4.3 %collective-permute-start.31 = (bf16[4,128,256]{2,1,0:T(8,128)(2,1)S(1)}, bf16[4,128,256]{2,1,0:T(8,128)(2,1)S(1)}, u32[]{:S(2)}, u32[]{:S(2)}) collective-permute-start(bf16[4,128,256]{2,1,0:T(8,128)(2,1)S(1)} %get-tuple-element.93), channel_id=1, source_target_pairs={{0,8},{1,16},{2,10},{3,18},{4,12},{5,20},{6,14},{7,22},{8,24},{9,0... | collective-permute-start | bytes 786440 | tf_op jit(solution)/shard_map/ppermute | solution.py:491
  167.1 4.5 %collective-permute-done.29.refs_1_ = bf16[4,128,256]{2,1,0:T(8,128)(2,1)S(1)} collective-permute-done((bf16[4,128,256]{2,1,0:T(8,128)(2,1)S(1)}, bf16[4,128,256]{2,1,0:T(8,128)(2,1)S(1)}, u32[]{:S(2)}, u32[]{:S(2)}) %collective-permute-start.29) | collective-permute-done | bytes 262176 | tf_op jit(solution)/shard_map/ppermute | solution.py:491
  171.7 6.6 %collective-permute-done.31.refs_3_ = bf16[4,128,256]{2,1,0:T(8,128)(2,1)S(1)} collective-permute-done((bf16[4,128,256]{2,1,0:T(8,128)(2,1)S(1)}, bf16[4,128,256]{2,1,0:T(8,128)(2,1)S(1)}, u32[]{:S(2)}, u32[]{:S(2)}) %collective-permute-start.31) | collective-permute-done | bytes 262176 | tf_op jit(solution)/shard_map/ppermute | solution.py:491
  (94 shorter events, 60.0 us)
Async XLA Ops:
  6.5 112.8 %all-gather.3.cloned.1.call-start = ((), (), s32[]{:S(2)}) async-start(), calls=%async_computation | async-start | bytes 20971520 | tf_op jit(solution)/shard_map/all_gather | solution.py:325
  7.3 66.0 %collective-permute-start.16 = (bf16[4096,512]{1,0:T(8,128)(2,1)}, bf16[4096,512]{1,0:T(8,128)(2,1)}, u32[]{:S(2)}, u32[]{:S(2)}) collective-permute-start(bf16[4096,512]{1,0:T(8,128)(2,1)} %refs_1_.5), channel_id=1, source_target_pairs={{0,2},{2,0},{4,6},{6,4},{8,10},{10,8},{12,14},{14,12},{16,18},{18,... | collective-permute-start | bytes 12582920 | tf_op jit(solution)/shard_map/ppermute | solution.py:304
  7.4 7.2 %collective-permute-start = (f32[33,256]{1,0:T(8,128)S(1)}, f32[33,256]{1,0:T(8,128)S(1)}, u32[]{:S(2)}, u32[]{:S(2)}) collective-permute-start(f32[33,256]{1,0:T(8,128)S(1)} %get-tuple-element.101), channel_id=1, source_target_pairs={{0,24},{2,26},{4,28},{6,30},{8,0},{10,2},{12,4},{14,6},{16,8},{18,... | collective-permute-start | bytes 101384 | tf_op jit(solution)/shard_map/ppermute | solution.py:307
  11.1 5.8 %collective-permute-start.2 = (f32[33,256]{1,0:T(8,128)S(1)}, f32[33,256]{1,0:T(8,128)S(1)}, u32[]{:S(2)}, u32[]{:S(2)}) collective-permute-start(f32[33,256]{1,0:T(8,128)S(1)} %get-tuple-element.101), channel_id=1, source_target_pairs={{0,8},{2,10},{4,12},{6,14},{8,16},{10,18},{12,20},{14,22},{16,24},... | collective-permute-start | bytes 101384 | tf_op jit(solution)/shard_map/ppermute | solution.py:307
  16.9 9.3 %collective-permute-start.4 = (f32[4,33,256]{2,1,0:T(8,128)S(1)}, f32[4,33,256]{2,1,0:T(8,128)S(1)}, u32[]{:S(2)}, u32[]{:S(2)}) collective-permute-start(f32[4,33,256]{2,1,0:T(8,128)S(1)} %pad_maximum_fusion.3.refs_0_.rates), channel_id=1, source_target_pairs={{0,4},{2,6},{4,0},{6,2},{8,12},{10,14},{12,8},{14,10},{16,20},{18,... | collective-permute-start | bytes 405512 | tf_op jit(solution)/shard_map/ppermute | solution.py:304
  20.0 6.3 %collective-permute-start.5 = (f32[4,33,256]{2,1,0:T(8,128)S(1)}, f32[4,33,256]{2,1,0:T(8,128)S(1)}, u32[]{:S(2)}, u32[]{:S(2)}) collective-permute-start(f32[4,33,256]{2,1,0:T(8,128)S(1)} %pad_maximum_fusion.3.refs_0_.rates), channel_id=1, source_target_pairs={{0,2},{2,0},{4,6},{6,4},{8,10},{10,8},{12,14},{14,12},{16,18},{18,... | collective-permute-start | bytes 405512 | tf_op jit(solution)/shard_map/ppermute | solution.py:304
  30.9 8.3 %collective-permute-start.7 = (bf16[4,16,256]{2,1,0:T(8,128)(2,1)S(1)}, bf16[4,16,256]{2,1,0:T(8,128)(2,1)S(1)}, u32[]{:S(2)}, u32[]{:S(2)}) collective-permute-start(bf16[4,16,256]{2,1,0:T(8,128)(2,1)S(1)} %get-tuple-element.56), channel_id=1, source_target_pairs={{0,2},{2,0},{4,6},{6,4},{8,10},{10,8},{12,14},{14,12},{16,18},{18,... | collective-permute-start | bytes 98312 | tf_op jit(solution)/shard_map/ppermute | solution.py:304
  31.2 8.1 %collective-permute-start.8 = (bf16[4,16,256]{2,1,0:T(8,128)(2,1)S(1)}, bf16[4,16,256]{2,1,0:T(8,128)(2,1)S(1)}, u32[]{:S(2)}, u32[]{:S(2)}) collective-permute-start(bf16[4,16,256]{2,1,0:T(8,128)(2,1)S(1)} %get-tuple-element.57), channel_id=1, source_target_pairs={{0,4},{2,6},{4,0},{6,2},{8,12},{10,14},{12,8},{14,10},{16,20},{18,... | collective-permute-start | bytes 98312 | tf_op jit(solution)/shard_map/ppermute | solution.py:304
  39.9 5.8 %collective-permute-start.10 = (bf16[4,16,256]{2,1,0:T(8,128)(2,1)S(1)}, bf16[4,16,256]{2,1,0:T(8,128)(2,1)S(1)}, u32[]{:S(2)}, u32[]{:S(2)}) collective-permute-start(bf16[4,16,256]{2,1,0:T(8,128)(2,1)S(1)} %slab_states.1), channel_id=1, source_target_pairs={{0,8},{2,10},{4,12},{6,14},{8,16},{10,18},{12,20},{14,22},{16,24},... | collective-permute-start | bytes 98312 | tf_op jit(solution)/shard_map/ppermute | solution.py:307
  57.4 15.7 %collective-permute-start.17 = (bf16[128,2048]{1,0:T(8,128)(2,1)S(1)}, bf16[128,2048]{1,0:T(8,128)(2,1)S(1)}, u32[]{:S(2)}, u32[]{:S(2)}) collective-permute-start(bf16[128,2048]{1,0:T(8,128)(2,1)S(1)} %gated_block.2.refs_0_), channel_id=1, source_target_pairs={{0,8},{2,10},{4,12},{6,14},{8,24},{10,26},{12,28},{14,30},{16,0},{... | collective-permute-start | bytes 1572872 | tf_op jit(solution)/shard_map/ppermute | solution.py:314
  60.8 23.6 %collective-permute-start.18 = (bf16[128,2048]{1,0:T(8,128)(2,1)S(1)}, bf16[128,2048]{1,0:T(8,128)(2,1)S(1)}, u32[]{:S(2)}, u32[]{:S(2)}) collective-permute-start(bf16[128,2048]{1,0:T(8,128)(2,1)S(1)} %gated_block.3.refs_1_), channel_id=1, source_target_pairs={{0,8},{2,10},{4,12},{6,14},{8,24},{10,26},{12,28},{14,30},{16,0},{... | collective-permute-start | bytes 1572872 | tf_op jit(solution)/shard_map/ppermute | solution.py:314
  73.1 22.5 %collective-permute-start.19 = (bf16[128,2048]{1,0:T(8,128)(2,1)S(1)}, bf16[128,2048]{1,0:T(8,128)(2,1)S(1)}, u32[]{:S(2)}, u32[]{:S(2)}) collective-permute-start(bf16[128,2048]{1,0:T(8,128)(2,1)S(1)} %collective-permute-done.17.refs_0_.refs_2_), channel_id=1, source_target_pairs={{0,8},{2,10},{4,12},{6,14},{8,24},{10,26},{12,28},{14,30},{16,0},{... | collective-permute-start | bytes 1572872 | tf_op jit(solution)/shard_map/ppermute | solution.py:314
  84.3 22.5 %collective-permute-start.20 = (bf16[128,2048]{1,0:T(8,128)(2,1)S(1)}, bf16[128,2048]{1,0:T(8,128)(2,1)S(1)}, u32[]{:S(2)}, u32[]{:S(2)}) collective-permute-start(bf16[128,2048]{1,0:T(8,128)(2,1)S(1)} %collective-permute-done.18.refs_1_.refs_3_), channel_id=1, source_target_pairs={{0,8},{2,10},{4,12},{6,14},{8,24},{10,26},{12,28},{14,30},{16,0},{... | collective-permute-start | bytes 1572872 | tf_op jit(solution)/shard_map/ppermute | solution.py:314
  84.9 14.5 %collective-permute-start.23 = (bf16[1,2,128,256]{3,2,1,0:T(8,128)(2,1)S(1)}, bf16[1,2,128,256]{3,2,1,0:T(8,128)(2,1)S(1)}, u32[]{:S(2)}, u32[]{:S(2)}) collective-permute-start(bf16[1,2,128,256]{3,2,1,0:T(8,128)(2,1)S(1)} %project_block.11), channel_id=1, source_target_pairs={{0,1},{1,0},{2,3},{3,2},{4,5},{5,4},{6,7},{7,6},{8,9},{9,8},{10,11... | collective-permute-start | bytes 393224 | tf_op jit(solution)/shard_map/ppermute | solution.py:472
  95.6 38.4 %collective-permute-start.26 = (bf16[128,2048]{1,0:T(8,128)(2,1)S(1)}, bf16[128,2048]{1,0:T(8,128)(2,1)}, u32[]{:S(2)}, u32[]{:S(2)}) collective-permute-start(bf16[128,2048]{1,0:T(8,128)(2,1)S(1)} %collective-permute-done.19.refs_0_.refs_4_), channel_id=1, source_target_pairs={{0,8},{2,10},{4,12},{6,14},{8,24},{10,26},{12,28},{14,30},{16,0},{... | collective-permute-start | bytes 1572872 | tf_op jit(solution)/shard_map/ppermute | solution.py:314
  98.7 11.9 %collective-permute-start.21 = (bf16[1,2,128,256]{3,2,1,0:T(8,128)(2,1)S(1)}, bf16[1,2,128,256]{3,2,1,0:T(8,128)(2,1)}, u32[]{:S(2)}, u32[]{:S(2)}) collective-permute-start(bf16[1,2,128,256]{3,2,1,0:T(8,128)(2,1)S(1)} %project_block.14), channel_id=1, source_target_pairs={{0,1},{1,0},{2,3},{3,2},{4,5},{5,4},{6,7},{7,6},{8,9},{9,8},{10,11... | collective-permute-start | bytes 393224 | tf_op jit(solution)/shard_map/ppermute | solution.py:472
  106.8 31.7 %collective-permute-start.25 = (bf16[128,2048]{1,0:T(8,128)(2,1)S(1)}, bf16[128,2048]{1,0:T(8,128)(2,1)}, u32[]{:S(2)}, u32[]{:S(2)}) collective-permute-start(bf16[128,2048]{1,0:T(8,128)(2,1)S(1)} %collective-permute-done.20.refs_1_.refs_5_), channel_id=1, source_target_pairs={{0,8},{2,10},{4,12},{6,14},{8,24},{10,26},{12,28},{14,30},{16,0},{... | collective-permute-start | bytes 1572872 | tf_op jit(solution)/shard_map/ppermute | solution.py:314
  125.8 16.4 %collective-permute-start.22 = (bf16[3,2,128,256]{3,2,1,0:T(8,128)(2,1)}, bf16[3,2,128,256]{3,2,1,0:T(8,128)(2,1)}, u32[]{:S(2)}, u32[]{:S(2)}) collective-permute-start(bf16[3,2,128,256]{3,2,1,0:T(8,128)(2,1)} %project_block.16), channel_id=1, source_target_pairs={{0,1},{1,0},{2,3},{3,2},{4,5},{5,4},{6,7},{7,6},{8,9},{9,8},{10,11... | collective-permute-start | bytes 1179656 | tf_op jit(solution)/shard_map/ppermute | solution.py:472
  126.4 15.8 %collective-permute-start.24 = (bf16[1,2,128,256]{3,2,1,0:T(8,128)(2,1)}, bf16[1,2,128,256]{3,2,1,0:T(8,128)(2,1)}, u32[]{:S(2)}, u32[]{:S(2)}) collective-permute-start(bf16[1,2,128,256]{3,2,1,0:T(8,128)(2,1)} %project_block.13), channel_id=1, source_target_pairs={{0,1},{1,0},{2,3},{3,2},{4,5},{5,4},{6,7},{7,6},{8,9},{9,8},{10,11... | collective-permute-start | bytes 393224 | tf_op jit(solution)/shard_map/ppermute | solution.py:472
  144.5 11.7 %collective-permute-start.27 = (bf16[4,128,256]{2,1,0:T(8,128)(2,1)S(1)}, bf16[4,128,256]{2,1,0:T(8,128)(2,1)S(1)}, u32[]{:S(2)}, u32[]{:S(2)}) collective-permute-start(bf16[4,128,256]{2,1,0:T(8,128)(2,1)S(1)} %get-tuple-element.96), channel_id=1, source_target_pairs={{0,0},{1,24},{2,2},{3,26},{4,4},{5,28},{6,6},{7,30},{8,8},{9,16},{... | collective-permute-start | bytes 786440 | tf_op jit(solution)/shard_map/ppermute | solution.py:491
  149.3 13.3 %collective-permute-start.28 = (bf16[1,4,128,256]{3,2,1,0:T(8,128)(2,1)S(1)}, bf16[1,4,128,256]{3,2,1,0:T(8,128)(2,1)S(1)}, u32[]{:S(2)}, u32[]{:S(2)}) collective-permute-start(bf16[1,4,128,256]{3,2,1,0:T(8,128)(2,1)S(1)} %project_block.20), channel_id=1, source_target_pairs={{0,1},{1,0},{2,3},{3,2},{4,5},{5,4},{6,7},{7,6},{8,9},{9,8},{10,11... | collective-permute-start | bytes 786440 | tf_op jit(solution)/shard_map/ppermute | solution.py:520
  149.3 17.8 %collective-permute-start.30 = (bf16[4,128,256]{2,1,0:T(8,128)(2,1)S(1)}, bf16[4,128,256]{2,1,0:T(8,128)(2,1)S(1)}, u32[]{:S(2)}, u32[]{:S(2)}) collective-permute-start(bf16[4,128,256]{2,1,0:T(8,128)(2,1)S(1)} %get-tuple-element.95), channel_id=1, source_target_pairs={{0,24},{1,0},{2,26},{3,2},{4,28},{5,4},{6,30},{7,6},{8,16},{9,8},{... | collective-permute-start | bytes 786440 | tf_op jit(solution)/shard_map/ppermute | solution.py:491
  162.7 8.9 %collective-permute-start.29 = (bf16[4,128,256]{2,1,0:T(8,128)(2,1)S(1)}, bf16[4,128,256]{2,1,0:T(8,128)(2,1)S(1)}, u32[]{:S(2)}, u32[]{:S(2)}) collective-permute-start(bf16[4,128,256]{2,1,0:T(8,128)(2,1)S(1)} %get-tuple-element.94), channel_id=1, source_target_pairs={{0,16},{1,8},{2,18},{3,10},{4,20},{5,12},{6,22},{7,14},{8,0},{9,24... | collective-permute-start | bytes 786440 | tf_op jit(solution)/shard_map/ppermute | solution.py:491
  162.8 15.5 %collective-permute-start.31 = (bf16[4,128,256]{2,1,0:T(8,128)(2,1)S(1)}, bf16[4,128,256]{2,1,0:T(8,128)(2,1)S(1)}, u32[]{:S(2)}, u32[]{:S(2)}) collective-permute-start(bf16[4,128,256]{2,1,0:T(8,128)(2,1)S(1)} %get-tuple-element.93), channel_id=1, source_target_pairs={{0,8},{1,16},{2,10},{3,18},{4,12},{5,20},{6,14},{7,22},{8,24},{9,0... | collective-permute-start | bytes 786440 | tf_op jit(solution)/shard_map/ppermute | solution.py:491
  (18 other events, 73.0 us)
Sparse Core Ops, SparseCore 0:
  8.9 110.4 all-gather.2

commit v6 on v4

--- a/solution.py
+++ b/solution.py
@@ -187,18 +187,24 @@
 
 
 def project_kernel(count, picks, first, added, here, *refs):
-    out_ref, slots, sems = refs[-3:]
+    out_ref, slots, held, sems = refs[-4:]
     depth, share = slots.shape[1:]
-    blocks, sources = refs[:-3], refs[:-3]
-    runs = depth // blocks[0].shape[1]
-    blocks, sources = blocks[: runs * count], sources[runs * count :]
+    runs = held.shape[0] // count
+    blocks, sources = refs[: runs * count], refs[runs * count : -4]
     rows = pl.ds(first, depth)
     columns = pl.ds(pl.multiple_of(here[0] * share, share), share)
     copies = []
     for i, (which, rank) in enumerate(picks):
         source = sources[which] if rank is None else sources[which].at[here[rank]]
         copies.append(pltpu.make_async_copy(source.at[rows, columns], slots.at[i], sems.at[i]))
-        copies[-1].start()
+    fetches = [
+        pltpu.make_async_copy(block, held.at[k], sems.at[len(picks) + k]) for k, block in enumerate(blocks)
+    ]
+    copies[0].start()
+    for copy in fetches + copies[1:]:
+        copy.start()
+    for copy in fetches:
+        copy.wait()
     for i in range(len(picks)):
         copies[i].wait()
         for j in range(count):
@@ -206,7 +212,7 @@
             for h in range(runs):
                 size = depth // runs
                 term = jnp.dot(
-                    blocks[runs * j + h][...],
+                    held[runs * j + h],
                     slots[i, h * size : (h + 1) * size],
                     preferred_element_type=F32,
                 )
@@ -444,14 +450,15 @@
                 project_kernel, len(blocks), picks, halves[0] * run, partial is not None
             ),
             in_specs=[smem]
-            + [vmem] * (len(halves) * len(blocks))
+            + [pl.BlockSpec(memory_space=pl.ANY)] * (len(halves) * len(blocks))
             + [pl.BlockSpec(memory_space=pltpu.HBM)] * len(sources)
             + ([vmem] if partial is not None else []),
             out_specs=vmem,
             out_shape=out,
             scratch_shapes=[
                 pltpu.VMEM((len(picks), len(halves) * run, wide_share), BF16),
-                pltpu.SemaphoreType.DMA((len(picks),)),
+                pltpu.VMEM((len(halves) * len(blocks), tokens, run), BF16),
+                pltpu.SemaphoreType.DMA((len(picks) + len(halves) * len(blocks),)),
             ],
             compiler_params=large,
             cost_estimate=light,
@@ -486,11 +493,6 @@
         moved = jnp.where(tp_me == 0, classes[by], classes[(by + slabs // tp) % slabs])
         return lax.ppermute(moved, ("ctx", "tp"), pairs)
 
-    near, far, both = (
-        ((0, None), (1, None)),
-        ((0, 1), (0, 2)),
-        ((0, None), (1, None), (2, 1), (2, 2)),
-    )
     near, far, both = (
         ((0, None), (1, None)),
         ((0, 1), (0, 2)),

time: 187 us -> 186 us (level)
  no operation moved by 1% of the time
where the time goes in v6:
time: 186 us; the launch traced here: 184 us
  Pallas kernels  60.5 us (33%)
  waiting for transfers between devices  59.5 us (32%)
  starting transfers between devices  41 us (22%)
  between operations  13.8 us (7%)
  local copies, waits for them, and re-layouts  5.78 us (3%)
  other arithmetic  3.52 us (2%)
    pallas_call x11, Pallas kernels, project(): pl.pallas_call(functools.partial(project_kernel, len(blocks), picks, halv...  40.5 us
    ppermute x6, waiting for transfers between devices, ring(): return lax.ppermute(array, 'ctx', pairs)  26.5 us
    ppermute x4, waiting for transfers between devices, deliver(): return lax.ppermute(moved, ('ctx', 'tp'), pairs)  13.1 us
    ppermute x4, starting transfers between devices, deliver(): return lax.ppermute(moved, ('ctx', 'tp'), pairs)  12.8 us
    ppermute x6, starting transfers between devices, from_slab(): lax.ppermute(array, 'ctx', [(i, (i - by * SLAB) % ctx) for i in range(ctx)])  10.4 us
    ppermute x10, starting transfers between devices, within_slab(): return lax.ppermute(array, 'ctx', [(i, i ^ mask) for i in range(ctx)])  8.01 us
    ppermute x10, waiting for transfers between devices, within_slab(): return lax.ppermute(array, 'ctx', [(i, i ^ mask) for i in range(ctx)])  5.62 us
    pallas_call x1, Pallas kernels, per_device(): grouped(functools.partial(local_kernel, modes), 'local_convolution', [ser...  5.61 us
  transfers between devices with their start and end apart: 33, of which 16 were waited for; matrix products, arithmetic and copies ran while one was open for 1% of the time, Pallas kernels for 32%

profile of v6, /device:TPU:4, one launch (start us, length us, event | category | flops | bytes accessed | tf_op | source)
XLA Modules:
  0.0 184.0 jit_solution(10589197807232524908)
XLA Ops:
  7.4 3.7 %collective-permute-start = (f32[33,256]{1,0:T(8,128)S(1)}, f32[33,256]{1,0:T(8,128)S(1)}, u32[]{:S(2)}, u32[]{:S(2)}) collective-permute-start(f32[33,256]{1,0:T(8,128)S(1)} %get-tuple-element.101), channel_id=1, source_target_pairs={{0,24},{2,26},{4,28},{6,30},{8,0},{10,2},{12,4},{14,6},{16,8},{18,... | collective-permute-start | bytes 101384 | tf_op jit(solution)/shard_map/ppermute | solution.py:309
  22.5 3.3 %short_filters.1 = (f32[4,128,8,128]{3,2,1,0:T(8,128)S(1)}, f32[4,128,8,128]{3,2,1,0:T(8,128)S(1)}) custom-call(s32[3]{0:T(128)S(1)} %pad_add_fusion.here, bf16[3,128,4096]{2,1,0:T(8,128)(2,1)S(1)} %copy-done.2, bf16[3,2,4096]{2,1,0:T(2,128)(2,1)S(1)} %collective-permute-done.3.halo, f32[3,3,8192]{2,1,0:T(4,128)S(1)} %copy-done.3), custom_call_target="tpu_custom_call" | custom-call | flops 1 | bytes 1 | tf_op jit(solution)/shard_map/short_filters/pallas_call | solution.py:362
  27.8 3.1 %block_states.1 = (bf16[4,16,256]{2,1,0:T(8,128)(2,1)S(1)}, bf16[4,16,256]{2,1,0:T(8,128)(2,1)S(1)}, bf16[4,16,256]{2,1,0:T(8,128)(2,1)S(1)}, bf16[4,16,256]{2,1,0:T(8,128)(2,1)S(1)}) custom-call(s32[3]{0:T(128)S(1)} %pad_add_fusion.here, f32[4,128,8,128]{3,2,1,0:T(8,128)S(1)} %get-tuple-element.53.u_ref, f32[4,33,256]{2,1,0:T(8,128)S(1)} %pad_maximum_fusion.3.refs_0_.rates, ...), custom_call_target="tpu_custom_call" | custom-call | flops 1 | bytes 1 | tf_op jit(solution)/shard_map/block_states/pallas_call | solution.py:378
  33.6 5.6 %local_convolution.1.y_ref = f32[4,128,8,128]{3,2,1,0:T(8,128)S(1)} custom-call(s32[3]{0:T(128)S(1)} %pad_add_fusion.here, f32[4,128,8,128]{3,2,1,0:T(8,128)S(1)} %get-tuple-element.53.u_ref, f32[4,33,256]{2,1,0:T(8,128)S(1)} %pad_maximum_fusion.3.refs_0_.rates, f32[4,33,256]{2,1,0:T(8,128)S(1)} %collective-permute-done.5.refs_1_, ...), custom_call_target="tpu_custom_call" | custom-call | flops 1 | bytes 1 | tf_op jit(solution)/shard_map/local_convolution/pallas_call | solution.py:388
  39.9 3.3 %collective-permute-start.10 = (bf16[4,16,256]{2,1,0:T(8,128)(2,1)S(1)}, bf16[4,16,256]{2,1,0:T(8,128)(2,1)S(1)}, u32[]{:S(2)}, u32[]{:S(2)}) collective-permute-start(bf16[4,16,256]{2,1,0:T(8,128)(2,1)S(1)} %slab_states.1), channel_id=1, source_target_pairs={{0,8},{2,10},{4,12},{6,14},{8,16},{10,18},{12,20},{14,22},{16,24},... | collective-permute-start | bytes 98312 | tf_op jit(solution)/shard_map/ppermute | solution.py:309
  51.1 3.1 %collective-permute-done.14.refs_6_ = bf16[4,16,256]{2,1,0:T(8,128)(2,1)S(1)} collective-permute-done((bf16[4,16,256]{2,1,0:T(8,128)(2,1)S(1)}, bf16[4,16,256]{2,1,0:T(8,128)(2,1)S(1)}, u32[]{:S(2)}, u32[]{:S(2)}) %collective-permute-start.14) | collective-permute-done | bytes 32800 | tf_op jit(solution)/shard_map/ppermute | solution.py:306
  63.6 9.5 %collective-permute-done.17.refs_0_.refs_2_ = bf16[128,2048]{1,0:T(8,128)(2,1)S(1)} collective-permute-done((bf16[128,2048]{1,0:T(8,128)(2,1)S(1)}, bf16[128,2048]{1,0:T(8,128)(2,1)S(1)}, u32[]{:S(2)}, u32[]{:S(2)}) %collective-permute-start.17) | collective-permute-done | bytes 524320 | tf_op jit(solution)/shard_map/ppermute | solution.py:316
  75.5 3.1 %project_block.11 = bf16[1,2,128,256]{3,2,1,0:T(8,128)(2,1)S(1)} custom-call(s32[3]{0:T(128)S(1)} %add_add_fusion.1.here, bf16[128,2048]{1,0:T(8,128)(2,1)S(1)} %gated_block.2.refs_0_, bf16[128,2048]{1,0:T(8,128)(2,1)S(1)} %gated_block.3.refs_1_, bf16[4096,512]{1,0:T(8,128)(2,1)S(1)} %copy-done, bf16[4096,512]{1,0:T(8,128)(2,1)} %collective-permute-done.16.refs_3_.refs_2_), custom_call_target="tpu_custom_call" | custom-call | flops 1 | bytes 1 | tf_op jit(solution)/shard_map/project_block/pallas_call | solution.py:448
  78.6 3.1 %project_block.12 = bf16[1,2,128,256]{3,2,1,0:T(8,128)(2,1)S(1)} custom-call(s32[3]{0:T(128)S(1)} %add_add_fusion.here, bf16[128,2048]{1,0:T(8,128)(2,1)S(1)} %gated_block.2.refs_0_, bf16[128,2048]{1,0:T(8,128)(2,1)S(1)} %gated_block.3.refs_1_, bf16[4096,512]{1,0:T(8,128)(2,1)S(1)} %copy-done, bf16[4096,512]{1,0:T(8,128)(2,1)} %collective-permute-done.16.refs_3_.refs_2_), custom_call_target="tpu_custom_call" | custom-call | flops 1 | bytes 1 | tf_op jit(solution)/shard_map/project_block/pallas_call | solution.py:448
  85.6 10.0 %collective-permute-done.19.refs_0_.refs_4_ = bf16[128,2048]{1,0:T(8,128)(2,1)S(1)} collective-permute-done((bf16[128,2048]{1,0:T(8,128)(2,1)S(1)}, bf16[128,2048]{1,0:T(8,128)(2,1)S(1)}, u32[]{:S(2)}, u32[]{:S(2)}) %collective-permute-start.19) | collective-permute-done | bytes 524320 | tf_op jit(solution)/shard_map/ppermute | solution.py:316
  102.5 4.3 %collective-permute-done.20.refs_1_.refs_5_ = bf16[128,2048]{1,0:T(8,128)(2,1)S(1)} collective-permute-done((bf16[128,2048]{1,0:T(8,128)(2,1)S(1)}, bf16[128,2048]{1,0:T(8,128)(2,1)S(1)}, u32[]{:S(2)}, u32[]{:S(2)}) %collective-permute-start.20) | collective-permute-done | bytes 524320 | tf_op jit(solution)/shard_map/ppermute | solution.py:316
  107.0 3.7 %project_block.13 = bf16[1,2,128,256]{3,2,1,0:T(8,128)(2,1)} custom-call(s32[3]{0:T(128)S(1)} %add_add_fusion.1.here, bf16[128,2048]{1,0:T(8,128)(2,1)S(1)} %collective-permute-done.19.refs_0_.refs_4_, bf16[128,2048]{1,0:T(8,128)(2,1)S(1)} %collective-permute-done.20.refs_1_.refs_5_, bf16[4096,512]{1,0:T(8,128)(2,1)S(1)} %copy-done, ...), custom_call_target="tpu_custom_call" | custom-call | flops 1 | bytes 1 | tf_op jit(solution)/shard_map/project_block/pallas_call | solution.py:448
  110.7 3.1 %project_block.15 = bf16[1,2,128,256]{3,2,1,0:T(8,128)(2,1)S(1)} custom-call(s32[3]{0:T(128)S(1)} %add_add_fusion.here, bf16[128,2048]{1,0:T(8,128)(2,1)S(1)} %collective-permute-done.19.refs_0_.refs_4_, bf16[128,2048]{1,0:T(8,128)(2,1)S(1)} %collective-permute-done.20.refs_1_.refs_5_, bf16[4096,512]{1,0:T(8,128)(2,1)S(1)} %copy-done, ...), custom_call_target="tpu_custom_call" | custom-call | flops 1 | bytes 1 | tf_op jit(solution)/shard_map/project_block/pallas_call | solution.py:448
  113.8 5.6 %all-gather.3.cloned.1.call-done = bf16[16384,512]{1,0:T(8,128)(2,1)} async-done(((bf16[4096,512]{1,0:T(8,128)(2,1)}), bf16[16384,512]{1,0:T(8,128)(2,1)}) %all-gather.3.cloned.1.call-update) | async-done | bytes 16777232 | tf_op jit(solution)/shard_map/all_gather | solution.py:327
  119.4 5.5 %project_block.16 = bf16[3,2,128,256]{3,2,1,0:T(8,128)(2,1)} custom-call(s32[3]{0:T(128)S(1)} %add_add_fusion.1.here, bf16[128,2048]{1,0:T(8,128)(2,1)S(1)} %gated_block.2.refs_0_, bf16[128,2048]{1,0:T(8,128)(2,1)S(1)} %gated_block.3.refs_1_, bf16[128,2048]{1,0:T(8,128)(2,1)S(1)} %collective-permute-done.17.refs_0_.refs_2_, ...), custom_call_target="tpu_custom_call" | custom-call | flops 1 | bytes 1 | tf_op jit(solution)/shard_map/project_block/pallas_call | solution.py:448
  127.0 5.0 %project_block.18 = bf16[3,2,128,256]{3,2,1,0:T(8,128)(2,1)S(1)} custom-call(s32[3]{0:T(128)S(1)} %add_add_fusion.here, bf16[128,2048]{1,0:T(8,128)(2,1)S(1)} %gated_block.2.refs_0_, bf16[128,2048]{1,0:T(8,128)(2,1)S(1)} %gated_block.3.refs_1_, bf16[128,2048]{1,0:T(8,128)(2,1)S(1)} %collective-permute-done.17.refs_0_.refs_2_, ...), custom_call_target="tpu_custom_call" | custom-call | flops 1 | bytes 1 | tf_op jit(solution)/shard_map/project_block/pallas_call | solution.py:448
  132.1 4.2 %project_block.19.refs_4_ = f32[2,1,4,128,256]{4,3,2,1,0:T(8,128)S(1)} custom-call(s32[3]{0:T(128)S(1)} %add_add_fusion.2.here, bf16[128,2048]{1,0:T(8,128)(2,1)} %collective-permute-done.26.refs_0_, bf16[4096,512]{1,0:T(8,128)(2,1)S(1)} %copy-done.1, bf16[4096,512]{1,0:T(8,128)(2,1)} %collective-permute-done.16.refs_3_.refs_2_, bf16[4,4096,512]{2,1,0:T(8,128)(2,1)} %bitcast.37), custom_call_target="tpu_custom_call" | custom-call | flops 1 | bytes 1 | tf_op jit(solution)/shard_map/project_block/pallas_call | solution.py:448
  136.3 3.4 %project_block.20 = bf16[1,4,128,256]{3,2,1,0:T(8,128)(2,1)S(1)} custom-call(s32[3]{0:T(128)S(1)} %add_add_fusion.1.here, bf16[128,2048]{1,0:T(8,128)(2,1)} %collective-permute-done.25.refs_0_, bf16[4096,512]{1,0:T(8,128)(2,1)S(1)} %copy-done.1, bf16[4096,512]{1,0:T(8,128)(2,1)} %collective-permute-done.16.refs_3_.refs_2_, bf16[4,4096,512]{2,1,0:T(8,128)(2,1)} %bitcast.38, ...), custom_call_target="tpu_custom_call" | custom-call | flops 1 | bytes 1 | tf_op jit(solution)/shard_map/project_block/pallas_call | solution.py:448
  141.9 4.8 %collective-permute-start.27 = (bf16[4,128,256]{2,1,0:T(8,128)(2,1)S(1)}, bf16[4,128,256]{2,1,0:T(8,128)(2,1)S(1)}, u32[]{:S(2)}, u32[]{:S(2)}) collective-permute-start(bf16[4,128,256]{2,1,0:T(8,128)(2,1)S(1)} %get-tuple-element.96), channel_id=1, source_target_pairs={{0,0},{1,24},{2,2},{3,26},{4,4},{5,28},{6,6},{7,30},{8,8},{9,16},{... | collective-permute-start | bytes 786440 | tf_op jit(solution)/shard_map/ppermute | solution.py:494
  146.8 3.9 %collective-permute-start.30 = (bf16[4,128,256]{2,1,0:T(8,128)(2,1)S(1)}, bf16[4,128,256]{2,1,0:T(8,128)(2,1)S(1)}, u32[]{:S(2)}, u32[]{:S(2)}) collective-permute-start(bf16[4,128,256]{2,1,0:T(8,128)(2,1)S(1)} %get-tuple-element.95), channel_id=1, source_target_pairs={{0,24},{1,0},{2,26},{3,2},{4,28},{5,4},{6,30},{7,6},{8,16},{9,8},{... | collective-permute-start | bytes 786440 | tf_op jit(solution)/shard_map/ppermute | solution.py:494
  153.6 3.4 %project_block.21 = bf16[1,4,128,256]{3,2,1,0:T(8,128)(2,1)S(1)} custom-call(s32[3]{0:T(128)S(1)} %add_add_fusion.here, bf16[128,2048]{1,0:T(8,128)(2,1)} %collective-permute-done.25.refs_0_, bf16[4096,512]{1,0:T(8,128)(2,1)S(1)} %copy-done.1, bf16[4096,512]{1,0:T(8,128)(2,1)} %collective-permute-done.16.refs_3_.refs_2_, bf16[4,4096,512]{2,1,0:T(8,128)(2,1)} %bitcast.39, ...), custom_call_target="tpu_custom_call" | custom-call | flops 1 | bytes 1 | tf_op jit(solution)/shard_map/project_block/pallas_call | solution.py:448
  160.2 4.0 %collective-permute-start.31 = (bf16[4,128,256]{2,1,0:T(8,128)(2,1)S(1)}, bf16[4,128,256]{2,1,0:T(8,128)(2,1)S(1)}, u32[]{:S(2)}, u32[]{:S(2)}) collective-permute-start(bf16[4,128,256]{2,1,0:T(8,128)(2,1)S(1)} %get-tuple-element.93), channel_id=1, source_target_pairs={{0,8},{1,16},{2,10},{3,18},{4,12},{5,20},{6,14},{7,22},{8,24},{9,0... | collective-permute-start | bytes 786440 | tf_op jit(solution)/shard_map/ppermute | solution.py:494
  164.3 4.5 %collective-permute-done.29.refs_1_ = bf16[4,128,256]{2,1,0:T(8,128)(2,1)S(1)} collective-permute-done((bf16[4,128,256]{2,1,0:T(8,128)(2,1)S(1)}, bf16[4,128,256]{2,1,0:T(8,128)(2,1)S(1)}, u32[]{:S(2)}, u32[]{:S(2)}) %collective-permute-start.29) | collective-permute-done | bytes 262176 | tf_op jit(solution)/shard_map/ppermute | solution.py:494
  168.8 6.6 %collective-permute-done.31.refs_3_ = bf16[4,128,256]{2,1,0:T(8,128)(2,1)S(1)} collective-permute-done((bf16[4,128,256]{2,1,0:T(8,128)(2,1)S(1)}, bf16[4,128,256]{2,1,0:T(8,128)(2,1)S(1)}, u32[]{:S(2)}, u32[]{:S(2)}) %collective-permute-start.31) | collective-permute-done | bytes 262176 | tf_op jit(solution)/shard_map/ppermute | solution.py:494
  (94 shorter events, 60.5 us)
Async XLA Ops:
  6.5 112.8 %all-gather.3.cloned.1.call-start = ((), (), s32[]{:S(2)}) async-start(), calls=%async_computation | async-start | bytes 20971520 | tf_op jit(solution)/shard_map/all_gather | solution.py:327
  7.3 66.0 %collective-permute-start.16 = (bf16[4096,512]{1,0:T(8,128)(2,1)}, bf16[4096,512]{1,0:T(8,128)(2,1)}, u32[]{:S(2)}, u32[]{:S(2)}) collective-permute-start(bf16[4096,512]{1,0:T(8,128)(2,1)} %refs_1_.5), channel_id=1, source_target_pairs={{0,2},{2,0},{4,6},{6,4},{8,10},{10,8},{12,14},{14,12},{16,18},{18,... | collective-permute-start | bytes 12582920 | tf_op jit(solution)/shard_map/ppermute | solution.py:306
  7.4 7.2 %collective-permute-start = (f32[33,256]{1,0:T(8,128)S(1)}, f32[33,256]{1,0:T(8,128)S(1)}, u32[]{:S(2)}, u32[]{:S(2)}) collective-permute-start(f32[33,256]{1,0:T(8,128)S(1)} %get-tuple-element.101), channel_id=1, source_target_pairs={{0,24},{2,26},{4,28},{6,30},{8,0},{10,2},{12,4},{14,6},{16,8},{18,... | collective-permute-start | bytes 101384 | tf_op jit(solution)/shard_map/ppermute | solution.py:309
  11.1 5.8 %collective-permute-start.2 = (f32[33,256]{1,0:T(8,128)S(1)}, f32[33,256]{1,0:T(8,128)S(1)}, u32[]{:S(2)}, u32[]{:S(2)}) collective-permute-start(f32[33,256]{1,0:T(8,128)S(1)} %get-tuple-element.101), channel_id=1, source_target_pairs={{0,8},{2,10},{4,12},{6,14},{8,16},{10,18},{12,20},{14,22},{16,24},... | collective-permute-start | bytes 101384 | tf_op jit(solution)/shard_map/ppermute | solution.py:309
  16.9 9.3 %collective-permute-start.4 = (f32[4,33,256]{2,1,0:T(8,128)S(1)}, f32[4,33,256]{2,1,0:T(8,128)S(1)}, u32[]{:S(2)}, u32[]{:S(2)}) collective-permute-start(f32[4,33,256]{2,1,0:T(8,128)S(1)} %pad_maximum_fusion.3.refs_0_.rates), channel_id=1, source_target_pairs={{0,4},{2,6},{4,0},{6,2},{8,12},{10,14},{12,8},{14,10},{16,20},{18,... | collective-permute-start | bytes 405512 | tf_op jit(solution)/shard_map/ppermute | solution.py:306
  20.0 6.3 %collective-permute-start.5 = (f32[4,33,256]{2,1,0:T(8,128)S(1)}, f32[4,33,256]{2,1,0:T(8,128)S(1)}, u32[]{:S(2)}, u32[]{:S(2)}) collective-permute-start(f32[4,33,256]{2,1,0:T(8,128)S(1)} %pad_maximum_fusion.3.refs_0_.rates), channel_id=1, source_target_pairs={{0,2},{2,0},{4,6},{6,4},{8,10},{10,8},{12,14},{14,12},{16,18},{18,... | collective-permute-start | bytes 405512 | tf_op jit(solution)/shard_map/ppermute | solution.py:306
  30.9 8.3 %collective-permute-start.7 = (bf16[4,16,256]{2,1,0:T(8,128)(2,1)S(1)}, bf16[4,16,256]{2,1,0:T(8,128)(2,1)S(1)}, u32[]{:S(2)}, u32[]{:S(2)}) collective-permute-start(bf16[4,16,256]{2,1,0:T(8,128)(2,1)S(1)} %get-tuple-element.56), channel_id=1, source_target_pairs={{0,2},{2,0},{4,6},{6,4},{8,10},{10,8},{12,14},{14,12},{16,18},{18,... | collective-permute-start | bytes 98312 | tf_op jit(solution)/shard_map/ppermute | solution.py:306
  31.2 8.1 %collective-permute-start.8 = (bf16[4,16,256]{2,1,0:T(8,128)(2,1)S(1)}, bf16[4,16,256]{2,1,0:T(8,128)(2,1)S(1)}, u32[]{:S(2)}, u32[]{:S(2)}) collective-permute-start(bf16[4,16,256]{2,1,0:T(8,128)(2,1)S(1)} %get-tuple-element.57), channel_id=1, source_target_pairs={{0,4},{2,6},{4,0},{6,2},{8,12},{10,14},{12,8},{14,10},{16,20},{18,... | collective-permute-start | bytes 98312 | tf_op jit(solution)/shard_map/ppermute | solution.py:306
  39.9 5.8 %collective-permute-start.10 = (bf16[4,16,256]{2,1,0:T(8,128)(2,1)S(1)}, bf16[4,16,256]{2,1,0:T(8,128)(2,1)S(1)}, u32[]{:S(2)}, u32[]{:S(2)}) collective-permute-start(bf16[4,16,256]{2,1,0:T(8,128)(2,1)S(1)} %slab_states.1), channel_id=1, source_target_pairs={{0,8},{2,10},{4,12},{6,14},{8,16},{10,18},{12,20},{14,22},{16,24},... | collective-permute-start | bytes 98312 | tf_op jit(solution)/shard_map/ppermute | solution.py:309
  57.4 15.7 %collective-permute-start.17 = (bf16[128,2048]{1,0:T(8,128)(2,1)S(1)}, bf16[128,2048]{1,0:T(8,128)(2,1)S(1)}, u32[]{:S(2)}, u32[]{:S(2)}) collective-permute-start(bf16[128,2048]{1,0:T(8,128)(2,1)S(1)} %gated_block.2.refs_0_), channel_id=1, source_target_pairs={{0,8},{2,10},{4,12},{6,14},{8,24},{10,26},{12,28},{14,30},{16,0},{... | collective-permute-start | bytes 1572872 | tf_op jit(solution)/shard_map/ppermute | solution.py:316
  60.8 23.6 %collective-permute-start.18 = (bf16[128,2048]{1,0:T(8,128)(2,1)S(1)}, bf16[128,2048]{1,0:T(8,128)(2,1)S(1)}, u32[]{:S(2)}, u32[]{:S(2)}) collective-permute-start(bf16[128,2048]{1,0:T(8,128)(2,1)S(1)} %gated_block.3.refs_1_), channel_id=1, source_target_pairs={{0,8},{2,10},{4,12},{6,14},{8,24},{10,26},{12,28},{14,30},{16,0},{... | collective-permute-start | bytes 1572872 | tf_op jit(solution)/shard_map/ppermute | solution.py:316
  73.1 22.5 %collective-permute-start.19 = (bf16[128,2048]{1,0:T(8,128)(2,1)S(1)}, bf16[128,2048]{1,0:T(8,128)(2,1)S(1)}, u32[]{:S(2)}, u32[]{:S(2)}) collective-permute-start(bf16[128,2048]{1,0:T(8,128)(2,1)S(1)} %collective-permute-done.17.refs_0_.refs_2_), channel_id=1, source_target_pairs={{0,8},{2,10},{4,12},{6,14},{8,24},{10,26},{12,28},{14,30},{16,0},{... | collective-permute-start | bytes 1572872 | tf_op jit(solution)/shard_map/ppermute | solution.py:316
  84.3 22.5 %collective-permute-start.20 = (bf16[128,2048]{1,0:T(8,128)(2,1)S(1)}, bf16[128,2048]{1,0:T(8,128)(2,1)S(1)}, u32[]{:S(2)}, u32[]{:S(2)}) collective-permute-start(bf16[128,2048]{1,0:T(8,128)(2,1)S(1)} %collective-permute-done.18.refs_1_.refs_3_), channel_id=1, source_target_pairs={{0,8},{2,10},{4,12},{6,14},{8,24},{10,26},{12,28},{14,30},{16,0},{... | collective-permute-start | bytes 1572872 | tf_op jit(solution)/shard_map/ppermute | solution.py:316
  85.1 14.4 %collective-permute-start.23 = (bf16[1,2,128,256]{3,2,1,0:T(8,128)(2,1)S(1)}, bf16[1,2,128,256]{3,2,1,0:T(8,128)(2,1)S(1)}, u32[]{:S(2)}, u32[]{:S(2)}) collective-permute-start(bf16[1,2,128,256]{3,2,1,0:T(8,128)(2,1)S(1)} %project_block.11), channel_id=1, source_target_pairs={{0,1},{1,0},{2,3},{3,2},{4,5},{5,4},{6,7},{7,6},{8,9},{9,8},{10,11... | collective-permute-start | bytes 393224 | tf_op jit(solution)/shard_map/ppermute | solution.py:475
  95.6 36.4 %collective-permute-start.26 = (bf16[128,2048]{1,0:T(8,128)(2,1)S(1)}, bf16[128,2048]{1,0:T(8,128)(2,1)}, u32[]{:S(2)}, u32[]{:S(2)}) collective-permute-start(bf16[128,2048]{1,0:T(8,128)(2,1)S(1)} %collective-permute-done.19.refs_0_.refs_4_), channel_id=1, source_target_pairs={{0,8},{2,10},{4,12},{6,14},{8,24},{10,26},{12,28},{14,30},{16,0},{... | collective-permute-start | bytes 1572872 | tf_op jit(solution)/shard_map/ppermute | solution.py:316
  98.8 11.9 %collective-permute-start.21 = (bf16[1,2,128,256]{3,2,1,0:T(8,128)(2,1)S(1)}, bf16[1,2,128,256]{3,2,1,0:T(8,128)(2,1)}, u32[]{:S(2)}, u32[]{:S(2)}) collective-permute-start(bf16[1,2,128,256]{3,2,1,0:T(8,128)(2,1)S(1)} %project_block.14), channel_id=1, source_target_pairs={{0,1},{1,0},{2,3},{3,2},{4,5},{5,4},{6,7},{7,6},{8,9},{9,8},{10,11... | collective-permute-start | bytes 393224 | tf_op jit(solution)/shard_map/ppermute | solution.py:475
  106.8 29.5 %collective-permute-start.25 = (bf16[128,2048]{1,0:T(8,128)(2,1)S(1)}, bf16[128,2048]{1,0:T(8,128)(2,1)}, u32[]{:S(2)}, u32[]{:S(2)}) collective-permute-start(bf16[128,2048]{1,0:T(8,128)(2,1)S(1)} %collective-permute-done.20.refs_1_.refs_5_), channel_id=1, source_target_pairs={{0,8},{2,10},{4,12},{6,14},{8,24},{10,26},{12,28},{14,30},{16,0},{... | collective-permute-start | bytes 1572872 | tf_op jit(solution)/shard_map/ppermute | solution.py:316
  124.9 14.8 %collective-permute-start.22 = (bf16[3,2,128,256]{3,2,1,0:T(8,128)(2,1)}, bf16[3,2,128,256]{3,2,1,0:T(8,128)(2,1)}, u32[]{:S(2)}, u32[]{:S(2)}) collective-permute-start(bf16[3,2,128,256]{3,2,1,0:T(8,128)(2,1)} %project_block.16), channel_id=1, source_target_pairs={{0,1},{1,0},{2,3},{3,2},{4,5},{5,4},{6,7},{7,6},{8,9},{9,8},{10,11... | collective-permute-start | bytes 1179656 | tf_op jit(solution)/shard_map/ppermute | solution.py:475
  125.4 14.3 %collective-permute-start.24 = (bf16[1,2,128,256]{3,2,1,0:T(8,128)(2,1)}, bf16[1,2,128,256]{3,2,1,0:T(8,128)(2,1)}, u32[]{:S(2)}, u32[]{:S(2)}) collective-permute-start(bf16[1,2,128,256]{3,2,1,0:T(8,128)(2,1)} %project_block.13), channel_id=1, source_target_pairs={{0,1},{1,0},{2,3},{3,2},{4,5},{5,4},{6,7},{7,6},{8,9},{9,8},{10,11... | collective-permute-start | bytes 393224 | tf_op jit(solution)/shard_map/ppermute | solution.py:475
  141.9 11.7 %collective-permute-start.27 = (bf16[4,128,256]{2,1,0:T(8,128)(2,1)S(1)}, bf16[4,128,256]{2,1,0:T(8,128)(2,1)S(1)}, u32[]{:S(2)}, u32[]{:S(2)}) collective-permute-start(bf16[4,128,256]{2,1,0:T(8,128)(2,1)S(1)} %get-tuple-element.96), channel_id=1, source_target_pairs={{0,0},{1,24},{2,2},{3,26},{4,4},{5,28},{6,6},{7,30},{8,8},{9,16},{... | collective-permute-start | bytes 786440 | tf_op jit(solution)/shard_map/ppermute | solution.py:494
  146.7 13.3 %collective-permute-start.28 = (bf16[1,4,128,256]{3,2,1,0:T(8,128)(2,1)S(1)}, bf16[1,4,128,256]{3,2,1,0:T(8,128)(2,1)S(1)}, u32[]{:S(2)}, u32[]{:S(2)}) collective-permute-start(bf16[1,4,128,256]{3,2,1,0:T(8,128)(2,1)S(1)} %project_block.20), channel_id=1, source_target_pairs={{0,1},{1,0},{2,3},{3,2},{4,5},{5,4},{6,7},{7,6},{8,9},{9,8},{10,11... | collective-permute-start | bytes 786440 | tf_op jit(solution)/shard_map/ppermute | solution.py:523
  146.8 17.5 %collective-permute-start.30 = (bf16[4,128,256]{2,1,0:T(8,128)(2,1)S(1)}, bf16[4,128,256]{2,1,0:T(8,128)(2,1)S(1)}, u32[]{:S(2)}, u32[]{:S(2)}) collective-permute-start(bf16[4,128,256]{2,1,0:T(8,128)(2,1)S(1)} %get-tuple-element.95), channel_id=1, source_target_pairs={{0,24},{1,0},{2,26},{3,2},{4,28},{5,4},{6,30},{7,6},{8,16},{9,8},{... | collective-permute-start | bytes 786440 | tf_op jit(solution)/shard_map/ppermute | solution.py:494
  160.2 8.7 %collective-permute-start.29 = (bf16[4,128,256]{2,1,0:T(8,128)(2,1)S(1)}, bf16[4,128,256]{2,1,0:T(8,128)(2,1)S(1)}, u32[]{:S(2)}, u32[]{:S(2)}) collective-permute-start(bf16[4,128,256]{2,1,0:T(8,128)(2,1)S(1)} %get-tuple-element.94), channel_id=1, source_target_pairs={{0,16},{1,8},{2,18},{3,10},{4,20},{5,12},{6,22},{7,14},{8,0},{9,24... | collective-permute-start | bytes 786440 | tf_op jit(solution)/shard_map/ppermute | solution.py:494
  160.2 15.3 %collective-permute-start.31 = (bf16[4,128,256]{2,1,0:T(8,128)(2,1)S(1)}, bf16[4,128,256]{2,1,0:T(8,128)(2,1)S(1)}, u32[]{:S(2)}, u32[]{:S(2)}) collective-permute-start(bf16[4,128,256]{2,1,0:T(8,128)(2,1)S(1)} %get-tuple-element.93), channel_id=1, source_target_pairs={{0,8},{1,16},{2,10},{3,18},{4,12},{5,20},{6,14},{7,22},{8,24},{9,0... | collective-permute-start | bytes 786440 | tf_op jit(solution)/shard_map/ppermute | solution.py:494
  (18 other events, 71.8 us)
Sparse Core Ops, SparseCore 0:
  8.9 110.4 all-gather.2

commit v7 on v6

--- a/solution.py
+++ b/solution.py
@@ -514,19 +514,19 @@
         got_parts.append(got)
     slab_weights, _ = lax.optimization_barrier((slab_weights, mine))
     away, batch_got = project_away(blocks[: slabs - 1], [slab_weights], far)
-    batch_mine = project_mine(blocks[: slabs - 1], [slab_weights], far, away)
     sources = [out_weight, beside, slab_weights]
-    head, _ = lax.optimization_barrier((blocks[-1][0], batch_mine))
+    head, _ = lax.optimization_barrier((blocks[-1][0], away))
     partial = project([[head]], sources, both, None, None, (0,))
     tail = blocks[-1][1]
     last_away = project([[None, tail]], sources, both, 1 - tp_me, partial, (1,))
     last_got = lax.ppermute(last_away, "tp", [(0, 1), (1, 0)])
+    batch_mine = project_mine(blocks[: slabs - 1], [slab_weights], far, last_away)
     batch_got, got_parts, _ = lax.optimization_barrier((batch_got, got_parts, last_away))
     near_sums = [total(m, g)[0] for m, g in zip(kept_parts, got_parts)]
     sums = [jnp.concatenate(parts) for parts in zip(near_sums, total(batch_mine, batch_got))]
     late = ((slabs - 1) % (slabs // tp), slabs - 1)
     arrived = {by: [deliver(sums, by)] for by in range(slabs) if by not in late}
-    tail, _ = lax.optimization_barrier((tail, (last_away, arrived[0])))
+    tail, _ = lax.optimization_barrier((tail, batch_mine))
     last_mine = project([[None, tail]], sources, both, tp_me, partial, (1,))
     sums.append(total(last_mine, last_got)[0])
     for by in late:

time: 186 us -> 188 us (1.011)
  waiting for transfers between devices: 59.5 us -> 69.7 us
  starting transfers between devices: 41 us -> 31.6 us
  local copies, waits for them, and re-layouts: 5.78 us -> 8.06 us
    ppermute x4, waiting for transfers between devices: 13.1 us -> 20.7 us  [deliver(): return lax.ppermute(moved, ('ctx', 'tp'), pairs)]
    ppermute x6, waiting for transfers between devices: 26.5 us -> 30.2 us  [ring(): return lax.ppermute(array, 'ctx', pairs)]
    ppermute x4, starting transfers between devices: 12.8 us -> 9.16 us  [deliver(): return lax.ppermute(moved, ('ctx', 'tp'), pairs)]
    ppermute x6, starting transfers between devices: 4.89 us -> 1.39 us  [ring(): return lax.ppermute(array, 'ctx', pairs)]
    ppermute x1, waiting for transfers between devices: 3.03 us -> 0.01 us  [per_device(): last_got = lax.ppermute(last_away, 'tp', [(0, 1), (1, 0)])]
    ppermute x6, waiting for transfers between devices: 4.98 us -> 7.68 us  [from_slab(): lax.ppermute(array, 'ctx', [(i, (i - by * SLAB) % ctx) for i in range(ctx)])]
    unnamed x18 -> x20, local copies, waits for them, and re-layouts: 4.69 us -> 6.96 us
    ppermute x6, starting transfers between devices: 10.4 us -> 8.52 us  [from_slab(): lax.ppermute(array, 'ctx', [(i, (i - by * SLAB) % ctx) for i in range(ctx)])]
  transfers between devices with their start and end apart: 33 -> 33, of which waited for: 16 -> 17; matrix products, arithmetic and copies ran while one was open for 1% -> 2% of each run, Pallas kernels for 32% -> 31%
where the time goes in v7:
time: 188 us; the launch traced here: 187 us
  waiting for transfers between devices  69.7 us (37%)
  Pallas kernels  60.3 us (32%)
  starting transfers between devices  31.6 us (17%)
  between operations  13.9 us (7%)
  local copies, waits for them, and re-layouts  8.06 us (4%)
  other arithmetic  3.52 us (2%)
    pallas_call x11, Pallas kernels, project(): pl.pallas_call(functools.partial(project_kernel, len(blocks), picks, halv...  40.3 us
    ppermute x6, waiting for transfers between devices, ring(): return lax.ppermute(array, 'ctx', pairs)  30.2 us
    ppermute x4, waiting for transfers between devices, deliver(): return lax.ppermute(moved, ('ctx', 'tp'), pairs)  20.7 us
    ppermute x4, starting transfers between devices, deliver(): return lax.ppermute(moved, ('ctx', 'tp'), pairs)  9.16 us
    ppermute x6, starting transfers between devices, from_slab(): lax.ppermute(array, 'ctx', [(i, (i - by * SLAB) % ctx) for i in range(ctx)])  8.52 us
    ppermute x6, waiting for transfers between devices, from_slab(): lax.ppermute(array, 'ctx', [(i, (i - by * SLAB) % ctx) for i in range(ctx)])  7.68 us
    ppermute x10, starting transfers between devices, within_slab(): return lax.ppermute(array, 'ctx', [(i, i ^ mask) for i in range(ctx)])  7.22 us
    unnamed x20, local copies, waits for them, and re-layouts  6.96 us
  transfers between devices with their start and end apart: 33, of which 17 were waited for; matrix products, arithmetic and copies ran while one was open for 2% of the time, Pallas kernels for 31%

profile of v7, /device:TPU:4, one launch (start us, length us, event | category | flops | bytes accessed | tf_op | source)
XLA Modules:
  0.0 187.0 jit_solution(8645403828552227272)
XLA Ops:
  22.5 3.3 %short_filters.1 = (f32[4,128,8,128]{3,2,1,0:T(8,128)S(1)}, f32[4,128,8,128]{3,2,1,0:T(8,128)S(1)}) custom-call(s32[3]{0:T(128)S(1)} %pad_add_fusion.here, bf16[3,128,4096]{2,1,0:T(8,128)(2,1)S(1)} %copy-done.3, bf16[3,2,4096]{2,1,0:T(2,128)(2,1)S(1)} %collective-permute-done.3.halo, f32[3,3,8192]{2,1,0:T(4,128)S(1)} %copy-done.4), custom_call_target="tpu_custom_call" | custom-call | flops 1 | bytes 1 | tf_op jit(solution)/shard_map/short_filters/pallas_call | solution.py:362
  27.6 3.1 %block_states.1 = (bf16[4,16,256]{2,1,0:T(8,128)(2,1)S(1)}, bf16[4,16,256]{2,1,0:T(8,128)(2,1)S(1)}, bf16[4,16,256]{2,1,0:T(8,128)(2,1)S(1)}, bf16[4,16,256]{2,1,0:T(8,128)(2,1)S(1)}) custom-call(s32[3]{0:T(128)S(1)} %pad_add_fusion.here, f32[4,128,8,128]{3,2,1,0:T(8,128)S(1)} %get-tuple-element.53.u_ref, f32[4,33,256]{2,1,0:T(8,128)S(1)} %pad_maximum_fusion.3.refs_0_.rates, ...), custom_call_target="tpu_custom_call" | custom-call | flops 1 | bytes 1 | tf_op jit(solution)/shard_map/block_states/pallas_call | solution.py:378
  32.7 5.6 %local_convolution.1.y_ref = f32[4,128,8,128]{3,2,1,0:T(8,128)S(1)} custom-call(s32[3]{0:T(128)S(1)} %pad_add_fusion.here, f32[4,128,8,128]{3,2,1,0:T(8,128)S(1)} %get-tuple-element.53.u_ref, f32[4,33,256]{2,1,0:T(8,128)S(1)} %pad_maximum_fusion.3.refs_0_.rates, f32[4,33,256]{2,1,0:T(8,128)S(1)} %collective-permute-done.5.refs_1_, ...), custom_call_target="tpu_custom_call" | custom-call | flops 1 | bytes 1 | tf_op jit(solution)/shard_map/local_convolution/pallas_call | solution.py:388
  38.9 3.2 %collective-permute-start.12 = (bf16[4,16,256]{2,1,0:T(8,128)(2,1)S(1)}, bf16[4,16,256]{2,1,0:T(8,128)(2,1)S(1)}, u32[]{:S(2)}, u32[]{:S(2)}) collective-permute-start(bf16[4,16,256]{2,1,0:T(8,128)(2,1)S(1)} %slab_states.1), channel_id=1, source_target_pairs={{0,24},{2,26},{4,28},{6,30},{8,0},{10,2},{12,4},{14,6},{16,8},{18,... | collective-permute-start | bytes 98312 | tf_op jit(solution)/shard_map/ppermute | solution.py:309
  50.6 3.1 %collective-permute-done.14.refs_6_ = bf16[4,16,256]{2,1,0:T(8,128)(2,1)S(1)} collective-permute-done((bf16[4,16,256]{2,1,0:T(8,128)(2,1)S(1)}, bf16[4,16,256]{2,1,0:T(8,128)(2,1)S(1)}, u32[]{:S(2)}, u32[]{:S(2)}) %collective-permute-start.14) | collective-permute-done | bytes 32800 | tf_op jit(solution)/shard_map/ppermute | solution.py:306
  61.0 11.7 %collective-permute-done.17.refs_0_.refs_2_ = bf16[128,2048]{1,0:T(8,128)(2,1)S(1)} collective-permute-done((bf16[128,2048]{1,0:T(8,128)(2,1)S(1)}, bf16[128,2048]{1,0:T(8,128)(2,1)S(1)}, u32[]{:S(2)}, u32[]{:S(2)}) %collective-permute-start.17) | collective-permute-done | bytes 524320 | tf_op jit(solution)/shard_map/ppermute | solution.py:316
  75.0 3.1 %project_block.11 = bf16[1,2,128,256]{3,2,1,0:T(8,128)(2,1)S(1)} custom-call(s32[3]{0:T(128)S(1)} %add_add_fusion.1.here, bf16[128,2048]{1,0:T(8,128)(2,1)S(1)} %gated_block.2.refs_0_, bf16[128,2048]{1,0:T(8,128)(2,1)S(1)} %gated_block.3.refs_1_, bf16[4096,512]{1,0:T(8,128)(2,1)S(1)} %copy-done, bf16[4096,512]{1,0:T(8,128)(2,1)} %collective-permute-done.16.refs_3_.refs_2_), custom_call_target="tpu_custom_call" | custom-call | flops 1 | bytes 1 | tf_op jit(solution)/shard_map/project_block/pallas_call | solution.py:448
  78.1 3.1 %project_block.12 = bf16[1,2,128,256]{3,2,1,0:T(8,128)(2,1)S(1)} custom-call(s32[3]{0:T(128)S(1)} %add_add_fusion.here, bf16[128,2048]{1,0:T(8,128)(2,1)S(1)} %gated_block.2.refs_0_, bf16[128,2048]{1,0:T(8,128)(2,1)S(1)} %gated_block.3.refs_1_, bf16[4096,512]{1,0:T(8,128)(2,1)S(1)} %copy-done, bf16[4096,512]{1,0:T(8,128)(2,1)} %collective-permute-done.16.refs_3_.refs_2_), custom_call_target="tpu_custom_call" | custom-call | flops 1 | bytes 1 | tf_op jit(solution)/shard_map/project_block/pallas_call | solution.py:448
  84.4 10.7 %collective-permute-done.19.refs_0_.refs_4_ = bf16[128,2048]{1,0:T(8,128)(2,1)S(1)} collective-permute-done((bf16[128,2048]{1,0:T(8,128)(2,1)S(1)}, bf16[128,2048]{1,0:T(8,128)(2,1)S(1)}, u32[]{:S(2)}, u32[]{:S(2)}) %collective-permute-start.19) | collective-permute-done | bytes 524320 | tf_op jit(solution)/shard_map/ppermute | solution.py:316
  95.2 3.1 %project_block.14 = bf16[1,2,128,256]{3,2,1,0:T(8,128)(2,1)S(1)} custom-call(s32[3]{0:T(128)S(1)} %add_add_fusion.1.here, bf16[128,2048]{1,0:T(8,128)(2,1)S(1)} %collective-permute-done.17.refs_0_.refs_2_, bf16[128,2048]{1,0:T(8,128)(2,1)S(1)} %collective-permute-done.18.refs_1_.refs_3_, bf16[4096,512]{1,0:T(8,128)(2,1)S(1)} %copy-done, ...), custom_call_target="tpu_custom_call" | custom-call | flops 1 | bytes 1 | tf_op jit(solution)/shard_map/project_block/pallas_call | solution.py:448
  98.2 3.1 %project_block.17 = bf16[1,2,128,256]{3,2,1,0:T(8,128)(2,1)S(1)} custom-call(s32[3]{0:T(128)S(1)} %add_add_fusion.here, bf16[128,2048]{1,0:T(8,128)(2,1)S(1)} %collective-permute-done.17.refs_0_.refs_2_, bf16[128,2048]{1,0:T(8,128)(2,1)S(1)} %collective-permute-done.18.refs_1_.refs_3_, bf16[4096,512]{1,0:T(8,128)(2,1)S(1)} %copy-done, ...), custom_call_target="tpu_custom_call" | custom-call | flops 1 | bytes 1 | tf_op jit(solution)/shard_map/project_block/pallas_call | solution.py:448
  101.3 5.0 %collective-permute-done.20.refs_1_.refs_5_ = bf16[128,2048]{1,0:T(8,128)(2,1)S(1)} collective-permute-done((bf16[128,2048]{1,0:T(8,128)(2,1)S(1)}, bf16[128,2048]{1,0:T(8,128)(2,1)S(1)}, u32[]{:S(2)}, u32[]{:S(2)}) %collective-permute-start.20) | collective-permute-done | bytes 524320 | tf_op jit(solution)/shard_map/ppermute | solution.py:316
  106.9 3.7 %project_block.13 = bf16[1,2,128,256]{3,2,1,0:T(8,128)(2,1)} custom-call(s32[3]{0:T(128)S(1)} %add_add_fusion.1.here, bf16[128,2048]{1,0:T(8,128)(2,1)S(1)} %collective-permute-done.19.refs_0_.refs_4_, bf16[128,2048]{1,0:T(8,128)(2,1)S(1)} %collective-permute-done.20.refs_1_.refs_5_, bf16[4096,512]{1,0:T(8,128)(2,1)S(1)} %copy-done, ...), custom_call_target="tpu_custom_call" | custom-call | flops 1 | bytes 1 | tf_op jit(solution)/shard_map/project_block/pallas_call | solution.py:448
  111.5 3.1 %project_block.15 = bf16[1,2,128,256]{3,2,1,0:T(8,128)(2,1)S(1)} custom-call(s32[3]{0:T(128)S(1)} %add_add_fusion.here, bf16[128,2048]{1,0:T(8,128)(2,1)S(1)} %collective-permute-done.19.refs_0_.refs_4_, bf16[128,2048]{1,0:T(8,128)(2,1)S(1)} %collective-permute-done.20.refs_1_.refs_5_, bf16[4096,512]{1,0:T(8,128)(2,1)S(1)} %copy-done, ...), custom_call_target="tpu_custom_call" | custom-call | flops 1 | bytes 1 | tf_op jit(solution)/shard_map/project_block/pallas_call | solution.py:448
  114.6 4.3 %all-gather.3.cloned.1.call-done = bf16[16384,512]{1,0:T(8,128)(2,1)} async-done(((bf16[4096,512]{1,0:T(8,128)(2,1)}), bf16[16384,512]{1,0:T(8,128)(2,1)}) %all-gather.3.cloned.1.call-update) | async-done | bytes 16777232 | tf_op jit(solution)/shard_map/all_gather | solution.py:327
  118.9 5.5 %project_block.16 = bf16[3,2,128,256]{3,2,1,0:T(8,128)(2,1)} custom-call(s32[3]{0:T(128)S(1)} %add_add_fusion.1.here, bf16[128,2048]{1,0:T(8,128)(2,1)S(1)} %gated_block.2.refs_0_, bf16[128,2048]{1,0:T(8,128)(2,1)S(1)} %gated_block.3.refs_1_, bf16[128,2048]{1,0:T(8,128)(2,1)S(1)} %collective-permute-done.17.refs_0_.refs_2_, ...), custom_call_target="tpu_custom_call" | custom-call | flops 1 | bytes 1 | tf_op jit(solution)/shard_map/project_block/pallas_call | solution.py:448
  128.7 4.2 %project_block.18.refs_4_ = f32[2,1,4,128,256]{4,3,2,1,0:T(8,128)S(1)} custom-call(s32[3]{0:T(128)S(1)} %add_add_fusion.2.here, bf16[128,2048]{1,0:T(8,128)(2,1)} %collective-permute-done.26.refs_0_, bf16[4096,512]{1,0:T(8,128)(2,1)S(1)} %copy-done.1, bf16[4096,512]{1,0:T(8,128)(2,1)} %collective-permute-done.16.refs_3_.refs_2_, bf16[4,4096,512]{2,1,0:T(8,128)(2,1)} %bitcast.36), custom_call_target="tpu_custom_call" | custom-call | flops 1 | bytes 1 | tf_op jit(solution)/shard_map/project_block/pallas_call | solution.py:448
  133.0 3.4 %project_block.19 = bf16[1,4,128,256]{3,2,1,0:T(8,128)(2,1)S(1)} custom-call(s32[3]{0:T(128)S(1)} %add_add_fusion.1.here, bf16[128,2048]{1,0:T(8,128)(2,1)} %collective-permute-done.25.refs_0_, bf16[4096,512]{1,0:T(8,128)(2,1)S(1)} %copy-done.1, bf16[4096,512]{1,0:T(8,128)(2,1)} %collective-permute-done.16.refs_3_.refs_2_, bf16[4,4096,512]{2,1,0:T(8,128)(2,1)} %bitcast.37, ...), custom_call_target="tpu_custom_call" | custom-call | flops 1 | bytes 1 | tf_op jit(solution)/shard_map/project_block/pallas_call | solution.py:448
  137.0 4.8 %project_block.20 = bf16[3,2,128,256]{3,2,1,0:T(8,128)(2,1)S(1)} custom-call(s32[3]{0:T(128)S(1)} %add_add_fusion.here, bf16[128,2048]{1,0:T(8,128)(2,1)S(1)} %gated_block.2.refs_0_, bf16[128,2048]{1,0:T(8,128)(2,1)S(1)} %gated_block.3.refs_1_, bf16[128,2048]{1,0:T(8,128)(2,1)S(1)} %collective-permute-done.17.refs_0_.refs_2_, ...), custom_call_target="tpu_custom_call" | custom-call | flops 1 | bytes 1 | tf_op jit(solution)/shard_map/project_block/pallas_call | solution.py:448
  141.8 3.4 %project_block.21 = bf16[1,4,128,256]{3,2,1,0:T(8,128)(2,1)S(1)} custom-call(s32[3]{0:T(128)S(1)} %add_add_fusion.here, bf16[128,2048]{1,0:T(8,128)(2,1)} %collective-permute-done.25.refs_0_, bf16[4096,512]{1,0:T(8,128)(2,1)S(1)} %copy-done.2, bf16[4096,512]{1,0:T(8,128)(2,1)} %collective-permute-done.16.refs_3_.refs_2_, bf16[4,4096,512]{2,1,0:T(8,128)(2,1)} %bitcast.39, ...), custom_call_target="tpu_custom_call" | custom-call | flops 1 | bytes 1 | tf_op jit(solution)/shard_map/project_block/pallas_call | solution.py:448
  147.4 3.3 %collective-permute-start.30 = (bf16[4,128,256]{2,1,0:T(8,128)(2,1)S(1)}, bf16[4,128,256]{2,1,0:T(8,128)(2,1)S(1)}, u32[]{:S(2)}, u32[]{:S(2)}) collective-permute-start(bf16[4,128,256]{2,1,0:T(8,128)(2,1)S(1)} %get-tuple-element.95), channel_id=1, source_target_pairs={{0,24},{1,0},{2,26},{3,2},{4,28},{5,4},{6,30},{7,6},{8,16},{9,8},{... | collective-permute-start | bytes 786440 | tf_op jit(solution)/shard_map/ppermute | solution.py:494
  150.7 5.2 %collective-permute-start.27 = (bf16[4,128,256]{2,1,0:T(8,128)(2,1)S(1)}, bf16[4,128,256]{2,1,0:T(8,128)(2,1)S(1)}, u32[]{:S(2)}, u32[]{:S(2)}) collective-permute-start(bf16[4,128,256]{2,1,0:T(8,128)(2,1)S(1)} %get-tuple-element.96), channel_id=1, source_target_pairs={{0,0},{1,24},{2,2},{3,26},{4,4},{5,28},{6,6},{7,30},{8,8},{9,16},{... | collective-permute-start | bytes 786440 | tf_op jit(solution)/shard_map/ppermute | solution.py:494
  160.7 3.1 %collective-permute-done.27.refs_0_ = bf16[4,128,256]{2,1,0:T(8,128)(2,1)S(1)} collective-permute-done((bf16[4,128,256]{2,1,0:T(8,128)(2,1)S(1)}, bf16[4,128,256]{2,1,0:T(8,128)(2,1)S(1)}, u32[]{:S(2)}, u32[]{:S(2)}) %collective-permute-start.27) | collective-permute-done | bytes 262176 | tf_op jit(solution)/shard_map/ppermute | solution.py:494
  163.8 12.9 %collective-permute-done.31.refs_3_ = bf16[4,128,256]{2,1,0:T(8,128)(2,1)S(1)} collective-permute-done((bf16[4,128,256]{2,1,0:T(8,128)(2,1)S(1)}, bf16[4,128,256]{2,1,0:T(8,128)(2,1)S(1)}, u32[]{:S(2)}, u32[]{:S(2)}) %collective-permute-start.31) | collective-permute-done | bytes 262176 | tf_op jit(solution)/shard_map/ppermute | solution.py:494
  (96 shorter events, 58.3 us)
Async XLA Ops:
  6.5 112.4 %all-gather.3.cloned.1.call-start = ((), (), s32[]{:S(2)}) async-start(), calls=%async_computation | async-start | bytes 20971520 | tf_op jit(solution)/shard_map/all_gather | solution.py:327
  7.3 65.4 %collective-permute-start.16 = (bf16[4096,512]{1,0:T(8,128)(2,1)}, bf16[4096,512]{1,0:T(8,128)(2,1)}, u32[]{:S(2)}, u32[]{:S(2)}) collective-permute-start(bf16[4096,512]{1,0:T(8,128)(2,1)} %refs_1_.5), channel_id=1, source_target_pairs={{0,2},{2,0},{4,6},{6,4},{8,10},{10,8},{12,14},{14,12},{16,18},{18,... | collective-permute-start | bytes 12582920 | tf_op jit(solution)/shard_map/ppermute | solution.py:306
  7.4 7.2 %collective-permute-start.1 = (f32[33,256]{1,0:T(8,128)S(1)}, f32[33,256]{1,0:T(8,128)S(1)}, u32[]{:S(2)}, u32[]{:S(2)}) collective-permute-start(f32[33,256]{1,0:T(8,128)S(1)} %get-tuple-element.101), channel_id=1, source_target_pairs={{0,16},{2,18},{4,20},{6,22},{8,24},{10,26},{12,28},{14,30},{16,0},... | collective-permute-start | bytes 101384 | tf_op jit(solution)/shard_map/ppermute | solution.py:309
  11.4 5.8 %collective-permute-start.2 = (f32[33,256]{1,0:T(8,128)S(1)}, f32[33,256]{1,0:T(8,128)S(1)}, u32[]{:S(2)}, u32[]{:S(2)}) collective-permute-start(f32[33,256]{1,0:T(8,128)S(1)} %get-tuple-element.101), channel_id=1, source_target_pairs={{0,8},{2,10},{4,12},{6,14},{8,16},{10,18},{12,20},{14,22},{16,24},... | collective-permute-start | bytes 101384 | tf_op jit(solution)/shard_map/ppermute | solution.py:309
  17.2 8.6 %collective-permute-start.4 = (f32[4,33,256]{2,1,0:T(8,128)S(1)}, f32[4,33,256]{2,1,0:T(8,128)S(1)}, u32[]{:S(2)}, u32[]{:S(2)}) collective-permute-start(f32[4,33,256]{2,1,0:T(8,128)S(1)} %pad_maximum_fusion.3.refs_0_.rates), channel_id=1, source_target_pairs={{0,4},{2,6},{4,0},{6,2},{8,12},{10,14},{12,8},{14,10},{16,20},{18,... | collective-permute-start | bytes 405512 | tf_op jit(solution)/shard_map/ppermute | solution.py:306
  20.0 6.3 %collective-permute-start.5 = (f32[4,33,256]{2,1,0:T(8,128)S(1)}, f32[4,33,256]{2,1,0:T(8,128)S(1)}, u32[]{:S(2)}, u32[]{:S(2)}) collective-permute-start(f32[4,33,256]{2,1,0:T(8,128)S(1)} %pad_maximum_fusion.3.refs_0_.rates), channel_id=1, source_target_pairs={{0,2},{2,0},{4,6},{6,4},{8,10},{10,8},{12,14},{14,12},{16,18},{18,... | collective-permute-start | bytes 405512 | tf_op jit(solution)/shard_map/ppermute | solution.py:306
  30.7 7.5 %collective-permute-start.7 = (bf16[4,16,256]{2,1,0:T(8,128)(2,1)S(1)}, bf16[4,16,256]{2,1,0:T(8,128)(2,1)S(1)}, u32[]{:S(2)}, u32[]{:S(2)}) collective-permute-start(bf16[4,16,256]{2,1,0:T(8,128)(2,1)S(1)} %get-tuple-element.56), channel_id=1, source_target_pairs={{0,2},{2,0},{4,6},{6,4},{8,10},{10,8},{12,14},{14,12},{16,18},{18,... | collective-permute-start | bytes 98312 | tf_op jit(solution)/shard_map/ppermute | solution.py:306
  31.2 7.1 %collective-permute-start.8 = (bf16[4,16,256]{2,1,0:T(8,128)(2,1)S(1)}, bf16[4,16,256]{2,1,0:T(8,128)(2,1)S(1)}, u32[]{:S(2)}, u32[]{:S(2)}) collective-permute-start(bf16[4,16,256]{2,1,0:T(8,128)(2,1)S(1)} %get-tuple-element.57), channel_id=1, source_target_pairs={{0,4},{2,6},{4,0},{6,2},{8,12},{10,14},{12,8},{14,10},{16,20},{18,... | collective-permute-start | bytes 98312 | tf_op jit(solution)/shard_map/ppermute | solution.py:306
  31.9 6.4 %collective-permute-start.9 = (bf16[4,16,256]{2,1,0:T(8,128)(2,1)S(1)}, bf16[4,16,256]{2,1,0:T(8,128)(2,1)S(1)}, u32[]{:S(2)}, u32[]{:S(2)}) collective-permute-start(bf16[4,16,256]{2,1,0:T(8,128)(2,1)S(1)} %get-tuple-element.58), channel_id=1, source_target_pairs={{0,6},{2,4},{4,2},{6,0},{8,14},{10,12},{12,10},{14,8},{16,22},{18,... | collective-permute-start | bytes 98312 | tf_op jit(solution)/shard_map/ppermute | solution.py:306
  42.2 5.7 %collective-permute-start.10 = (bf16[4,16,256]{2,1,0:T(8,128)(2,1)S(1)}, bf16[4,16,256]{2,1,0:T(8,128)(2,1)S(1)}, u32[]{:S(2)}, u32[]{:S(2)}) collective-permute-start(bf16[4,16,256]{2,1,0:T(8,128)(2,1)S(1)} %slab_states.1), channel_id=1, source_target_pairs={{0,8},{2,10},{4,12},{6,14},{8,16},{10,18},{12,20},{14,22},{16,24},... | collective-permute-start | bytes 98312 | tf_op jit(solution)/shard_map/ppermute | solution.py:309
  57.0 15.7 %collective-permute-start.17 = (bf16[128,2048]{1,0:T(8,128)(2,1)S(1)}, bf16[128,2048]{1,0:T(8,128)(2,1)S(1)}, u32[]{:S(2)}, u32[]{:S(2)}) collective-permute-start(bf16[128,2048]{1,0:T(8,128)(2,1)S(1)} %gated_block.2.refs_0_), channel_id=1, source_target_pairs={{0,8},{2,10},{4,12},{6,14},{8,24},{10,26},{12,28},{14,30},{16,0},{... | collective-permute-start | bytes 1572872 | tf_op jit(solution)/shard_map/ppermute | solution.py:316
  59.5 24.4 %collective-permute-start.18 = (bf16[128,2048]{1,0:T(8,128)(2,1)S(1)}, bf16[128,2048]{1,0:T(8,128)(2,1)S(1)}, u32[]{:S(2)}, u32[]{:S(2)}) collective-permute-start(bf16[128,2048]{1,0:T(8,128)(2,1)S(1)} %gated_block.3.refs_1_), channel_id=1, source_target_pairs={{0,8},{2,10},{4,12},{6,14},{8,24},{10,26},{12,28},{14,30},{16,0},{... | collective-permute-start | bytes 1572872 | tf_op jit(solution)/shard_map/ppermute | solution.py:316
  72.7 22.5 %collective-permute-start.19 = (bf16[128,2048]{1,0:T(8,128)(2,1)S(1)}, bf16[128,2048]{1,0:T(8,128)(2,1)S(1)}, u32[]{:S(2)}, u32[]{:S(2)}) collective-permute-start(bf16[128,2048]{1,0:T(8,128)(2,1)S(1)} %collective-permute-done.17.refs_0_.refs_2_), channel_id=1, source_target_pairs={{0,8},{2,10},{4,12},{6,14},{8,24},{10,26},{12,28},{14,30},{16,0},{... | collective-permute-start | bytes 1572872 | tf_op jit(solution)/shard_map/ppermute | solution.py:316
  83.9 22.5 %collective-permute-start.20 = (bf16[128,2048]{1,0:T(8,128)(2,1)S(1)}, bf16[128,2048]{1,0:T(8,128)(2,1)S(1)}, u32[]{:S(2)}, u32[]{:S(2)}) collective-permute-start(bf16[128,2048]{1,0:T(8,128)(2,1)S(1)} %collective-permute-done.18.refs_1_.refs_3_), channel_id=1, source_target_pairs={{0,8},{2,10},{4,12},{6,14},{8,24},{10,26},{12,28},{14,30},{16,0},{... | collective-permute-start | bytes 1572872 | tf_op jit(solution)/shard_map/ppermute | solution.py:316
  83.9 14.3 %collective-permute-start.23 = (bf16[1,2,128,256]{3,2,1,0:T(8,128)(2,1)S(1)}, bf16[1,2,128,256]{3,2,1,0:T(8,128)(2,1)S(1)}, u32[]{:S(2)}, u32[]{:S(2)}) collective-permute-start(bf16[1,2,128,256]{3,2,1,0:T(8,128)(2,1)S(1)} %project_block.11), channel_id=1, source_target_pairs={{0,1},{1,0},{2,3},{3,2},{4,5},{5,4},{6,7},{7,6},{8,9},{9,8},{10,11... | collective-permute-start | bytes 393224 | tf_op jit(solution)/shard_map/ppermute | solution.py:475
  95.1 31.4 %collective-permute-start.26 = (bf16[128,2048]{1,0:T(8,128)(2,1)S(1)}, bf16[128,2048]{1,0:T(8,128)(2,1)}, u32[]{:S(2)}, u32[]{:S(2)}) collective-permute-start(bf16[128,2048]{1,0:T(8,128)(2,1)S(1)} %collective-permute-done.19.refs_0_.refs_4_), channel_id=1, source_target_pairs={{0,8},{2,10},{4,12},{6,14},{8,24},{10,26},{12,28},{14,30},{16,0},{... | collective-permute-start | bytes 1572872 | tf_op jit(solution)/shard_map/ppermute | solution.py:316
  106.4 26.6 %collective-permute-start.25 = (bf16[128,2048]{1,0:T(8,128)(2,1)S(1)}, bf16[128,2048]{1,0:T(8,128)(2,1)}, u32[]{:S(2)}, u32[]{:S(2)}) collective-permute-start(bf16[128,2048]{1,0:T(8,128)(2,1)S(1)} %collective-permute-done.20.refs_1_.refs_5_), channel_id=1, source_target_pairs={{0,8},{2,10},{4,12},{6,14},{8,24},{10,26},{12,28},{14,30},{16,0},{... | collective-permute-start | bytes 1572872 | tf_op jit(solution)/shard_map/ppermute | solution.py:316
  124.4 20.9 %collective-permute-start.22 = (bf16[3,2,128,256]{3,2,1,0:T(8,128)(2,1)}, bf16[3,2,128,256]{3,2,1,0:T(8,128)(2,1)}, u32[]{:S(2)}, u32[]{:S(2)}) collective-permute-start(bf16[3,2,128,256]{3,2,1,0:T(8,128)(2,1)} %project_block.16), channel_id=1, source_target_pairs={{0,1},{1,0},{2,3},{3,2},{4,5},{5,4},{6,7},{7,6},{8,9},{9,8},{10,11... | collective-permute-start | bytes 1179656 | tf_op jit(solution)/shard_map/ppermute | solution.py:475
  125.0 20.2 %collective-permute-start.24 = (bf16[1,2,128,256]{3,2,1,0:T(8,128)(2,1)}, bf16[1,2,128,256]{3,2,1,0:T(8,128)(2,1)}, u32[]{:S(2)}, u32[]{:S(2)}) collective-permute-start(bf16[1,2,128,256]{3,2,1,0:T(8,128)(2,1)} %project_block.13), channel_id=1, source_target_pairs={{0,1},{1,0},{2,3},{3,2},{4,5},{5,4},{6,7},{7,6},{8,9},{9,8},{10,11... | collective-permute-start | bytes 393224 | tf_op jit(solution)/shard_map/ppermute | solution.py:475
  136.4 20.6 %collective-permute-start.28 = (bf16[1,4,128,256]{3,2,1,0:T(8,128)(2,1)S(1)}, bf16[1,4,128,256]{3,2,1,0:T(8,128)(2,1)S(1)}, u32[]{:S(2)}, u32[]{:S(2)}) collective-permute-start(bf16[1,4,128,256]{3,2,1,0:T(8,128)(2,1)S(1)} %project_block.19), channel_id=1, source_target_pairs={{0,1},{1,0},{2,3},{3,2},{4,5},{5,4},{6,7},{7,6},{8,9},{9,8},{10,11... | collective-permute-start | bytes 786440 | tf_op jit(solution)/shard_map/ppermute | solution.py:522
  147.4 13.2 %collective-permute-start.30 = (bf16[4,128,256]{2,1,0:T(8,128)(2,1)S(1)}, bf16[4,128,256]{2,1,0:T(8,128)(2,1)S(1)}, u32[]{:S(2)}, u32[]{:S(2)}) collective-permute-start(bf16[4,128,256]{2,1,0:T(8,128)(2,1)S(1)} %get-tuple-element.95), channel_id=1, source_target_pairs={{0,24},{1,0},{2,26},{3,2},{4,28},{5,4},{6,30},{7,6},{8,16},{9,8},{... | collective-permute-start | bytes 786440 | tf_op jit(solution)/shard_map/ppermute | solution.py:494
  150.7 13.0 %collective-permute-start.27 = (bf16[4,128,256]{2,1,0:T(8,128)(2,1)S(1)}, bf16[4,128,256]{2,1,0:T(8,128)(2,1)S(1)}, u32[]{:S(2)}, u32[]{:S(2)}) collective-permute-start(bf16[4,128,256]{2,1,0:T(8,128)(2,1)S(1)} %get-tuple-element.96), channel_id=1, source_target_pairs={{0,0},{1,24},{2,2},{3,26},{4,4},{5,28},{6,6},{7,30},{8,8},{9,16},{... | collective-permute-start | bytes 786440 | tf_op jit(solution)/shard_map/ppermute | solution.py:494
  157.1 19.6 %collective-permute-start.31 = (bf16[4,128,256]{2,1,0:T(8,128)(2,1)S(1)}, bf16[4,128,256]{2,1,0:T(8,128)(2,1)S(1)}, u32[]{:S(2)}, u32[]{:S(2)}) collective-permute-start(bf16[4,128,256]{2,1,0:T(8,128)(2,1)S(1)} %get-tuple-element.93), channel_id=1, source_target_pairs={{0,8},{1,16},{2,10},{3,18},{4,12},{5,20},{6,14},{7,22},{8,24},{9,0... | collective-permute-start | bytes 786440 | tf_op jit(solution)/shard_map/ppermute | solution.py:494
  157.1 21.3 %collective-permute-start.29 = (bf16[4,128,256]{2,1,0:T(8,128)(2,1)S(1)}, bf16[4,128,256]{2,1,0:T(8,128)(2,1)S(1)}, u32[]{:S(2)}, u32[]{:S(2)}) collective-permute-start(bf16[4,128,256]{2,1,0:T(8,128)(2,1)S(1)} %get-tuple-element.94), channel_id=1, source_target_pairs={{0,16},{1,8},{2,18},{3,10},{4,20},{5,12},{6,22},{7,14},{8,0},{9,24... | collective-permute-start | bytes 786440 | tf_op jit(solution)/shard_map/ppermute | solution.py:494
  (19 other events, 72.7 us)
Sparse Core Ops, SparseCore 0:
  8.9 109.9 all-gather.2

commit v8 on v6

--- a/solution.py
+++ b/solution.py
@@ -14,6 +14,7 @@
 TAPS = 3
 SIDE = 2
 SLAB = SIDE * SIDE
+WIDE = 512
 F32 = jnp.float32
 BF16 = jnp.bfloat16
 
@@ -188,41 +189,50 @@
 
 def project_kernel(count, picks, first, added, here, *refs):
     out_ref, slots, held, sems = refs[-4:]
-    depth, share = slots.shape[1:]
-    runs = held.shape[0] // count
+    pieces = len(picks)
+    depth, share = slots.shape[0], slots.shape[1] // pieces
+    runs, size = held.shape[0] // count, held.shape[2]
     blocks, sources = refs[: runs * count], refs[runs * count : -4]
-    rows = pl.ds(first, depth)
     columns = pl.ds(pl.multiple_of(here[0] * share, share), share)
     copies = []
-    for i, (which, rank) in enumerate(picks):
-        source = sources[which] if rank is None else sources[which].at[here[rank]]
-        copies.append(pltpu.make_async_copy(source.at[rows, columns], slots.at[i], sems.at[i]))
+    for h in range(runs):
+        for i, (which, rank) in enumerate(picks):
+            source = sources[which] if rank is None else sources[which].at[here[rank]]
+            source = source.at[pl.ds(first + h * size, size), columns]
+            target = slots.at[pl.ds(h * size, size), pl.ds(i * share, share)]
+            copies.append(pltpu.make_async_copy(source, target, sems.at[h * pieces + i]))
     fetches = [
-        pltpu.make_async_copy(block, held.at[k], sems.at[len(picks) + k]) for k, block in enumerate(blocks)
+        pltpu.make_async_copy(block, held.at[k], sems.at[runs * pieces + k])
+        for k, block in enumerate(blocks)
     ]
-    copies[0].start()
-    for copy in fetches + copies[1:]:
+    for copy in copies[:pieces] + fetches + copies[pieces:]:
         copy.start()
     for copy in fetches:
         copy.wait()
-    for i in range(len(picks)):
-        copies[i].wait()
-        for j in range(count):
-            total = sources[-1][here[0], j, i] if added else None
-            for h in range(runs):
-                size = depth // runs
+    together = max(WIDE // share, 1)
+    for start in range(0, pieces, together):
+        totals = [None] * count
+        for h in range(runs):
+            for i in range(start, start + together):
+                copies[h * pieces + i].wait()
+            for j in range(count):
                 term = jnp.dot(
                     held[runs * j + h],
-                    slots[i, h * size : (h + 1) * size],
+                    slots[h * size : (h + 1) * size, start * share : (start + together) * share],
                     preferred_element_type=F32,
                 )
-                total = term if total is None else total + term
-            if out_ref.ndim == 4:
-                out_ref[j, i] = total.astype(out_ref.dtype)
-            else:
-                part = out_ref.shape[-1]
-                for t in range(out_ref.shape[0]):
-                    out_ref[t, j, i] = total[:, t * part : (t + 1) * part].astype(out_ref.dtype)
+                totals[j] = term if totals[j] is None else totals[j] + term
+        for j in range(count):
+            for i in range(start, start + together):
+                total = totals[j][:, (i - start) * share : (i - start + 1) * share]
+                if added:
+                    total = sources[-1][here[0], j, i] + total
+                if out_ref.ndim == 4:
+                    out_ref[j, i] = total.astype(out_ref.dtype)
+                else:
+                    part = out_ref.shape[-1]
+                    for t in range(out_ref.shape[0]):
+                        out_ref[t, j, i] = total[:, t * part : (t + 1) * part].astype(out_ref.dtype)
 
 
 def place_kernel(kept, counts, here, *refs):
@@ -456,9 +466,9 @@
             out_specs=vmem,
             out_shape=out,
             scratch_shapes=[
-                pltpu.VMEM((len(picks), len(halves) * run, wide_share), BF16),
+                pltpu.VMEM((len(halves) * run, len(picks) * wide_share), BF16),
                 pltpu.VMEM((len(halves) * len(blocks), tokens, run), BF16),
-                pltpu.SemaphoreType.DMA((len(picks) + len(halves) * len(blocks),)),
+                pltpu.SemaphoreType.DMA((len(halves) * (len(picks) + len(blocks)),)),
             ],
             compiler_params=large,
             cost_estimate=light,

time: 186 us -> 188 us (1.011)
  no operation moved by 1% of the time
where the time goes in v8:
time: 188 us; the launch traced here: 186 us
  Pallas kernels  61.5 us (33%)
  waiting for transfers between devices  60.1 us (32%)
  starting transfers between devices  41 us (22%)
  between operations  13.8 us (7%)
  local copies, waits for them, and re-layouts  5.78 us (3%)
  other arithmetic  3.52 us (2%)
    pallas_call x11, Pallas kernels, project(): pl.pallas_call(functools.partial(project_kernel, len(blocks), picks, halv...  41.6 us
    ppermute x6, waiting for transfers between devices, ring(): return lax.ppermute(array, 'ctx', pairs)  27.1 us
    ppermute x4, waiting for transfers between devices, deliver(): return lax.ppermute(moved, ('ctx', 'tp'), pairs)  13.1 us
    ppermute x4, starting transfers between devices, deliver(): return lax.ppermute(moved, ('ctx', 'tp'), pairs)  13 us
    ppermute x6, starting transfers between devices, from_slab(): lax.ppermute(array, 'ctx', [(i, (i - by * SLAB) % ctx) for i in range(ctx)])  10.4 us
    ppermute x10, starting transfers between devices, within_slab(): return lax.ppermute(array, 'ctx', [(i, i ^ mask) for i in range(ctx)])  8.01 us
    all_gather x1, waiting for transfers between devices, per_device(): lax.all_gather(out_weight, 'ctx', axis_index_groups=[list(range(z * SLAB,...  5.8 us
    ppermute x10, waiting for transfers between devices, within_slab(): return lax.ppermute(array, 'ctx', [(i, i ^ mask) for i in range(ctx)])  5.62 us
  transfers between devices with their start and end apart: 33, of which 16 were waited for; matrix products, arithmetic and copies ran while one was open for 1% of the time, Pallas kernels for 32%

profile of v8, /device:TPU:4, one launch (start us, length us, event | category | flops | bytes accessed | tf_op | source)
XLA Modules:
  0.0 185.7 jit_solution(18325787180669881373)
XLA Ops:
  7.4 3.7 %collective-permute-start = (f32[33,256]{1,0:T(8,128)S(1)}, f32[33,256]{1,0:T(8,128)S(1)}, u32[]{:S(2)}, u32[]{:S(2)}) collective-permute-start(f32[33,256]{1,0:T(8,128)S(1)} %get-tuple-element.101), channel_id=1, source_target_pairs={{0,24},{2,26},{4,28},{6,30},{8,0},{10,2},{12,4},{14,6},{16,8},{18,... | collective-permute-start | bytes 101384 | tf_op jit(solution)/shard_map/ppermute | solution.py:319
  16.9 3.1 %collective-permute-start.4 = (f32[4,33,256]{2,1,0:T(8,128)S(1)}, f32[4,33,256]{2,1,0:T(8,128)S(1)}, u32[]{:S(2)}, u32[]{:S(2)}) collective-permute-start(f32[4,33,256]{2,1,0:T(8,128)S(1)} %pad_maximum_fusion.3.refs_0_.rates), channel_id=1, source_target_pairs={{0,4},{2,6},{4,0},{6,2},{8,12},{10,14},{12,8},{14,10},{16,20},{18,... | collective-permute-start | bytes 405512 | tf_op jit(solution)/shard_map/ppermute | solution.py:316
  22.5 3.3 %short_filters.1 = (f32[4,128,8,128]{3,2,1,0:T(8,128)S(1)}, f32[4,128,8,128]{3,2,1,0:T(8,128)S(1)}) custom-call(s32[3]{0:T(128)S(1)} %pad_add_fusion.here, bf16[3,128,4096]{2,1,0:T(8,128)(2,1)S(1)} %copy-done.2, bf16[3,2,4096]{2,1,0:T(2,128)(2,1)S(1)} %collective-permute-done.3.halo, f32[3,3,8192]{2,1,0:T(4,128)S(1)} %copy-done.3), custom_call_target="tpu_custom_call" | custom-call | flops 1 | bytes 1 | tf_op jit(solution)/shard_map/short_filters/pallas_call | solution.py:372
  27.8 3.1 %block_states.1 = (bf16[4,16,256]{2,1,0:T(8,128)(2,1)S(1)}, bf16[4,16,256]{2,1,0:T(8,128)(2,1)S(1)}, bf16[4,16,256]{2,1,0:T(8,128)(2,1)S(1)}, bf16[4,16,256]{2,1,0:T(8,128)(2,1)S(1)}) custom-call(s32[3]{0:T(128)S(1)} %pad_add_fusion.here, f32[4,128,8,128]{3,2,1,0:T(8,128)S(1)} %get-tuple-element.53.u_ref, f32[4,33,256]{2,1,0:T(8,128)S(1)} %pad_maximum_fusion.3.refs_0_.rates, ...), custom_call_target="tpu_custom_call" | custom-call | flops 1 | bytes 1 | tf_op jit(solution)/shard_map/block_states/pallas_call | solution.py:388
  33.6 5.6 %local_convolution.1.y_ref = f32[4,128,8,128]{3,2,1,0:T(8,128)S(1)} custom-call(s32[3]{0:T(128)S(1)} %pad_add_fusion.here, f32[4,128,8,128]{3,2,1,0:T(8,128)S(1)} %get-tuple-element.53.u_ref, f32[4,33,256]{2,1,0:T(8,128)S(1)} %pad_maximum_fusion.3.refs_0_.rates, f32[4,33,256]{2,1,0:T(8,128)S(1)} %collective-permute-done.5.refs_1_, ...), custom_call_target="tpu_custom_call" | custom-call | flops 1 | bytes 1 | tf_op jit(solution)/shard_map/local_convolution/pallas_call | solution.py:398
  39.9 3.3 %collective-permute-start.10 = (bf16[4,16,256]{2,1,0:T(8,128)(2,1)S(1)}, bf16[4,16,256]{2,1,0:T(8,128)(2,1)S(1)}, u32[]{:S(2)}, u32[]{:S(2)}) collective-permute-start(bf16[4,16,256]{2,1,0:T(8,128)(2,1)S(1)} %slab_states.1), channel_id=1, source_target_pairs={{0,8},{2,10},{4,12},{6,14},{8,16},{10,18},{12,20},{14,22},{16,24},... | collective-permute-start | bytes 98312 | tf_op jit(solution)/shard_map/ppermute | solution.py:319
  51.1 3.1 %collective-permute-done.14.refs_6_ = bf16[4,16,256]{2,1,0:T(8,128)(2,1)S(1)} collective-permute-done((bf16[4,16,256]{2,1,0:T(8,128)(2,1)S(1)}, bf16[4,16,256]{2,1,0:T(8,128)(2,1)S(1)}, u32[]{:S(2)}, u32[]{:S(2)}) %collective-permute-start.14) | collective-permute-done | bytes 32800 | tf_op jit(solution)/shard_map/ppermute | solution.py:316
  63.6 9.5 %collective-permute-done.17.refs_0_.refs_2_ = bf16[128,2048]{1,0:T(8,128)(2,1)S(1)} collective-permute-done((bf16[128,2048]{1,0:T(8,128)(2,1)S(1)}, bf16[128,2048]{1,0:T(8,128)(2,1)S(1)}, u32[]{:S(2)}, u32[]{:S(2)}) %collective-permute-start.17) | collective-permute-done | bytes 524320 | tf_op jit(solution)/shard_map/ppermute | solution.py:326
  78.5 3.0 %project_block.12 = bf16[1,2,128,256]{3,2,1,0:T(8,128)(2,1)S(1)} custom-call(s32[3]{0:T(128)S(1)} %add_add_fusion.here, bf16[128,2048]{1,0:T(8,128)(2,1)S(1)} %gated_block.2.refs_0_, bf16[128,2048]{1,0:T(8,128)(2,1)S(1)} %gated_block.3.refs_1_, bf16[4096,512]{1,0:T(8,128)(2,1)S(1)} %copy-done, bf16[4096,512]{1,0:T(8,128)(2,1)} %collective-permute-done.16.refs_3_.refs_2_), custom_call_target="tpu_custom_call" | custom-call | flops 1 | bytes 1 | tf_op jit(solution)/shard_map/project_block/pallas_call | solution.py:458
  85.4 10.2 %collective-permute-done.19.refs_0_.refs_4_ = bf16[128,2048]{1,0:T(8,128)(2,1)S(1)} collective-permute-done((bf16[128,2048]{1,0:T(8,128)(2,1)S(1)}, bf16[128,2048]{1,0:T(8,128)(2,1)S(1)}, u32[]{:S(2)}, u32[]{:S(2)}) %collective-permute-start.19) | collective-permute-done | bytes 524320 | tf_op jit(solution)/shard_map/ppermute | solution.py:326
  102.3 4.5 %collective-permute-done.20.refs_1_.refs_5_ = bf16[128,2048]{1,0:T(8,128)(2,1)S(1)} collective-permute-done((bf16[128,2048]{1,0:T(8,128)(2,1)S(1)}, bf16[128,2048]{1,0:T(8,128)(2,1)S(1)}, u32[]{:S(2)}, u32[]{:S(2)}) %collective-permute-start.20) | collective-permute-done | bytes 524320 | tf_op jit(solution)/shard_map/ppermute | solution.py:326
  107.0 3.6 %project_block.13 = bf16[1,2,128,256]{3,2,1,0:T(8,128)(2,1)} custom-call(s32[3]{0:T(128)S(1)} %add_add_fusion.1.here, bf16[128,2048]{1,0:T(8,128)(2,1)S(1)} %collective-permute-done.19.refs_0_.refs_4_, bf16[128,2048]{1,0:T(8,128)(2,1)S(1)} %collective-permute-done.20.refs_1_.refs_5_, bf16[4096,512]{1,0:T(8,128)(2,1)S(1)} %copy-done, ...), custom_call_target="tpu_custom_call" | custom-call | flops 1 | bytes 1 | tf_op jit(solution)/shard_map/project_block/pallas_call | solution.py:458
  110.6 3.0 %project_block.15 = bf16[1,2,128,256]{3,2,1,0:T(8,128)(2,1)S(1)} custom-call(s32[3]{0:T(128)S(1)} %add_add_fusion.here, bf16[128,2048]{1,0:T(8,128)(2,1)S(1)} %collective-permute-done.19.refs_0_.refs_4_, bf16[128,2048]{1,0:T(8,128)(2,1)S(1)} %collective-permute-done.20.refs_1_.refs_5_, bf16[4096,512]{1,0:T(8,128)(2,1)S(1)} %copy-done, ...), custom_call_target="tpu_custom_call" | custom-call | flops 1 | bytes 1 | tf_op jit(solution)/shard_map/project_block/pallas_call | solution.py:458
  113.6 5.8 %all-gather.3.cloned.1.call-done = bf16[16384,512]{1,0:T(8,128)(2,1)} async-done(((bf16[4096,512]{1,0:T(8,128)(2,1)}), bf16[16384,512]{1,0:T(8,128)(2,1)}) %all-gather.3.cloned.1.call-update) | async-done | bytes 16777232 | tf_op jit(solution)/shard_map/all_gather | solution.py:337
  119.4 5.4 %project_block.16 = bf16[3,2,128,256]{3,2,1,0:T(8,128)(2,1)} custom-call(s32[3]{0:T(128)S(1)} %add_add_fusion.1.here, bf16[128,2048]{1,0:T(8,128)(2,1)S(1)} %gated_block.2.refs_0_, bf16[128,2048]{1,0:T(8,128)(2,1)S(1)} %gated_block.3.refs_1_, bf16[128,2048]{1,0:T(8,128)(2,1)S(1)} %collective-permute-done.17.refs_0_.refs_2_, ...), custom_call_target="tpu_custom_call" | custom-call | flops 1 | bytes 1 | tf_op jit(solution)/shard_map/project_block/pallas_call | solution.py:458
  127.0 4.9 %project_block.18 = bf16[3,2,128,256]{3,2,1,0:T(8,128)(2,1)S(1)} custom-call(s32[3]{0:T(128)S(1)} %add_add_fusion.here, bf16[128,2048]{1,0:T(8,128)(2,1)S(1)} %gated_block.2.refs_0_, bf16[128,2048]{1,0:T(8,128)(2,1)S(1)} %gated_block.3.refs_1_, bf16[128,2048]{1,0:T(8,128)(2,1)S(1)} %collective-permute-done.17.refs_0_.refs_2_, ...), custom_call_target="tpu_custom_call" | custom-call | flops 1 | bytes 1 | tf_op jit(solution)/shard_map/project_block/pallas_call | solution.py:458
  131.9 5.6 %project_block.19.refs_4_ = f32[2,1,4,128,256]{4,3,2,1,0:T(8,128)S(1)} custom-call(s32[3]{0:T(128)S(1)} %add_add_fusion.2.here, bf16[128,2048]{1,0:T(8,128)(2,1)} %collective-permute-done.26.refs_0_, bf16[4096,512]{1,0:T(8,128)(2,1)S(1)} %copy-done.1, bf16[4096,512]{1,0:T(8,128)(2,1)} %collective-permute-done.16.refs_3_.refs_2_, bf16[4,4096,512]{2,1,0:T(8,128)(2,1)} %bitcast.37), custom_call_target="tpu_custom_call" | custom-call | flops 1 | bytes 1 | tf_op jit(solution)/shard_map/project_block/pallas_call | solution.py:458
  137.5 3.6 %project_block.20 = bf16[1,4,128,256]{3,2,1,0:T(8,128)(2,1)S(1)} custom-call(s32[3]{0:T(128)S(1)} %add_add_fusion.1.here, bf16[128,2048]{1,0:T(8,128)(2,1)} %collective-permute-done.25.refs_0_, bf16[4096,512]{1,0:T(8,128)(2,1)S(1)} %copy-done.1, bf16[4096,512]{1,0:T(8,128)(2,1)} %collective-permute-done.16.refs_3_.refs_2_, bf16[4,4096,512]{2,1,0:T(8,128)(2,1)} %bitcast.38, ...), custom_call_target="tpu_custom_call" | custom-call | flops 1 | bytes 1 | tf_op jit(solution)/shard_map/project_block/pallas_call | solution.py:458
  143.3 4.8 %collective-permute-start.27 = (bf16[4,128,256]{2,1,0:T(8,128)(2,1)S(1)}, bf16[4,128,256]{2,1,0:T(8,128)(2,1)S(1)}, u32[]{:S(2)}, u32[]{:S(2)}) collective-permute-start(bf16[4,128,256]{2,1,0:T(8,128)(2,1)S(1)} %get-tuple-element.96), channel_id=1, source_target_pairs={{0,0},{1,24},{2,2},{3,26},{4,4},{5,28},{6,6},{7,30},{8,8},{9,16},{... | collective-permute-start | bytes 786440 | tf_op jit(solution)/shard_map/ppermute | solution.py:504
  148.3 3.9 %collective-permute-start.30 = (bf16[4,128,256]{2,1,0:T(8,128)(2,1)S(1)}, bf16[4,128,256]{2,1,0:T(8,128)(2,1)S(1)}, u32[]{:S(2)}, u32[]{:S(2)}) collective-permute-start(bf16[4,128,256]{2,1,0:T(8,128)(2,1)S(1)} %get-tuple-element.95), channel_id=1, source_target_pairs={{0,24},{1,0},{2,26},{3,2},{4,28},{5,4},{6,30},{7,6},{8,16},{9,8},{... | collective-permute-start | bytes 786440 | tf_op jit(solution)/shard_map/ppermute | solution.py:504
  155.0 3.7 %project_block.21 = bf16[1,4,128,256]{3,2,1,0:T(8,128)(2,1)S(1)} custom-call(s32[3]{0:T(128)S(1)} %add_add_fusion.here, bf16[128,2048]{1,0:T(8,128)(2,1)} %collective-permute-done.25.refs_0_, bf16[4096,512]{1,0:T(8,128)(2,1)S(1)} %copy-done.1, bf16[4096,512]{1,0:T(8,128)(2,1)} %collective-permute-done.16.refs_3_.refs_2_, bf16[4,4096,512]{2,1,0:T(8,128)(2,1)} %bitcast.39, ...), custom_call_target="tpu_custom_call" | custom-call | flops 1 | bytes 1 | tf_op jit(solution)/shard_map/project_block/pallas_call | solution.py:458
  161.7 4.2 %collective-permute-start.31 = (bf16[4,128,256]{2,1,0:T(8,128)(2,1)S(1)}, bf16[4,128,256]{2,1,0:T(8,128)(2,1)S(1)}, u32[]{:S(2)}, u32[]{:S(2)}) collective-permute-start(bf16[4,128,256]{2,1,0:T(8,128)(2,1)S(1)} %get-tuple-element.93), channel_id=1, source_target_pairs={{0,8},{1,16},{2,10},{3,18},{4,12},{5,20},{6,14},{7,22},{8,24},{9,0... | collective-permute-start | bytes 786440 | tf_op jit(solution)/shard_map/ppermute | solution.py:504
  166.0 4.6 %collective-permute-done.29.refs_1_ = bf16[4,128,256]{2,1,0:T(8,128)(2,1)S(1)} collective-permute-done((bf16[4,128,256]{2,1,0:T(8,128)(2,1)S(1)}, bf16[4,128,256]{2,1,0:T(8,128)(2,1)S(1)}, u32[]{:S(2)}, u32[]{:S(2)}) %collective-permute-start.29) | collective-permute-done | bytes 262176 | tf_op jit(solution)/shard_map/ppermute | solution.py:504
  170.6 6.6 %collective-permute-done.31.refs_3_ = bf16[4,128,256]{2,1,0:T(8,128)(2,1)S(1)} collective-permute-done((bf16[4,128,256]{2,1,0:T(8,128)(2,1)S(1)}, bf16[4,128,256]{2,1,0:T(8,128)(2,1)S(1)}, u32[]{:S(2)}, u32[]{:S(2)}) %collective-permute-start.31) | collective-permute-done | bytes 262176 | tf_op jit(solution)/shard_map/ppermute | solution.py:504
  (94 shorter events, 59.9 us)
Async XLA Ops:
  6.5 112.8 %all-gather.3.cloned.1.call-start = ((), (), s32[]{:S(2)}) async-start(), calls=%async_computation | async-start | bytes 20971520 | tf_op jit(solution)/shard_map/all_gather | solution.py:337
  7.3 66.0 %collective-permute-start.16 = (bf16[4096,512]{1,0:T(8,128)(2,1)}, bf16[4096,512]{1,0:T(8,128)(2,1)}, u32[]{:S(2)}, u32[]{:S(2)}) collective-permute-start(bf16[4096,512]{1,0:T(8,128)(2,1)} %refs_1_.5), channel_id=1, source_target_pairs={{0,2},{2,0},{4,6},{6,4},{8,10},{10,8},{12,14},{14,12},{16,18},{18,... | collective-permute-start | bytes 12582920 | tf_op jit(solution)/shard_map/ppermute | solution.py:316
  7.4 7.2 %collective-permute-start = (f32[33,256]{1,0:T(8,128)S(1)}, f32[33,256]{1,0:T(8,128)S(1)}, u32[]{:S(2)}, u32[]{:S(2)}) collective-permute-start(f32[33,256]{1,0:T(8,128)S(1)} %get-tuple-element.101), channel_id=1, source_target_pairs={{0,24},{2,26},{4,28},{6,30},{8,0},{10,2},{12,4},{14,6},{16,8},{18,... | collective-permute-start | bytes 101384 | tf_op jit(solution)/shard_map/ppermute | solution.py:319
  11.1 5.8 %collective-permute-start.2 = (f32[33,256]{1,0:T(8,128)S(1)}, f32[33,256]{1,0:T(8,128)S(1)}, u32[]{:S(2)}, u32[]{:S(2)}) collective-permute-start(f32[33,256]{1,0:T(8,128)S(1)} %get-tuple-element.101), channel_id=1, source_target_pairs={{0,8},{2,10},{4,12},{6,14},{8,16},{10,18},{12,20},{14,22},{16,24},... | collective-permute-start | bytes 101384 | tf_op jit(solution)/shard_map/ppermute | solution.py:319
  16.9 9.3 %collective-permute-start.4 = (f32[4,33,256]{2,1,0:T(8,128)S(1)}, f32[4,33,256]{2,1,0:T(8,128)S(1)}, u32[]{:S(2)}, u32[]{:S(2)}) collective-permute-start(f32[4,33,256]{2,1,0:T(8,128)S(1)} %pad_maximum_fusion.3.refs_0_.rates), channel_id=1, source_target_pairs={{0,4},{2,6},{4,0},{6,2},{8,12},{10,14},{12,8},{14,10},{16,20},{18,... | collective-permute-start | bytes 405512 | tf_op jit(solution)/shard_map/ppermute | solution.py:316
  20.0 6.3 %collective-permute-start.5 = (f32[4,33,256]{2,1,0:T(8,128)S(1)}, f32[4,33,256]{2,1,0:T(8,128)S(1)}, u32[]{:S(2)}, u32[]{:S(2)}) collective-permute-start(f32[4,33,256]{2,1,0:T(8,128)S(1)} %pad_maximum_fusion.3.refs_0_.rates), channel_id=1, source_target_pairs={{0,2},{2,0},{4,6},{6,4},{8,10},{10,8},{12,14},{14,12},{16,18},{18,... | collective-permute-start | bytes 405512 | tf_op jit(solution)/shard_map/ppermute | solution.py:316
  30.9 8.3 %collective-permute-start.7 = (bf16[4,16,256]{2,1,0:T(8,128)(2,1)S(1)}, bf16[4,16,256]{2,1,0:T(8,128)(2,1)S(1)}, u32[]{:S(2)}, u32[]{:S(2)}) collective-permute-start(bf16[4,16,256]{2,1,0:T(8,128)(2,1)S(1)} %get-tuple-element.56), channel_id=1, source_target_pairs={{0,2},{2,0},{4,6},{6,4},{8,10},{10,8},{12,14},{14,12},{16,18},{18,... | collective-permute-start | bytes 98312 | tf_op jit(solution)/shard_map/ppermute | solution.py:316
  31.2 8.1 %collective-permute-start.8 = (bf16[4,16,256]{2,1,0:T(8,128)(2,1)S(1)}, bf16[4,16,256]{2,1,0:T(8,128)(2,1)S(1)}, u32[]{:S(2)}, u32[]{:S(2)}) collective-permute-start(bf16[4,16,256]{2,1,0:T(8,128)(2,1)S(1)} %get-tuple-element.57), channel_id=1, source_target_pairs={{0,4},{2,6},{4,0},{6,2},{8,12},{10,14},{12,8},{14,10},{16,20},{18,... | collective-permute-start | bytes 98312 | tf_op jit(solution)/shard_map/ppermute | solution.py:316
  39.9 5.8 %collective-permute-start.10 = (bf16[4,16,256]{2,1,0:T(8,128)(2,1)S(1)}, bf16[4,16,256]{2,1,0:T(8,128)(2,1)S(1)}, u32[]{:S(2)}, u32[]{:S(2)}) collective-permute-start(bf16[4,16,256]{2,1,0:T(8,128)(2,1)S(1)} %slab_states.1), channel_id=1, source_target_pairs={{0,8},{2,10},{4,12},{6,14},{8,16},{10,18},{12,20},{14,22},{16,24},... | collective-permute-start | bytes 98312 | tf_op jit(solution)/shard_map/ppermute | solution.py:319
  57.4 15.7 %collective-permute-start.17 = (bf16[128,2048]{1,0:T(8,128)(2,1)S(1)}, bf16[128,2048]{1,0:T(8,128)(2,1)S(1)}, u32[]{:S(2)}, u32[]{:S(2)}) collective-permute-start(bf16[128,2048]{1,0:T(8,128)(2,1)S(1)} %gated_block.2.refs_0_), channel_id=1, source_target_pairs={{0,8},{2,10},{4,12},{6,14},{8,24},{10,26},{12,28},{14,30},{16,0},{... | collective-permute-start | bytes 1572872 | tf_op jit(solution)/shard_map/ppermute | solution.py:326
  60.8 23.6 %collective-permute-start.18 = (bf16[128,2048]{1,0:T(8,128)(2,1)S(1)}, bf16[128,2048]{1,0:T(8,128)(2,1)S(1)}, u32[]{:S(2)}, u32[]{:S(2)}) collective-permute-start(bf16[128,2048]{1,0:T(8,128)(2,1)S(1)} %gated_block.3.refs_1_), channel_id=1, source_target_pairs={{0,8},{2,10},{4,12},{6,14},{8,24},{10,26},{12,28},{14,30},{16,0},{... | collective-permute-start | bytes 1572872 | tf_op jit(solution)/shard_map/ppermute | solution.py:326
  73.1 22.5 %collective-permute-start.19 = (bf16[128,2048]{1,0:T(8,128)(2,1)S(1)}, bf16[128,2048]{1,0:T(8,128)(2,1)S(1)}, u32[]{:S(2)}, u32[]{:S(2)}) collective-permute-start(bf16[128,2048]{1,0:T(8,128)(2,1)S(1)} %collective-permute-done.17.refs_0_.refs_2_), channel_id=1, source_target_pairs={{0,8},{2,10},{4,12},{6,14},{8,24},{10,26},{12,28},{14,30},{16,0},{... | collective-permute-start | bytes 1572872 | tf_op jit(solution)/shard_map/ppermute | solution.py:326
  84.3 22.5 %collective-permute-start.20 = (bf16[128,2048]{1,0:T(8,128)(2,1)S(1)}, bf16[128,2048]{1,0:T(8,128)(2,1)S(1)}, u32[]{:S(2)}, u32[]{:S(2)}) collective-permute-start(bf16[128,2048]{1,0:T(8,128)(2,1)S(1)} %collective-permute-done.18.refs_1_.refs_3_), channel_id=1, source_target_pairs={{0,8},{2,10},{4,12},{6,14},{8,24},{10,26},{12,28},{14,30},{16,0},{... | collective-permute-start | bytes 1572872 | tf_op jit(solution)/shard_map/ppermute | solution.py:326
  84.9 14.5 %collective-permute-start.23 = (bf16[1,2,128,256]{3,2,1,0:T(8,128)(2,1)S(1)}, bf16[1,2,128,256]{3,2,1,0:T(8,128)(2,1)S(1)}, u32[]{:S(2)}, u32[]{:S(2)}) collective-permute-start(bf16[1,2,128,256]{3,2,1,0:T(8,128)(2,1)S(1)} %project_block.11), channel_id=1, source_target_pairs={{0,1},{1,0},{2,3},{3,2},{4,5},{5,4},{6,7},{7,6},{8,9},{9,8},{10,11... | collective-permute-start | bytes 393224 | tf_op jit(solution)/shard_map/ppermute | solution.py:485
  95.6 36.3 %collective-permute-start.26 = (bf16[128,2048]{1,0:T(8,128)(2,1)S(1)}, bf16[128,2048]{1,0:T(8,128)(2,1)}, u32[]{:S(2)}, u32[]{:S(2)}) collective-permute-start(bf16[128,2048]{1,0:T(8,128)(2,1)S(1)} %collective-permute-done.19.refs_0_.refs_4_), channel_id=1, source_target_pairs={{0,8},{2,10},{4,12},{6,14},{8,24},{10,26},{12,28},{14,30},{16,0},{... | collective-permute-start | bytes 1572872 | tf_op jit(solution)/shard_map/ppermute | solution.py:326
  98.7 11.9 %collective-permute-start.21 = (bf16[1,2,128,256]{3,2,1,0:T(8,128)(2,1)S(1)}, bf16[1,2,128,256]{3,2,1,0:T(8,128)(2,1)}, u32[]{:S(2)}, u32[]{:S(2)}) collective-permute-start(bf16[1,2,128,256]{3,2,1,0:T(8,128)(2,1)S(1)} %project_block.14), channel_id=1, source_target_pairs={{0,1},{1,0},{2,3},{3,2},{4,5},{5,4},{6,7},{7,6},{8,9},{9,8},{10,11... | collective-permute-start | bytes 393224 | tf_op jit(solution)/shard_map/ppermute | solution.py:485
  106.8 30.7 %collective-permute-start.25 = (bf16[128,2048]{1,0:T(8,128)(2,1)S(1)}, bf16[128,2048]{1,0:T(8,128)(2,1)}, u32[]{:S(2)}, u32[]{:S(2)}) collective-permute-start(bf16[128,2048]{1,0:T(8,128)(2,1)S(1)} %collective-permute-done.20.refs_1_.refs_5_), channel_id=1, source_target_pairs={{0,8},{2,10},{4,12},{6,14},{8,24},{10,26},{12,28},{14,30},{16,0},{... | collective-permute-start | bytes 1572872 | tf_op jit(solution)/shard_map/ppermute | solution.py:326
  124.8 16.3 %collective-permute-start.22 = (bf16[3,2,128,256]{3,2,1,0:T(8,128)(2,1)}, bf16[3,2,128,256]{3,2,1,0:T(8,128)(2,1)}, u32[]{:S(2)}, u32[]{:S(2)}) collective-permute-start(bf16[3,2,128,256]{3,2,1,0:T(8,128)(2,1)} %project_block.16), channel_id=1, source_target_pairs={{0,1},{1,0},{2,3},{3,2},{4,5},{5,4},{6,7},{7,6},{8,9},{9,8},{10,11... | collective-permute-start | bytes 1179656 | tf_op jit(solution)/shard_map/ppermute | solution.py:485
  125.4 15.8 %collective-permute-start.24 = (bf16[1,2,128,256]{3,2,1,0:T(8,128)(2,1)}, bf16[1,2,128,256]{3,2,1,0:T(8,128)(2,1)}, u32[]{:S(2)}, u32[]{:S(2)}) collective-permute-start(bf16[1,2,128,256]{3,2,1,0:T(8,128)(2,1)} %project_block.13), channel_id=1, source_target_pairs={{0,1},{1,0},{2,3},{3,2},{4,5},{5,4},{6,7},{7,6},{8,9},{9,8},{10,11... | collective-permute-start | bytes 393224 | tf_op jit(solution)/shard_map/ppermute | solution.py:485
  143.3 11.7 %collective-permute-start.27 = (bf16[4,128,256]{2,1,0:T(8,128)(2,1)S(1)}, bf16[4,128,256]{2,1,0:T(8,128)(2,1)S(1)}, u32[]{:S(2)}, u32[]{:S(2)}) collective-permute-start(bf16[4,128,256]{2,1,0:T(8,128)(2,1)S(1)} %get-tuple-element.96), channel_id=1, source_target_pairs={{0,0},{1,24},{2,2},{3,26},{4,4},{5,28},{6,6},{7,30},{8,8},{9,16},{... | collective-permute-start | bytes 786440 | tf_op jit(solution)/shard_map/ppermute | solution.py:504
  148.2 13.3 %collective-permute-start.28 = (bf16[1,4,128,256]{3,2,1,0:T(8,128)(2,1)S(1)}, bf16[1,4,128,256]{3,2,1,0:T(8,128)(2,1)S(1)}, u32[]{:S(2)}, u32[]{:S(2)}) collective-permute-start(bf16[1,4,128,256]{3,2,1,0:T(8,128)(2,1)S(1)} %project_block.20), channel_id=1, source_target_pairs={{0,1},{1,0},{2,3},{3,2},{4,5},{5,4},{6,7},{7,6},{8,9},{9,8},{10,11... | collective-permute-start | bytes 786440 | tf_op jit(solution)/shard_map/ppermute | solution.py:533
  148.3 17.7 %collective-permute-start.30 = (bf16[4,128,256]{2,1,0:T(8,128)(2,1)S(1)}, bf16[4,128,256]{2,1,0:T(8,128)(2,1)S(1)}, u32[]{:S(2)}, u32[]{:S(2)}) collective-permute-start(bf16[4,128,256]{2,1,0:T(8,128)(2,1)S(1)} %get-tuple-element.95), channel_id=1, source_target_pairs={{0,24},{1,0},{2,26},{3,2},{4,28},{5,4},{6,30},{7,6},{8,16},{9,8},{... | collective-permute-start | bytes 786440 | tf_op jit(solution)/shard_map/ppermute | solution.py:504
  161.6 8.9 %collective-permute-start.29 = (bf16[4,128,256]{2,1,0:T(8,128)(2,1)S(1)}, bf16[4,128,256]{2,1,0:T(8,128)(2,1)S(1)}, u32[]{:S(2)}, u32[]{:S(2)}) collective-permute-start(bf16[4,128,256]{2,1,0:T(8,128)(2,1)S(1)} %get-tuple-element.94), channel_id=1, source_target_pairs={{0,16},{1,8},{2,18},{3,10},{4,20},{5,12},{6,22},{7,14},{8,0},{9,24... | collective-permute-start | bytes 786440 | tf_op jit(solution)/shard_map/ppermute | solution.py:504
  161.7 15.5 %collective-permute-start.31 = (bf16[4,128,256]{2,1,0:T(8,128)(2,1)S(1)}, bf16[4,128,256]{2,1,0:T(8,128)(2,1)S(1)}, u32[]{:S(2)}, u32[]{:S(2)}) collective-permute-start(bf16[4,128,256]{2,1,0:T(8,128)(2,1)S(1)} %get-tuple-element.93), channel_id=1, source_target_pairs={{0,8},{1,16},{2,10},{3,18},{4,12},{5,20},{6,14},{7,22},{8,24},{9,0... | collective-permute-start | bytes 786440 | tf_op jit(solution)/shard_map/ppermute | solution.py:504
  (18 other events, 71.9 us)
Sparse Core Ops, SparseCore 0:
  8.9 110.4 all-gather.2

commit v9 on v6

--- a/solution.py
+++ b/solution.py
@@ -521,13 +521,14 @@
     tail = blocks[-1][1]
     last_away = project([[None, tail]], sources, both, 1 - tp_me, partial, (1,))
     last_got = lax.ppermute(last_away, "tp", [(0, 1), (1, 0)])
-    batch_got, got_parts, _ = lax.optimization_barrier((batch_got, got_parts, last_away))
+    tail, _ = lax.optimization_barrier((tail, last_away))
+    last_mine = project([[None, tail]], sources, both, tp_me, partial, (1,))
+    batch_got, got_parts, _ = lax.optimization_barrier((batch_got, got_parts, last_mine))
     near_sums = [total(m, g)[0] for m, g in zip(kept_parts, got_parts)]
     sums = [jnp.concatenate(parts) for parts in zip(near_sums, total(batch_mine, batch_got))]
     late = ((slabs - 1) % (slabs // tp), slabs - 1)
     arrived = {by: [deliver(sums, by)] for by in range(slabs) if by not in late}
-    tail, _ = lax.optimization_barrier((tail, (last_away, arrived[0])))
-    last_mine = project([[None, tail]], sources, both, tp_me, partial, (1,))
+    last_got, _ = lax.optimization_barrier((last_got, arrived[0]))
     sums.append(total(last_mine, last_got)[0])
     for by in late:
         arrived[by] = [deliver(sums, by)]

time: 186 us -> 187 us (level)
  starting transfers between devices: 41 us -> 44.1 us
    ppermute x1, waiting for transfers between devices: 3.03 us -> 0.01 us  [per_device(): last_got = lax.ppermute(last_away, 'tp', [(0, 1), (1, 0)])]
    ppermute x4, starting transfers between devices: 12.8 us -> 15.4 us  [deliver(): return lax.ppermute(moved, ('ctx', 'tp'), pairs)]
    ppermute x4, waiting for transfers between devices: 13.1 us -> 15.3 us  [deliver(): return lax.ppermute(moved, ('ctx', 'tp'), pairs)]
  transfers between devices with their start and end apart: 33 -> 33, of which waited for: 16 -> 15; matrix products, arithmetic and copies ran while one was open for 1% -> 2% of each run, Pallas kernels for 32% -> 32%
where the time goes in v9:
time: 187 us; the launch traced here: 186 us
  Pallas kernels  60.5 us (32%)
  waiting for transfers between devices  58.7 us (31%)
  starting transfers between devices  44.1 us (24%)
  between operations  13.8 us (7%)
  local copies, waits for them, and re-layouts  5.78 us (3%)
  other arithmetic  3.52 us (2%)
    pallas_call x11, Pallas kernels, project(): pl.pallas_call(functools.partial(project_kernel, len(blocks), picks, halv...  40.5 us
    ppermute x6, waiting for transfers between devices, ring(): return lax.ppermute(array, 'ctx', pairs)  26.4 us
    ppermute x4, starting transfers between devices, deliver(): return lax.ppermute(moved, ('ctx', 'tp'), pairs)  15.4 us
    ppermute x4, waiting for transfers between devices, deliver(): return lax.ppermute(moved, ('ctx', 'tp'), pairs)  15.3 us
    ppermute x6, starting transfers between devices, from_slab(): lax.ppermute(array, 'ctx', [(i, (i - by * SLAB) % ctx) for i in range(ctx)])  10.4 us
    ppermute x10, starting transfers between devices, within_slab(): return lax.ppermute(array, 'ctx', [(i, i ^ mask) for i in range(ctx)])  8.01 us
    ppermute x10, waiting for transfers between devices, within_slab(): return lax.ppermute(array, 'ctx', [(i, i ^ mask) for i in range(ctx)])  5.62 us
    pallas_call x1, Pallas kernels, per_device(): grouped(functools.partial(local_kernel, modes), 'local_convolution', [ser...  5.61 us
  transfers between devices with their start and end apart: 33, of which 15 were waited for; matrix products, arithmetic and copies ran while one was open for 2% of the time, Pallas kernels for 32%

profile of v9, /device:TPU:4, one launch (start us, length us, event | category | flops | bytes accessed | tf_op | source)
XLA Modules:
  0.0 186.3 jit_solution(15226083912291900544)
XLA Ops:
  7.4 3.7 %collective-permute-start = (f32[33,256]{1,0:T(8,128)S(1)}, f32[33,256]{1,0:T(8,128)S(1)}, u32[]{:S(2)}, u32[]{:S(2)}) collective-permute-start(f32[33,256]{1,0:T(8,128)S(1)} %get-tuple-element.103), channel_id=1, source_target_pairs={{0,24},{2,26},{4,28},{6,30},{8,0},{10,2},{12,4},{14,6},{16,8},{18,... | collective-permute-start | bytes 101384 | tf_op jit(solution)/shard_map/ppermute | solution.py:309
  22.5 3.3 %short_filters.1 = (f32[4,128,8,128]{3,2,1,0:T(8,128)S(1)}, f32[4,128,8,128]{3,2,1,0:T(8,128)S(1)}) custom-call(s32[3]{0:T(128)S(1)} %pad_add_fusion.here, bf16[3,128,4096]{2,1,0:T(8,128)(2,1)S(1)} %copy-done.2, bf16[3,2,4096]{2,1,0:T(2,128)(2,1)S(1)} %collective-permute-done.3.halo, f32[3,3,8192]{2,1,0:T(4,128)S(1)} %copy-done.3), custom_call_target="tpu_custom_call" | custom-call | flops 1 | bytes 1 | tf_op jit(solution)/shard_map/short_filters/pallas_call | solution.py:362
  27.8 3.1 %block_states.1 = (bf16[4,16,256]{2,1,0:T(8,128)(2,1)S(1)}, bf16[4,16,256]{2,1,0:T(8,128)(2,1)S(1)}, bf16[4,16,256]{2,1,0:T(8,128)(2,1)S(1)}, bf16[4,16,256]{2,1,0:T(8,128)(2,1)S(1)}) custom-call(s32[3]{0:T(128)S(1)} %pad_add_fusion.here, f32[4,128,8,128]{3,2,1,0:T(8,128)S(1)} %get-tuple-element.54.u_ref, f32[4,33,256]{2,1,0:T(8,128)S(1)} %pad_maximum_fusion.3.refs_0_.rates, ...), custom_call_target="tpu_custom_call" | custom-call | flops 1 | bytes 1 | tf_op jit(solution)/shard_map/block_states/pallas_call | solution.py:378
  33.6 5.6 %local_convolution.1.y_ref = f32[4,128,8,128]{3,2,1,0:T(8,128)S(1)} custom-call(s32[3]{0:T(128)S(1)} %pad_add_fusion.here, f32[4,128,8,128]{3,2,1,0:T(8,128)S(1)} %get-tuple-element.54.u_ref, f32[4,33,256]{2,1,0:T(8,128)S(1)} %pad_maximum_fusion.3.refs_0_.rates, f32[4,33,256]{2,1,0:T(8,128)S(1)} %collective-permute-done.5.refs_1_, ...), custom_call_target="tpu_custom_call" | custom-call | flops 1 | bytes 1 | tf_op jit(solution)/shard_map/local_convolution/pallas_call | solution.py:388
  39.9 3.3 %collective-permute-start.10 = (bf16[4,16,256]{2,1,0:T(8,128)(2,1)S(1)}, bf16[4,16,256]{2,1,0:T(8,128)(2,1)S(1)}, u32[]{:S(2)}, u32[]{:S(2)}) collective-permute-start(bf16[4,16,256]{2,1,0:T(8,128)(2,1)S(1)} %slab_states.1), channel_id=1, source_target_pairs={{0,8},{2,10},{4,12},{6,14},{8,16},{10,18},{12,20},{14,22},{16,24},... | collective-permute-start | bytes 98312 | tf_op jit(solution)/shard_map/ppermute | solution.py:309
  51.1 3.1 %collective-permute-done.14.refs_6_ = bf16[4,16,256]{2,1,0:T(8,128)(2,1)S(1)} collective-permute-done((bf16[4,16,256]{2,1,0:T(8,128)(2,1)S(1)}, bf16[4,16,256]{2,1,0:T(8,128)(2,1)S(1)}, u32[]{:S(2)}, u32[]{:S(2)}) %collective-permute-start.14) | collective-permute-done | bytes 32800 | tf_op jit(solution)/shard_map/ppermute | solution.py:306
  63.6 9.5 %collective-permute-done.17.refs_0_.refs_2_ = bf16[128,2048]{1,0:T(8,128)(2,1)S(1)} collective-permute-done((bf16[128,2048]{1,0:T(8,128)(2,1)S(1)}, bf16[128,2048]{1,0:T(8,128)(2,1)S(1)}, u32[]{:S(2)}, u32[]{:S(2)}) %collective-permute-start.17) | collective-permute-done | bytes 524320 | tf_op jit(solution)/shard_map/ppermute | solution.py:316
  75.5 3.1 %project_block.11 = bf16[1,2,128,256]{3,2,1,0:T(8,128)(2,1)S(1)} custom-call(s32[3]{0:T(128)S(1)} %add_add_fusion.1.here, bf16[128,2048]{1,0:T(8,128)(2,1)S(1)} %gated_block.2.refs_0_, bf16[128,2048]{1,0:T(8,128)(2,1)S(1)} %gated_block.3.refs_1_, bf16[4096,512]{1,0:T(8,128)(2,1)S(1)} %copy-done, bf16[4096,512]{1,0:T(8,128)(2,1)} %collective-permute-done.16.refs_3_.refs_2_), custom_call_target="tpu_custom_call" | custom-call | flops 1 | bytes 1 | tf_op jit(solution)/shard_map/project_block/pallas_call | solution.py:448
  78.6 3.1 %project_block.12 = bf16[1,2,128,256]{3,2,1,0:T(8,128)(2,1)S(1)} custom-call(s32[3]{0:T(128)S(1)} %add_add_fusion.here, bf16[128,2048]{1,0:T(8,128)(2,1)S(1)} %gated_block.2.refs_0_, bf16[128,2048]{1,0:T(8,128)(2,1)S(1)} %gated_block.3.refs_1_, bf16[4096,512]{1,0:T(8,128)(2,1)S(1)} %copy-done, bf16[4096,512]{1,0:T(8,128)(2,1)} %collective-permute-done.16.refs_3_.refs_2_), custom_call_target="tpu_custom_call" | custom-call | flops 1 | bytes 1 | tf_op jit(solution)/shard_map/project_block/pallas_call | solution.py:448
  85.6 10.0 %collective-permute-done.19.refs_0_.refs_4_ = bf16[128,2048]{1,0:T(8,128)(2,1)S(1)} collective-permute-done((bf16[128,2048]{1,0:T(8,128)(2,1)S(1)}, bf16[128,2048]{1,0:T(8,128)(2,1)S(1)}, u32[]{:S(2)}, u32[]{:S(2)}) %collective-permute-start.19) | collective-permute-done | bytes 524320 | tf_op jit(solution)/shard_map/ppermute | solution.py:316
  99.5 3.1 %project_block.17 = bf16[1,2,128,256]{3,2,1,0:T(8,128)(2,1)S(1)} custom-call(s32[3]{0:T(128)S(1)} %add_add_fusion.here, bf16[128,2048]{1,0:T(8,128)(2,1)S(1)} %collective-permute-done.17.refs_0_.refs_2_, bf16[128,2048]{1,0:T(8,128)(2,1)S(1)} %collective-permute-done.18.refs_1_.refs_3_, bf16[4096,512]{1,0:T(8,128)(2,1)S(1)} %copy-done, ...), custom_call_target="tpu_custom_call" | custom-call | flops 1 | bytes 1 | tf_op jit(solution)/shard_map/project_block/pallas_call | solution.py:448
  102.5 4.3 %collective-permute-done.20.refs_1_.refs_5_ = bf16[128,2048]{1,0:T(8,128)(2,1)S(1)} collective-permute-done((bf16[128,2048]{1,0:T(8,128)(2,1)S(1)}, bf16[128,2048]{1,0:T(8,128)(2,1)S(1)}, u32[]{:S(2)}, u32[]{:S(2)}) %collective-permute-start.20) | collective-permute-done | bytes 524320 | tf_op jit(solution)/shard_map/ppermute | solution.py:316
  107.0 3.7 %project_block.13 = bf16[1,2,128,256]{3,2,1,0:T(8,128)(2,1)} custom-call(s32[3]{0:T(128)S(1)} %add_add_fusion.1.here, bf16[128,2048]{1,0:T(8,128)(2,1)S(1)} %collective-permute-done.19.refs_0_.refs_4_, bf16[128,2048]{1,0:T(8,128)(2,1)S(1)} %collective-permute-done.20.refs_1_.refs_5_, bf16[4096,512]{1,0:T(8,128)(2,1)S(1)} %copy-done, ...), custom_call_target="tpu_custom_call" | custom-call | flops 1 | bytes 1 | tf_op jit(solution)/shard_map/project_block/pallas_call | solution.py:448
  110.7 3.1 %project_block.15 = bf16[1,2,128,256]{3,2,1,0:T(8,128)(2,1)S(1)} custom-call(s32[3]{0:T(128)S(1)} %add_add_fusion.here, bf16[128,2048]{1,0:T(8,128)(2,1)S(1)} %collective-permute-done.19.refs_0_.refs_4_, bf16[128,2048]{1,0:T(8,128)(2,1)S(1)} %collective-permute-done.20.refs_1_.refs_5_, bf16[4096,512]{1,0:T(8,128)(2,1)S(1)} %copy-done, ...), custom_call_target="tpu_custom_call" | custom-call | flops 1 | bytes 1 | tf_op jit(solution)/shard_map/project_block/pallas_call | solution.py:448
  113.8 5.6 %all-gather.3.cloned.1.call-done = bf16[16384,512]{1,0:T(8,128)(2,1)} async-done(((bf16[4096,512]{1,0:T(8,128)(2,1)}), bf16[16384,512]{1,0:T(8,128)(2,1)}) %all-gather.3.cloned.1.call-update) | async-done | bytes 16777232 | tf_op jit(solution)/shard_map/all_gather | solution.py:327
  119.4 5.5 %project_block.16 = bf16[3,2,128,256]{3,2,1,0:T(8,128)(2,1)} custom-call(s32[3]{0:T(128)S(1)} %add_add_fusion.1.here, bf16[128,2048]{1,0:T(8,128)(2,1)S(1)} %gated_block.2.refs_0_, bf16[128,2048]{1,0:T(8,128)(2,1)S(1)} %gated_block.3.refs_1_, bf16[128,2048]{1,0:T(8,128)(2,1)S(1)} %collective-permute-done.17.refs_0_.refs_2_, ...), custom_call_target="tpu_custom_call" | custom-call | flops 1 | bytes 1 | tf_op jit(solution)/shard_map/project_block/pallas_call | solution.py:448
  127.0 5.0 %project_block.18 = bf16[3,2,128,256]{3,2,1,0:T(8,128)(2,1)S(1)} custom-call(s32[3]{0:T(128)S(1)} %add_add_fusion.here, bf16[128,2048]{1,0:T(8,128)(2,1)S(1)} %gated_block.2.refs_0_, bf16[128,2048]{1,0:T(8,128)(2,1)S(1)} %gated_block.3.refs_1_, bf16[128,2048]{1,0:T(8,128)(2,1)S(1)} %collective-permute-done.17.refs_0_.refs_2_, ...), custom_call_target="tpu_custom_call" | custom-call | flops 1 | bytes 1 | tf_op jit(solution)/shard_map/project_block/pallas_call | solution.py:448
  132.1 4.2 %project_block.19.refs_4_ = f32[2,1,4,128,256]{4,3,2,1,0:T(8,128)S(1)} custom-call(s32[3]{0:T(128)S(1)} %add_add_fusion.2.here, bf16[128,2048]{1,0:T(8,128)(2,1)} %collective-permute-done.26.refs_0_, bf16[4096,512]{1,0:T(8,128)(2,1)S(1)} %copy-done.1, bf16[4096,512]{1,0:T(8,128)(2,1)} %collective-permute-done.16.refs_3_.refs_2_, bf16[4,4096,512]{2,1,0:T(8,128)(2,1)} %bitcast.37), custom_call_target="tpu_custom_call" | custom-call | flops 1 | bytes 1 | tf_op jit(solution)/shard_map/project_block/pallas_call | solution.py:448
  136.3 3.4 %project_block.20 = bf16[1,4,128,256]{3,2,1,0:T(8,128)(2,1)S(1)} custom-call(s32[3]{0:T(128)S(1)} %add_add_fusion.1.here, bf16[128,2048]{1,0:T(8,128)(2,1)} %collective-permute-done.25.refs_0_, bf16[4096,512]{1,0:T(8,128)(2,1)S(1)} %copy-done.1, bf16[4096,512]{1,0:T(8,128)(2,1)} %collective-permute-done.16.refs_3_.refs_2_, bf16[4,4096,512]{2,1,0:T(8,128)(2,1)} %bitcast.38, ...), custom_call_target="tpu_custom_call" | custom-call | flops 1 | bytes 1 | tf_op jit(solution)/shard_map/project_block/pallas_call | solution.py:448
  140.3 3.4 %project_block.21 = bf16[1,4,128,256]{3,2,1,0:T(8,128)(2,1)S(1)} custom-call(s32[3]{0:T(128)S(1)} %add_add_fusion.here, bf16[128,2048]{1,0:T(8,128)(2,1)} %collective-permute-done.25.refs_0_, bf16[4096,512]{1,0:T(8,128)(2,1)S(1)} %copy-done.1, bf16[4096,512]{1,0:T(8,128)(2,1)} %collective-permute-done.16.refs_3_.refs_2_, bf16[4,4096,512]{2,1,0:T(8,128)(2,1)} %bitcast.39, ...), custom_call_target="tpu_custom_call" | custom-call | flops 1 | bytes 1 | tf_op jit(solution)/shard_map/project_block/pallas_call | solution.py:448
  145.9 5.8 %collective-permute-start.27 = (bf16[4,128,256]{2,1,0:T(8,128)(2,1)S(1)}, bf16[4,128,256]{2,1,0:T(8,128)(2,1)S(1)}, u32[]{:S(2)}, u32[]{:S(2)}) collective-permute-start(bf16[4,128,256]{2,1,0:T(8,128)(2,1)S(1)} %get-tuple-element.98), channel_id=1, source_target_pairs={{0,0},{1,24},{2,2},{3,26},{4,4},{5,28},{6,6},{7,30},{8,8},{9,16},{... | collective-permute-start | bytes 786440 | tf_op jit(solution)/shard_map/ppermute | solution.py:494
  157.6 7.6 %collective-permute-start.31 = (bf16[4,128,256]{2,1,0:T(8,128)(2,1)S(1)}, bf16[4,128,256]{2,1,0:T(8,128)(2,1)S(1)}, u32[]{:S(2)}, u32[]{:S(2)}) collective-permute-start(bf16[4,128,256]{2,1,0:T(8,128)(2,1)S(1)} %get-tuple-element.95), channel_id=1, source_target_pairs={{0,8},{1,16},{2,10},{3,18},{4,12},{5,20},{6,14},{7,22},{8,24},{9,0... | collective-permute-start | bytes 786440 | tf_op jit(solution)/shard_map/ppermute | solution.py:494
  165.2 3.9 %collective-permute-done.29.refs_1_ = bf16[4,128,256]{2,1,0:T(8,128)(2,1)S(1)} collective-permute-done((bf16[4,128,256]{2,1,0:T(8,128)(2,1)S(1)}, bf16[4,128,256]{2,1,0:T(8,128)(2,1)S(1)}, u32[]{:S(2)}, u32[]{:S(2)}) %collective-permute-start.29) | collective-permute-done | bytes 262176 | tf_op jit(solution)/shard_map/ppermute | solution.py:494
  169.1 8.7 %collective-permute-done.31.refs_3_ = bf16[4,128,256]{2,1,0:T(8,128)(2,1)S(1)} collective-permute-done((bf16[4,128,256]{2,1,0:T(8,128)(2,1)S(1)}, bf16[4,128,256]{2,1,0:T(8,128)(2,1)S(1)}, u32[]{:S(2)}, u32[]{:S(2)}) %collective-permute-start.31) | collective-permute-done | bytes 262176 | tf_op jit(solution)/shard_map/ppermute | solution.py:494
  (94 shorter events, 57.7 us)
Async XLA Ops:
  6.5 112.8 %all-gather.3.cloned.1.call-start = ((), (), s32[]{:S(2)}) async-start(), calls=%async_computation | async-start | bytes 20971520 | tf_op jit(solution)/shard_map/all_gather | solution.py:327
  7.3 66.0 %collective-permute-start.16 = (bf16[4096,512]{1,0:T(8,128)(2,1)}, bf16[4096,512]{1,0:T(8,128)(2,1)}, u32[]{:S(2)}, u32[]{:S(2)}) collective-permute-start(bf16[4096,512]{1,0:T(8,128)(2,1)} %refs_1_.5), channel_id=1, source_target_pairs={{0,2},{2,0},{4,6},{6,4},{8,10},{10,8},{12,14},{14,12},{16,18},{18,... | collective-permute-start | bytes 12582920 | tf_op jit(solution)/shard_map/ppermute | solution.py:306
  7.4 7.2 %collective-permute-start = (f32[33,256]{1,0:T(8,128)S(1)}, f32[33,256]{1,0:T(8,128)S(1)}, u32[]{:S(2)}, u32[]{:S(2)}) collective-permute-start(f32[33,256]{1,0:T(8,128)S(1)} %get-tuple-element.103), channel_id=1, source_target_pairs={{0,24},{2,26},{4,28},{6,30},{8,0},{10,2},{12,4},{14,6},{16,8},{18,... | collective-permute-start | bytes 101384 | tf_op jit(solution)/shard_map/ppermute | solution.py:309
  11.1 5.8 %collective-permute-start.2 = (f32[33,256]{1,0:T(8,128)S(1)}, f32[33,256]{1,0:T(8,128)S(1)}, u32[]{:S(2)}, u32[]{:S(2)}) collective-permute-start(f32[33,256]{1,0:T(8,128)S(1)} %get-tuple-element.103), channel_id=1, source_target_pairs={{0,8},{2,10},{4,12},{6,14},{8,16},{10,18},{12,20},{14,22},{16,24},... | collective-permute-start | bytes 101384 | tf_op jit(solution)/shard_map/ppermute | solution.py:309
  16.9 9.3 %collective-permute-start.4 = (f32[4,33,256]{2,1,0:T(8,128)S(1)}, f32[4,33,256]{2,1,0:T(8,128)S(1)}, u32[]{:S(2)}, u32[]{:S(2)}) collective-permute-start(f32[4,33,256]{2,1,0:T(8,128)S(1)} %pad_maximum_fusion.3.refs_0_.rates), channel_id=1, source_target_pairs={{0,4},{2,6},{4,0},{6,2},{8,12},{10,14},{12,8},{14,10},{16,20},{18,... | collective-permute-start | bytes 405512 | tf_op jit(solution)/shard_map/ppermute | solution.py:306
  20.0 6.3 %collective-permute-start.5 = (f32[4,33,256]{2,1,0:T(8,128)S(1)}, f32[4,33,256]{2,1,0:T(8,128)S(1)}, u32[]{:S(2)}, u32[]{:S(2)}) collective-permute-start(f32[4,33,256]{2,1,0:T(8,128)S(1)} %pad_maximum_fusion.3.refs_0_.rates), channel_id=1, source_target_pairs={{0,2},{2,0},{4,6},{6,4},{8,10},{10,8},{12,14},{14,12},{16,18},{18,... | collective-permute-start | bytes 405512 | tf_op jit(solution)/shard_map/ppermute | solution.py:306
  30.9 8.3 %collective-permute-start.7 = (bf16[4,16,256]{2,1,0:T(8,128)(2,1)S(1)}, bf16[4,16,256]{2,1,0:T(8,128)(2,1)S(1)}, u32[]{:S(2)}, u32[]{:S(2)}) collective-permute-start(bf16[4,16,256]{2,1,0:T(8,128)(2,1)S(1)} %get-tuple-element.57), channel_id=1, source_target_pairs={{0,2},{2,0},{4,6},{6,4},{8,10},{10,8},{12,14},{14,12},{16,18},{18,... | collective-permute-start | bytes 98312 | tf_op jit(solution)/shard_map/ppermute | solution.py:306
  31.2 8.1 %collective-permute-start.8 = (bf16[4,16,256]{2,1,0:T(8,128)(2,1)S(1)}, bf16[4,16,256]{2,1,0:T(8,128)(2,1)S(1)}, u32[]{:S(2)}, u32[]{:S(2)}) collective-permute-start(bf16[4,16,256]{2,1,0:T(8,128)(2,1)S(1)} %get-tuple-element.58), channel_id=1, source_target_pairs={{0,4},{2,6},{4,0},{6,2},{8,12},{10,14},{12,8},{14,10},{16,20},{18,... | collective-permute-start | bytes 98312 | tf_op jit(solution)/shard_map/ppermute | solution.py:306
  39.9 5.8 %collective-permute-start.10 = (bf16[4,16,256]{2,1,0:T(8,128)(2,1)S(1)}, bf16[4,16,256]{2,1,0:T(8,128)(2,1)S(1)}, u32[]{:S(2)}, u32[]{:S(2)}) collective-permute-start(bf16[4,16,256]{2,1,0:T(8,128)(2,1)S(1)} %slab_states.1), channel_id=1, source_target_pairs={{0,8},{2,10},{4,12},{6,14},{8,16},{10,18},{12,20},{14,22},{16,24},... | collective-permute-start | bytes 98312 | tf_op jit(solution)/shard_map/ppermute | solution.py:309
  57.4 15.7 %collective-permute-start.17 = (bf16[128,2048]{1,0:T(8,128)(2,1)S(1)}, bf16[128,2048]{1,0:T(8,128)(2,1)S(1)}, u32[]{:S(2)}, u32[]{:S(2)}) collective-permute-start(bf16[128,2048]{1,0:T(8,128)(2,1)S(1)} %gated_block.2.refs_0_), channel_id=1, source_target_pairs={{0,8},{2,10},{4,12},{6,14},{8,24},{10,26},{12,28},{14,30},{16,0},{... | collective-permute-start | bytes 1572872 | tf_op jit(solution)/shard_map/ppermute | solution.py:316
  60.8 23.6 %collective-permute-start.18 = (bf16[128,2048]{1,0:T(8,128)(2,1)S(1)}, bf16[128,2048]{1,0:T(8,128)(2,1)S(1)}, u32[]{:S(2)}, u32[]{:S(2)}) collective-permute-start(bf16[128,2048]{1,0:T(8,128)(2,1)S(1)} %gated_block.3.refs_1_), channel_id=1, source_target_pairs={{0,8},{2,10},{4,12},{6,14},{8,24},{10,26},{12,28},{14,30},{16,0},{... | collective-permute-start | bytes 1572872 | tf_op jit(solution)/shard_map/ppermute | solution.py:316
  73.1 22.5 %collective-permute-start.19 = (bf16[128,2048]{1,0:T(8,128)(2,1)S(1)}, bf16[128,2048]{1,0:T(8,128)(2,1)S(1)}, u32[]{:S(2)}, u32[]{:S(2)}) collective-permute-start(bf16[128,2048]{1,0:T(8,128)(2,1)S(1)} %collective-permute-done.17.refs_0_.refs_2_), channel_id=1, source_target_pairs={{0,8},{2,10},{4,12},{6,14},{8,24},{10,26},{12,28},{14,30},{16,0},{... | collective-permute-start | bytes 1572872 | tf_op jit(solution)/shard_map/ppermute | solution.py:316
  84.3 22.5 %collective-permute-start.20 = (bf16[128,2048]{1,0:T(8,128)(2,1)S(1)}, bf16[128,2048]{1,0:T(8,128)(2,1)S(1)}, u32[]{:S(2)}, u32[]{:S(2)}) collective-permute-start(bf16[128,2048]{1,0:T(8,128)(2,1)S(1)} %collective-permute-done.18.refs_1_.refs_3_), channel_id=1, source_target_pairs={{0,8},{2,10},{4,12},{6,14},{8,24},{10,26},{12,28},{14,30},{16,0},{... | collective-permute-start | bytes 1572872 | tf_op jit(solution)/shard_map/ppermute | solution.py:316
  85.1 14.4 %collective-permute-start.23 = (bf16[1,2,128,256]{3,2,1,0:T(8,128)(2,1)S(1)}, bf16[1,2,128,256]{3,2,1,0:T(8,128)(2,1)S(1)}, u32[]{:S(2)}, u32[]{:S(2)}) collective-permute-start(bf16[1,2,128,256]{3,2,1,0:T(8,128)(2,1)S(1)} %project_block.11), channel_id=1, source_target_pairs={{0,1},{1,0},{2,3},{3,2},{4,5},{5,4},{6,7},{7,6},{8,9},{9,8},{10,11... | collective-permute-start | bytes 393224 | tf_op jit(solution)/shard_map/ppermute | solution.py:475
  95.6 36.4 %collective-permute-start.26 = (bf16[128,2048]{1,0:T(8,128)(2,1)S(1)}, bf16[128,2048]{1,0:T(8,128)(2,1)}, u32[]{:S(2)}, u32[]{:S(2)}) collective-permute-start(bf16[128,2048]{1,0:T(8,128)(2,1)S(1)} %collective-permute-done.19.refs_0_.refs_4_), channel_id=1, source_target_pairs={{0,8},{2,10},{4,12},{6,14},{8,24},{10,26},{12,28},{14,30},{16,0},{... | collective-permute-start | bytes 1572872 | tf_op jit(solution)/shard_map/ppermute | solution.py:316
  98.8 11.9 %collective-permute-start.21 = (bf16[1,2,128,256]{3,2,1,0:T(8,128)(2,1)S(1)}, bf16[1,2,128,256]{3,2,1,0:T(8,128)(2,1)}, u32[]{:S(2)}, u32[]{:S(2)}) collective-permute-start(bf16[1,2,128,256]{3,2,1,0:T(8,128)(2,1)S(1)} %project_block.14), channel_id=1, source_target_pairs={{0,1},{1,0},{2,3},{3,2},{4,5},{5,4},{6,7},{7,6},{8,9},{9,8},{10,11... | collective-permute-start | bytes 393224 | tf_op jit(solution)/shard_map/ppermute | solution.py:475
  106.8 29.5 %collective-permute-start.25 = (bf16[128,2048]{1,0:T(8,128)(2,1)S(1)}, bf16[128,2048]{1,0:T(8,128)(2,1)}, u32[]{:S(2)}, u32[]{:S(2)}) collective-permute-start(bf16[128,2048]{1,0:T(8,128)(2,1)S(1)} %collective-permute-done.20.refs_1_.refs_5_), channel_id=1, source_target_pairs={{0,8},{2,10},{4,12},{6,14},{8,24},{10,26},{12,28},{14,30},{16,0},{... | collective-permute-start | bytes 1572872 | tf_op jit(solution)/shard_map/ppermute | solution.py:316
  124.9 18.8 %collective-permute-start.22 = (bf16[3,2,128,256]{3,2,1,0:T(8,128)(2,1)}, bf16[3,2,128,256]{3,2,1,0:T(8,128)(2,1)}, u32[]{:S(2)}, u32[]{:S(2)}) collective-permute-start(bf16[3,2,128,256]{3,2,1,0:T(8,128)(2,1)} %project_block.16), channel_id=1, source_target_pairs={{0,1},{1,0},{2,3},{3,2},{4,5},{5,4},{6,7},{7,6},{8,9},{9,8},{10,11... | collective-permute-start | bytes 1179656 | tf_op jit(solution)/shard_map/ppermute | solution.py:475
  125.4 18.2 %collective-permute-start.24 = (bf16[1,2,128,256]{3,2,1,0:T(8,128)(2,1)}, bf16[1,2,128,256]{3,2,1,0:T(8,128)(2,1)}, u32[]{:S(2)}, u32[]{:S(2)}) collective-permute-start(bf16[1,2,128,256]{3,2,1,0:T(8,128)(2,1)} %project_block.13), channel_id=1, source_target_pairs={{0,1},{1,0},{2,3},{3,2},{4,5},{5,4},{6,7},{7,6},{8,9},{9,8},{10,11... | collective-permute-start | bytes 393224 | tf_op jit(solution)/shard_map/ppermute | solution.py:475
  139.7 14.9 %collective-permute-start.28 = (bf16[1,4,128,256]{3,2,1,0:T(8,128)(2,1)S(1)}, bf16[1,4,128,256]{3,2,1,0:T(8,128)(2,1)S(1)}, u32[]{:S(2)}, u32[]{:S(2)}) collective-permute-start(bf16[1,4,128,256]{3,2,1,0:T(8,128)(2,1)S(1)} %project_block.20), channel_id=1, source_target_pairs={{0,1},{1,0},{2,3},{3,2},{4,5},{5,4},{6,7},{7,6},{8,9},{9,8},{10,11... | collective-permute-start | bytes 786440 | tf_op jit(solution)/shard_map/ppermute | solution.py:523
  145.9 11.5 %collective-permute-start.27 = (bf16[4,128,256]{2,1,0:T(8,128)(2,1)S(1)}, bf16[4,128,256]{2,1,0:T(8,128)(2,1)S(1)}, u32[]{:S(2)}, u32[]{:S(2)}) collective-permute-start(bf16[4,128,256]{2,1,0:T(8,128)(2,1)S(1)} %get-tuple-element.98), channel_id=1, source_target_pairs={{0,0},{1,24},{2,2},{3,26},{4,4},{5,28},{6,6},{7,30},{8,8},{9,16},{... | collective-permute-start | bytes 786440 | tf_op jit(solution)/shard_map/ppermute | solution.py:494
  151.7 13.6 %collective-permute-start.30 = (bf16[4,128,256]{2,1,0:T(8,128)(2,1)S(1)}, bf16[4,128,256]{2,1,0:T(8,128)(2,1)S(1)}, u32[]{:S(2)}, u32[]{:S(2)}) collective-permute-start(bf16[4,128,256]{2,1,0:T(8,128)(2,1)S(1)} %get-tuple-element.97), channel_id=1, source_target_pairs={{0,24},{1,0},{2,26},{3,2},{4,28},{5,4},{6,30},{7,6},{8,16},{9,8},{... | collective-permute-start | bytes 786440 | tf_op jit(solution)/shard_map/ppermute | solution.py:494
  157.5 11.6 %collective-permute-start.29 = (bf16[4,128,256]{2,1,0:T(8,128)(2,1)S(1)}, bf16[4,128,256]{2,1,0:T(8,128)(2,1)S(1)}, u32[]{:S(2)}, u32[]{:S(2)}) collective-permute-start(bf16[4,128,256]{2,1,0:T(8,128)(2,1)S(1)} %get-tuple-element.96), channel_id=1, source_target_pairs={{0,16},{1,8},{2,18},{3,10},{4,20},{5,12},{6,22},{7,14},{8,0},{9,24... | collective-permute-start | bytes 786440 | tf_op jit(solution)/shard_map/ppermute | solution.py:494
  157.6 20.2 %collective-permute-start.31 = (bf16[4,128,256]{2,1,0:T(8,128)(2,1)S(1)}, bf16[4,128,256]{2,1,0:T(8,128)(2,1)S(1)}, u32[]{:S(2)}, u32[]{:S(2)}) collective-permute-start(bf16[4,128,256]{2,1,0:T(8,128)(2,1)S(1)} %get-tuple-element.95), channel_id=1, source_target_pairs={{0,8},{1,16},{2,10},{3,18},{4,12},{5,20},{6,14},{7,22},{8,24},{9,0... | collective-permute-start | bytes 786440 | tf_op jit(solution)/shard_map/ppermute | solution.py:494
  (18 other events, 72.4 us)
Sparse Core Ops, SparseCore 0:
  8.9 110.4 all-gather.2

commit v10 on v6

--- a/solution.py
+++ b/solution.py
@@ -526,7 +526,7 @@
     sums = [jnp.concatenate(parts) for parts in zip(near_sums, total(batch_mine, batch_got))]
     late = ((slabs - 1) % (slabs // tp), slabs - 1)
     arrived = {by: [deliver(sums, by)] for by in range(slabs) if by not in late}
-    tail, _ = lax.optimization_barrier((tail, (last_away, arrived[0])))
+    tail, _ = lax.optimization_barrier((tail, last_away))
     last_mine = project([[None, tail]], sources, both, tp_me, partial, (1,))
     sums.append(total(last_mine, last_got)[0])
     for by in late:

time: 186 us -> 184 us (0.989)
  the two profiles are of different devices: /device:TPU:4 before, /device:TPU:13 now
where the time goes in v10:
time: 184 us; the launch traced here: 183 us
  Pallas kernels  60.5 us (33%)
  waiting for transfers between devices  55 us (30%)
  starting transfers between devices  44.7 us (24%)
  between operations  13.8 us (8%)
  local copies, waits for them, and re-layouts  5.81 us (3%)
  other arithmetic  3.55 us (2%)
    pallas_call x11, Pallas kernels, project(): pl.pallas_call(functools.partial(project_kernel, len(blocks), picks, halv...  40.5 us
    ppermute x6, waiting for transfers between devices, ring(): return lax.ppermute(array, 'ctx', pairs)  18.4 us
    ppermute x4, waiting for transfers between devices, deliver(): return lax.ppermute(moved, ('ctx', 'tp'), pairs)  18.4 us
    ppermute x6, starting transfers between devices, ring(): return lax.ppermute(array, 'ctx', pairs)  14.6 us
    ppermute x10, starting transfers between devices, within_slab(): return lax.ppermute(array, 'ctx', [(i, i ^ mask) for i in range(ctx)])  10.1 us
    ppermute x4, starting transfers between devices, deliver(): return lax.ppermute(moved, ('ctx', 'tp'), pairs)  7.37 us
    ppermute x6, starting transfers between devices, from_slab(): lax.ppermute(array, 'ctx', [(i, (i - by * SLAB) % ctx) for i in range(ctx)])  6.24 us
    all_gather x1, waiting for transfers between devices, per_device(): lax.all_gather(out_weight, 'ctx', axis_index_groups=[list(range(z * SLAB,...  5.7 us
  transfers between devices with their start and end apart: 33, of which 15 were waited for; matrix products, arithmetic and copies ran while one was open for 2% of the time, Pallas kernels for 32%

profile of v10, /device:TPU:13, one launch (start us, length us, event | category | flops | bytes accessed | tf_op | source)
XLA Modules:
  0.0 183.3 jit_solution(6008518575328194032)
XLA Ops:
  13.7 3.9 %collective-permute-start.3 = (bf16[3,2,4096]{2,1,0:T(2,128)(2,1)S(1)}, bf16[3,2,4096]{2,1,0:T(2,128)(2,1)S(1)}, u32[]{:S(2)}, u32[]{:S(2)}) collective-permute-start(bf16[3,2,4096]{2,1,0:T(2,128)(2,1)S(1)} %slice.3), channel_id=1, source_target_pairs={{0,2},{2,4},{4,6},{6,8},{8,10},{10,12},{12,14},{14,16},{16,18},{18... | collective-permute-start | bytes 147464 | tf_op jit(solution)/shard_map/ppermute | solution.py:318
  24.1 3.3 %short_filters.1 = (f32[4,128,8,128]{3,2,1,0:T(8,128)S(1)}, f32[4,128,8,128]{3,2,1,0:T(8,128)S(1)}) custom-call(s32[3]{0:T(128)S(1)} %pad_add_fusion.here, bf16[3,128,4096]{2,1,0:T(8,128)(2,1)S(1)} %copy-done.2, bf16[3,2,4096]{2,1,0:T(2,128)(2,1)S(1)} %collective-permute-done.3.halo, f32[3,3,8192]{2,1,0:T(4,128)S(1)} %copy-done.3), custom_call_target="tpu_custom_call" | custom-call | flops 1 | bytes 1 | tf_op jit(solution)/shard_map/short_filters/pallas_call | solution.py:362
  30.6 3.1 %block_states.1 = (bf16[4,16,256]{2,1,0:T(8,128)(2,1)S(1)}, bf16[4,16,256]{2,1,0:T(8,128)(2,1)S(1)}, bf16[4,16,256]{2,1,0:T(8,128)(2,1)S(1)}, bf16[4,16,256]{2,1,0:T(8,128)(2,1)S(1)}) custom-call(s32[3]{0:T(128)S(1)} %pad_add_fusion.here, f32[4,128,8,128]{3,2,1,0:T(8,128)S(1)} %get-tuple-element.53.u_ref, f32[4,33,256]{2,1,0:T(8,128)S(1)} %pad_maximum_fusion.3.refs_0_.rates, ...), custom_call_target="tpu_custom_call" | custom-call | flops 1 | bytes 1 | tf_op jit(solution)/shard_map/block_states/pallas_call | solution.py:378
  35.9 5.6 %local_convolution.1.y_ref = f32[4,128,8,128]{3,2,1,0:T(8,128)S(1)} custom-call(s32[3]{0:T(128)S(1)} %pad_add_fusion.here, f32[4,128,8,128]{3,2,1,0:T(8,128)S(1)} %get-tuple-element.53.u_ref, f32[4,33,256]{2,1,0:T(8,128)S(1)} %pad_maximum_fusion.3.refs_0_.rates, f32[4,33,256]{2,1,0:T(8,128)S(1)} %collective-permute-done.5.refs_1_, ...), custom_call_target="tpu_custom_call" | custom-call | flops 1 | bytes 1 | tf_op jit(solution)/shard_map/local_convolution/pallas_call | solution.py:388
  62.6 8.9 %collective-permute-done.17.refs_0_.refs_2_ = bf16[128,2048]{1,0:T(8,128)(2,1)S(1)} collective-permute-done((bf16[128,2048]{1,0:T(8,128)(2,1)S(1)}, bf16[128,2048]{1,0:T(8,128)(2,1)S(1)}, u32[]{:S(2)}, u32[]{:S(2)}) %collective-permute-start.17) | collective-permute-done | bytes 524320 | tf_op jit(solution)/shard_map/ppermute | solution.py:316
  71.5 3.1 %collective-permute-start.19 = (bf16[128,2048]{1,0:T(8,128)(2,1)S(1)}, bf16[128,2048]{1,0:T(8,128)(2,1)S(1)}, u32[]{:S(2)}, u32[]{:S(2)}) collective-permute-start(bf16[128,2048]{1,0:T(8,128)(2,1)S(1)} %collective-permute-done.17.refs_0_.refs_2_), channel_id=1, source_target_pairs={{0,8},{2,10},{4,12},{6,14},{8,24},{10,26},{12,28},{14,30},{16,0},{... | collective-permute-start | bytes 1572872 | tf_op jit(solution)/shard_map/ppermute | solution.py:316
  76.8 3.1 %project_block.11 = bf16[1,2,128,256]{3,2,1,0:T(8,128)(2,1)S(1)} custom-call(s32[3]{0:T(128)S(1)} %add_add_fusion.1.here, bf16[128,2048]{1,0:T(8,128)(2,1)S(1)} %gated_block.2.refs_0_, bf16[128,2048]{1,0:T(8,128)(2,1)S(1)} %gated_block.3.refs_1_, bf16[4096,512]{1,0:T(8,128)(2,1)S(1)} %copy-done, bf16[4096,512]{1,0:T(8,128)(2,1)} %collective-permute-done.16.refs_3_.refs_2_), custom_call_target="tpu_custom_call" | custom-call | flops 1 | bytes 1 | tf_op jit(solution)/shard_map/project_block/pallas_call | solution.py:448
  79.9 3.1 %project_block.12 = bf16[1,2,128,256]{3,2,1,0:T(8,128)(2,1)S(1)} custom-call(s32[3]{0:T(128)S(1)} %add_add_fusion.here, bf16[128,2048]{1,0:T(8,128)(2,1)S(1)} %gated_block.2.refs_0_, bf16[128,2048]{1,0:T(8,128)(2,1)S(1)} %gated_block.3.refs_1_, bf16[4096,512]{1,0:T(8,128)(2,1)S(1)} %copy-done, bf16[4096,512]{1,0:T(8,128)(2,1)} %collective-permute-done.16.refs_3_.refs_2_), custom_call_target="tpu_custom_call" | custom-call | flops 1 | bytes 1 | tf_op jit(solution)/shard_map/project_block/pallas_call | solution.py:448
  86.1 7.9 %collective-permute-done.19.refs_0_.refs_4_ = bf16[128,2048]{1,0:T(8,128)(2,1)S(1)} collective-permute-done((bf16[128,2048]{1,0:T(8,128)(2,1)S(1)}, bf16[128,2048]{1,0:T(8,128)(2,1)S(1)}, u32[]{:S(2)}, u32[]{:S(2)}) %collective-permute-start.19) | collective-permute-done | bytes 524320 | tf_op jit(solution)/shard_map/ppermute | solution.py:316
  94.0 3.1 %collective-permute-start.26 = (bf16[128,2048]{1,0:T(8,128)(2,1)S(1)}, bf16[128,2048]{1,0:T(8,128)(2,1)}, u32[]{:S(2)}, u32[]{:S(2)}) collective-permute-start(bf16[128,2048]{1,0:T(8,128)(2,1)S(1)} %collective-permute-done.19.refs_0_.refs_4_), channel_id=1, source_target_pairs={{0,8},{2,10},{4,12},{6,14},{8,24},{10,26},{12,28},{14,30},{16,0},{... | collective-permute-start | bytes 1572872 | tf_op jit(solution)/shard_map/ppermute | solution.py:316
  100.5 3.1 %project_block.17 = bf16[1,2,128,256]{3,2,1,0:T(8,128)(2,1)S(1)} custom-call(s32[3]{0:T(128)S(1)} %add_add_fusion.here, bf16[128,2048]{1,0:T(8,128)(2,1)S(1)} %collective-permute-done.17.refs_0_.refs_2_, bf16[128,2048]{1,0:T(8,128)(2,1)S(1)} %collective-permute-done.18.refs_1_.refs_3_, bf16[4096,512]{1,0:T(8,128)(2,1)S(1)} %copy-done, ...), custom_call_target="tpu_custom_call" | custom-call | flops 1 | bytes 1 | tf_op jit(solution)/shard_map/project_block/pallas_call | solution.py:448
  105.2 3.1 %collective-permute-start.25 = (bf16[128,2048]{1,0:T(8,128)(2,1)S(1)}, bf16[128,2048]{1,0:T(8,128)(2,1)}, u32[]{:S(2)}, u32[]{:S(2)}) collective-permute-start(bf16[128,2048]{1,0:T(8,128)(2,1)S(1)} %collective-permute-done.20.refs_1_.refs_5_), channel_id=1, source_target_pairs={{0,8},{2,10},{4,12},{6,14},{8,24},{10,26},{12,28},{14,30},{16,0},{... | collective-permute-start | bytes 1572872 | tf_op jit(solution)/shard_map/ppermute | solution.py:316
  108.3 3.7 %project_block.13 = bf16[1,2,128,256]{3,2,1,0:T(8,128)(2,1)} custom-call(s32[3]{0:T(128)S(1)} %add_add_fusion.1.here, bf16[128,2048]{1,0:T(8,128)(2,1)S(1)} %collective-permute-done.19.refs_0_.refs_4_, bf16[128,2048]{1,0:T(8,128)(2,1)S(1)} %collective-permute-done.20.refs_1_.refs_5_, bf16[4096,512]{1,0:T(8,128)(2,1)S(1)} %copy-done, ...), custom_call_target="tpu_custom_call" | custom-call | flops 1 | bytes 1 | tf_op jit(solution)/shard_map/project_block/pallas_call | solution.py:448
  112.1 3.1 %project_block.15 = bf16[1,2,128,256]{3,2,1,0:T(8,128)(2,1)S(1)} custom-call(s32[3]{0:T(128)S(1)} %add_add_fusion.here, bf16[128,2048]{1,0:T(8,128)(2,1)S(1)} %collective-permute-done.19.refs_0_.refs_4_, bf16[128,2048]{1,0:T(8,128)(2,1)S(1)} %collective-permute-done.20.refs_1_.refs_5_, bf16[4096,512]{1,0:T(8,128)(2,1)S(1)} %copy-done, ...), custom_call_target="tpu_custom_call" | custom-call | flops 1 | bytes 1 | tf_op jit(solution)/shard_map/project_block/pallas_call | solution.py:448
  115.2 5.7 %all-gather.3.cloned.1.call-done = bf16[16384,512]{1,0:T(8,128)(2,1)} async-done(((bf16[4096,512]{1,0:T(8,128)(2,1)}), bf16[16384,512]{1,0:T(8,128)(2,1)}) %all-gather.3.cloned.1.call-update) | async-done | bytes 16777232 | tf_op jit(solution)/shard_map/all_gather | solution.py:327
  120.9 5.5 %project_block.16 = bf16[3,2,128,256]{3,2,1,0:T(8,128)(2,1)} custom-call(s32[3]{0:T(128)S(1)} %add_add_fusion.1.here, bf16[128,2048]{1,0:T(8,128)(2,1)S(1)} %gated_block.2.refs_0_, bf16[128,2048]{1,0:T(8,128)(2,1)S(1)} %gated_block.3.refs_1_, bf16[128,2048]{1,0:T(8,128)(2,1)S(1)} %collective-permute-done.17.refs_0_.refs_2_, ...), custom_call_target="tpu_custom_call" | custom-call | flops 1 | bytes 1 | tf_op jit(solution)/shard_map/project_block/pallas_call | solution.py:448
  127.9 5.0 %project_block.18 = bf16[3,2,128,256]{3,2,1,0:T(8,128)(2,1)S(1)} custom-call(s32[3]{0:T(128)S(1)} %add_add_fusion.here, bf16[128,2048]{1,0:T(8,128)(2,1)S(1)} %gated_block.2.refs_0_, bf16[128,2048]{1,0:T(8,128)(2,1)S(1)} %gated_block.3.refs_1_, bf16[128,2048]{1,0:T(8,128)(2,1)S(1)} %collective-permute-done.17.refs_0_.refs_2_, ...), custom_call_target="tpu_custom_call" | custom-call | flops 1 | bytes 1 | tf_op jit(solution)/shard_map/project_block/pallas_call | solution.py:448
  133.0 4.2 %project_block.19.refs_4_ = f32[2,1,4,128,256]{4,3,2,1,0:T(8,128)S(1)} custom-call(s32[3]{0:T(128)S(1)} %add_add_fusion.2.here, bf16[128,2048]{1,0:T(8,128)(2,1)} %collective-permute-done.26.refs_0_, bf16[4096,512]{1,0:T(8,128)(2,1)S(1)} %copy-done.1, bf16[4096,512]{1,0:T(8,128)(2,1)} %collective-permute-done.16.refs_3_.refs_2_, bf16[4,4096,512]{2,1,0:T(8,128)(2,1)} %bitcast.37), custom_call_target="tpu_custom_call" | custom-call | flops 1 | bytes 1 | tf_op jit(solution)/shard_map/project_block/pallas_call | solution.py:448
  137.2 3.4 %project_block.20 = bf16[1,4,128,256]{3,2,1,0:T(8,128)(2,1)S(1)} custom-call(s32[3]{0:T(128)S(1)} %add_add_fusion.1.here, bf16[128,2048]{1,0:T(8,128)(2,1)} %collective-permute-done.25.refs_0_, bf16[4096,512]{1,0:T(8,128)(2,1)S(1)} %copy-done.1, bf16[4096,512]{1,0:T(8,128)(2,1)} %collective-permute-done.16.refs_3_.refs_2_, bf16[4,4096,512]{2,1,0:T(8,128)(2,1)} %bitcast.38, ...), custom_call_target="tpu_custom_call" | custom-call | flops 1 | bytes 1 | tf_op jit(solution)/shard_map/project_block/pallas_call | solution.py:448
  140.9 3.4 %project_block.21 = bf16[1,4,128,256]{3,2,1,0:T(8,128)(2,1)S(1)} custom-call(s32[3]{0:T(128)S(1)} %add_add_fusion.here, bf16[128,2048]{1,0:T(8,128)(2,1)} %collective-permute-done.25.refs_0_, bf16[4096,512]{1,0:T(8,128)(2,1)S(1)} %copy-done.1, bf16[4096,512]{1,0:T(8,128)(2,1)} %collective-permute-done.16.refs_3_.refs_2_, bf16[4,4096,512]{2,1,0:T(8,128)(2,1)} %bitcast.39, ...), custom_call_target="tpu_custom_call" | custom-call | flops 1 | bytes 1 | tf_op jit(solution)/shard_map/project_block/pallas_call | solution.py:448
  149.7 4.6 %collective-permute-start.27 = (bf16[4,128,256]{2,1,0:T(8,128)(2,1)S(1)}, bf16[4,128,256]{2,1,0:T(8,128)(2,1)S(1)}, u32[]{:S(2)}, u32[]{:S(2)}) collective-permute-start(bf16[4,128,256]{2,1,0:T(8,128)(2,1)S(1)} %get-tuple-element.96), channel_id=1, source_target_pairs={{0,0},{1,24},{2,2},{3,26},{4,4},{5,28},{6,6},{7,30},{8,8},{9,16},{... | collective-permute-start | bytes 786440 | tf_op jit(solution)/shard_map/ppermute | solution.py:494
  156.4 3.6 %collective-permute-done.31.refs_3_ = bf16[4,128,256]{2,1,0:T(8,128)(2,1)S(1)} collective-permute-done((bf16[4,128,256]{2,1,0:T(8,128)(2,1)S(1)}, bf16[4,128,256]{2,1,0:T(8,128)(2,1)S(1)}, u32[]{:S(2)}, u32[]{:S(2)}) %collective-permute-start.31) | collective-permute-done | bytes 262176 | tf_op jit(solution)/shard_map/ppermute | solution.py:494
  160.0 10.8 %collective-permute-done.27.refs_0_ = bf16[4,128,256]{2,1,0:T(8,128)(2,1)S(1)} collective-permute-done((bf16[4,128,256]{2,1,0:T(8,128)(2,1)S(1)}, bf16[4,128,256]{2,1,0:T(8,128)(2,1)S(1)}, u32[]{:S(2)}, u32[]{:S(2)}) %collective-permute-start.27) | collective-permute-done | bytes 262176 | tf_op jit(solution)/shard_map/ppermute | solution.py:494
  170.8 4.0 %collective-permute-done.30.refs_2_ = bf16[4,128,256]{2,1,0:T(8,128)(2,1)S(1)} collective-permute-done((bf16[4,128,256]{2,1,0:T(8,128)(2,1)S(1)}, bf16[4,128,256]{2,1,0:T(8,128)(2,1)S(1)}, u32[]{:S(2)}, u32[]{:S(2)}) %collective-permute-start.30) | collective-permute-done | bytes 262176 | tf_op jit(solution)/shard_map/ppermute | solution.py:494
  (94 shorter events, 61.5 us)
Async XLA Ops:
  6.5 114.3 %all-gather.3.cloned.1.call-start = ((), (), s32[]{:S(2)}) async-start(), calls=%async_computation | async-start | bytes 20971520 | tf_op jit(solution)/shard_map/all_gather | solution.py:327
  7.3 67.4 %collective-permute-start.16 = (bf16[4096,512]{1,0:T(8,128)(2,1)}, bf16[4096,512]{1,0:T(8,128)(2,1)}, u32[]{:S(2)}, u32[]{:S(2)}) collective-permute-start(bf16[4096,512]{1,0:T(8,128)(2,1)} %refs_1_.5), channel_id=1, source_target_pairs={{0,2},{2,0},{4,6},{6,4},{8,10},{10,8},{12,14},{14,12},{16,18},{18,... | collective-permute-start | bytes 12582920 | tf_op jit(solution)/shard_map/ppermute | solution.py:306
  8.0 9.6 %collective-permute-start = (f32[33,256]{1,0:T(8,128)S(1)}, f32[33,256]{1,0:T(8,128)S(1)}, u32[]{:S(2)}, u32[]{:S(2)}) collective-permute-start(f32[33,256]{1,0:T(8,128)S(1)} %get-tuple-element.101), channel_id=1, source_target_pairs={{0,24},{2,26},{4,28},{6,30},{8,0},{10,2},{12,4},{14,6},{16,8},{18,... | collective-permute-start | bytes 101384 | tf_op jit(solution)/shard_map/ppermute | solution.py:309
  8.3 9.4 %collective-permute-start.1 = (f32[33,256]{1,0:T(8,128)S(1)}, f32[33,256]{1,0:T(8,128)S(1)}, u32[]{:S(2)}, u32[]{:S(2)}) collective-permute-start(f32[33,256]{1,0:T(8,128)S(1)} %get-tuple-element.101), channel_id=1, source_target_pairs={{0,16},{2,18},{4,20},{6,22},{8,24},{10,26},{12,28},{14,30},{16,0},... | collective-permute-start | bytes 101384 | tf_op jit(solution)/shard_map/ppermute | solution.py:309
  10.6 7.1 %collective-permute-start.2 = (f32[33,256]{1,0:T(8,128)S(1)}, f32[33,256]{1,0:T(8,128)S(1)}, u32[]{:S(2)}, u32[]{:S(2)}) collective-permute-start(f32[33,256]{1,0:T(8,128)S(1)} %get-tuple-element.101), channel_id=1, source_target_pairs={{0,8},{2,10},{4,12},{6,14},{8,16},{10,18},{12,20},{14,22},{16,24},... | collective-permute-start | bytes 101384 | tf_op jit(solution)/shard_map/ppermute | solution.py:309
  18.8 8.6 %collective-permute-start.4 = (f32[4,33,256]{2,1,0:T(8,128)S(1)}, f32[4,33,256]{2,1,0:T(8,128)S(1)}, u32[]{:S(2)}, u32[]{:S(2)}) collective-permute-start(f32[4,33,256]{2,1,0:T(8,128)S(1)} %pad_maximum_fusion.3.refs_0_.rates), channel_id=1, source_target_pairs={{0,4},{2,6},{4,0},{6,2},{8,12},{10,14},{12,8},{14,10},{16,20},{18,... | collective-permute-start | bytes 405512 | tf_op jit(solution)/shard_map/ppermute | solution.py:306
  18.9 10.6 %collective-permute-start.5 = (f32[4,33,256]{2,1,0:T(8,128)S(1)}, f32[4,33,256]{2,1,0:T(8,128)S(1)}, u32[]{:S(2)}, u32[]{:S(2)}) collective-permute-start(f32[4,33,256]{2,1,0:T(8,128)S(1)} %pad_maximum_fusion.3.refs_0_.rates), channel_id=1, source_target_pairs={{0,2},{2,0},{4,6},{6,4},{8,10},{10,8},{12,14},{14,12},{16,18},{18,... | collective-permute-start | bytes 405512 | tf_op jit(solution)/shard_map/ppermute | solution.py:306
  33.7 7.8 %collective-permute-start.7 = (bf16[4,16,256]{2,1,0:T(8,128)(2,1)S(1)}, bf16[4,16,256]{2,1,0:T(8,128)(2,1)S(1)}, u32[]{:S(2)}, u32[]{:S(2)}) collective-permute-start(bf16[4,16,256]{2,1,0:T(8,128)(2,1)S(1)} %get-tuple-element.56), channel_id=1, source_target_pairs={{0,2},{2,0},{4,6},{6,4},{8,10},{10,8},{12,14},{14,12},{16,18},{18,... | collective-permute-start | bytes 98312 | tf_op jit(solution)/shard_map/ppermute | solution.py:306
  34.1 7.4 %collective-permute-start.8 = (bf16[4,16,256]{2,1,0:T(8,128)(2,1)S(1)}, bf16[4,16,256]{2,1,0:T(8,128)(2,1)S(1)}, u32[]{:S(2)}, u32[]{:S(2)}) collective-permute-start(bf16[4,16,256]{2,1,0:T(8,128)(2,1)S(1)} %get-tuple-element.57), channel_id=1, source_target_pairs={{0,4},{2,6},{4,0},{6,2},{8,12},{10,14},{12,8},{14,10},{16,20},{18,... | collective-permute-start | bytes 98312 | tf_op jit(solution)/shard_map/ppermute | solution.py:306
  57.7 13.9 %collective-permute-start.17 = (bf16[128,2048]{1,0:T(8,128)(2,1)S(1)}, bf16[128,2048]{1,0:T(8,128)(2,1)S(1)}, u32[]{:S(2)}, u32[]{:S(2)}) collective-permute-start(bf16[128,2048]{1,0:T(8,128)(2,1)S(1)} %gated_block.2.refs_0_), channel_id=1, source_target_pairs={{0,8},{2,10},{4,12},{6,14},{8,24},{10,26},{12,28},{14,30},{16,0},{... | collective-permute-start | bytes 1572872 | tf_op jit(solution)/shard_map/ppermute | solution.py:316
  62.4 20.6 %collective-permute-start.18 = (bf16[128,2048]{1,0:T(8,128)(2,1)S(1)}, bf16[128,2048]{1,0:T(8,128)(2,1)S(1)}, u32[]{:S(2)}, u32[]{:S(2)}) collective-permute-start(bf16[128,2048]{1,0:T(8,128)(2,1)S(1)} %gated_block.3.refs_1_), channel_id=1, source_target_pairs={{0,8},{2,10},{4,12},{6,14},{8,24},{10,26},{12,28},{14,30},{16,0},{... | collective-permute-start | bytes 1572872 | tf_op jit(solution)/shard_map/ppermute | solution.py:316
  71.5 22.5 %collective-permute-start.19 = (bf16[128,2048]{1,0:T(8,128)(2,1)S(1)}, bf16[128,2048]{1,0:T(8,128)(2,1)S(1)}, u32[]{:S(2)}, u32[]{:S(2)}) collective-permute-start(bf16[128,2048]{1,0:T(8,128)(2,1)S(1)} %collective-permute-done.17.refs_0_.refs_2_), channel_id=1, source_target_pairs={{0,8},{2,10},{4,12},{6,14},{8,24},{10,26},{12,28},{14,30},{16,0},{... | collective-permute-start | bytes 1572872 | tf_op jit(solution)/shard_map/ppermute | solution.py:316
  83.0 22.2 %collective-permute-start.20 = (bf16[128,2048]{1,0:T(8,128)(2,1)S(1)}, bf16[128,2048]{1,0:T(8,128)(2,1)S(1)}, u32[]{:S(2)}, u32[]{:S(2)}) collective-permute-start(bf16[128,2048]{1,0:T(8,128)(2,1)S(1)} %collective-permute-done.18.refs_1_.refs_3_), channel_id=1, source_target_pairs={{0,8},{2,10},{4,12},{6,14},{8,24},{10,26},{12,28},{14,30},{16,0},{... | collective-permute-start | bytes 1572872 | tf_op jit(solution)/shard_map/ppermute | solution.py:316
  85.9 14.7 %collective-permute-start.23 = (bf16[1,2,128,256]{3,2,1,0:T(8,128)(2,1)S(1)}, bf16[1,2,128,256]{3,2,1,0:T(8,128)(2,1)S(1)}, u32[]{:S(2)}, u32[]{:S(2)}) collective-permute-start(bf16[1,2,128,256]{3,2,1,0:T(8,128)(2,1)S(1)} %project_block.11), channel_id=1, source_target_pairs={{0,1},{1,0},{2,3},{3,2},{4,5},{5,4},{6,7},{7,6},{8,9},{9,8},{10,11... | collective-permute-start | bytes 393224 | tf_op jit(solution)/shard_map/ppermute | solution.py:475
  94.0 38.9 %collective-permute-start.26 = (bf16[128,2048]{1,0:T(8,128)(2,1)S(1)}, bf16[128,2048]{1,0:T(8,128)(2,1)}, u32[]{:S(2)}, u32[]{:S(2)}) collective-permute-start(bf16[128,2048]{1,0:T(8,128)(2,1)S(1)} %collective-permute-done.19.refs_0_.refs_4_), channel_id=1, source_target_pairs={{0,8},{2,10},{4,12},{6,14},{8,24},{10,26},{12,28},{14,30},{16,0},{... | collective-permute-start | bytes 1572872 | tf_op jit(solution)/shard_map/ppermute | solution.py:316
  100.2 11.9 %collective-permute-start.21 = (bf16[1,2,128,256]{3,2,1,0:T(8,128)(2,1)S(1)}, bf16[1,2,128,256]{3,2,1,0:T(8,128)(2,1)}, u32[]{:S(2)}, u32[]{:S(2)}) collective-permute-start(bf16[1,2,128,256]{3,2,1,0:T(8,128)(2,1)S(1)} %project_block.14), channel_id=1, source_target_pairs={{0,1},{1,0},{2,3},{3,2},{4,5},{5,4},{6,7},{7,6},{8,9},{9,8},{10,11... | collective-permute-start | bytes 393224 | tf_op jit(solution)/shard_map/ppermute | solution.py:475
  105.2 32.0 %collective-permute-start.25 = (bf16[128,2048]{1,0:T(8,128)(2,1)S(1)}, bf16[128,2048]{1,0:T(8,128)(2,1)}, u32[]{:S(2)}, u32[]{:S(2)}) collective-permute-start(bf16[128,2048]{1,0:T(8,128)(2,1)S(1)} %collective-permute-done.20.refs_1_.refs_5_), channel_id=1, source_target_pairs={{0,8},{2,10},{4,12},{6,14},{8,24},{10,26},{12,28},{14,30},{16,0},{... | collective-permute-start | bytes 1572872 | tf_op jit(solution)/shard_map/ppermute | solution.py:316
  126.3 18.0 %collective-permute-start.22 = (bf16[3,2,128,256]{3,2,1,0:T(8,128)(2,1)}, bf16[3,2,128,256]{3,2,1,0:T(8,128)(2,1)}, u32[]{:S(2)}, u32[]{:S(2)}) collective-permute-start(bf16[3,2,128,256]{3,2,1,0:T(8,128)(2,1)} %project_block.16), channel_id=1, source_target_pairs={{0,1},{1,0},{2,3},{3,2},{4,5},{5,4},{6,7},{7,6},{8,9},{9,8},{10,11... | collective-permute-start | bytes 1179656 | tf_op jit(solution)/shard_map/ppermute | solution.py:475
  126.6 17.7 %collective-permute-start.24 = (bf16[1,2,128,256]{3,2,1,0:T(8,128)(2,1)}, bf16[1,2,128,256]{3,2,1,0:T(8,128)(2,1)}, u32[]{:S(2)}, u32[]{:S(2)}) collective-permute-start(bf16[1,2,128,256]{3,2,1,0:T(8,128)(2,1)} %project_block.13), channel_id=1, source_target_pairs={{0,1},{1,0},{2,3},{3,2},{4,5},{5,4},{6,7},{7,6},{8,9},{9,8},{10,11... | collective-permute-start | bytes 393224 | tf_op jit(solution)/shard_map/ppermute | solution.py:475
  140.6 7.1 %collective-permute-start.28 = (bf16[1,4,128,256]{3,2,1,0:T(8,128)(2,1)S(1)}, bf16[1,4,128,256]{3,2,1,0:T(8,128)(2,1)S(1)}, u32[]{:S(2)}, u32[]{:S(2)}) collective-permute-start(bf16[1,4,128,256]{3,2,1,0:T(8,128)(2,1)S(1)} %project_block.20), channel_id=1, source_target_pairs={{0,1},{1,0},{2,3},{3,2},{4,5},{5,4},{6,7},{7,6},{8,9},{9,8},{10,11... | collective-permute-start | bytes 786440 | tf_op jit(solution)/shard_map/ppermute | solution.py:523
  147.8 8.6 %collective-permute-start.29 = (bf16[4,128,256]{2,1,0:T(8,128)(2,1)S(1)}, bf16[4,128,256]{2,1,0:T(8,128)(2,1)S(1)}, u32[]{:S(2)}, u32[]{:S(2)}) collective-permute-start(bf16[4,128,256]{2,1,0:T(8,128)(2,1)S(1)} %get-tuple-element.94), channel_id=1, source_target_pairs={{0,16},{1,8},{2,18},{3,10},{4,20},{5,12},{6,22},{7,14},{8,0},{9,24... | collective-permute-start | bytes 786440 | tf_op jit(solution)/shard_map/ppermute | solution.py:494
  148.4 11.5 %collective-permute-start.31 = (bf16[4,128,256]{2,1,0:T(8,128)(2,1)S(1)}, bf16[4,128,256]{2,1,0:T(8,128)(2,1)S(1)}, u32[]{:S(2)}, u32[]{:S(2)}) collective-permute-start(bf16[4,128,256]{2,1,0:T(8,128)(2,1)S(1)} %get-tuple-element.93), channel_id=1, source_target_pairs={{0,8},{1,16},{2,10},{3,18},{4,12},{5,20},{6,14},{7,22},{8,24},{9,0... | collective-permute-start | bytes 786440 | tf_op jit(solution)/shard_map/ppermute | solution.py:494
  149.7 21.0 %collective-permute-start.27 = (bf16[4,128,256]{2,1,0:T(8,128)(2,1)S(1)}, bf16[4,128,256]{2,1,0:T(8,128)(2,1)S(1)}, u32[]{:S(2)}, u32[]{:S(2)}) collective-permute-start(bf16[4,128,256]{2,1,0:T(8,128)(2,1)S(1)} %get-tuple-element.96), channel_id=1, source_target_pairs={{0,0},{1,24},{2,2},{3,26},{4,4},{5,28},{6,6},{7,30},{8,8},{9,16},{... | collective-permute-start | bytes 786440 | tf_op jit(solution)/shard_map/ppermute | solution.py:494
  154.3 20.4 %collective-permute-start.30 = (bf16[4,128,256]{2,1,0:T(8,128)(2,1)S(1)}, bf16[4,128,256]{2,1,0:T(8,128)(2,1)S(1)}, u32[]{:S(2)}, u32[]{:S(2)}) collective-permute-start(bf16[4,128,256]{2,1,0:T(8,128)(2,1)S(1)} %get-tuple-element.95), channel_id=1, source_target_pairs={{0,24},{1,0},{2,26},{3,2},{4,28},{5,4},{6,30},{7,6},{8,16},{9,8},{... | collective-permute-start | bytes 786440 | tf_op jit(solution)/shard_map/ppermute | solution.py:494
  (18 other events, 75.9 us)
Sparse Core Ops, SparseCore 0:
  8.9 111.8 all-gather.2
